TPU v7x, 32 devices: a whole 2x2x4 slice. The times are simulated.
32 devices in a mesh: tok: 8 (over z, x), head: 4 (over y, core).
Axes of the slice: x: 2, y: 2, z: 4, core: 2. Of those that a mesh axis runs over, the one named last changes fastest.
Arguments:
- queries: bfloat16 [8192, 4096], P(('tok', 'head')), may hold values from -32 to 32
- key_states: bfloat16 [8192, 512], P(('tok', 'head')), may hold values from -10 to 10
- value_states: bfloat16 [8192, 512], P(('tok', 'head')), may hold values from -6 to 6
- out_grad: bfloat16 [8192, 4096], P(('tok', 'head')), may hold values from -15 to 15
- sink_logits: float32 [64], P('head'), may hold values from 0 to 5
- branch_start: int32 [16], replicated, may hold values from 0 to 8064, as said below
- branch_len: int32 [16], replicated, may hold values from 128 to 384, as said below
- parent_list: int32 [16, 2], replicated, may hold values from -1 to 256, as said below
Outputs:
- attn_out: bfloat16 [8192, 4096], P(('tok', 'head'))
- query_grad: bfloat16 [8192, 4096], P(('tok', 'head'))
- key_grad: bfloat16 [8192, 512], P(('tok', 'head'))
- value_grad: bfloat16 [8192, 512], P(('tok', 'head'))
- sink_grad: float32 [64], P('head')
Inputs may be any that keep to these rules, and one draw needn't show every extreme that they name: `branch_start`: branch b lies within the tokens of index b // 2 of tok. The branches of one index follow one another in order, begin at multiples of 128 and do not intersect; tokens between them belong to no branch. `branch_len`: A multiple of 128. `parent_list`: row b is (parent branch, tail offset). The branches of index 0 of tok have parent -1 and offset 0; the parent of a branch on index d lies on index d - s for some s from 1 to min(3, d), and each s from 1 to 3 occurs. Branches 2m and 2m + 1 are siblings with equal rows. The offset is a multiple of 128 and the 128 tokens of the parent that begin there lie inside the parent.
All inputs are finite; a program needn't handle non-finite values.
Results may differ from a plain program's by a relative error of at most 0.02.
Values may be sent and summed in bfloat16 or wider, within the bound.
No kernel may reach another device: no remote copies, remote signals or barrier semaphores. Data moves between devices by JAX's collectives and lax.ppermute only.
A program may use at most 64 MiB of HBM per device.

v0:
```python
import functools

import jax
import jax.numpy as jnp
from jax import lax
from jax.experimental import pallas as pl
from jax.experimental.pallas import tpu as pltpu
from jax.sharding import PartitionSpec as P

HEAD_DIM = 64
KV_HEADS = 8
GROUP = 8
WINDOW = 128
HALF = WINDOW // 2
LAG = 3
BR_DEV = 2
PAIRS = KV_HEADS // 2
FACTOR = 0.125
LOW = -1e30
EXTRA = 16
BF16 = jnp.bfloat16
F32 = jnp.float32

SMEM = pl.BlockSpec(memory_space=pltpu.SMEM)
VMEM = pl.BlockSpec(memory_space=pltpu.VMEM)
HBM = pl.BlockSpec(memory_space=pltpu.HBM)
PARAMS = pltpu.CompilerParams(vmem_limit_bytes=24 * 1024 * 1024)


def shift(value, axis, steps):
    count = lax.axis_size(axis)
    leading, last = (max(0, -steps), min(count, count - steps))
    return lax.ppermute(value, axis, [(source, source + steps) for source in range(leading, last)])


def ring(value, axis, steps):
    count = lax.axis_size(axis)
    return lax.ppermute(value, axis, [(source, (source + steps) % count) for source in range(count)])


def row_split(row, dims):
    high = row.astype(BF16).astype(F32)
    middle = (row - high).astype(BF16).astype(F32)
    low = row - high - middle
    place = lax.broadcasted_iota(jnp.int32, dims, 0)
    rest = jnp.where(place == 2, low, 0.0)
    return jnp.where(place == 0, high, jnp.where(place == 1, middle, rest)).astype(BF16)


def row_join(rows):
    rows = rows.astype(F32)
    return rows[0:1] + rows[1:2] + rows[2:3]


def child_tail(table, tok, distance, tok_count, blocks):
    branches = tok_count * BR_DEV
    child = jnp.minimum(tok + distance, tok_count - 1) * BR_DEV
    parent = table[2 * branches + child]
    safe = jnp.maximum(parent, 0)
    valid = (tok + distance < tok_count) & (parent >= 0) & (safe // BR_DEV == tok)
    place = (table[safe] + table[3 * branches + child]) // WINDOW - tok * blocks
    return valid, jnp.where(valid, place, 0)


def block_state(table, tok, tok_count, block):
    branches = tok_count * BR_DEV
    position = block * WINDOW
    alive, opening = jnp.bool_(False), jnp.bool_(False)
    for branch in range(BR_DEV):
        start = table[tok * BR_DEV + branch]
        length = table[branches + tok * BR_DEV + branch]
        alive = alive | ((start <= position) & (position < start + length))
        opening = opening | (start == position)
    has_tail = table[2 * branches + tok * BR_DEV] >= 0
    return alive, opening, jnp.logical_not(opening) | has_tail


def take(ref, slot, width):
    if width % 128 == 0:
        return ref[:, pl.ds(pl.multiple_of(slot * width, width), width)]
    value = ref[:, :width]
    for other in range(1, ref.shape[1] // width):
        value = jnp.where(slot == other, ref[:, other * width : (other + 1) * width], value)
    return value


def pack_kernel(sink_hbm, key_hbm, value_hbm, *refs):
    *slot_refs, halo_ref, sinks, keys, values, sems = refs
    copies = [
        pltpu.make_async_copy(source, target, sems.at[place])
        for place, (source, target) in enumerate(
            ((sink_hbm, sinks), (key_hbm, keys), (value_hbm, values))
        )
    ]
    for copy in copies:
        copy.start()
    for copy in copies:
        copy.wait()
    slots, rows = len(slot_refs), keys.shape[0]
    head = lax.axis_index("head")
    width = KV_HEADS * HEAD_DIM // slots
    lane = lax.broadcasted_iota(jnp.int32, (1, 2 * width), 1)
    sink_row = jnp.zeros((1, 2 * width), F32)
    for place in range(sinks.shape[0]):
        sink_row = jnp.where(lane == place, sinks[place], sink_row)
    extra = row_split(sink_row, (EXTRA, 2 * width))
    for step, slot_ref in enumerate(slot_refs):
        slot = lax.rem(head + step, slots)
        slot_ref[:rows] = jnp.concatenate(
            [take(keys, slot, width), take(values, slot, width)], axis=1
        )
        slot_ref[rows:] = extra
    for pair in range(PAIRS):
        lanes = slice(pair * 128, (pair + 1) * 128)
        last = slice(rows - WINDOW, rows)
        halo_ref[pair] = jnp.concatenate([keys[last, lanes], values[last, lanes]], axis=1)


def choose_kernel(tok_count, blocks, table, *refs):
    slots = len(refs) - LAG - 1
    slot_refs, out_refs, sink_ref = refs[:slots], refs[slots:-1], refs[-1]
    tok, head = lax.axis_index("tok"), lax.axis_index("head")
    rows = slot_refs[0].shape[0] - EXTRA
    blocks_here = rows // WINDOW
    heads = sink_ref.shape[0] // slots
    for distance, out_ref in zip(range(LAG, 0, -1), out_refs):
        _, place = child_tail(table, tok, distance, tok_count, blocks)
        begin = pl.multiple_of(place % blocks_here * WINDOW, WINDOW)
        wanted = lax.rem(head - place // blocks_here + slots, slots)
        for step, slot_ref in enumerate(slot_refs):

            @pl.when(wanted == step)
            def _(out_ref=out_ref, slot_ref=slot_ref, begin=begin):
                out_ref[...] = slot_ref[pl.ds(begin, WINDOW), :]

    for step, slot_ref in enumerate(slot_refs):
        source = lax.rem(head - step + slots, slots)
        sink_row = row_join(slot_ref[rows:, :])[:, :128]
        turned = jnp.broadcast_to(sink_row, (128, 128)).T
        sink_ref[pl.ds(pl.multiple_of(source * heads, heads), heads), :] = turned[:heads]


def arrive_kernel(tok_count, table, *refs):
    tok = lax.axis_index("tok")
    *in_refs, out_ref = refs
    parent = table[2 * tok_count * BR_DEV + tok * BR_DEV]
    mine = jnp.where(parent >= 0, tok - jnp.maximum(parent, 0) // BR_DEV, 1)
    for distance, in_ref in zip(range(LAG, 0, -1), in_refs):

        @pl.when(mine == distance)
        def _(in_ref=in_ref):
            out_ref[...] = in_ref[...]


def own_pair(turn_of, offset):
    return lax.rem(lax.axis_index("head") + turn_of + offset, PAIRS)


def attend_kernel(
    tok_count,
    blocks_here,
    slots,
    steps,
    offset,
    joins,
    table,
    sink_ref,
    q_ref,
    g_ref,
    k_ref,
    v_ref,
    halo_ref,
    *refs,
):
    tail_refs, refs = refs[: len(steps)], refs[len(steps) + joins :]
    o_ref, dq_ref, dk_ref, dv_ref, dhalo_ref = refs[:5]
    dtail_refs, refs = refs[5 : 5 + len(steps)], refs[5 + len(steps) :]
    tails, tail_sum, sink_rows, prob2, slope2 = refs
    per_slot = KV_HEADS // slots
    turn_of, block = pl.program_id(0), pl.program_id(1)
    pair = turn_of if offset is None else own_pair(turn_of, offset)
    tok, head = lax.axis_index("tok"), lax.axis_index("head")
    number = (tok * lax.axis_size("head") + head) * blocks_here + block
    alive, opening, prev_ok = block_state(table, tok, tok_count, number)
    here = pl.ds(pl.multiple_of(block * WINDOW, WINDOW), WINDOW)
    before = pl.ds(pl.multiple_of(jnp.maximum(block - 1, 0) * WINDOW, WINDOW), WINDOW)
    first = block == 0

    @pl.when(first & (turn_of == 0))
    def _():
        for step, tail_ref in zip(steps, tail_refs):
            tails[lax.rem(head - step + slots, slots)] = tail_ref[...]

    @pl.when(first)
    def _():
        tail_sum[...] = jnp.zeros_like(tail_sum)
        dhalo_ref[...] = jnp.zeros_like(dhalo_ref)
        sink_rows[...] = jnp.zeros_like(sink_rows)

    @pl.when(jnp.logical_not(alive))
    def _():
        o_ref[...] = jnp.zeros_like(o_ref)
        dq_ref[...] = jnp.zeros_like(dq_ref)
        dk_ref[here, :] = jnp.zeros((WINDOW, 128), F32)
        dv_ref[here, :] = jnp.zeros((WINDOW, 128), F32)

    @pl.when(alive)
    def _():
        halo = halo_ref[...] if len(halo_ref.shape) == 2 else halo_ref[0]
        if per_slot == 2:
            tail = tails[pair]
            tail_k, tail_v = tail[:, :128], tail[:, 128:]
        else:
            tail_a, tail_b = tails[2 * pair], tails[2 * pair + 1]
            tail_k = jnp.concatenate([tail_a[:, :64], tail_b[:, :64]], axis=1)
            tail_v = jnp.concatenate([tail_a[:, 64:], tail_b[:, 64:]], axis=1)
        near_k = jnp.where(first, halo[:, :128], k_ref[before, :])
        near_v = jnp.where(first, halo[:, 128:], v_ref[before, :])
        prev_k = jnp.where(opening, tail_k, near_k)
        prev_v = jnp.where(opening, tail_v, near_v)
        own_k, own_v = k_ref[here, :], v_ref[here, :]

        def halves(own, prev):
            return (
                jnp.concatenate([own[:HALF], prev[:HALF], prev[HALF:]], axis=0),
                jnp.concatenate([own[HALF:], prev[HALF:], own[:HALF]], axis=0),
            )

        left = lax.broadcasted_iota(jnp.int32, (1, 128), 1) < HALF
        low16 = left.astype(F32).astype(BF16)
        high16 = BF16(1) - low16

        def padded(seen):
            swapped = jnp.concatenate([seen[:, 64:], seen[:, :64]], axis=1)
            return (
                jnp.concatenate([seen * low16, swapped * high16], axis=0),
                jnp.concatenate([swapped * low16, seen * high16], axis=0),
            )

        seen_k = halves(own_k * BF16(FACTOR), prev_k * BF16(FACTOR))
        seen_v = halves(own_v, prev_v)
        padded_k = tuple(padded(value) for value in seen_k)
        padded_v = tuple(padded(value) for value in seen_v)
        turned_k = tuple(value.T for value in seen_k)
        turned_v = tuple(value.T for value in seen_v)
        bias = jnp.where(prev_ok, 0.0, LOW)
        key_place = lax.broadcasted_iota(jnp.int32, (HALF, 4 * HALF), 0)
        query_place = lax.broadcasted_iota(jnp.int32, (HALF, 4 * HALF), 1) & (HALF - 1)
        own = key_place <= query_place
        own16 = own.astype(F32).astype(BF16)
        turn = (((1,), (1,)), ((), ()))
        items = [(unit, half) for unit in range(2) for half in range(2)]
        seen = 3 * HALF

        def wide(index):
            return slice(index * 256, (index + 1) * 256)

        def feats(index):
            unit = items[index][0]
            return slice(unit * HEAD_DIM, (unit + 1) * HEAD_DIM)

        def corners(unit, half):
            rows = slice(half * HALF, (half + 1) * HALF)
            return [
                (rows, slice(unit * 512 + at * 128, unit * 512 + (at + 1) * 128)) for at in range(4)
            ]

        def stacked(ref, unit, half):
            return jnp.concatenate([ref[corner] for corner in corners(unit, half)], axis=0)

        def products(index):
            unit, half = items[index]
            score, dp = (
                lax.dot_general(
                    padded[half][unit],
                    stacked(ref, unit, half),
                    turn,
                    preferred_element_type=F32,
                )
                for padded, ref in ((padded_k, q_ref), (padded_v, g_ref))
            )
            parts = []
            for base in (0, seen):
                near, far = slice(base, base + HALF), slice(base + HALF, base + 2 * HALF)
                rest = slice(base + 2 * HALF, base + 3 * HALF)
                edge = jnp.where(own, score[near], score[far] + bias)
                whole = score[rest] + bias if half == 0 else score[rest]
                parts.append((edge, whole, jnp.where(own, dp[near], dp[far]), dp[rest]))
            return parts

        def weigh(index, odd, edge, whole, dp_edge, dp_whole):
            unit, half = items[index]
            base = odd * seen
            row = unit * GROUP + odd
            sink = jnp.concatenate(
                [
                    jnp.where(left, sink_ref[at : at + 1], sink_ref[at + 2 : at + 3])
                    for at in (row, row + 4)
                ],
                axis=1,
            )
            peak = jnp.max(jnp.maximum(edge, whole), axis=0, keepdims=True)
            peak = jnp.maximum(peak, sink)
            edge, whole = jnp.exp(edge - peak), jnp.exp(whole - peak)
            sink_weight = jnp.exp(sink - peak)
            inverse = 1.0 / (jnp.sum(edge + whole, axis=0, keepdims=True) + sink_weight)
            edge, whole = edge * inverse, whole * inverse
            term_edge, term_whole = edge * dp_edge, whole * dp_whole
            delta = jnp.sum(term_edge + term_whole, axis=0, keepdims=True)
            for target, at_edge, at_whole in (
                (prob2, edge, whole),
                (slope2, term_edge - edge * delta, term_whole - whole * delta),
            ):
                edge16 = at_edge.astype(BF16)
                edge_own = edge16 * own16
                target[base : base + HALF, wide(index)] = edge_own
                target[base + HALF : base + 2 * HALF, wide(index)] = edge16 - edge_own
                target[base + 2 * HALF : base + seen, wide(index)] = at_whole.astype(BF16)
            sink_term = sink_weight * inverse * delta
            for at, lanes in ((row, slice(0, 128)), (row + 4, slice(128, 256))):
                part = sink_term[:, lanes]
                sink_rows[at : at + 1] += jnp.where(left, part, 0.0)
                sink_rows[at + 2 : at + 3] += jnp.where(left, 0.0, part)

        def finish(index):
            unit, half = items[index]
            for source, across, out_ref in ((prob2, turned_v, o_ref), (slope2, turned_k, dq_ref)):
                out_t = [
                    jnp.dot(
                        across[half][feats(index)],
                        source[base : base + seen, wide(index)],
                        preferred_element_type=F32,
                    ).astype(BF16)
                    for base in (0, seen)
                ]
                out = jnp.concatenate(out_t, axis=0).T
                for at, corner in enumerate(corners(unit, half)):
                    out_ref[corner] = out[at * HALF : (at + 1) * HALF]

        def reduce(index):
            unit, half = items[index]
            parts = []
            for weights, ref in ((slope2, q_ref), (prob2, g_ref)):
                part = jnp.dot(
                    weights[:, wide(index)], stacked(ref, unit, half), preferred_element_type=F32
                )
                parts.append(jnp.where(left, part[:seen], part[seen:]))
            return parts

        def join(first_half, second_half):
            total = jnp.concatenate(
                [
                    first_half[:HALF] + second_half[2 * HALF :],
                    second_half[:HALF],
                    first_half[HALF : 2 * HALF],
                    first_half[2 * HALF :] + second_half[HALF : 2 * HALF],
                ],
                axis=0,
            )
            return total + pltpu.roll(total, HEAD_DIM, 1)

        ahead, parts = products(0), []
        for index in range(len(items)):
            now = ahead
            weigh(index, 0, *now[0])
            if index + 1 < len(items):
                ahead = products(index + 1)
            weigh(index, 1, *now[1])
            if index >= 1:
                finish(index - 1)
            parts.append(reduce(index))
        finish(len(items) - 1)
        grads = [
            [join(parts[2 * unit][place], parts[2 * unit + 1][place]) for place in range(2)]
            for unit in range(2)
        ]
        dk = jnp.where(left, grads[0][0], grads[1][0]) * FACTOR
        dv = jnp.where(left, grads[0][1], grads[1][1])
        dk_ref[here, :] = dk[:WINDOW]
        dv_ref[here, :] = dv[:WINDOW]

        @pl.when(opening & prev_ok)
        def _():
            tail_sum[:, :128] += dk[WINDOW:]
            tail_sum[:, 128:] += dv[WINDOW:]

        @pl.when(jnp.logical_not(opening) & first)
        def _():
            dhalo_ref[0, :, :128] = dk[WINDOW:].astype(BF16)
            dhalo_ref[0, :, 128:] = dv[WINDOW:].astype(BF16)

        @pl.when(jnp.logical_not(opening) & jnp.logical_not(first))
        def _():
            dk_ref[before, :] += dk[WINDOW:]
            dv_ref[before, :] += dv[WINDOW:]

    @pl.when(block == blocks_here - 1)
    def _():
        width = dtail_refs[0].shape[1]
        heads = per_slot * GROUP
        total = tail_sum[...].astype(BF16)
        for part in range(2 // per_slot):
            feats = slice(part * width // 2, (part + 1) * width // 2)
            tail = jnp.concatenate([total[:, :128][:, feats], total[:, 128:][:, feats]], axis=1)
            rows = sink_rows[part * heads : (part + 1) * heads]
            rows = jnp.concatenate([rows, jnp.zeros((128 - heads, WINDOW), F32)], axis=0)
            sink_row = jnp.sum(rows.T, axis=0, keepdims=True)
            if width > 128:
                sink_row = jnp.concatenate([sink_row, jnp.zeros((1, width - 128), F32)], axis=1)
            extra = row_split(sink_row, (EXTRA, width))
            wanted = lax.rem(pair * (2 // per_slot) + part - head + slots, slots)
            for step, dtail_ref in zip(steps, dtail_refs):

                @pl.when(wanted == step)
                def _(dtail_ref=dtail_ref, tail=tail, extra=extra):
                    dtail_ref[:WINDOW] = tail
                    dtail_ref[WINDOW:] = extra


def gather_kernel(*refs):
    *in_refs, out_ref = refs
    total, sink_row = 0.0, 0.0
    for in_ref in in_refs:
        total = total + in_ref[:WINDOW].astype(F32)
        sink_row = sink_row + row_join(in_ref[WINDOW:])
    out_ref[:WINDOW] = total.astype(BF16)
    out_ref[WINDOW:] = row_split(sink_row, (EXTRA, out_ref.shape[1]))


def land_kernel(tok_count, blocks, table, here_ref, *refs):
    tok, head = lax.axis_index("tok"), lax.axis_index("head")
    in_refs, out_refs, sink_ref = refs[:LAG], refs[LAG:-1], refs[-1]
    slots = len(out_refs)
    blocks_here = blocks // slots
    for out_ref in out_refs:
        out_ref[...] = jnp.zeros_like(out_ref)
    sink_row = row_join(here_ref[WINDOW:])
    for distance, in_ref in enumerate(in_refs, 1):
        valid, place = child_tail(table, tok, distance, tok_count, blocks)
        sink_row = sink_row + row_join(in_ref[WINDOW:])
        wanted = lax.rem(place // blocks_here - head + slots, slots)
        here = pl.ds(pl.multiple_of(place % blocks_here * WINDOW, WINDOW), WINDOW)
        for step, out_ref in enumerate(out_refs):

            @pl.when(valid & (wanted == step))
            def _(out_ref=out_ref, in_ref=in_ref, here=here):
                total = out_ref[here, :].astype(F32) + in_ref[:WINDOW].astype(F32)
                out_ref[here, :] = total.astype(BF16)

    sink_ref[...] = jnp.broadcast_to(sink_row[:, :128], sink_ref.shape)


def total_kernel(dk_ref, dv_ref, halo_ref, sink_ref, far_ref, *refs):
    *tail_refs, key_ref, value_ref, sink_grad, tails = refs
    slots, rows = len(tail_refs), dk_ref.shape[0]
    width = tails.shape[2] // 2
    head = lax.axis_index("head")
    for step, tail_ref in enumerate(tail_refs):
        tails[lax.rem(head - step + slots, slots)] = tail_ref[...]
    halo_k = jnp.concatenate([halo_ref[pair][:, :128] for pair in range(PAIRS)], axis=1)
    halo_v = jnp.concatenate([halo_ref[pair][:, 128:] for pair in range(PAIRS)], axis=1)
    for in_ref, halo, at, out_ref in (
        (dk_ref, halo_k, 0, key_ref),
        (dv_ref, halo_v, width, value_ref),
    ):
        for begin in range(0, rows, WINDOW):
            here = slice(begin, begin + WINDOW)
            parts = [tails[slot, here, at : at + width] for slot in range(slots)]
            total = in_ref[here, :] + jnp.concatenate(parts, axis=1).astype(F32)
            if begin == rows - WINDOW:
                total = total + halo.astype(F32)
            out_ref[here, :] = total.astype(BF16)
    sink_row = -(sink_ref[0:1] + far_ref[0:1])
    for place in range(sink_grad.shape[0]):
        sink_grad[place] = sink_row[0, place]


def swap(values, axis):
    return [values[0]] + [ring(values[step], axis, step) for step in range(1, len(values))]


def local(
    queries, key_states, value_states, out_grad, sink_logits, branch_start, branch_len, parent_list
):
    tok_count, head_count = lax.axis_size("tok"), lax.axis_size("head")
    rows = queries.shape[0]
    blocks_here = rows // WINDOW
    blocks = blocks_here * head_count
    per_slot = KV_HEADS // head_count
    width = 2 * per_slot * HEAD_DIM

    def shape(dims, kind=BF16):
        return jax.ShapeDtypeStruct(dims, kind)

    queries, out_grad, key_states, value_states, sink_logits = (
        pltpu.with_memory_space_constraint(value, pltpu.HBM)
        for value in (queries, out_grad, key_states, value_states, sink_logits)
    )
    table = jnp.concatenate([branch_start, branch_len, parent_list[:, 0], parent_list[:, 1]])
    *slots, halo_out = pl.pallas_call(
        pack_kernel,
        out_shape=(shape((rows + EXTRA, width)),) * head_count + (shape((PAIRS, WINDOW, 256)),),
        in_specs=[HBM] * 3,
        out_specs=(VMEM,) * (head_count + 1),
        scratch_shapes=[
            pltpu.SMEM(sink_logits.shape, F32),
            pltpu.VMEM(key_states.shape, BF16),
            pltpu.VMEM(key_states.shape, BF16),
            pltpu.SemaphoreType.DMA((3,)),
        ],
        compiler_params=PARAMS,
        name="pack",
    )(sink_logits, key_states, value_states)
    spread = swap(slots, "head")
    *chosen, sinks = pl.pallas_call(
        functools.partial(choose_kernel, tok_count, blocks),
        out_shape=(shape((WINDOW, width)),) * LAG + (shape((KV_HEADS * GROUP, 128), F32),),
        in_specs=[SMEM] + [VMEM] * head_count,
        out_specs=(VMEM,) * (LAG + 1),
        compiler_params=PARAMS,
        name="choose",
    )(table, *spread)
    arrived = [ring(chosen[LAG - s], "tok", s) for s in range(LAG, 0, -1)]
    quarter = pl.pallas_call(
        functools.partial(arrive_kernel, tok_count),
        out_shape=shape((WINDOW, width)),
        in_specs=[SMEM] + [VMEM] * LAG,
        out_specs=VMEM,
        compiler_params=PARAMS,
        name="arrive",
    )(table, *arrived)
    tails = swap([quarter] * head_count, "head")
    halo_out, _ = lax.optimization_barrier((halo_out, quarter))
    halo = shift(halo_out, "head", 1)

    def attend(steps, pairs, offset, halo, joined):
        def at(index):
            def place(p, b):
                return index(p if offset is None else own_pair(p, offset), b)

            return place

        big = pl.BlockSpec((WINDOW, 1024), at(lambda p, b: (b, p)))
        small = pl.BlockSpec((rows, 128), at(lambda p, b: (0, p)))
        near = pl.BlockSpec((1, WINDOW, 256), at(lambda p, b: (p, 0, 0)))
        last = pl.BlockSpec((WINDOW, width), lambda p, b: (blocks_here - 1, 0))
        whole = pl.BlockSpec((WINDOW, width), lambda p, b: (0, 0))
        whole_back = pl.BlockSpec((WINDOW + EXTRA, width), lambda p, b: (0, 0))
        inputs = (
            (table, SMEM),
            (sinks, pl.BlockSpec((2 * GROUP, 128), at(lambda p, b: (p, 0)))),
            (queries, big),
            (out_grad, big),
            (key_states, small),
            (value_states, small),
            (halo, near if halo.ndim == 3 else last),
            *((tails[step], whole) for step in steps),
            *((value, pl.BlockSpec(memory_space=pl.ANY)) for value in joined),
        )
        base = len(inputs) - len(joined)
        return pl.pallas_call(
            functools.partial(
                attend_kernel, tok_count, blocks_here, head_count, steps, offset, len(joined)
            ),
            grid=(pairs, blocks_here),
            out_shape=(
                shape(queries.shape),
                shape(queries.shape),
                shape(key_states.shape, F32),
                shape(key_states.shape, F32),
                shape((PAIRS, WINDOW, 256)),
            )
            + (shape((WINDOW + EXTRA, width)),) * len(steps),
            in_specs=[spec for _, spec in inputs],
            out_specs=(big, big, small, small, near) + (whole_back,) * len(steps),
            scratch_shapes=[
                pltpu.VMEM((head_count, WINDOW, width), BF16),
                pltpu.VMEM((WINDOW, 256), F32),
                pltpu.VMEM((2 * GROUP, WINDOW), F32),
                pltpu.VMEM((6 * HALF, 1024), BF16),
                pltpu.VMEM((6 * HALF, 1024), BF16),
            ],
            input_output_aliases={base + place: place for place in range(len(joined))},
            compiler_params=PARAMS,
            name="attend",
        )(*(value for value, _ in inputs))

    if per_slot == 2:
        *joined, own_tail = attend((0,), 1, 0, spread[1], ())
        *results, tail_1, tail_2, tail_3 = attend((1, 2, 3), PAIRS - 1, 1, halo, joined)
        dtail = [own_tail, tail_1, tail_2, tail_3]
    else:
        results = attend(tuple(range(head_count)), PAIRS, None, halo, ())
        results, dtail = results[:5], list(results[5:])
    attended, query_grad, dk, dv, dhalo = results
    parts = swap(dtail, "head")
    quarter_grad = pl.pallas_call(
        gather_kernel,
        out_shape=shape((WINDOW + EXTRA, width)),
        in_specs=[VMEM] * head_count,
        out_specs=VMEM,
        compiler_params=PARAMS,
        name="gather",
    )(*parts)
    returned = [ring(quarter_grad, "tok", -s) for s in range(LAG, 0, -1)][::-1]
    halo_back = shift(dhalo, "head", -1)
    *landed, sink_near = pl.pallas_call(
        functools.partial(land_kernel, tok_count, blocks),
        out_shape=(shape((rows, width)),) * head_count + (shape((8, 128), F32),),
        in_specs=[SMEM] + [VMEM] * (LAG + 1),
        out_specs=(VMEM,) * (head_count + 1),
        compiler_params=PARAMS,
        name="land",
    )(table, quarter_grad, *returned)
    tails_back = swap(landed, "head")
    span = LAG + 1
    while 2 * span < tok_count:
        sink_near = sink_near + ring(sink_near, "tok", -span)
        span *= 2
    sink_far = ring(sink_near, "tok", -span)
    key_grad, value_grad, sink_grad = pl.pallas_call(
        total_kernel,
        out_shape=(
            shape(key_states.shape),
            shape(value_states.shape),
            shape(sink_logits.shape, F32),
        ),
        in_specs=[VMEM] * (5 + head_count),
        out_specs=(VMEM, VMEM, SMEM),
        scratch_shapes=[pltpu.VMEM((head_count, rows, width), BF16)],
        compiler_params=PARAMS,
        name="total",
    )(dk, dv, halo_back, sink_near, sink_far, *tails_back)
    return attended, query_grad, key_grad, value_grad, sink_grad


def solution(mesh):
    rows = P(("tok", "head"), None)
    return jax.shard_map(
        local,
        mesh=mesh,
        in_specs=(rows, rows, rows, rows, P("head"), P(), P(), P()),
        out_specs=(rows, rows, rows, rows, P("head")),
        check_vma=False,
    )
```

profile of v0, /device:TPU:3, one launch (start us, length us, event | category | flops | bytes accessed | tf_op | source)
XLA Modules:
  0.0 69.4 jit_solution(4467928097095770093)
XLA Ops:
  0.6 1.2 %pack.1 = (bf16[272,256]{1,0:T(8,128)(2,1)S(1)}, bf16[272,256]{1,0:T(8,128)(2,1)S(1)}, bf16[272,256]{1,0:T(8,128)(2,1)S(1)}, bf16[272,256]{1,0:T(8,128)(2,1)S(1)}, bf16[4,128,256]{2,1,0:T(8,128)(2,1)S(1)}) custom-call(f32[16]{0:T(128)} %sink_hbm.1, bf16[256,512]{1,0:T(8,128)(2,1)} %k_ref.3, bf16[256,512]{1,0:T(8,128)(2,1)} %v_ref.3), custom_call_target="tpu_custom_call" | custom-call | tf_op jit(solution)/shard_map/pack/pallas_call | solution.py:500
  1.8 1.9 %collective-permute-start = (bf16[272,256]{1,0:T(8,128)(2,1)S(1)}, bf16[272,256]{1,0:T(8,128)(2,1)S(1)}, u32[]{:S(2)}, u32[]{:S(2)}) collective-permute-start(bf16[272,256]{1,0:T(8,128)(2,1)S(1)} %get-tuple-element.38), channel_id=1, source_target_pairs={{0,1},{1,2},{2,3},{3,0},{4,5},{5,6},{6,7},{7,4},{8,9},{9,10},{10,1... | collective-permute-start | bytes 417800 | tf_op jit(solution)/shard_map/ppermute | solution.py:38
  5.6 0.9 %collective-permute-done.refs_1_.halo_ref = bf16[272,256]{1,0:T(8,128)(2,1)S(1)} collective-permute-done((bf16[272,256]{1,0:T(8,128)(2,1)S(1)}, bf16[272,256]{1,0:T(8,128)(2,1)S(1)}, u32[]{:S(2)}, u32[]{:S(2)}) %collective-permute-start) | collective-permute-done | bytes 139296 | tf_op jit(solution)/shard_map/ppermute | solution.py:38
  6.5 3.6 %collective-permute-done.1.refs_2_ = bf16[272,256]{1,0:T(8,128)(2,1)S(1)} collective-permute-done((bf16[272,256]{1,0:T(8,128)(2,1)S(1)}, bf16[272,256]{1,0:T(8,128)(2,1)S(1)}, u32[]{:S(2)}, u32[]{:S(2)}) %collective-permute-start.1) | collective-permute-done | bytes 139296 | tf_op jit(solution)/shard_map/ppermute | solution.py:38
  10.8 0.8 %choose.1 = (bf16[128,256]{1,0:T(8,128)(2,1)S(1)}, bf16[128,256]{1,0:T(8,128)(2,1)S(1)}, bf16[128,256]{1,0:T(8,128)(2,1)S(1)}, f32[64,128]{1,0:T(8,128)S(1)}) custom-call(s32[64]{0:T(128)S(1)} %pad_add_fusion.table, bf16[272,256]{1,0:T(8,128)(2,1)S(1)} %get-tuple-element.37.refs_0_, bf16[272,256]{1,0:T(8,128)(2,1)S(1)} %collective-permute-done.refs_1_.halo_ref, ...), custom_call_target="tpu_custom_call" | custom-call | tf_op jit(solution)/shard_map/choose/pallas_call | solution.py:515
  11.6 2.3 %collective-permute-start.3 = (bf16[128,256]{1,0:T(8,128)(2,1)S(1)}, bf16[128,256]{1,0:T(8,128)(2,1)S(1)}, u32[]{:S(2)}, u32[]{:S(2)}) collective-permute-start(bf16[128,256]{1,0:T(8,128)(2,1)S(1)} %get-tuple-element.43), channel_id=1, source_target_pairs={{0,12},{4,16},{8,20},{12,24},{16,28},{20,0},{24,4},{28,8},{1,13},{... | collective-permute-start | bytes 196616 | tf_op jit(solution)/shard_map/ppermute | solution.py:38
  13.9 1.3 %collective-permute-start.4 = (bf16[128,256]{1,0:T(8,128)(2,1)S(1)}, bf16[128,256]{1,0:T(8,128)(2,1)S(1)}, u32[]{:S(2)}, u32[]{:S(2)}) collective-permute-start(bf16[128,256]{1,0:T(8,128)(2,1)S(1)} %get-tuple-element.44), channel_id=1, source_target_pairs={{0,8},{4,12},{8,16},{12,20},{16,24},{20,28},{24,0},{28,4},{1,9},{5... | collective-permute-start | bytes 196616 | tf_op jit(solution)/shard_map/ppermute | solution.py:38
  15.2 1.2 %collective-permute-start.5 = (bf16[128,256]{1,0:T(8,128)(2,1)S(1)}, bf16[128,256]{1,0:T(8,128)(2,1)S(1)}, u32[]{:S(2)}, u32[]{:S(2)}) collective-permute-start(bf16[128,256]{1,0:T(8,128)(2,1)S(1)} %get-tuple-element.45), channel_id=1, source_target_pairs={{0,4},{4,8},{8,12},{12,16},{16,20},{20,24},{24,28},{28,0},{1,5},{5... | collective-permute-start | bytes 196616 | tf_op jit(solution)/shard_map/ppermute | solution.py:38
  16.4 1.8 %collective-permute-done.3.refs_0_ = bf16[128,256]{1,0:T(8,128)(2,1)S(1)} collective-permute-done((bf16[128,256]{1,0:T(8,128)(2,1)S(1)}, bf16[128,256]{1,0:T(8,128)(2,1)S(1)}, u32[]{:S(2)}, u32[]{:S(2)}) %collective-permute-start.3) | collective-permute-done | bytes 65568 | tf_op jit(solution)/shard_map/ppermute | solution.py:38
  18.3 1.2 %collective-permute-done.4.refs_1_ = bf16[128,256]{1,0:T(8,128)(2,1)S(1)} collective-permute-done((bf16[128,256]{1,0:T(8,128)(2,1)S(1)}, bf16[128,256]{1,0:T(8,128)(2,1)S(1)}, u32[]{:S(2)}, u32[]{:S(2)}) %collective-permute-start.4) | collective-permute-done | bytes 65568 | tf_op jit(solution)/shard_map/ppermute | solution.py:38
  20.2 2.8 %collective-permute-start.6 = (bf16[4,128,256]{2,1,0:T(8,128)(2,1)S(1)}, bf16[4,128,256]{2,1,0:T(8,128)(2,1)S(1)}, u32[]{:S(2)}, u32[]{:S(2)}) collective-permute-start(bf16[4,128,256]{2,1,0:T(8,128)(2,1)S(1)} %get-tuple-element.46), channel_id=1, source_target_pairs={{0,1},{1,2},{2,3},{4,5},{5,6},{6,7},{8,9},{9,10},{10,11},{12,13},{... | collective-permute-start | bytes 786440 | tf_op jit(solution)/shard_map/ppermute | solution.py:33
  23.3 1.5 %collective-permute-start.7 = (bf16[128,256]{1,0:T(8,128)(2,1)S(1)}, bf16[128,256]{1,0:T(8,128)(2,1)S(1)}, u32[]{:S(2)}, u32[]{:S(2)}) collective-permute-start(bf16[128,256]{1,0:T(8,128)(2,1)S(1)} %arrive.1.refs_0_), channel_id=1, source_target_pairs={{0,1},{1,2},{2,3},{3,0},{4,5},{5,6},{6,7},{7,4},{8,9},{9,10},{10,1... | collective-permute-start | bytes 196616 | tf_op jit(solution)/shard_map/ppermute | solution.py:38
  24.8 3.8 %attend.2 = (bf16[256,4096]{1,0:T(8,128)(2,1)}, bf16[256,4096]{1,0:T(8,128)(2,1)}, f32[256,512]{1,0:T(8,128)S(1)}, f32[256,512]{1,0:T(8,128)S(1)}, bf16[4,128,25...) custom-call(s32[64]{0:T(128)S(1)} %pad_add_fusion.table, f32[64,128]{1,0:T(8,128)S(1)} %get-tuple-element.41.sink_ref, ...), custom_call_target="tpu_custom_call" | custom-call | tf_op jit(solution)/shard_map/attend/pallas_call | solution.py:561
  29.0 9.9 %attend.3 = (bf16[256,4096]{1,0:T(8,128)(2,1)}, bf16[256,4096]{1,0:T(8,128)(2,1)}, f32[256,512]{1,0:T(8,128)S(1)}, f32[256,512]{1,0:T(8,128)S(1)}, bf16[4,128,25...) custom-call(s32[64]{0:T(128)S(1)} %pad_add_fusion.table, ...), custom_call_target="tpu_custom_call", output_to_operand_aliasing={{0}: (10, {}), {1}: (11, {}), {2}: (12, {}), {3}: (13, {}),... | custom-call | tf_op jit(solution)/shard_map/attend/pallas_call | solution.py:561
  38.9 5.4 %collective-permute-start.11 = (bf16[144,256]{1,0:T(8,128)(2,1)S(1)}, bf16[144,256]{1,0:T(8,128)(2,1)S(1)}, u32[]{:S(2)}, u32[]{:S(2)}) collective-permute-start(bf16[144,256]{1,0:T(8,128)(2,1)S(1)} %get-tuple-element.58), channel_id=1, source_target_pairs={{0,1},{1,2},{2,3},{3,0},{4,5},{5,6},{6,7},{7,4},{8,9},{9,10},{10,1... | collective-permute-start | bytes 221192 | tf_op jit(solution)/shard_map/ppermute | solution.py:38
  44.7 3.3 %collective-permute-start.10 = (bf16[4,128,256]{2,1,0:T(8,128)(2,1)S(1)}, bf16[4,128,256]{2,1,0:T(8,128)(2,1)S(1)}, u32[]{:S(2)}, u32[]{:S(2)}) collective-permute-start(bf16[4,128,256]{2,1,0:T(8,128)(2,1)S(1)} %get-tuple-element.56), channel_id=1, source_target_pairs={{1,0},{2,1},{3,2},{5,4},{6,5},{7,6},{9,8},{10,9},{11,10},{13,12},{... | collective-permute-start | bytes 786440 | tf_op jit(solution)/shard_map/ppermute | solution.py:33
  48.8 3.7 %collective-permute-start.16 = (bf16[144,256]{1,0:T(8,128)(2,1)S(1)}, bf16[144,256]{1,0:T(8,128)(2,1)S(1)}, u32[]{:S(2)}, u32[]{:S(2)}) collective-permute-start(bf16[144,256]{1,0:T(8,128)(2,1)S(1)} %gather.1.here_ref), channel_id=1, source_target_pairs={{0,20},{4,24},{8,28},{12,0},{16,4},{20,8},{24,12},{28,16},{1,21},{... | collective-permute-start | bytes 221192 | tf_op jit(solution)/shard_map/ppermute | solution.py:38
  52.5 1.7 %collective-permute-start.15 = (bf16[144,256]{1,0:T(8,128)(2,1)S(1)}, bf16[144,256]{1,0:T(8,128)(2,1)S(1)}, u32[]{:S(2)}, u32[]{:S(2)}) collective-permute-start(bf16[144,256]{1,0:T(8,128)(2,1)S(1)} %gather.1.here_ref), channel_id=1, source_target_pairs={{0,24},{4,28},{8,0},{12,4},{16,8},{20,12},{24,16},{28,20},{1,25},{... | collective-permute-start | bytes 221192 | tf_op jit(solution)/shard_map/ppermute | solution.py:38
  54.2 2.9 %collective-permute-done.16.refs_2_ = bf16[144,256]{1,0:T(8,128)(2,1)S(1)} collective-permute-done((bf16[144,256]{1,0:T(8,128)(2,1)S(1)}, bf16[144,256]{1,0:T(8,128)(2,1)S(1)}, u32[]{:S(2)}, u32[]{:S(2)}) %collective-permute-start.16) | collective-permute-done | bytes 73760 | tf_op jit(solution)/shard_map/ppermute | solution.py:38
  57.1 1.6 %collective-permute-done.14.refs_0_ = bf16[144,256]{1,0:T(8,128)(2,1)S(1)} collective-permute-done((bf16[144,256]{1,0:T(8,128)(2,1)S(1)}, bf16[144,256]{1,0:T(8,128)(2,1)S(1)}, u32[]{:S(2)}, u32[]{:S(2)}) %collective-permute-start.14) | collective-permute-done | bytes 73760 | tf_op jit(solution)/shard_map/ppermute | solution.py:38
  59.5 2.1 %collective-permute-start.18 = (bf16[256,256]{1,0:T(8,128)(2,1)S(1)}, bf16[256,256]{1,0:T(8,128)(2,1)S(1)}, u32[]{:S(2)}, u32[]{:S(2)}) collective-permute-start(bf16[256,256]{1,0:T(8,128)(2,1)S(1)} %get-tuple-element.63), channel_id=1, source_target_pairs={{0,1},{1,2},{2,3},{3,0},{4,5},{5,6},{6,7},{7,4},{8,9},{9,10},{10,1... | collective-permute-start | bytes 393224 | tf_op jit(solution)/shard_map/ppermute | solution.py:38
  62.2 3.2 %collective-permute-done.17.far_ref = f32[8,128]{1,0:T(8,128)S(1)} collective-permute-done((f32[8,128]{1,0:T(8,128)S(1)}, f32[8,128]{1,0:T(8,128)S(1)}, u32[]{:S(2)}, u32[]{:S(2)}) %collective-permute-start.17) | collective-permute-done | bytes 4128 | tf_op jit(solution)/shard_map/ppermute | solution.py:38
  65.4 2.4 %collective-permute-done.19.refs_2_ = bf16[256,256]{1,0:T(8,128)(2,1)S(1)} collective-permute-done((bf16[256,256]{1,0:T(8,128)(2,1)S(1)}, bf16[256,256]{1,0:T(8,128)(2,1)S(1)}, u32[]{:S(2)}, u32[]{:S(2)}) %collective-permute-start.19) | collective-permute-done | bytes 131104 | tf_op jit(solution)/shard_map/ppermute | solution.py:38
  68.5 1.0 %total.1 = (bf16[256,512]{1,0:T(8,128)(2,1)}, bf16[256,512]{1,0:T(8,128)(2,1)}, f32[16]{0:T(128)}) custom-call(f32[256,512]{1,0:T(8,128)S(1)} %get-tuple-element.54.dk_ref, f32[256,512]{1,0:T(8,128)S(1)} %get-tuple-element.55.dv_ref, bf16[4,128,256]{2,1,0:T(8,128)(2,1)S(1)} %collective-permute-done.10.halo_ref, f32[8,128]{1,0:T(8,128)S(1)} %get-tuple-element.61.sink_ref, ...), custom_call_target="tpu_custom_call" | custom-call | tf_op jit(solution)/shard_map/total/pallas_call | solution.py:621
  (28 shorter events, 7.2 us)
Async XLA Ops:
  1.8 4.7 %collective-permute-start = (bf16[272,256]{1,0:T(8,128)(2,1)S(1)}, bf16[272,256]{1,0:T(8,128)(2,1)S(1)}, u32[]{:S(2)}, u32[]{:S(2)}) collective-permute-start(bf16[272,256]{1,0:T(8,128)(2,1)S(1)} %get-tuple-element.38), channel_id=1, source_target_pairs={{0,1},{1,2},{2,3},{3,0},{4,5},{5,6},{6,7},{7,4},{8,9},{9,10},{10,1... | collective-permute-start | bytes 417800 | tf_op jit(solution)/shard_map/ppermute | solution.py:38
  3.7 6.5 %collective-permute-start.1 = (bf16[272,256]{1,0:T(8,128)(2,1)S(1)}, bf16[272,256]{1,0:T(8,128)(2,1)S(1)}, u32[]{:S(2)}, u32[]{:S(2)}) collective-permute-start(bf16[272,256]{1,0:T(8,128)(2,1)S(1)} %get-tuple-element.39), channel_id=1, source_target_pairs={{0,2},{1,3},{2,0},{3,1},{4,6},{5,7},{6,4},{7,5},{8,10},{9,11},{10,... | collective-permute-start | bytes 417800 | tf_op jit(solution)/shard_map/ppermute | solution.py:38
  3.9 6.9 %collective-permute-start.2 = (bf16[272,256]{1,0:T(8,128)(2,1)S(1)}, bf16[272,256]{1,0:T(8,128)(2,1)S(1)}, u32[]{:S(2)}, u32[]{:S(2)}) collective-permute-start(bf16[272,256]{1,0:T(8,128)(2,1)S(1)} %get-tuple-element.40), channel_id=1, source_target_pairs={{0,3},{1,0},{2,1},{3,2},{4,7},{5,4},{6,5},{7,6},{8,11},{9,8},{10,9... | collective-permute-start | bytes 417800 | tf_op jit(solution)/shard_map/ppermute | solution.py:38
  11.6 6.7 %collective-permute-start.3 = (bf16[128,256]{1,0:T(8,128)(2,1)S(1)}, bf16[128,256]{1,0:T(8,128)(2,1)S(1)}, u32[]{:S(2)}, u32[]{:S(2)}) collective-permute-start(bf16[128,256]{1,0:T(8,128)(2,1)S(1)} %get-tuple-element.43), channel_id=1, source_target_pairs={{0,12},{4,16},{8,20},{12,24},{16,28},{20,0},{24,4},{28,8},{1,13},{... | collective-permute-start | bytes 196616 | tf_op jit(solution)/shard_map/ppermute | solution.py:38
  13.9 5.5 %collective-permute-start.4 = (bf16[128,256]{1,0:T(8,128)(2,1)S(1)}, bf16[128,256]{1,0:T(8,128)(2,1)S(1)}, u32[]{:S(2)}, u32[]{:S(2)}) collective-permute-start(bf16[128,256]{1,0:T(8,128)(2,1)S(1)} %get-tuple-element.44), channel_id=1, source_target_pairs={{0,8},{4,12},{8,16},{12,20},{16,24},{20,28},{24,0},{28,4},{1,9},{5... | collective-permute-start | bytes 196616 | tf_op jit(solution)/shard_map/ppermute | solution.py:38
  15.2 4.4 %collective-permute-start.5 = (bf16[128,256]{1,0:T(8,128)(2,1)S(1)}, bf16[128,256]{1,0:T(8,128)(2,1)S(1)}, u32[]{:S(2)}, u32[]{:S(2)}) collective-permute-start(bf16[128,256]{1,0:T(8,128)(2,1)S(1)} %get-tuple-element.45), channel_id=1, source_target_pairs={{0,4},{4,8},{8,12},{12,16},{16,20},{20,24},{24,28},{28,0},{1,5},{5... | collective-permute-start | bytes 196616 | tf_op jit(solution)/shard_map/ppermute | solution.py:38
  20.2 8.8 %collective-permute-start.6 = (bf16[4,128,256]{2,1,0:T(8,128)(2,1)S(1)}, bf16[4,128,256]{2,1,0:T(8,128)(2,1)S(1)}, u32[]{:S(2)}, u32[]{:S(2)}) collective-permute-start(bf16[4,128,256]{2,1,0:T(8,128)(2,1)S(1)} %get-tuple-element.46), channel_id=1, source_target_pairs={{0,1},{1,2},{2,3},{4,5},{5,6},{6,7},{8,9},{9,10},{10,11},{12,13},{... | collective-permute-start | bytes 786440 | tf_op jit(solution)/shard_map/ppermute | solution.py:33
  23.0 5.6 %collective-permute-start.9 = (bf16[128,256]{1,0:T(8,128)(2,1)S(1)}, bf16[128,256]{1,0:T(8,128)(2,1)S(1)}, u32[]{:S(2)}, u32[]{:S(2)}) collective-permute-start(bf16[128,256]{1,0:T(8,128)(2,1)S(1)} %arrive.1.refs_0_), channel_id=1, source_target_pairs={{0,3},{1,0},{2,1},{3,2},{4,7},{5,4},{6,5},{7,6},{8,11},{9,8},{10,9... | collective-permute-start | bytes 196616 | tf_op jit(solution)/shard_map/ppermute | solution.py:38
  23.1 5.5 %collective-permute-start.8 = (bf16[128,256]{1,0:T(8,128)(2,1)S(1)}, bf16[128,256]{1,0:T(8,128)(2,1)S(1)}, u32[]{:S(2)}, u32[]{:S(2)}) collective-permute-start(bf16[128,256]{1,0:T(8,128)(2,1)S(1)} %arrive.1.refs_0_), channel_id=1, source_target_pairs={{0,2},{1,3},{2,0},{3,1},{4,6},{5,7},{6,4},{7,5},{8,10},{9,11},{10,... | collective-permute-start | bytes 196616 | tf_op jit(solution)/shard_map/ppermute | solution.py:38
  23.3 5.7 %collective-permute-start.7 = (bf16[128,256]{1,0:T(8,128)(2,1)S(1)}, bf16[128,256]{1,0:T(8,128)(2,1)S(1)}, u32[]{:S(2)}, u32[]{:S(2)}) collective-permute-start(bf16[128,256]{1,0:T(8,128)(2,1)S(1)} %arrive.1.refs_0_), channel_id=1, source_target_pairs={{0,1},{1,2},{2,3},{3,0},{4,5},{5,6},{6,7},{7,4},{8,9},{9,10},{10,1... | collective-permute-start | bytes 196616 | tf_op jit(solution)/shard_map/ppermute | solution.py:38
  38.9 9.1 %collective-permute-start.11 = (bf16[144,256]{1,0:T(8,128)(2,1)S(1)}, bf16[144,256]{1,0:T(8,128)(2,1)S(1)}, u32[]{:S(2)}, u32[]{:S(2)}) collective-permute-start(bf16[144,256]{1,0:T(8,128)(2,1)S(1)} %get-tuple-element.58), channel_id=1, source_target_pairs={{0,1},{1,2},{2,3},{3,0},{4,5},{5,6},{6,7},{7,4},{8,9},{9,10},{10,1... | collective-permute-start | bytes 221192 | tf_op jit(solution)/shard_map/ppermute | solution.py:38
  44.3 4.0 %collective-permute-start.12 = (bf16[144,256]{1,0:T(8,128)(2,1)S(1)}, bf16[144,256]{1,0:T(8,128)(2,1)S(1)}, u32[]{:S(2)}, u32[]{:S(2)}) collective-permute-start(bf16[144,256]{1,0:T(8,128)(2,1)S(1)} %get-tuple-element.59), channel_id=1, source_target_pairs={{0,2},{1,3},{2,0},{3,1},{4,6},{5,7},{6,4},{7,5},{8,10},{9,11},{10,... | collective-permute-start | bytes 221192 | tf_op jit(solution)/shard_map/ppermute | solution.py:38
  44.7 4.1 %collective-permute-start.13 = (bf16[144,256]{1,0:T(8,128)(2,1)S(1)}, bf16[144,256]{1,0:T(8,128)(2,1)S(1)}, u32[]{:S(2)}, u32[]{:S(2)}) collective-permute-start(bf16[144,256]{1,0:T(8,128)(2,1)S(1)} %get-tuple-element.60), channel_id=1, source_target_pairs={{0,3},{1,0},{2,1},{3,2},{4,7},{5,4},{6,5},{7,6},{8,11},{9,8},{10,9... | collective-permute-start | bytes 221192 | tf_op jit(solution)/shard_map/ppermute | solution.py:38
  44.7 20.7 %collective-permute-start.10 = (bf16[4,128,256]{2,1,0:T(8,128)(2,1)S(1)}, bf16[4,128,256]{2,1,0:T(8,128)(2,1)S(1)}, u32[]{:S(2)}, u32[]{:S(2)}) collective-permute-start(bf16[4,128,256]{2,1,0:T(8,128)(2,1)S(1)} %get-tuple-element.56), channel_id=1, source_target_pairs={{1,0},{2,1},{3,2},{5,4},{6,5},{7,6},{9,8},{10,9},{11,10},{13,12},{... | collective-permute-start | bytes 786440 | tf_op jit(solution)/shard_map/ppermute | solution.py:33
  48.8 8.3 %collective-permute-start.16 = (bf16[144,256]{1,0:T(8,128)(2,1)S(1)}, bf16[144,256]{1,0:T(8,128)(2,1)S(1)}, u32[]{:S(2)}, u32[]{:S(2)}) collective-permute-start(bf16[144,256]{1,0:T(8,128)(2,1)S(1)} %gather.1.here_ref), channel_id=1, source_target_pairs={{0,20},{4,24},{8,28},{12,0},{16,4},{20,8},{24,12},{28,16},{1,21},{... | collective-permute-start | bytes 221192 | tf_op jit(solution)/shard_map/ppermute | solution.py:38
  52.5 4.6 %collective-permute-start.15 = (bf16[144,256]{1,0:T(8,128)(2,1)S(1)}, bf16[144,256]{1,0:T(8,128)(2,1)S(1)}, u32[]{:S(2)}, u32[]{:S(2)}) collective-permute-start(bf16[144,256]{1,0:T(8,128)(2,1)S(1)} %gather.1.here_ref), channel_id=1, source_target_pairs={{0,24},{4,28},{8,0},{12,4},{16,8},{20,12},{24,16},{28,20},{1,25},{... | collective-permute-start | bytes 221192 | tf_op jit(solution)/shard_map/ppermute | solution.py:38
  54.2 4.6 %collective-permute-start.14 = (bf16[144,256]{1,0:T(8,128)(2,1)S(1)}, bf16[144,256]{1,0:T(8,128)(2,1)S(1)}, u32[]{:S(2)}, u32[]{:S(2)}) collective-permute-start(bf16[144,256]{1,0:T(8,128)(2,1)S(1)} %gather.1.here_ref), channel_id=1, source_target_pairs={{0,28},{4,0},{8,4},{12,8},{16,12},{20,16},{24,20},{28,24},{1,29},{... | collective-permute-start | bytes 221192 | tf_op jit(solution)/shard_map/ppermute | solution.py:38
  59.5 6.0 %collective-permute-start.18 = (bf16[256,256]{1,0:T(8,128)(2,1)S(1)}, bf16[256,256]{1,0:T(8,128)(2,1)S(1)}, u32[]{:S(2)}, u32[]{:S(2)}) collective-permute-start(bf16[256,256]{1,0:T(8,128)(2,1)S(1)} %get-tuple-element.63), channel_id=1, source_target_pairs={{0,1},{1,2},{2,3},{3,0},{4,5},{5,6},{6,7},{7,4},{8,9},{9,10},{10,1... | collective-permute-start | bytes 393224 | tf_op jit(solution)/shard_map/ppermute | solution.py:38
  61.6 6.3 %collective-permute-start.19 = (bf16[256,256]{1,0:T(8,128)(2,1)S(1)}, bf16[256,256]{1,0:T(8,128)(2,1)S(1)}, u32[]{:S(2)}, u32[]{:S(2)}) collective-permute-start(bf16[256,256]{1,0:T(8,128)(2,1)S(1)} %get-tuple-element.64), channel_id=1, source_target_pairs={{0,2},{1,3},{2,0},{3,1},{4,6},{5,7},{6,4},{7,5},{8,10},{9,11},{10,... | collective-permute-start | bytes 393224 | tf_op jit(solution)/shard_map/ppermute | solution.py:38
  61.9 6.6 %collective-permute-start.20 = (bf16[256,256]{1,0:T(8,128)(2,1)S(1)}, bf16[256,256]{1,0:T(8,128)(2,1)S(1)}, u32[]{:S(2)}, u32[]{:S(2)}) collective-permute-start(bf16[256,256]{1,0:T(8,128)(2,1)S(1)} %get-tuple-element.65), channel_id=1, source_target_pairs={{0,3},{1,0},{2,1},{3,2},{4,7},{5,4},{6,5},{7,6},{8,11},{9,8},{10,9... | collective-permute-start | bytes 393224 | tf_op jit(solution)/shard_map/ppermute | solution.py:38
  62.1 3.4 %collective-permute-start.17 = (f32[8,128]{1,0:T(8,128)S(1)}, f32[8,128]{1,0:T(8,128)S(1)}, u32[]{:S(2)}, u32[]{:S(2)}) collective-permute-start(f32[8,128]{1,0:T(8,128)S(1)} %get-tuple-element.61.sink_ref), channel_id=1, source_target_pairs={{0,16},{4,20},{8,24},{12,28},{16,0},{20,4},{24,8},{28,12},{1,17},{... | collective-permute-start | bytes 12296 | tf_op jit(solution)/shard_map/ppermute | solution.py:38
where the time goes:
time: 69.5 us; the launch traced here: 69.4 us
  starting transfers between devices  28.9 us (42%)
  waiting for transfers between devices  20.3 us (29%)
  Pallas kernels  18 us (26%)
  local copies, waits for them, and re-layouts  0.76 us (1%)
  other arithmetic  0.75 us (1%)
  between operations  0.72 us (1%)
    ppermute x19, starting transfers between devices, ring(): lax.ppermute(value, axis, [(source, (source + steps) % count) for source...  22.9 us
    ppermute x19, waiting for transfers between devices, ring(): lax.ppermute(value, axis, [(source, (source + steps) % count) for source...  20.3 us
    pallas_call x2, Pallas kernels, attend(): pl.pallas_call(functools.partial(attend_kernel, tok_count, blocks_here, h...  13.6 us
    ppermute x2, starting transfers between devices, shift(): lax.ppermute(value, axis, [(source, source + steps) for source in range(l...  6.07 us
  transfers between devices with their start and end apart: 21, of which 14 were waited for; matrix products, arithmetic and copies ran while one was open for 2% of the time, Pallas kernels for 7%

commit v1 on v0

--- a/solution.py
+++ b/solution.py
@@ -85,7 +85,7 @@
 
 
 def pack_kernel(sink_hbm, key_hbm, value_hbm, *refs):
-    *slot_refs, halo_ref, sinks, keys, values, sems = refs
+    *slot_refs, halo_ref, keys, values, sinks, sems = refs
     copies = [
         pltpu.make_async_copy(source, target, sems.at[place])
         for place, (source, target) in enumerate(
@@ -152,61 +152,90 @@
             out_ref[...] = in_ref[...]
 
 
-def own_pair(turn_of, offset):
-    return lax.rem(lax.axis_index("head") + turn_of + offset, PAIRS)
-
-
-def attend_kernel(
-    tok_count,
-    blocks_here,
-    slots,
-    steps,
-    offset,
-    joins,
-    table,
-    sink_ref,
-    q_ref,
-    g_ref,
-    k_ref,
-    v_ref,
-    halo_ref,
-    *refs,
+def stage_kernel(*refs):
+    *arrays, sems = refs
+    half = len(arrays) // 2
+    copies = [
+        pltpu.make_async_copy(source, target, sems.at[place])
+        for place, (source, target) in enumerate(zip(arrays[:half], arrays[half:]))
+    ]
+    for copy in copies:
+        copy.start()
+    for copy in copies:
+        copy.wait()
+
+
+def attend_kernel(tok_count, blocks_here, slots, steps, offset, pairs, joins, *refs):
+    inputs, refs = refs[:7], refs[7:]
+    tail_refs, refs = refs[: len(steps)], refs[len(steps) + joins :]
+    outputs, refs = refs[:5], refs[5:]
+    dtail_refs, refs = refs[: len(steps)], refs[len(steps) :]
+    tails, *scratch = refs
+    head = lax.axis_index("head")
+    for step, tail_ref in zip(steps, tail_refs):
+        tails[lax.rem(head - step + slots, slots)] = tail_ref[...]
+
+    def step(place, carry):
+        pair = place // blocks_here
+        if offset is not None:
+            pair = lax.rem(head + pair + offset, PAIRS)
+        attend_block(
+            tok_count,
+            blocks_here,
+            slots,
+            pair,
+            place % blocks_here,
+            inputs,
+            outputs,
+            tails,
+            tuple(zip(steps, dtail_refs)),
+            scratch,
+        )
+        return carry
+
+    lax.fori_loop(0, pairs * blocks_here, step, 0)
+
+
+def attend_block(
+    tok_count, blocks_here, slots, pair, block, inputs, outputs, tails, dtails, scratch
 ):
-    tail_refs, refs = refs[: len(steps)], refs[len(steps) + joins :]
-    o_ref, dq_ref, dk_ref, dv_ref, dhalo_ref = refs[:5]
-    dtail_refs, refs = refs[5 : 5 + len(steps)], refs[5 + len(steps) :]
-    tails, tail_sum, sink_rows, prob2, slope2 = refs
+    table, sink_ref, q_ref, g_ref, k_ref, v_ref, halo_ref = inputs
+    o_ref, dq_ref, dk_ref, dv_ref, dhalo_ref = outputs
+    tail_sum, sink_rows, prob2, slope2 = scratch
     per_slot = KV_HEADS // slots
-    turn_of, block = pl.program_id(0), pl.program_id(1)
-    pair = turn_of if offset is None else own_pair(turn_of, offset)
     tok, head = lax.axis_index("tok"), lax.axis_index("head")
     number = (tok * lax.axis_size("head") + head) * blocks_here + block
     alive, opening, prev_ok = block_state(table, tok, tok_count, number)
     here = pl.ds(pl.multiple_of(block * WINDOW, WINDOW), WINDOW)
     before = pl.ds(pl.multiple_of(jnp.maximum(block - 1, 0) * WINDOW, WINDOW), WINDOW)
     first = block == 0
-
-    @pl.when(first & (turn_of == 0))
-    def _():
-        for step, tail_ref in zip(steps, tail_refs):
-            tails[lax.rem(head - step + slots, slots)] = tail_ref[...]
+    near = pl.ds(pl.multiple_of(pair * 128, 128), 128)
+    big = pl.ds(pl.multiple_of(pair * 1024, 1024), 1024)
+    q_ref, g_ref, o_ref, dq_ref = (ref.at[here, big] for ref in (q_ref, g_ref, o_ref, dq_ref))
+    k_ref, v_ref, dk_ref, dv_ref = (ref.at[:, near] for ref in (k_ref, v_ref, dk_ref, dv_ref))
+    sink_ref = sink_ref.at[pl.ds(pl.multiple_of(pair * 16, 16), 16)]
+    dhalo_ref = dhalo_ref.at[pair]
 
     @pl.when(first)
     def _():
         tail_sum[...] = jnp.zeros_like(tail_sum)
-        dhalo_ref[...] = jnp.zeros_like(dhalo_ref)
+        dhalo_ref[...] = jnp.zeros((WINDOW, 256), BF16)
         sink_rows[...] = jnp.zeros_like(sink_rows)
 
     @pl.when(jnp.logical_not(alive))
     def _():
-        o_ref[...] = jnp.zeros_like(o_ref)
-        dq_ref[...] = jnp.zeros_like(dq_ref)
+        o_ref[...] = jnp.zeros((WINDOW, 1024), BF16)
+        dq_ref[...] = jnp.zeros((WINDOW, 1024), BF16)
         dk_ref[here, :] = jnp.zeros((WINDOW, 128), F32)
         dv_ref[here, :] = jnp.zeros((WINDOW, 128), F32)
 
     @pl.when(alive)
     def _():
-        halo = halo_ref[...] if len(halo_ref.shape) == 2 else halo_ref[0]
+        if len(halo_ref.shape) == 2:
+            last = halo_ref.shape[0] - EXTRA
+            halo = halo_ref[last - WINDOW : last]
+        else:
+            halo = halo_ref[pair]
         if per_slot == 2:
             tail = tails[pair]
             tail_k, tail_v = tail[:, :128], tail[:, 128:]
@@ -386,8 +415,8 @@
 
         @pl.when(jnp.logical_not(opening) & first)
         def _():
-            dhalo_ref[0, :, :128] = dk[WINDOW:].astype(BF16)
-            dhalo_ref[0, :, 128:] = dv[WINDOW:].astype(BF16)
+            dhalo_ref[:, :128] = dk[WINDOW:].astype(BF16)
+            dhalo_ref[:, 128:] = dv[WINDOW:].astype(BF16)
 
         @pl.when(jnp.logical_not(opening) & jnp.logical_not(first))
         def _():
@@ -396,7 +425,7 @@
 
     @pl.when(block == blocks_here - 1)
     def _():
-        width = dtail_refs[0].shape[1]
+        width = 2 * per_slot * HEAD_DIM
         heads = per_slot * GROUP
         total = tail_sum[...].astype(BF16)
         for part in range(2 // per_slot):
@@ -409,7 +438,7 @@
                 sink_row = jnp.concatenate([sink_row, jnp.zeros((1, width - 128), F32)], axis=1)
             extra = row_split(sink_row, (EXTRA, width))
             wanted = lax.rem(pair * (2 // per_slot) + part - head + slots, slots)
-            for step, dtail_ref in zip(steps, dtail_refs):
+            for step, dtail_ref in dtails:
 
                 @pl.when(wanted == step)
                 def _(dtail_ref=dtail_ref, tail=tail, extra=extra):
@@ -492,25 +521,27 @@
     def shape(dims, kind=BF16):
         return jax.ShapeDtypeStruct(dims, kind)
 
-    queries, out_grad, key_states, value_states, sink_logits = (
-        pltpu.with_memory_space_constraint(value, pltpu.HBM)
-        for value in (queries, out_grad, key_states, value_states, sink_logits)
-    )
+    def far(value):
+        return pltpu.with_memory_space_constraint(value, pltpu.HBM)
+
+    def close(value):
+        return pltpu.with_memory_space_constraint(value, pltpu.VMEM)
+
     table = jnp.concatenate([branch_start, branch_len, parent_list[:, 0], parent_list[:, 1]])
-    *slots, halo_out = pl.pallas_call(
+    *slots, halo_out, keys, values = pl.pallas_call(
         pack_kernel,
-        out_shape=(shape((rows + EXTRA, width)),) * head_count + (shape((PAIRS, WINDOW, 256)),),
+        out_shape=(shape((rows + EXTRA, width)),) * head_count
+        + (shape((PAIRS, WINDOW, 256)),)
+        + (pltpu.VMEM(key_states.shape, BF16),) * 2,
         in_specs=[HBM] * 3,
-        out_specs=(VMEM,) * (head_count + 1),
+        out_specs=(VMEM,) * (head_count + 3),
         scratch_shapes=[
             pltpu.SMEM(sink_logits.shape, F32),
-            pltpu.VMEM(key_states.shape, BF16),
-            pltpu.VMEM(key_states.shape, BF16),
             pltpu.SemaphoreType.DMA((3,)),
         ],
         compiler_params=PARAMS,
         name="pack",
-    )(sink_logits, key_states, value_states)
+    )(far(sink_logits), far(key_states), far(value_states))
     spread = swap(slots, "head")
     *chosen, sinks = pl.pallas_call(
         functools.partial(choose_kernel, tok_count, blocks),
@@ -521,6 +552,19 @@
         name="choose",
     )(table, *spread)
     arrived = [ring(chosen[LAG - s], "tok", s) for s in range(LAG, 0, -1)]
+    queries, out_grad, _ = lax.optimization_barrier((queries, out_grad, sinks))
+    near_queries, near_grad = pl.pallas_call(
+        stage_kernel,
+        out_shape=(pltpu.VMEM(queries.shape, BF16),) * 2,
+        in_specs=[HBM] * 2,
+        out_specs=(VMEM,) * 2,
+        scratch_shapes=[pltpu.SemaphoreType.DMA((2,))],
+        compiler_params=PARAMS,
+        name="stage",
+    )(far(queries), far(out_grad))
+    *arrived, near_queries, near_grad = lax.optimization_barrier(
+        (*arrived, near_queries, near_grad)
+    )
     quarter = pl.pallas_call(
         functools.partial(arrive_kernel, tok_count),
         out_shape=shape((WINDOW, width)),
@@ -534,45 +578,38 @@
     halo = shift(halo_out, "head", 1)
 
     def attend(steps, pairs, offset, halo, joined):
-        def at(index):
-            def place(p, b):
-                return index(p if offset is None else own_pair(p, offset), b)
-
-            return place
-
-        big = pl.BlockSpec((WINDOW, 1024), at(lambda p, b: (b, p)))
-        small = pl.BlockSpec((rows, 128), at(lambda p, b: (0, p)))
-        near = pl.BlockSpec((1, WINDOW, 256), at(lambda p, b: (p, 0, 0)))
-        last = pl.BlockSpec((WINDOW, width), lambda p, b: (blocks_here - 1, 0))
-        whole = pl.BlockSpec((WINDOW, width), lambda p, b: (0, 0))
-        whole_back = pl.BlockSpec((WINDOW + EXTRA, width), lambda p, b: (0, 0))
         inputs = (
-            (table, SMEM),
-            (sinks, pl.BlockSpec((2 * GROUP, 128), at(lambda p, b: (p, 0)))),
-            (queries, big),
-            (out_grad, big),
-            (key_states, small),
-            (value_states, small),
-            (halo, near if halo.ndim == 3 else last),
-            *((tails[step], whole) for step in steps),
-            *((value, pl.BlockSpec(memory_space=pl.ANY)) for value in joined),
+            sinks,
+            close(near_queries),
+            close(near_grad),
+            close(keys),
+            close(values),
+            halo,
+            *(tails[step] for step in steps),
+            *(close(value) for value in joined),
         )
-        base = len(inputs) - len(joined)
+        base = 1 + len(inputs) - len(joined)
         return pl.pallas_call(
             functools.partial(
-                attend_kernel, tok_count, blocks_here, head_count, steps, offset, len(joined)
+                attend_kernel,
+                tok_count,
+                blocks_here,
+                head_count,
+                steps,
+                offset,
+                pairs,
+                len(joined),
             ),
-            grid=(pairs, blocks_here),
             out_shape=(
-                shape(queries.shape),
-                shape(queries.shape),
-                shape(key_states.shape, F32),
-                shape(key_states.shape, F32),
-                shape((PAIRS, WINDOW, 256)),
+                pltpu.VMEM(queries.shape, BF16),
+                pltpu.VMEM(queries.shape, BF16),
+                pltpu.VMEM(key_states.shape, F32),
+                pltpu.VMEM(key_states.shape, F32),
+                pltpu.VMEM((PAIRS, WINDOW, 256), BF16),
             )
             + (shape((WINDOW + EXTRA, width)),) * len(steps),
-            in_specs=[spec for _, spec in inputs],
-            out_specs=(big, big, small, small, near) + (whole_back,) * len(steps),
+            in_specs=[SMEM] + [VMEM] * len(inputs),
+            out_specs=(VMEM,) * (5 + len(steps)),
             scratch_shapes=[
                 pltpu.VMEM((head_count, WINDOW, width), BF16),
                 pltpu.VMEM((WINDOW, 256), F32),
@@ -583,7 +620,7 @@
             input_output_aliases={base + place: place for place in range(len(joined))},
             compiler_params=PARAMS,
             name="attend",
-        )(*(value for value, _ in inputs))
+        )(table, *inputs)
 
     if per_slot == 2:
         *joined, own_tail = attend((0,), 1, 0, spread[1], ())
@@ -602,6 +639,16 @@
         compiler_params=PARAMS,
         name="gather",
     )(*parts)
+    attended, query_grad, _ = lax.optimization_barrier((attended, query_grad, quarter_grad))
+    attended, query_grad = pl.pallas_call(
+        stage_kernel,
+        out_shape=(pltpu.HBM(queries.shape, BF16),) * 2,
+        in_specs=[VMEM] * 2,
+        out_specs=(HBM,) * 2,
+        scratch_shapes=[pltpu.SemaphoreType.DMA((2,))],
+        compiler_params=PARAMS,
+        name="flush",
+    )(close(attended), close(query_grad))
     returned = [ring(quarter_grad, "tok", -s) for s in range(LAG, 0, -1)][::-1]
     halo_back = shift(dhalo, "head", -1)
     *landed, sink_near = pl.pallas_call(

time: 69.5 us -> 66.7 us (0.960)
  waiting for transfers between devices: 20.3 us -> 13.4 us
  Pallas kernels: 18 us -> 23 us
  starting transfers between devices: 28.9 us -> 27.4 us
    ppermute x19, waiting for transfers between devices: 20.3 us -> 13.4 us  [ring(): lax.ppermute(value, axis, [(source, (source + steps) % count) for source...]
    pallas_call x0 -> x2, Pallas kernels: none -> 4.26 us  [the longest x1 2.24 us: local(): pl.pallas_call(stage_kernel, out_shape=(pltpu.VMEM(queries.shape, BF16),)...]
    ppermute x19, starting transfers between devices: 22.9 us -> 21.3 us  [ring(): lax.ppermute(value, axis, [(source, (source + steps) % count) for source...]
    pallas_call x2, Pallas kernels: 13.6 us -> 14.4 us  [attend(): pl.pallas_call(functools.partial(attend_kernel, tok_count, blocks_here, h...]
  transfers between devices with their start and end apart: 21 -> 21, of which waited for: 14 -> 12; matrix products, arithmetic and copies ran while one was open for 2% -> 2% of each run, Pallas kernels for 7% -> 13%
where the time goes in v1:
time: 66.7 us; the launch traced here: 66 us
  starting transfers between devices  27.4 us (41%)
  Pallas kernels  23 us (34%)
  waiting for transfers between devices  13.4 us (20%)
  between operations  0.79 us (1%)
  local copies, waits for them, and re-layouts  0.76 us (1%)
  other arithmetic  0.75 us (1%)
    ppermute x19, starting transfers between devices, ring(): lax.ppermute(value, axis, [(source, (source + steps) % count) for source...  21.3 us
    pallas_call x2, Pallas kernels, attend(): pl.pallas_call(functools.partial(attend_kernel, tok_count, blocks_here, h...  14.4 us
    ppermute x19, waiting for transfers between devices, ring(): lax.ppermute(value, axis, [(source, (source + steps) % count) for source...  13.4 us
    ppermute x2, starting transfers between devices, shift(): lax.ppermute(value, axis, [(source, source + steps) for source in range(l...  6.06 us
    pallas_call x1, Pallas kernels, local(): pl.pallas_call(stage_kernel, out_shape=(pltpu.VMEM(queries.shape, BF16),)...  2.24 us
    pallas_call x1, Pallas kernels, local(): pl.pallas_call(stage_kernel, out_shape=(pltpu.HBM(queries.shape, BF16),)...  2.02 us
  transfers between devices with their start and end apart: 21, of which 12 were waited for; matrix products, arithmetic and copies ran while one was open for 2% of the time, Pallas kernels for 13%

profile of v1, /device:TPU:3, one launch (start us, length us, event | category | flops | bytes accessed | tf_op | source)
XLA Modules:
  0.0 66.0 jit_solution(18317467256422648330)
XLA Ops:
  0.6 1.2 %pack.1 = (bf16[272,256]{1,0:T(8,128)(2,1)S(1)}, bf16[272,256]{1,0:T(8,128)(2,1)S(1)}, bf16[272,256]{1,0:T(8,128)(2,1)S(1)}, bf16[272,256]{1,0:T(8,128)(2,1)S(1)...) custom-call(f32[16]{0:T(128)} %sink_hbm.1, ...), custom_call_target="tpu_custom_call" | custom-call | tf_op jit(solution)/shard_map/pack/pallas_call | solution.py:531
  1.8 1.8 %collective-permute-start = (bf16[272,256]{1,0:T(8,128)(2,1)S(1)}, bf16[272,256]{1,0:T(8,128)(2,1)S(1)}, u32[]{:S(2)}, u32[]{:S(2)}) collective-permute-start(bf16[272,256]{1,0:T(8,128)(2,1)S(1)} %get-tuple-element.53), channel_id=1, source_target_pairs={{0,1},{1,2},{2,3},{3,0},{4,5},{5,6},{6,7},{7,4},{8,9},{9,10},{10,1... | collective-permute-start | bytes 417800 | tf_op jit(solution)/shard_map/ppermute | solution.py:38
  5.6 0.9 %collective-permute-done.refs_1_.refs_6_ = bf16[272,256]{1,0:T(8,128)(2,1)S(1)} collective-permute-done((bf16[272,256]{1,0:T(8,128)(2,1)S(1)}, bf16[272,256]{1,0:T(8,128)(2,1)S(1)}, u32[]{:S(2)}, u32[]{:S(2)}) %collective-permute-start) | collective-permute-done | bytes 139296 | tf_op jit(solution)/shard_map/ppermute | solution.py:38
  6.5 3.6 %collective-permute-done.1.refs_2_ = bf16[272,256]{1,0:T(8,128)(2,1)S(1)} collective-permute-done((bf16[272,256]{1,0:T(8,128)(2,1)S(1)}, bf16[272,256]{1,0:T(8,128)(2,1)S(1)}, u32[]{:S(2)}, u32[]{:S(2)}) %collective-permute-start.1) | collective-permute-done | bytes 139296 | tf_op jit(solution)/shard_map/ppermute | solution.py:38
  10.8 0.8 %choose.1 = (bf16[128,256]{1,0:T(8,128)(2,1)S(1)}, bf16[128,256]{1,0:T(8,128)(2,1)S(1)}, bf16[128,256]{1,0:T(8,128)(2,1)S(1)}, f32[64,128]{1,0:T(8,128)S(1)}) custom-call(s32[64]{0:T(128)S(1)} %pad_add_fusion.table.refs_0_, bf16[272,256]{1,0:T(8,128)(2,1)S(1)} %get-tuple-element.52.refs_0_, bf16[272,256]{1,0:T(8,128)(2,1)S(1)} %collective-permute-done.refs_1_.refs_6_, ...), custom_call_target="tpu_custom_call" | custom-call | tf_op jit(solution)/shard_map/choose/pallas_call | solution.py:546
  11.6 2.3 %collective-permute-start.3 = (bf16[128,256]{1,0:T(8,128)(2,1)S(1)}, bf16[128,256]{1,0:T(8,128)(2,1)S(1)}, u32[]{:S(2)}, u32[]{:S(2)}) collective-permute-start(bf16[128,256]{1,0:T(8,128)(2,1)S(1)} %get-tuple-element.57), channel_id=1, source_target_pairs={{0,12},{4,16},{8,20},{12,24},{16,28},{20,0},{24,4},{28,8},{1,13},{... | collective-permute-start | bytes 196616 | tf_op jit(solution)/shard_map/ppermute | solution.py:38
  13.9 1.3 %collective-permute-start.4 = (bf16[128,256]{1,0:T(8,128)(2,1)S(1)}, bf16[128,256]{1,0:T(8,128)(2,1)S(1)}, u32[]{:S(2)}, u32[]{:S(2)}) collective-permute-start(bf16[128,256]{1,0:T(8,128)(2,1)S(1)} %get-tuple-element.58), channel_id=1, source_target_pairs={{0,8},{4,12},{8,16},{12,20},{16,24},{20,28},{24,0},{28,4},{1,9},{5... | collective-permute-start | bytes 196616 | tf_op jit(solution)/shard_map/ppermute | solution.py:38
  15.2 1.2 %collective-permute-start.5 = (bf16[128,256]{1,0:T(8,128)(2,1)S(1)}, bf16[128,256]{1,0:T(8,128)(2,1)S(1)}, u32[]{:S(2)}, u32[]{:S(2)}) collective-permute-start(bf16[128,256]{1,0:T(8,128)(2,1)S(1)} %get-tuple-element.59), channel_id=1, source_target_pairs={{0,4},{4,8},{8,12},{12,16},{16,20},{20,24},{24,28},{28,0},{1,5},{5... | collective-permute-start | bytes 196616 | tf_op jit(solution)/shard_map/ppermute | solution.py:38
  16.4 2.2 %stage.1 = (bf16[256,4096]{1,0:T(8,128)(2,1)S(1)}, bf16[256,4096]{1,0:T(8,128)(2,1)S(1)}) custom-call(bf16[256,4096]{1,0:T(8,128)(2,1)} %refs_0_, bf16[256,4096]{1,0:T(8,128)(2,1)} %refs_1_), custom_call_target="tpu_custom_call" | custom-call | tf_op jit(solution)/shard_map/stage/pallas_call | solution.py:556
  20.2 2.8 %collective-permute-start.6 = (bf16[4,128,256]{2,1,0:T(8,128)(2,1)S(1)}, bf16[4,128,256]{2,1,0:T(8,128)(2,1)S(1)}, u32[]{:S(2)}, u32[]{:S(2)}) collective-permute-start(bf16[4,128,256]{2,1,0:T(8,128)(2,1)S(1)} %get-tuple-element.72), channel_id=1, source_target_pairs={{0,1},{1,2},{2,3},{4,5},{5,6},{6,7},{8,9},{9,10},{10,11},{12,13},{... | collective-permute-start | bytes 786440 | tf_op jit(solution)/shard_map/ppermute | solution.py:33
  23.3 1.5 %collective-permute-start.7 = (bf16[128,256]{1,0:T(8,128)(2,1)S(1)}, bf16[128,256]{1,0:T(8,128)(2,1)S(1)}, u32[]{:S(2)}, u32[]{:S(2)}) collective-permute-start(bf16[128,256]{1,0:T(8,128)(2,1)S(1)} %arrive.1.refs_7_), channel_id=1, source_target_pairs={{0,1},{1,2},{2,3},{3,0},{4,5},{5,6},{6,7},{7,4},{8,9},{9,10},{10,1... | collective-permute-start | bytes 196616 | tf_op jit(solution)/shard_map/ppermute | solution.py:38
  24.8 3.9 %attend.2 = (bf16[256,4096]{1,0:T(8,128)(2,1)S(1)}, bf16[256,4096]{1,0:T(8,128)(2,1)S(1)}, f32[256,512]{1,0:T(8,128)S(1)}, f32[256,512]{1,0:T(8,128)S(1)}, bf16[...) custom-call(s32[64]{0:T(128)S(1)} %pad_add_fusion.table.refs_0_, f32[64,128]{1,0:T(8,128)S(1)} %get-tuple-element.56.refs_1_, ...), custom_call_target="tpu_custom_call" | custom-call | tf_op jit(solution)/shard_map/attend/pallas_call | solution.py:592
  29.0 10.5 %attend.3 = (bf16[256,4096]{1,0:T(8,128)(2,1)S(1)}, bf16[256,4096]{1,0:T(8,128)(2,1)S(1)}, f32[256,512]{1,0:T(8,128)S(1)}, f32[256,512]{1,0:T(8,128)S(1)}, bf16[...) custom-call(s32[64]{0:T(128)S(1)} %pad_add_fusion.table.refs_0_, ...), custom_call_target="tpu_custom_call", output_to_operand_aliasing={{0}: (10, {}), {1}: (11, {}), {2}: (12, {}), {3}: (13, {}),... | custom-call | tf_op jit(solution)/shard_map/attend/pallas_call | solution.py:592
  39.5 2.6 %collective-permute-start.10 = (bf16[144,256]{1,0:T(8,128)(2,1)S(1)}, bf16[144,256]{1,0:T(8,128)(2,1)S(1)}, u32[]{:S(2)}, u32[]{:S(2)}) collective-permute-start(bf16[144,256]{1,0:T(8,128)(2,1)S(1)} %get-tuple-element.81), channel_id=1, source_target_pairs={{0,1},{1,2},{2,3},{3,0},{4,5},{5,6},{6,7},{7,4},{8,9},{9,10},{10,1... | collective-permute-start | bytes 221192 | tf_op jit(solution)/shard_map/ppermute | solution.py:38
  42.6 3.3 %collective-permute-start.13 = (bf16[4,128,256]{2,1,0:T(8,128)(2,1)S(1)}, bf16[4,128,256]{2,1,0:T(8,128)(2,1)S(1)}, u32[]{:S(2)}, u32[]{:S(2)}) collective-permute-start(bf16[4,128,256]{2,1,0:T(8,128)(2,1)S(1)} %get-tuple-element.90), channel_id=1, source_target_pairs={{1,0},{2,1},{3,2},{5,4},{6,5},{7,6},{9,8},{10,9},{11,10},{13,12},{... | collective-permute-start | bytes 786440 | tf_op jit(solution)/shard_map/ppermute | solution.py:33
  46.2 2.1 %collective-permute-start.16 = (bf16[144,256]{1,0:T(8,128)(2,1)S(1)}, bf16[144,256]{1,0:T(8,128)(2,1)S(1)}, u32[]{:S(2)}, u32[]{:S(2)}) collective-permute-start(bf16[144,256]{1,0:T(8,128)(2,1)S(1)} %gather.1.here_ref), channel_id=1, source_target_pairs={{0,20},{4,24},{8,28},{12,0},{16,4},{20,8},{24,12},{28,16},{1,21},{... | collective-permute-start | bytes 221192 | tf_op jit(solution)/shard_map/ppermute | solution.py:38
  48.3 2.3 %collective-permute-start.15 = (bf16[144,256]{1,0:T(8,128)(2,1)S(1)}, bf16[144,256]{1,0:T(8,128)(2,1)S(1)}, u32[]{:S(2)}, u32[]{:S(2)}) collective-permute-start(bf16[144,256]{1,0:T(8,128)(2,1)S(1)} %gather.1.here_ref), channel_id=1, source_target_pairs={{0,24},{4,28},{8,0},{12,4},{16,8},{20,12},{24,16},{28,20},{1,25},{... | collective-permute-start | bytes 221192 | tf_op jit(solution)/shard_map/ppermute | solution.py:38
  50.9 0.9 %collective-permute-done.16.refs_2_ = bf16[144,256]{1,0:T(8,128)(2,1)S(1)} collective-permute-done((bf16[144,256]{1,0:T(8,128)(2,1)S(1)}, bf16[144,256]{1,0:T(8,128)(2,1)S(1)}, u32[]{:S(2)}, u32[]{:S(2)}) %collective-permute-start.16) | collective-permute-done | bytes 73760 | tf_op jit(solution)/shard_map/ppermute | solution.py:38
  52.5 2.3 %collective-permute-done.14.refs_0_ = bf16[144,256]{1,0:T(8,128)(2,1)S(1)} collective-permute-done((bf16[144,256]{1,0:T(8,128)(2,1)S(1)}, bf16[144,256]{1,0:T(8,128)(2,1)S(1)}, u32[]{:S(2)}, u32[]{:S(2)}) %collective-permute-start.14) | collective-permute-done | bytes 73760 | tf_op jit(solution)/shard_map/ppermute | solution.py:38
  55.5 2.6 %collective-permute-start.18 = (bf16[256,256]{1,0:T(8,128)(2,1)S(1)}, bf16[256,256]{1,0:T(8,128)(2,1)S(1)}, u32[]{:S(2)}, u32[]{:S(2)}) collective-permute-start(bf16[256,256]{1,0:T(8,128)(2,1)S(1)} %get-tuple-element.93), channel_id=1, source_target_pairs={{0,1},{1,2},{2,3},{3,0},{4,5},{5,6},{6,7},{7,4},{8,9},{9,10},{10,1... | collective-permute-start | bytes 393224 | tf_op jit(solution)/shard_map/ppermute | solution.py:38
  58.6 1.5 %collective-permute-start.17 = (f32[8,128]{1,0:T(8,128)S(1)}, f32[8,128]{1,0:T(8,128)S(1)}, u32[]{:S(2)}, u32[]{:S(2)}) collective-permute-start(f32[8,128]{1,0:T(8,128)S(1)} %get-tuple-element.91.sink_ref), channel_id=1, source_target_pairs={{0,16},{4,20},{8,24},{12,28},{16,0},{20,4},{24,8},{28,12},{1,17},{... | collective-permute-start | bytes 12296 | tf_op jit(solution)/shard_map/ppermute | solution.py:38
  60.1 2.0 %flush.1 = (bf16[256,4096]{1,0:T(8,128)(2,1)}, bf16[256,4096]{1,0:T(8,128)(2,1)}) custom-call(bf16[256,4096]{1,0:T(8,128)(2,1)S(1)} %get-tuple-element.84.refs_0_, bf16[256,4096]{1,0:T(8,128)(2,1)S(1)} %get-tuple-element.85.refs_1_), custom_call_target="tpu_custom_call" | custom-call | tf_op jit(solution)/shard_map/flush/pallas_call | solution.py:643
  62.1 2.3 %collective-permute-done.19.refs_2_ = bf16[256,256]{1,0:T(8,128)(2,1)S(1)} collective-permute-done((bf16[256,256]{1,0:T(8,128)(2,1)S(1)}, bf16[256,256]{1,0:T(8,128)(2,1)S(1)}, u32[]{:S(2)}, u32[]{:S(2)}) %collective-permute-start.19) | collective-permute-done | bytes 131104 | tf_op jit(solution)/shard_map/ppermute | solution.py:38
  65.0 1.0 %total.1 = (bf16[256,512]{1,0:T(8,128)(2,1)}, bf16[256,512]{1,0:T(8,128)(2,1)}, f32[16]{0:T(128)}) custom-call(f32[256,512]{1,0:T(8,128)S(1)} %get-tuple-element.88.dk_ref, f32[256,512]{1,0:T(8,128)S(1)} %get-tuple-element.89.dv_ref, bf16[4,128,256]{2,1,0:T(8,128)(2,1)S(1)} %collective-permute-done.13.halo_ref, f32[8,128]{1,0:T(8,128)S(1)} %get-tuple-element.91.sink_ref, ...), custom_call_target="tpu_custom_call" | custom-call | tf_op jit(solution)/shard_map/total/pallas_call | solution.py:668
  (30 shorter events, 8.2 us)
Async XLA Ops:
  1.8 4.7 %collective-permute-start = (bf16[272,256]{1,0:T(8,128)(2,1)S(1)}, bf16[272,256]{1,0:T(8,128)(2,1)S(1)}, u32[]{:S(2)}, u32[]{:S(2)}) collective-permute-start(bf16[272,256]{1,0:T(8,128)(2,1)S(1)} %get-tuple-element.53), channel_id=1, source_target_pairs={{0,1},{1,2},{2,3},{3,0},{4,5},{5,6},{6,7},{7,4},{8,9},{9,10},{10,1... | collective-permute-start | bytes 417800 | tf_op jit(solution)/shard_map/ppermute | solution.py:38
  3.7 6.5 %collective-permute-start.1 = (bf16[272,256]{1,0:T(8,128)(2,1)S(1)}, bf16[272,256]{1,0:T(8,128)(2,1)S(1)}, u32[]{:S(2)}, u32[]{:S(2)}) collective-permute-start(bf16[272,256]{1,0:T(8,128)(2,1)S(1)} %get-tuple-element.54), channel_id=1, source_target_pairs={{0,2},{1,3},{2,0},{3,1},{4,6},{5,7},{6,4},{7,5},{8,10},{9,11},{10,... | collective-permute-start | bytes 417800 | tf_op jit(solution)/shard_map/ppermute | solution.py:38
  3.9 6.9 %collective-permute-start.2 = (bf16[272,256]{1,0:T(8,128)(2,1)S(1)}, bf16[272,256]{1,0:T(8,128)(2,1)S(1)}, u32[]{:S(2)}, u32[]{:S(2)}) collective-permute-start(bf16[272,256]{1,0:T(8,128)(2,1)S(1)} %get-tuple-element.55), channel_id=1, source_target_pairs={{0,3},{1,0},{2,1},{3,2},{4,7},{5,4},{6,5},{7,6},{8,11},{9,8},{10,9... | collective-permute-start | bytes 417800 | tf_op jit(solution)/shard_map/ppermute | solution.py:38
  11.6 7.1 %collective-permute-start.3 = (bf16[128,256]{1,0:T(8,128)(2,1)S(1)}, bf16[128,256]{1,0:T(8,128)(2,1)S(1)}, u32[]{:S(2)}, u32[]{:S(2)}) collective-permute-start(bf16[128,256]{1,0:T(8,128)(2,1)S(1)} %get-tuple-element.57), channel_id=1, source_target_pairs={{0,12},{4,16},{8,20},{12,24},{16,28},{20,0},{24,4},{28,8},{1,13},{... | collective-permute-start | bytes 196616 | tf_op jit(solution)/shard_map/ppermute | solution.py:38
  13.9 5.5 %collective-permute-start.4 = (bf16[128,256]{1,0:T(8,128)(2,1)S(1)}, bf16[128,256]{1,0:T(8,128)(2,1)S(1)}, u32[]{:S(2)}, u32[]{:S(2)}) collective-permute-start(bf16[128,256]{1,0:T(8,128)(2,1)S(1)} %get-tuple-element.58), channel_id=1, source_target_pairs={{0,8},{4,12},{8,16},{12,20},{16,24},{20,28},{24,0},{28,4},{1,9},{5... | collective-permute-start | bytes 196616 | tf_op jit(solution)/shard_map/ppermute | solution.py:38
  15.2 4.4 %collective-permute-start.5 = (bf16[128,256]{1,0:T(8,128)(2,1)S(1)}, bf16[128,256]{1,0:T(8,128)(2,1)S(1)}, u32[]{:S(2)}, u32[]{:S(2)}) collective-permute-start(bf16[128,256]{1,0:T(8,128)(2,1)S(1)} %get-tuple-element.59), channel_id=1, source_target_pairs={{0,4},{4,8},{8,12},{12,16},{16,20},{20,24},{24,28},{28,0},{1,5},{5... | collective-permute-start | bytes 196616 | tf_op jit(solution)/shard_map/ppermute | solution.py:38
  20.2 8.8 %collective-permute-start.6 = (bf16[4,128,256]{2,1,0:T(8,128)(2,1)S(1)}, bf16[4,128,256]{2,1,0:T(8,128)(2,1)S(1)}, u32[]{:S(2)}, u32[]{:S(2)}) collective-permute-start(bf16[4,128,256]{2,1,0:T(8,128)(2,1)S(1)} %get-tuple-element.72), channel_id=1, source_target_pairs={{0,1},{1,2},{2,3},{4,5},{5,6},{6,7},{8,9},{9,10},{10,11},{12,13},{... | collective-permute-start | bytes 786440 | tf_op jit(solution)/shard_map/ppermute | solution.py:33
  23.0 5.7 %collective-permute-start.9 = (bf16[128,256]{1,0:T(8,128)(2,1)S(1)}, bf16[128,256]{1,0:T(8,128)(2,1)S(1)}, u32[]{:S(2)}, u32[]{:S(2)}) collective-permute-start(bf16[128,256]{1,0:T(8,128)(2,1)S(1)} %arrive.1.refs_7_), channel_id=1, source_target_pairs={{0,3},{1,0},{2,1},{3,2},{4,7},{5,4},{6,5},{7,6},{8,11},{9,8},{10,9... | collective-permute-start | bytes 196616 | tf_op jit(solution)/shard_map/ppermute | solution.py:38
  23.0 5.7 %collective-permute-start.8 = (bf16[128,256]{1,0:T(8,128)(2,1)S(1)}, bf16[128,256]{1,0:T(8,128)(2,1)S(1)}, u32[]{:S(2)}, u32[]{:S(2)}) collective-permute-start(bf16[128,256]{1,0:T(8,128)(2,1)S(1)} %arrive.1.refs_7_), channel_id=1, source_target_pairs={{0,2},{1,3},{2,0},{3,1},{4,6},{5,7},{6,4},{7,5},{8,10},{9,11},{10,... | collective-permute-start | bytes 196616 | tf_op jit(solution)/shard_map/ppermute | solution.py:38
  23.3 5.7 %collective-permute-start.7 = (bf16[128,256]{1,0:T(8,128)(2,1)S(1)}, bf16[128,256]{1,0:T(8,128)(2,1)S(1)}, u32[]{:S(2)}, u32[]{:S(2)}) collective-permute-start(bf16[128,256]{1,0:T(8,128)(2,1)S(1)} %arrive.1.refs_7_), channel_id=1, source_target_pairs={{0,1},{1,2},{2,3},{3,0},{4,5},{5,6},{6,7},{7,4},{8,9},{9,10},{10,1... | collective-permute-start | bytes 196616 | tf_op jit(solution)/shard_map/ppermute | solution.py:38
  39.5 6.3 %collective-permute-start.10 = (bf16[144,256]{1,0:T(8,128)(2,1)S(1)}, bf16[144,256]{1,0:T(8,128)(2,1)S(1)}, u32[]{:S(2)}, u32[]{:S(2)}) collective-permute-start(bf16[144,256]{1,0:T(8,128)(2,1)S(1)} %get-tuple-element.81), channel_id=1, source_target_pairs={{0,1},{1,2},{2,3},{3,0},{4,5},{5,6},{6,7},{7,4},{8,9},{9,10},{10,1... | collective-permute-start | bytes 221192 | tf_op jit(solution)/shard_map/ppermute | solution.py:38
  42.1 3.8 %collective-permute-start.11 = (bf16[144,256]{1,0:T(8,128)(2,1)S(1)}, bf16[144,256]{1,0:T(8,128)(2,1)S(1)}, u32[]{:S(2)}, u32[]{:S(2)}) collective-permute-start(bf16[144,256]{1,0:T(8,128)(2,1)S(1)} %get-tuple-element.82), channel_id=1, source_target_pairs={{0,2},{1,3},{2,0},{3,1},{4,6},{5,7},{6,4},{7,5},{8,10},{9,11},{10,... | collective-permute-start | bytes 221192 | tf_op jit(solution)/shard_map/ppermute | solution.py:38
  42.1 4.0 %collective-permute-start.12 = (bf16[144,256]{1,0:T(8,128)(2,1)S(1)}, bf16[144,256]{1,0:T(8,128)(2,1)S(1)}, u32[]{:S(2)}, u32[]{:S(2)}) collective-permute-start(bf16[144,256]{1,0:T(8,128)(2,1)S(1)} %get-tuple-element.83), channel_id=1, source_target_pairs={{0,3},{1,0},{2,1},{3,2},{4,7},{5,4},{6,5},{7,6},{8,11},{9,8},{10,9... | collective-permute-start | bytes 221192 | tf_op jit(solution)/shard_map/ppermute | solution.py:38
  42.6 19.5 %collective-permute-start.13 = (bf16[4,128,256]{2,1,0:T(8,128)(2,1)S(1)}, bf16[4,128,256]{2,1,0:T(8,128)(2,1)S(1)}, u32[]{:S(2)}, u32[]{:S(2)}) collective-permute-start(bf16[4,128,256]{2,1,0:T(8,128)(2,1)S(1)} %get-tuple-element.90), channel_id=1, source_target_pairs={{1,0},{2,1},{3,2},{5,4},{6,5},{7,6},{9,8},{10,9},{11,10},{13,12},{... | collective-permute-start | bytes 786440 | tf_op jit(solution)/shard_map/ppermute | solution.py:33
  46.2 5.7 %collective-permute-start.16 = (bf16[144,256]{1,0:T(8,128)(2,1)S(1)}, bf16[144,256]{1,0:T(8,128)(2,1)S(1)}, u32[]{:S(2)}, u32[]{:S(2)}) collective-permute-start(bf16[144,256]{1,0:T(8,128)(2,1)S(1)} %gather.1.here_ref), channel_id=1, source_target_pairs={{0,20},{4,24},{8,28},{12,0},{16,4},{20,8},{24,12},{28,16},{1,21},{... | collective-permute-start | bytes 221192 | tf_op jit(solution)/shard_map/ppermute | solution.py:38
  48.3 4.2 %collective-permute-start.15 = (bf16[144,256]{1,0:T(8,128)(2,1)S(1)}, bf16[144,256]{1,0:T(8,128)(2,1)S(1)}, u32[]{:S(2)}, u32[]{:S(2)}) collective-permute-start(bf16[144,256]{1,0:T(8,128)(2,1)S(1)} %gather.1.here_ref), channel_id=1, source_target_pairs={{0,24},{4,28},{8,0},{12,4},{16,8},{20,12},{24,16},{28,20},{1,25},{... | collective-permute-start | bytes 221192 | tf_op jit(solution)/shard_map/ppermute | solution.py:38
  50.6 4.2 %collective-permute-start.14 = (bf16[144,256]{1,0:T(8,128)(2,1)S(1)}, bf16[144,256]{1,0:T(8,128)(2,1)S(1)}, u32[]{:S(2)}, u32[]{:S(2)}) collective-permute-start(bf16[144,256]{1,0:T(8,128)(2,1)S(1)} %gather.1.here_ref), channel_id=1, source_target_pairs={{0,28},{4,0},{8,4},{12,8},{16,12},{20,16},{24,20},{28,24},{1,29},{... | collective-permute-start | bytes 221192 | tf_op jit(solution)/shard_map/ppermute | solution.py:38
  55.5 6.6 %collective-permute-start.18 = (bf16[256,256]{1,0:T(8,128)(2,1)S(1)}, bf16[256,256]{1,0:T(8,128)(2,1)S(1)}, u32[]{:S(2)}, u32[]{:S(2)}) collective-permute-start(bf16[256,256]{1,0:T(8,128)(2,1)S(1)} %get-tuple-element.93), channel_id=1, source_target_pairs={{0,1},{1,2},{2,3},{3,0},{4,5},{5,6},{6,7},{7,4},{8,9},{9,10},{10,1... | collective-permute-start | bytes 393224 | tf_op jit(solution)/shard_map/ppermute | solution.py:38
  58.1 6.3 %collective-permute-start.19 = (bf16[256,256]{1,0:T(8,128)(2,1)S(1)}, bf16[256,256]{1,0:T(8,128)(2,1)S(1)}, u32[]{:S(2)}, u32[]{:S(2)}) collective-permute-start(bf16[256,256]{1,0:T(8,128)(2,1)S(1)} %get-tuple-element.94), channel_id=1, source_target_pairs={{0,2},{1,3},{2,0},{3,1},{4,6},{5,7},{6,4},{7,5},{8,10},{9,11},{10,... | collective-permute-start | bytes 393224 | tf_op jit(solution)/shard_map/ppermute | solution.py:38
  58.4 6.6 %collective-permute-start.20 = (bf16[256,256]{1,0:T(8,128)(2,1)S(1)}, bf16[256,256]{1,0:T(8,128)(2,1)S(1)}, u32[]{:S(2)}, u32[]{:S(2)}) collective-permute-start(bf16[256,256]{1,0:T(8,128)(2,1)S(1)} %get-tuple-element.95), channel_id=1, source_target_pairs={{0,3},{1,0},{2,1},{3,2},{4,7},{5,4},{6,5},{7,6},{8,11},{9,8},{10,9... | collective-permute-start | bytes 393224 | tf_op jit(solution)/shard_map/ppermute | solution.py:38
  58.6 3.5 %collective-permute-start.17 = (f32[8,128]{1,0:T(8,128)S(1)}, f32[8,128]{1,0:T(8,128)S(1)}, u32[]{:S(2)}, u32[]{:S(2)}) collective-permute-start(f32[8,128]{1,0:T(8,128)S(1)} %get-tuple-element.91.sink_ref), channel_id=1, source_target_pairs={{0,16},{4,20},{8,24},{12,28},{16,0},{20,4},{24,8},{28,12},{1,17},{... | collective-permute-start | bytes 12296 | tf_op jit(solution)/shard_map/ppermute | solution.py:38

commit v2 on v1

--- a/solution.py
+++ b/solution.py
@@ -73,6 +73,37 @@
         opening = opening | (start == position)
     has_tail = table[2 * branches + tok * BR_DEV] >= 0
     return alive, opening, jnp.logical_not(opening) | has_tail
+
+
+def plan_kernel(tok_count, blocks, blocks_here, table, plan_ref):
+    tok, head = lax.axis_index("tok"), lax.axis_index("head")
+    values = []
+    for distance in range(1, LAG + 1):
+        values += child_tail(table, tok, distance, tok_count, blocks)
+    parent = table[2 * tok_count * BR_DEV + tok * BR_DEV]
+    values.append(jnp.where(parent >= 0, tok - jnp.maximum(parent, 0) // BR_DEV, 1))
+    for block in range(blocks_here):
+        number = tok * blocks + head * blocks_here + block
+        values += block_state(table, tok, tok_count, number)
+    lane = lax.broadcasted_iota(jnp.int32, plan_ref.shape, 1)
+    plan = jnp.zeros(plan_ref.shape, jnp.int32)
+    for place, value in enumerate(values):
+        plan = jnp.where(lane == place, value.astype(jnp.int32), plan)
+    plan_ref[...] = plan
+
+
+def planned_tail(plan_ref, distance):
+    row = plan_ref[0:1, :]
+    return row[0, 2 * distance - 2] != 0, row[0, 2 * distance - 1]
+
+
+def planned_source(plan_ref):
+    return plan_ref[0:1, :][0, 2 * LAG]
+
+
+def planned_block(plan_ref, block):
+    row = plan_ref[0:1, :]
+    return tuple(row[0, 2 * LAG + 1 + 3 * block + place] for place in range(3))
 
 
 def take(ref, slot, width):
@@ -116,15 +147,15 @@
         halo_ref[pair] = jnp.concatenate([keys[last, lanes], values[last, lanes]], axis=1)
 
 
-def choose_kernel(tok_count, blocks, table, *refs):
+def choose_kernel(plan_ref, *refs):
     slots = len(refs) - LAG - 1
     slot_refs, out_refs, sink_ref = refs[:slots], refs[slots:-1], refs[-1]
-    tok, head = lax.axis_index("tok"), lax.axis_index("head")
+    head = lax.axis_index("head")
     rows = slot_refs[0].shape[0] - EXTRA
     blocks_here = rows // WINDOW
     heads = sink_ref.shape[0] // slots
     for distance, out_ref in zip(range(LAG, 0, -1), out_refs):
-        _, place = child_tail(table, tok, distance, tok_count, blocks)
+        _, place = planned_tail(plan_ref, distance)
         begin = pl.multiple_of(place % blocks_here * WINDOW, WINDOW)
         wanted = lax.rem(head - place // blocks_here + slots, slots)
         for step, slot_ref in enumerate(slot_refs):
@@ -140,11 +171,9 @@
         sink_ref[pl.ds(pl.multiple_of(source * heads, heads), heads), :] = turned[:heads]
 
 
-def arrive_kernel(tok_count, table, *refs):
-    tok = lax.axis_index("tok")
+def arrive_kernel(plan_ref, *refs):
     *in_refs, out_ref = refs
-    parent = table[2 * tok_count * BR_DEV + tok * BR_DEV]
-    mine = jnp.where(parent >= 0, tok - jnp.maximum(parent, 0) // BR_DEV, 1)
+    mine = planned_source(plan_ref)
     for distance, in_ref in zip(range(LAG, 0, -1), in_refs):
 
         @pl.when(mine == distance)
@@ -165,13 +194,14 @@
         copy.wait()
 
 
-def attend_kernel(tok_count, blocks_here, slots, steps, offset, pairs, joins, *refs):
+def attend_kernel(blocks_here, slots, steps, offset, pairs, joins, *refs):
     inputs, refs = refs[:7], refs[7:]
     tail_refs, refs = refs[: len(steps)], refs[len(steps) + joins :]
     outputs, refs = refs[:5], refs[5:]
     dtail_refs, refs = refs[: len(steps)], refs[len(steps) :]
     tails, *scratch = refs
     head = lax.axis_index("head")
+    states = [planned_block(inputs[0], block) for block in range(blocks_here)]
     for step, tail_ref in zip(steps, tail_refs):
         tails[lax.rem(head - step + slots, slots)] = tail_ref[...]
 
@@ -179,12 +209,16 @@
         pair = place // blocks_here
         if offset is not None:
             pair = lax.rem(head + pair + offset, PAIRS)
+        block = place % blocks_here
+        state = states[0]
+        for other in range(1, blocks_here):
+            state = [jnp.where(block == other, *two) for two in zip(states[other], state)]
         attend_block(
-            tok_count,
             blocks_here,
             slots,
             pair,
-            place % blocks_here,
+            block,
+            [value != 0 for value in state],
             inputs,
             outputs,
             tails,
@@ -197,15 +231,14 @@
 
 
 def attend_block(
-    tok_count, blocks_here, slots, pair, block, inputs, outputs, tails, dtails, scratch
+    blocks_here, slots, pair, block, state, inputs, outputs, tails, dtails, scratch
 ):
-    table, sink_ref, q_ref, g_ref, k_ref, v_ref, halo_ref = inputs
+    _, sink_ref, q_ref, g_ref, k_ref, v_ref, halo_ref = inputs
     o_ref, dq_ref, dk_ref, dv_ref, dhalo_ref = outputs
     tail_sum, sink_rows, prob2, slope2 = scratch
     per_slot = KV_HEADS // slots
-    tok, head = lax.axis_index("tok"), lax.axis_index("head")
-    number = (tok * lax.axis_size("head") + head) * blocks_here + block
-    alive, opening, prev_ok = block_state(table, tok, tok_count, number)
+    head = lax.axis_index("head")
+    alive, opening, prev_ok = state
     here = pl.ds(pl.multiple_of(block * WINDOW, WINDOW), WINDOW)
     before = pl.ds(pl.multiple_of(jnp.maximum(block - 1, 0) * WINDOW, WINDOW), WINDOW)
     first = block == 0
@@ -456,8 +489,8 @@
     out_ref[WINDOW:] = row_split(sink_row, (EXTRA, out_ref.shape[1]))
 
 
-def land_kernel(tok_count, blocks, table, here_ref, *refs):
-    tok, head = lax.axis_index("tok"), lax.axis_index("head")
+def land_kernel(blocks, plan_ref, here_ref, *refs):
+    head = lax.axis_index("head")
     in_refs, out_refs, sink_ref = refs[:LAG], refs[LAG:-1], refs[-1]
     slots = len(out_refs)
     blocks_here = blocks // slots
@@ -465,7 +498,7 @@
         out_ref[...] = jnp.zeros_like(out_ref)
     sink_row = row_join(here_ref[WINDOW:])
     for distance, in_ref in enumerate(in_refs, 1):
-        valid, place = child_tail(table, tok, distance, tok_count, blocks)
+        valid, place = planned_tail(plan_ref, distance)
         sink_row = sink_row + row_join(in_ref[WINDOW:])
         wanted = lax.rem(place // blocks_here - head + slots, slots)
         here = pl.ds(pl.multiple_of(place % blocks_here * WINDOW, WINDOW), WINDOW)
@@ -543,14 +576,24 @@
         name="pack",
     )(far(sink_logits), far(key_states), far(value_states))
     spread = swap(slots, "head")
+    halo = shift(halo_out, "head", 1)
+    plan = pl.pallas_call(
+        functools.partial(plan_kernel, tok_count, blocks, blocks_here),
+        out_shape=pltpu.VMEM((8, 128), jnp.int32),
+        in_specs=[SMEM],
+        out_specs=VMEM,
+        compiler_params=PARAMS,
+        name="plan",
+    )(table)
+    plan = close(plan)
     *chosen, sinks = pl.pallas_call(
-        functools.partial(choose_kernel, tok_count, blocks),
+        choose_kernel,
         out_shape=(shape((WINDOW, width)),) * LAG + (shape((KV_HEADS * GROUP, 128), F32),),
-        in_specs=[SMEM] + [VMEM] * head_count,
+        in_specs=[VMEM] * (1 + head_count),
         out_specs=(VMEM,) * (LAG + 1),
         compiler_params=PARAMS,
         name="choose",
-    )(table, *spread)
+    )(plan, *spread)
     arrived = [ring(chosen[LAG - s], "tok", s) for s in range(LAG, 0, -1)]
     queries, out_grad, _ = lax.optimization_barrier((queries, out_grad, sinks))
     near_queries, near_grad = pl.pallas_call(
@@ -566,16 +609,14 @@
         (*arrived, near_queries, near_grad)
     )
     quarter = pl.pallas_call(
-        functools.partial(arrive_kernel, tok_count),
+        arrive_kernel,
         out_shape=shape((WINDOW, width)),
-        in_specs=[SMEM] + [VMEM] * LAG,
+        in_specs=[VMEM] * (1 + LAG),
         out_specs=VMEM,
         compiler_params=PARAMS,
         name="arrive",
-    )(table, *arrived)
+    )(plan, *arrived)
     tails = swap([quarter] * head_count, "head")
-    halo_out, _ = lax.optimization_barrier((halo_out, quarter))
-    halo = shift(halo_out, "head", 1)
 
     def attend(steps, pairs, offset, halo, joined):
         inputs = (
@@ -592,7 +633,6 @@
         return pl.pallas_call(
             functools.partial(
                 attend_kernel,
-                tok_count,
                 blocks_here,
                 head_count,
                 steps,
@@ -608,7 +648,7 @@
                 pltpu.VMEM((PAIRS, WINDOW, 256), BF16),
             )
             + (shape((WINDOW + EXTRA, width)),) * len(steps),
-            in_specs=[SMEM] + [VMEM] * len(inputs),
+            in_specs=[VMEM] * (1 + len(inputs)),
             out_specs=(VMEM,) * (5 + len(steps)),
             scratch_shapes=[
                 pltpu.VMEM((head_count, WINDOW, width), BF16),
@@ -620,7 +660,7 @@
             input_output_aliases={base + place: place for place in range(len(joined))},
             compiler_params=PARAMS,
             name="attend",
-        )(table, *inputs)
+        )(plan, *inputs)
 
     if per_slot == 2:
         *joined, own_tail = attend((0,), 1, 0, spread[1], ())
@@ -639,27 +679,33 @@
         compiler_params=PARAMS,
         name="gather",
     )(*parts)
-    attended, query_grad, _ = lax.optimization_barrier((attended, query_grad, quarter_grad))
-    attended, query_grad = pl.pallas_call(
-        stage_kernel,
-        out_shape=(pltpu.HBM(queries.shape, BF16),) * 2,
-        in_specs=[VMEM] * 2,
-        out_specs=(HBM,) * 2,
-        scratch_shapes=[pltpu.SemaphoreType.DMA((2,))],
-        compiler_params=PARAMS,
-        name="flush",
-    )(close(attended), close(query_grad))
+    def flush(value):
+        return pl.pallas_call(
+            stage_kernel,
+            out_shape=pltpu.HBM(value.shape, BF16),
+            in_specs=[VMEM],
+            out_specs=HBM,
+            scratch_shapes=[pltpu.SemaphoreType.DMA((1,))],
+            compiler_params=PARAMS,
+            name="flush",
+        )(close(value))
+
     returned = [ring(quarter_grad, "tok", -s) for s in range(LAG, 0, -1)][::-1]
+    attended, _ = lax.optimization_barrier((attended, quarter_grad))
+    attended = flush(attended)
+    attended, *returned = lax.optimization_barrier((attended, *returned))
     halo_back = shift(dhalo, "head", -1)
     *landed, sink_near = pl.pallas_call(
-        functools.partial(land_kernel, tok_count, blocks),
+        functools.partial(land_kernel, blocks),
         out_shape=(shape((rows, width)),) * head_count + (shape((8, 128), F32),),
-        in_specs=[SMEM] + [VMEM] * (LAG + 1),
+        in_specs=[VMEM] * (LAG + 2),
         out_specs=(VMEM,) * (head_count + 1),
         compiler_params=PARAMS,
         name="land",
-    )(table, quarter_grad, *returned)
+    )(plan, quarter_grad, *returned)
     tails_back = swap(landed, "head")
+    query_grad, _ = lax.optimization_barrier((query_grad, sink_near))
+    query_grad = flush(query_grad)
     span = LAG + 1
     while 2 * span < tok_count:
         sink_near = sink_near + ring(sink_near, "tok", -span)

time: 66.7 us -> 62.3 us (0.934)
  waiting for transfers between devices: 13.4 us -> 10.8 us
  Pallas kernels: 23 us -> 22.2 us
    ppermute x19, waiting for transfers between devices: 13.4 us -> 10.8 us  [ring(): lax.ppermute(value, axis, [(source, (source + steps) % count) for source...]
    ppermute x19, starting transfers between devices: 21.3 us -> 20.2 us  [ring(): lax.ppermute(value, axis, [(source, (source + steps) % count) for source...]
    pallas_call x6 -> x8, Pallas kernels: 18.5 us -> 17.8 us  [the longest x2 13.5 us: attend(): pl.pallas_call(functools.partial(attend_kernel, blocks_here, head_count,...]
  transfers between devices with their start and end apart: 21 -> 21, of which waited for: 12 -> 10; matrix products, arithmetic and copies ran while one was open for 2% -> 2% of each run, Pallas kernels for 13% -> 16%
where the time goes in v2:
time: 62.3 us; the launch traced here: 62.1 us
  starting transfers between devices  26.8 us (43%)
  Pallas kernels  22.2 us (36%)
  waiting for transfers between devices  10.8 us (17%)
  between operations  0.81 us (1%)
  local copies, waits for them, and re-layouts  0.76 us (1%)
  other arithmetic  0.75 us (1%)
    ppermute x19, starting transfers between devices, ring(): lax.ppermute(value, axis, [(source, (source + steps) % count) for source...  20.2 us
    pallas_call x2, Pallas kernels, attend(): pl.pallas_call(functools.partial(attend_kernel, blocks_here, head_count,...  13.5 us
    ppermute x19, waiting for transfers between devices, ring(): lax.ppermute(value, axis, [(source, (source + steps) % count) for source...  10.8 us
    ppermute x2, starting transfers between devices, shift(): lax.ppermute(value, axis, [(source, source + steps) for source in range(l...  6.54 us
    pallas_call x2, Pallas kernels, flush(): pl.pallas_call(stage_kernel, out_shape=pltpu.HBM(value.shape, BF16), in_s...  2.65 us
    pallas_call x1, Pallas kernels, local(): pl.pallas_call(stage_kernel, out_shape=(pltpu.VMEM(queries.shape, BF16),)...  2.24 us
  transfers between devices with their start and end apart: 21, of which 10 were waited for; matrix products, arithmetic and copies ran while one was open for 2% of the time, Pallas kernels for 16%

profile of v2, /device:TPU:3, one launch (start us, length us, event | category | flops | bytes accessed | tf_op | source)
XLA Modules:
  0.0 62.1 jit_solution(7193419096468466635)
XLA Ops:
  0.6 1.2 %pack.1 = (bf16[272,256]{1,0:T(8,128)(2,1)S(1)}, bf16[272,256]{1,0:T(8,128)(2,1)S(1)}, bf16[272,256]{1,0:T(8,128)(2,1)S(1)}, bf16[272,256]{1,0:T(8,128)(2,1)S(1)...) custom-call(f32[16]{0:T(128)} %sink_hbm.1, ...), custom_call_target="tpu_custom_call" | custom-call | tf_op jit(solution)/shard_map/pack/pallas_call | solution.py:564
  1.8 1.9 %collective-permute-start = (bf16[272,256]{1,0:T(8,128)(2,1)S(1)}, bf16[272,256]{1,0:T(8,128)(2,1)S(1)}, u32[]{:S(2)}, u32[]{:S(2)}) collective-permute-start(bf16[272,256]{1,0:T(8,128)(2,1)S(1)} %get-tuple-element.54), channel_id=1, source_target_pairs={{0,1},{1,2},{2,3},{3,0},{4,5},{5,6},{6,7},{7,4},{8,9},{9,10},{10,1... | collective-permute-start | bytes 417800 | tf_op jit(solution)/shard_map/ppermute | solution.py:38
  4.1 3.4 %collective-permute-start.6 = (bf16[4,128,256]{2,1,0:T(8,128)(2,1)S(1)}, bf16[4,128,256]{2,1,0:T(8,128)(2,1)S(1)}, u32[]{:S(2)}, u32[]{:S(2)}) collective-permute-start(bf16[4,128,256]{2,1,0:T(8,128)(2,1)S(1)} %get-tuple-element.69), channel_id=1, source_target_pairs={{0,1},{1,2},{2,3},{4,5},{5,6},{6,7},{8,9},{9,10},{10,11},{12,13},{... | collective-permute-start | bytes 786440 | tf_op jit(solution)/shard_map/ppermute | solution.py:33
  11.3 2.3 %collective-permute-start.3 = (bf16[128,256]{1,0:T(8,128)(2,1)S(1)}, bf16[128,256]{1,0:T(8,128)(2,1)S(1)}, u32[]{:S(2)}, u32[]{:S(2)}) collective-permute-start(bf16[128,256]{1,0:T(8,128)(2,1)S(1)} %get-tuple-element.58), channel_id=1, source_target_pairs={{0,12},{4,16},{8,20},{12,24},{16,28},{20,0},{24,4},{28,8},{1,13},{... | collective-permute-start | bytes 196616 | tf_op jit(solution)/shard_map/ppermute | solution.py:38
  13.6 1.3 %collective-permute-start.4 = (bf16[128,256]{1,0:T(8,128)(2,1)S(1)}, bf16[128,256]{1,0:T(8,128)(2,1)S(1)}, u32[]{:S(2)}, u32[]{:S(2)}) collective-permute-start(bf16[128,256]{1,0:T(8,128)(2,1)S(1)} %get-tuple-element.59), channel_id=1, source_target_pairs={{0,8},{4,12},{8,16},{12,20},{16,24},{20,28},{24,0},{28,4},{1,9},{5... | collective-permute-start | bytes 196616 | tf_op jit(solution)/shard_map/ppermute | solution.py:38
  14.9 1.2 %collective-permute-start.5 = (bf16[128,256]{1,0:T(8,128)(2,1)S(1)}, bf16[128,256]{1,0:T(8,128)(2,1)S(1)}, u32[]{:S(2)}, u32[]{:S(2)}) collective-permute-start(bf16[128,256]{1,0:T(8,128)(2,1)S(1)} %get-tuple-element.60), channel_id=1, source_target_pairs={{0,4},{4,8},{8,12},{12,16},{16,20},{20,24},{24,28},{28,0},{1,5},{5... | collective-permute-start | bytes 196616 | tf_op jit(solution)/shard_map/ppermute | solution.py:38
  16.1 2.2 %stage.1 = (bf16[256,4096]{1,0:T(8,128)(2,1)S(1)}, bf16[256,4096]{1,0:T(8,128)(2,1)S(1)}) custom-call(bf16[256,4096]{1,0:T(8,128)(2,1)} %refs_0_, bf16[256,4096]{1,0:T(8,128)(2,1)} %refs_1_), custom_call_target="tpu_custom_call" | custom-call | tf_op jit(solution)/shard_map/stage/pallas_call | solution.py:599
  18.8 2.3 %collective-permute-start.9 = (bf16[128,256]{1,0:T(8,128)(2,1)S(1)}, bf16[128,256]{1,0:T(8,128)(2,1)S(1)}, u32[]{:S(2)}, u32[]{:S(2)}) collective-permute-start(bf16[128,256]{1,0:T(8,128)(2,1)S(1)} %arrive.1.refs_7_), channel_id=1, source_target_pairs={{0,3},{1,0},{2,1},{3,2},{4,7},{5,4},{6,5},{7,6},{8,11},{9,8},{10,9... | collective-permute-start | bytes 196616 | tf_op jit(solution)/shard_map/ppermute | solution.py:38
  21.6 1.9 %collective-permute-start.7 = (bf16[128,256]{1,0:T(8,128)(2,1)S(1)}, bf16[128,256]{1,0:T(8,128)(2,1)S(1)}, u32[]{:S(2)}, u32[]{:S(2)}) collective-permute-start(bf16[128,256]{1,0:T(8,128)(2,1)S(1)} %arrive.1.refs_7_), channel_id=1, source_target_pairs={{0,1},{1,2},{2,3},{3,0},{4,5},{5,6},{6,7},{7,4},{8,9},{9,10},{10,1... | collective-permute-start | bytes 196616 | tf_op jit(solution)/shard_map/ppermute | solution.py:38
  23.5 3.4 %attend.2 = (bf16[256,4096]{1,0:T(8,128)(2,1)S(1)}, bf16[256,4096]{1,0:T(8,128)(2,1)S(1)}, f32[256,512]{1,0:T(8,128)S(1)}, f32[256,512]{1,0:T(8,128)S(1)}, bf16[...) custom-call(s32[8,128]{1,0:T(8,128)S(1)} %plan.1.plan_ref.refs_0_, f32[64,128]{1,0:T(8,128)S(1)} %get-tuple-element.57.refs_1_, ...), custom_call_target="tpu_custom_call" | custom-call | tf_op jit(solution)/shard_map/attend/pallas_call | solution.py:633
  27.0 10.1 %attend.3 = (bf16[256,4096]{1,0:T(8,128)(2,1)S(1)}, bf16[256,4096]{1,0:T(8,128)(2,1)S(1)}, f32[256,512]{1,0:T(8,128)S(1)}, f32[256,512]{1,0:T(8,128)S(1)}, bf16[...) custom-call(s32[8,128]{1,0:T(8,128)S(1)} %plan.1.plan_ref.refs_0_, ...), custom_call_target="tpu_custom_call", output_to_operand_aliasing={{0}: (10, {}), {1}: (11, {}), {2}: (12, {}), {3}: (13, {}),... | custom-call | tf_op jit(solution)/shard_map/attend/pallas_call | solution.py:633
  37.8 3.1 %collective-permute-start.16 = (bf16[4,128,256]{2,1,0:T(8,128)(2,1)S(1)}, bf16[4,128,256]{2,1,0:T(8,128)(2,1)S(1)}, u32[]{:S(2)}, u32[]{:S(2)}) collective-permute-start(bf16[4,128,256]{2,1,0:T(8,128)(2,1)S(1)} %get-tuple-element.93), channel_id=1, source_target_pairs={{1,0},{2,1},{3,2},{5,4},{6,5},{7,6},{9,8},{10,9},{11,10},{13,12},{... | collective-permute-start | bytes 786440 | tf_op jit(solution)/shard_map/ppermute | solution.py:33
  41.0 1.1 %collective-permute-done.12.refs_3_ = bf16[144,256]{1,0:T(8,128)(2,1)S(1)} collective-permute-done((bf16[144,256]{1,0:T(8,128)(2,1)S(1)}, bf16[144,256]{1,0:T(8,128)(2,1)S(1)}, u32[]{:S(2)}, u32[]{:S(2)}) %collective-permute-start.12) | collective-permute-done | bytes 73760 | tf_op jit(solution)/shard_map/ppermute | solution.py:38
  42.1 1.9 %collective-permute-start.15 = (bf16[144,256]{1,0:T(8,128)(2,1)S(1)}, bf16[144,256]{1,0:T(8,128)(2,1)S(1)}, u32[]{:S(2)}, u32[]{:S(2)}) collective-permute-start(bf16[144,256]{1,0:T(8,128)(2,1)S(1)} %gather.1.here_ref), channel_id=1, source_target_pairs={{0,20},{4,24},{8,28},{12,0},{16,4},{20,8},{24,12},{28,16},{1,21},{... | collective-permute-start | bytes 221192 | tf_op jit(solution)/shard_map/ppermute | solution.py:38
  44.0 3.1 %collective-permute-start.14 = (bf16[144,256]{1,0:T(8,128)(2,1)S(1)}, bf16[144,256]{1,0:T(8,128)(2,1)S(1)}, u32[]{:S(2)}, u32[]{:S(2)}) collective-permute-start(bf16[144,256]{1,0:T(8,128)(2,1)S(1)} %gather.1.here_ref), channel_id=1, source_target_pairs={{0,24},{4,28},{8,0},{12,4},{16,8},{20,12},{24,16},{28,20},{1,25},{... | collective-permute-start | bytes 221192 | tf_op jit(solution)/shard_map/ppermute | solution.py:38
  47.1 1.3 %flush.2 = bf16[256,4096]{1,0:T(8,128)(2,1)} custom-call(bf16[256,4096]{1,0:T(8,128)(2,1)S(1)} %get-tuple-element.83.refs_0_), custom_call_target="tpu_custom_call" | custom-call | tf_op jit(solution)/shard_map/flush/pallas_call | solution.py:683
  48.4 1.7 %collective-permute-done.15.refs_2_ = bf16[144,256]{1,0:T(8,128)(2,1)S(1)} collective-permute-done((bf16[144,256]{1,0:T(8,128)(2,1)S(1)}, bf16[144,256]{1,0:T(8,128)(2,1)S(1)}, u32[]{:S(2)}, u32[]{:S(2)}) %collective-permute-start.15) | collective-permute-done | bytes 73760 | tf_op jit(solution)/shard_map/ppermute | solution.py:38
  50.1 1.5 %collective-permute-done.13.refs_0_ = bf16[144,256]{1,0:T(8,128)(2,1)S(1)} collective-permute-done((bf16[144,256]{1,0:T(8,128)(2,1)S(1)}, bf16[144,256]{1,0:T(8,128)(2,1)S(1)}, u32[]{:S(2)}, u32[]{:S(2)}) %collective-permute-start.13) | collective-permute-done | bytes 73760 | tf_op jit(solution)/shard_map/ppermute | solution.py:38
  52.0 1.4 %collective-permute-start.18 = (bf16[256,256]{1,0:T(8,128)(2,1)S(1)}, bf16[256,256]{1,0:T(8,128)(2,1)S(1)}, u32[]{:S(2)}, u32[]{:S(2)}) collective-permute-start(bf16[256,256]{1,0:T(8,128)(2,1)S(1)} %get-tuple-element.95), channel_id=1, source_target_pairs={{0,1},{1,2},{2,3},{3,0},{4,5},{5,6},{6,7},{7,4},{8,9},{9,10},{10,1... | collective-permute-start | bytes 393224 | tf_op jit(solution)/shard_map/ppermute | solution.py:38
  53.4 1.1 %collective-permute-start.19 = (bf16[256,256]{1,0:T(8,128)(2,1)S(1)}, bf16[256,256]{1,0:T(8,128)(2,1)S(1)}, u32[]{:S(2)}, u32[]{:S(2)}) collective-permute-start(bf16[256,256]{1,0:T(8,128)(2,1)S(1)} %get-tuple-element.96), channel_id=1, source_target_pairs={{0,2},{1,3},{2,0},{3,1},{4,6},{5,7},{6,4},{7,5},{8,10},{9,11},{10,... | collective-permute-start | bytes 393224 | tf_op jit(solution)/shard_map/ppermute | solution.py:38
  54.6 1.3 %flush.3 = bf16[256,4096]{1,0:T(8,128)(2,1)} custom-call(bf16[256,4096]{1,0:T(8,128)(2,1)S(1)} %get-tuple-element.90.refs_0_), custom_call_target="tpu_custom_call" | custom-call | tf_op jit(solution)/shard_map/flush/pallas_call | solution.py:683
  55.9 1.9 %collective-permute-done.17.far_ref = f32[8,128]{1,0:T(8,128)S(1)} collective-permute-done((f32[8,128]{1,0:T(8,128)S(1)}, f32[8,128]{1,0:T(8,128)S(1)}, u32[]{:S(2)}, u32[]{:S(2)}) %collective-permute-start.17) | collective-permute-done | bytes 4128 | tf_op jit(solution)/shard_map/ppermute | solution.py:38
  57.9 2.6 %collective-permute-done.19.refs_2_ = bf16[256,256]{1,0:T(8,128)(2,1)S(1)} collective-permute-done((bf16[256,256]{1,0:T(8,128)(2,1)S(1)}, bf16[256,256]{1,0:T(8,128)(2,1)S(1)}, u32[]{:S(2)}, u32[]{:S(2)}) %collective-permute-start.19) | collective-permute-done | bytes 131104 | tf_op jit(solution)/shard_map/ppermute | solution.py:38
  61.1 1.0 %total.1 = (bf16[256,512]{1,0:T(8,128)(2,1)}, bf16[256,512]{1,0:T(8,128)(2,1)}, f32[16]{0:T(128)}) custom-call(f32[256,512]{1,0:T(8,128)S(1)} %get-tuple-element.91.dk_ref, f32[256,512]{1,0:T(8,128)S(1)} %get-tuple-element.92.dv_ref, bf16[4,128,256]{2,1,0:T(8,128)(2,1)S(1)} %collective-permute-done.16.halo_ref, f32[8,128]{1,0:T(8,128)S(1)} %get-tuple-element.89.sink_ref, ...), custom_call_target="tpu_custom_call" | custom-call | tf_op jit(solution)/shard_map/total/pallas_call | solution.py:714
  (32 shorter events, 7.1 us)
Async XLA Ops:
  1.8 7.9 %collective-permute-start = (bf16[272,256]{1,0:T(8,128)(2,1)S(1)}, bf16[272,256]{1,0:T(8,128)(2,1)S(1)}, u32[]{:S(2)}, u32[]{:S(2)}) collective-permute-start(bf16[272,256]{1,0:T(8,128)(2,1)S(1)} %get-tuple-element.54), channel_id=1, source_target_pairs={{0,1},{1,2},{2,3},{3,0},{4,5},{5,6},{6,7},{7,4},{8,9},{9,10},{10,1... | collective-permute-start | bytes 417800 | tf_op jit(solution)/shard_map/ppermute | solution.py:38
  3.7 6.5 %collective-permute-start.1 = (bf16[272,256]{1,0:T(8,128)(2,1)S(1)}, bf16[272,256]{1,0:T(8,128)(2,1)S(1)}, u32[]{:S(2)}, u32[]{:S(2)}) collective-permute-start(bf16[272,256]{1,0:T(8,128)(2,1)S(1)} %get-tuple-element.55), channel_id=1, source_target_pairs={{0,2},{1,3},{2,0},{3,1},{4,6},{5,7},{6,4},{7,5},{8,10},{9,11},{10,... | collective-permute-start | bytes 417800 | tf_op jit(solution)/shard_map/ppermute | solution.py:38
  3.9 6.9 %collective-permute-start.2 = (bf16[272,256]{1,0:T(8,128)(2,1)S(1)}, bf16[272,256]{1,0:T(8,128)(2,1)S(1)}, u32[]{:S(2)}, u32[]{:S(2)}) collective-permute-start(bf16[272,256]{1,0:T(8,128)(2,1)S(1)} %get-tuple-element.56), channel_id=1, source_target_pairs={{0,3},{1,0},{2,1},{3,2},{4,7},{5,4},{6,5},{7,6},{8,11},{9,8},{10,9... | collective-permute-start | bytes 417800 | tf_op jit(solution)/shard_map/ppermute | solution.py:38
  4.1 22.8 %collective-permute-start.6 = (bf16[4,128,256]{2,1,0:T(8,128)(2,1)S(1)}, bf16[4,128,256]{2,1,0:T(8,128)(2,1)S(1)}, u32[]{:S(2)}, u32[]{:S(2)}) collective-permute-start(bf16[4,128,256]{2,1,0:T(8,128)(2,1)S(1)} %get-tuple-element.69), channel_id=1, source_target_pairs={{0,1},{1,2},{2,3},{4,5},{5,6},{6,7},{8,9},{9,10},{10,11},{12,13},{... | collective-permute-start | bytes 786440 | tf_op jit(solution)/shard_map/ppermute | solution.py:33
  11.3 7.1 %collective-permute-start.3 = (bf16[128,256]{1,0:T(8,128)(2,1)S(1)}, bf16[128,256]{1,0:T(8,128)(2,1)S(1)}, u32[]{:S(2)}, u32[]{:S(2)}) collective-permute-start(bf16[128,256]{1,0:T(8,128)(2,1)S(1)} %get-tuple-element.58), channel_id=1, source_target_pairs={{0,12},{4,16},{8,20},{12,24},{16,28},{20,0},{24,4},{28,8},{1,13},{... | collective-permute-start | bytes 196616 | tf_op jit(solution)/shard_map/ppermute | solution.py:38
  13.6 4.9 %collective-permute-start.4 = (bf16[128,256]{1,0:T(8,128)(2,1)S(1)}, bf16[128,256]{1,0:T(8,128)(2,1)S(1)}, u32[]{:S(2)}, u32[]{:S(2)}) collective-permute-start(bf16[128,256]{1,0:T(8,128)(2,1)S(1)} %get-tuple-element.59), channel_id=1, source_target_pairs={{0,8},{4,12},{8,16},{12,20},{16,24},{20,28},{24,0},{28,4},{1,9},{5... | collective-permute-start | bytes 196616 | tf_op jit(solution)/shard_map/ppermute | solution.py:38
  14.9 3.7 %collective-permute-start.5 = (bf16[128,256]{1,0:T(8,128)(2,1)S(1)}, bf16[128,256]{1,0:T(8,128)(2,1)S(1)}, u32[]{:S(2)}, u32[]{:S(2)}) collective-permute-start(bf16[128,256]{1,0:T(8,128)(2,1)S(1)} %get-tuple-element.60), channel_id=1, source_target_pairs={{0,4},{4,8},{8,12},{12,16},{16,20},{20,24},{24,28},{28,0},{1,5},{5... | collective-permute-start | bytes 196616 | tf_op jit(solution)/shard_map/ppermute | solution.py:38
  18.8 8.2 %collective-permute-start.9 = (bf16[128,256]{1,0:T(8,128)(2,1)S(1)}, bf16[128,256]{1,0:T(8,128)(2,1)S(1)}, u32[]{:S(2)}, u32[]{:S(2)}) collective-permute-start(bf16[128,256]{1,0:T(8,128)(2,1)S(1)} %arrive.1.refs_7_), channel_id=1, source_target_pairs={{0,3},{1,0},{2,1},{3,2},{4,7},{5,4},{6,5},{7,6},{8,11},{9,8},{10,9... | collective-permute-start | bytes 196616 | tf_op jit(solution)/shard_map/ppermute | solution.py:38
  21.0 5.9 %collective-permute-start.8 = (bf16[128,256]{1,0:T(8,128)(2,1)S(1)}, bf16[128,256]{1,0:T(8,128)(2,1)S(1)}, u32[]{:S(2)}, u32[]{:S(2)}) collective-permute-start(bf16[128,256]{1,0:T(8,128)(2,1)S(1)} %arrive.1.refs_7_), channel_id=1, source_target_pairs={{0,2},{1,3},{2,0},{3,1},{4,6},{5,7},{6,4},{7,5},{8,10},{9,11},{10,... | collective-permute-start | bytes 196616 | tf_op jit(solution)/shard_map/ppermute | solution.py:38
  21.6 5.4 %collective-permute-start.7 = (bf16[128,256]{1,0:T(8,128)(2,1)S(1)}, bf16[128,256]{1,0:T(8,128)(2,1)S(1)}, u32[]{:S(2)}, u32[]{:S(2)}) collective-permute-start(bf16[128,256]{1,0:T(8,128)(2,1)S(1)} %arrive.1.refs_7_), channel_id=1, source_target_pairs={{0,1},{1,2},{2,3},{3,0},{4,5},{5,6},{6,7},{7,4},{8,9},{9,10},{10,1... | collective-permute-start | bytes 196616 | tf_op jit(solution)/shard_map/ppermute | solution.py:38
  37.0 3.9 %collective-permute-start.10 = (bf16[144,256]{1,0:T(8,128)(2,1)S(1)}, bf16[144,256]{1,0:T(8,128)(2,1)S(1)}, u32[]{:S(2)}, u32[]{:S(2)}) collective-permute-start(bf16[144,256]{1,0:T(8,128)(2,1)S(1)} %get-tuple-element.80), channel_id=1, source_target_pairs={{0,1},{1,2},{2,3},{3,0},{4,5},{5,6},{6,7},{7,4},{8,9},{9,10},{10,1... | collective-permute-start | bytes 221192 | tf_op jit(solution)/shard_map/ppermute | solution.py:38
  37.1 3.8 %collective-permute-start.11 = (bf16[144,256]{1,0:T(8,128)(2,1)S(1)}, bf16[144,256]{1,0:T(8,128)(2,1)S(1)}, u32[]{:S(2)}, u32[]{:S(2)}) collective-permute-start(bf16[144,256]{1,0:T(8,128)(2,1)S(1)} %get-tuple-element.81), channel_id=1, source_target_pairs={{0,2},{1,3},{2,0},{3,1},{4,6},{5,7},{6,4},{7,5},{8,10},{9,11},{10,... | collective-permute-start | bytes 221192 | tf_op jit(solution)/shard_map/ppermute | solution.py:38
  37.8 4.3 %collective-permute-start.12 = (bf16[144,256]{1,0:T(8,128)(2,1)S(1)}, bf16[144,256]{1,0:T(8,128)(2,1)S(1)}, u32[]{:S(2)}, u32[]{:S(2)}) collective-permute-start(bf16[144,256]{1,0:T(8,128)(2,1)S(1)} %get-tuple-element.82), channel_id=1, source_target_pairs={{0,3},{1,0},{2,1},{3,2},{4,7},{5,4},{6,5},{7,6},{8,11},{9,8},{10,9... | collective-permute-start | bytes 221192 | tf_op jit(solution)/shard_map/ppermute | solution.py:38
  37.8 20.1 %collective-permute-start.16 = (bf16[4,128,256]{2,1,0:T(8,128)(2,1)S(1)}, bf16[4,128,256]{2,1,0:T(8,128)(2,1)S(1)}, u32[]{:S(2)}, u32[]{:S(2)}) collective-permute-start(bf16[4,128,256]{2,1,0:T(8,128)(2,1)S(1)} %get-tuple-element.93), channel_id=1, source_target_pairs={{1,0},{2,1},{3,2},{5,4},{6,5},{7,6},{9,8},{10,9},{11,10},{13,12},{... | collective-permute-start | bytes 786440 | tf_op jit(solution)/shard_map/ppermute | solution.py:33
  42.1 8.0 %collective-permute-start.15 = (bf16[144,256]{1,0:T(8,128)(2,1)S(1)}, bf16[144,256]{1,0:T(8,128)(2,1)S(1)}, u32[]{:S(2)}, u32[]{:S(2)}) collective-permute-start(bf16[144,256]{1,0:T(8,128)(2,1)S(1)} %gather.1.here_ref), channel_id=1, source_target_pairs={{0,20},{4,24},{8,28},{12,0},{16,4},{20,8},{24,12},{28,16},{1,21},{... | collective-permute-start | bytes 221192 | tf_op jit(solution)/shard_map/ppermute | solution.py:38
  44.0 6.1 %collective-permute-start.14 = (bf16[144,256]{1,0:T(8,128)(2,1)S(1)}, bf16[144,256]{1,0:T(8,128)(2,1)S(1)}, u32[]{:S(2)}, u32[]{:S(2)}) collective-permute-start(bf16[144,256]{1,0:T(8,128)(2,1)S(1)} %gather.1.here_ref), channel_id=1, source_target_pairs={{0,24},{4,28},{8,0},{12,4},{16,8},{20,12},{24,16},{28,20},{1,25},{... | collective-permute-start | bytes 221192 | tf_op jit(solution)/shard_map/ppermute | solution.py:38
  47.1 4.5 %collective-permute-start.13 = (bf16[144,256]{1,0:T(8,128)(2,1)S(1)}, bf16[144,256]{1,0:T(8,128)(2,1)S(1)}, u32[]{:S(2)}, u32[]{:S(2)}) collective-permute-start(bf16[144,256]{1,0:T(8,128)(2,1)S(1)} %gather.1.here_ref), channel_id=1, source_target_pairs={{0,28},{4,0},{8,4},{12,8},{16,12},{20,16},{24,20},{28,24},{1,29},{... | collective-permute-start | bytes 221192 | tf_op jit(solution)/shard_map/ppermute | solution.py:38
  52.0 5.9 %collective-permute-start.18 = (bf16[256,256]{1,0:T(8,128)(2,1)S(1)}, bf16[256,256]{1,0:T(8,128)(2,1)S(1)}, u32[]{:S(2)}, u32[]{:S(2)}) collective-permute-start(bf16[256,256]{1,0:T(8,128)(2,1)S(1)} %get-tuple-element.95), channel_id=1, source_target_pairs={{0,1},{1,2},{2,3},{3,0},{4,5},{5,6},{6,7},{7,4},{8,9},{9,10},{10,1... | collective-permute-start | bytes 393224 | tf_op jit(solution)/shard_map/ppermute | solution.py:38
  53.4 7.0 %collective-permute-start.19 = (bf16[256,256]{1,0:T(8,128)(2,1)S(1)}, bf16[256,256]{1,0:T(8,128)(2,1)S(1)}, u32[]{:S(2)}, u32[]{:S(2)}) collective-permute-start(bf16[256,256]{1,0:T(8,128)(2,1)S(1)} %get-tuple-element.96), channel_id=1, source_target_pairs={{0,2},{1,3},{2,0},{3,1},{4,6},{5,7},{6,4},{7,5},{8,10},{9,11},{10,... | collective-permute-start | bytes 393224 | tf_op jit(solution)/shard_map/ppermute | solution.py:38
  54.5 6.6 %collective-permute-start.20 = (bf16[256,256]{1,0:T(8,128)(2,1)S(1)}, bf16[256,256]{1,0:T(8,128)(2,1)S(1)}, u32[]{:S(2)}, u32[]{:S(2)}) collective-permute-start(bf16[256,256]{1,0:T(8,128)(2,1)S(1)} %get-tuple-element.97), channel_id=1, source_target_pairs={{0,3},{1,0},{2,1},{3,2},{4,7},{5,4},{6,5},{7,6},{8,11},{9,8},{10,9... | collective-permute-start | bytes 393224 | tf_op jit(solution)/shard_map/ppermute | solution.py:38
  54.5 3.4 %collective-permute-start.17 = (f32[8,128]{1,0:T(8,128)S(1)}, f32[8,128]{1,0:T(8,128)S(1)}, u32[]{:S(2)}, u32[]{:S(2)}) collective-permute-start(f32[8,128]{1,0:T(8,128)S(1)} %get-tuple-element.89.sink_ref), channel_id=1, source_target_pairs={{0,16},{4,20},{8,24},{12,28},{16,0},{20,4},{24,8},{28,12},{1,17},{... | collective-permute-start | bytes 12296 | tf_op jit(solution)/shard_map/ppermute | solution.py:38

commit v3 on v2

--- a/solution.py
+++ b/solution.py
@@ -17,7 +17,6 @@
 PAIRS = KV_HEADS // 2
 FACTOR = 0.125
 LOW = -1e30
-EXTRA = 16
 BF16 = jnp.bfloat16
 F32 = jnp.float32
 
@@ -38,18 +37,22 @@
     return lax.ppermute(value, axis, [(source, (source + steps) % count) for source in range(count)])
 
 
-def row_split(row, dims):
+def with_row(tile, row):
     high = row.astype(BF16).astype(F32)
     middle = (row - high).astype(BF16).astype(F32)
     low = row - high - middle
-    place = lax.broadcasted_iota(jnp.int32, dims, 0)
-    rest = jnp.where(place == 2, low, 0.0)
-    return jnp.where(place == 0, high, jnp.where(place == 1, middle, rest)).astype(BF16)
-
-
-def row_join(rows):
-    rows = rows.astype(F32)
-    return rows[0:1] + rows[1:2] + rows[2:3]
+    packed = high + pltpu.roll(middle, 32, 1) + pltpu.roll(low, 64, 1)
+    place = lax.broadcasted_iota(jnp.int32, (16, 128), 0)
+    top = jnp.where(place == 0, packed, tile[:16, :128].astype(F32)).astype(BF16)
+    if tile.shape[1] > 128:
+        top = jnp.concatenate([top, tile[:16, 128:]], axis=1)
+    return jnp.concatenate([top, tile[16:]], axis=0)
+
+
+def row_join(top):
+    packed = top[0:1, :128].astype(F32)
+    row = packed + pltpu.roll(packed, 96, 1) + pltpu.roll(packed, 64, 1)
+    return jnp.where(lax.broadcasted_iota(jnp.int32, (1, 128), 1) < 32, row, 0.0)
 
 
 def child_tail(table, tok, distance, tok_count, blocks):
@@ -130,17 +133,14 @@
     slots, rows = len(slot_refs), keys.shape[0]
     head = lax.axis_index("head")
     width = KV_HEADS * HEAD_DIM // slots
-    lane = lax.broadcasted_iota(jnp.int32, (1, 2 * width), 1)
-    sink_row = jnp.zeros((1, 2 * width), F32)
+    lane = lax.broadcasted_iota(jnp.int32, (1, 128), 1)
+    sink_row = jnp.zeros((1, 128), F32)
     for place in range(sinks.shape[0]):
         sink_row = jnp.where(lane == place, sinks[place], sink_row)
-    extra = row_split(sink_row, (EXTRA, 2 * width))
     for step, slot_ref in enumerate(slot_refs):
         slot = lax.rem(head + step, slots)
-        slot_ref[:rows] = jnp.concatenate(
-            [take(keys, slot, width), take(values, slot, width)], axis=1
-        )
-        slot_ref[rows:] = extra
+        both = jnp.concatenate([take(keys, slot, width), take(values, slot, width)], axis=1)
+        slot_ref[...] = with_row(both, sink_row)
     for pair in range(PAIRS):
         lanes = slice(pair * 128, (pair + 1) * 128)
         last = slice(rows - WINDOW, rows)
@@ -151,7 +151,7 @@
     slots = len(refs) - LAG - 1
     slot_refs, out_refs, sink_ref = refs[:slots], refs[slots:-1], refs[-1]
     head = lax.axis_index("head")
-    rows = slot_refs[0].shape[0] - EXTRA
+    rows = slot_refs[0].shape[0]
     blocks_here = rows // WINDOW
     heads = sink_ref.shape[0] // slots
     for distance, out_ref in zip(range(LAG, 0, -1), out_refs):
@@ -166,7 +166,7 @@
 
     for step, slot_ref in enumerate(slot_refs):
         source = lax.rem(head - step + slots, slots)
-        sink_row = row_join(slot_ref[rows:, :])[:, :128]
+        sink_row = row_join(slot_ref[:16])
         turned = jnp.broadcast_to(sink_row, (128, 128)).T
         sink_ref[pl.ds(pl.multiple_of(source * heads, heads), heads), :] = turned[:heads]
 
@@ -265,8 +265,7 @@
     @pl.when(alive)
     def _():
         if len(halo_ref.shape) == 2:
-            last = halo_ref.shape[0] - EXTRA
-            halo = halo_ref[last - WINDOW : last]
+            halo = halo_ref[halo_ref.shape[0] - WINDOW :]
         else:
             halo = halo_ref[pair]
         if per_slot == 2:
@@ -467,26 +466,22 @@
             rows = sink_rows[part * heads : (part + 1) * heads]
             rows = jnp.concatenate([rows, jnp.zeros((128 - heads, WINDOW), F32)], axis=0)
             sink_row = jnp.sum(rows.T, axis=0, keepdims=True)
-            if width > 128:
-                sink_row = jnp.concatenate([sink_row, jnp.zeros((1, width - 128), F32)], axis=1)
-            extra = row_split(sink_row, (EXTRA, width))
+            tail = with_row(tail, sink_row)
             wanted = lax.rem(pair * (2 // per_slot) + part - head + slots, slots)
             for step, dtail_ref in dtails:
 
                 @pl.when(wanted == step)
-                def _(dtail_ref=dtail_ref, tail=tail, extra=extra):
-                    dtail_ref[:WINDOW] = tail
-                    dtail_ref[WINDOW:] = extra
+                def _(dtail_ref=dtail_ref, tail=tail):
+                    dtail_ref[...] = tail
 
 
 def gather_kernel(*refs):
     *in_refs, out_ref = refs
     total, sink_row = 0.0, 0.0
     for in_ref in in_refs:
-        total = total + in_ref[:WINDOW].astype(F32)
-        sink_row = sink_row + row_join(in_ref[WINDOW:])
-    out_ref[:WINDOW] = total.astype(BF16)
-    out_ref[WINDOW:] = row_split(sink_row, (EXTRA, out_ref.shape[1]))
+        total = total + in_ref[...].astype(F32)
+        sink_row = sink_row + row_join(in_ref[:16])
+    out_ref[...] = with_row(total.astype(BF16), sink_row)
 
 
 def land_kernel(blocks, plan_ref, here_ref, *refs):
@@ -496,20 +491,21 @@
     blocks_here = blocks // slots
     for out_ref in out_refs:
         out_ref[...] = jnp.zeros_like(out_ref)
-    sink_row = row_join(here_ref[WINDOW:])
+    sink_row = row_join(here_ref[:16])
+    seen = lax.broadcasted_iota(jnp.int32, here_ref.shape, 0) > 0
     for distance, in_ref in enumerate(in_refs, 1):
         valid, place = planned_tail(plan_ref, distance)
-        sink_row = sink_row + row_join(in_ref[WINDOW:])
+        sink_row = sink_row + row_join(in_ref[:16])
         wanted = lax.rem(place // blocks_here - head + slots, slots)
         here = pl.ds(pl.multiple_of(place % blocks_here * WINDOW, WINDOW), WINDOW)
         for step, out_ref in enumerate(out_refs):
 
             @pl.when(valid & (wanted == step))
             def _(out_ref=out_ref, in_ref=in_ref, here=here):
-                total = out_ref[here, :].astype(F32) + in_ref[:WINDOW].astype(F32)
-                out_ref[here, :] = total.astype(BF16)
-
-    sink_ref[...] = jnp.broadcast_to(sink_row[:, :128], sink_ref.shape)
+                total = out_ref[here, :].astype(F32) + in_ref[...].astype(F32)
+                out_ref[here, :] = jnp.where(seen, total, 0.0).astype(BF16)
+
+    sink_ref[...] = jnp.broadcast_to(sink_row, sink_ref.shape)
 
 
 def total_kernel(dk_ref, dv_ref, halo_ref, sink_ref, far_ref, *refs):
@@ -563,7 +559,7 @@
     table = jnp.concatenate([branch_start, branch_len, parent_list[:, 0], parent_list[:, 1]])
     *slots, halo_out, keys, values = pl.pallas_call(
         pack_kernel,
-        out_shape=(shape((rows + EXTRA, width)),) * head_count
+        out_shape=(shape((rows, width)),) * head_count
         + (shape((PAIRS, WINDOW, 256)),)
         + (pltpu.VMEM(key_states.shape, BF16),) * 2,
         in_specs=[HBM] * 3,
@@ -647,7 +643,7 @@
                 pltpu.VMEM(key_states.shape, F32),
                 pltpu.VMEM((PAIRS, WINDOW, 256), BF16),
             )
-            + (shape((WINDOW + EXTRA, width)),) * len(steps),
+            + (shape((WINDOW, width)),) * len(steps),
             in_specs=[VMEM] * (1 + len(inputs)),
             out_specs=(VMEM,) * (5 + len(steps)),
             scratch_shapes=[
@@ -673,7 +669,7 @@
     parts = swap(dtail, "head")
     quarter_grad = pl.pallas_call(
         gather_kernel,
-        out_shape=shape((WINDOW + EXTRA, width)),
+        out_shape=shape((WINDOW, width)),
         in_specs=[VMEM] * head_count,
         out_specs=VMEM,
         compiler_params=PARAMS,

time: 62.3 us -> 61.1 us (0.981)
  starting transfers between devices: 26.8 us -> 33.3 us
  Pallas kernels: 22.2 us -> 16.5 us
  waiting for transfers between devices: 10.8 us -> 8.89 us
    ppermute x19, starting transfers between devices: 20.2 us -> 26.6 us  [ring(): lax.ppermute(value, axis, [(source, (source + steps) % count) for source...]
    pallas_call x2, Pallas kernels: 13.5 us -> 7.61 us  [attend(): pl.pallas_call(functools.partial(attend_kernel, blocks_here, head_count,...]
    ppermute x19, waiting for transfers between devices: 10.8 us -> 8.88 us  [ring(): lax.ppermute(value, axis, [(source, (source + steps) % count) for source...]
  transfers between devices with their start and end apart: 21 -> 21, of which waited for: 10 -> 9; matrix products, arithmetic and copies ran while one was open for 2% -> 2% of each run, Pallas kernels for 16% -> 14%
where the time goes in v3:
time: 61.1 us; the launch traced here: 61 us
  starting transfers between devices  33.3 us (55%)
  Pallas kernels  16.5 us (27%)
  waiting for transfers between devices  8.89 us (15%)
  between operations  0.77 us (1%)
  local copies, waits for them, and re-layouts  0.76 us (1%)
  other arithmetic  0.75 us (1%)
    ppermute x19, starting transfers between devices, ring(): lax.ppermute(value, axis, [(source, (source + steps) % count) for source...  26.6 us
    ppermute x19, waiting for transfers between devices, ring(): lax.ppermute(value, axis, [(source, (source + steps) % count) for source...  8.88 us
    pallas_call x2, Pallas kernels, attend(): pl.pallas_call(functools.partial(attend_kernel, blocks_here, head_count,...  7.61 us
    ppermute x2, starting transfers between devices, shift(): lax.ppermute(value, axis, [(source, source + steps) for source in range(l...  6.68 us
    pallas_call x2, Pallas kernels, flush(): pl.pallas_call(stage_kernel, out_shape=pltpu.HBM(value.shape, BF16), in_s...  2.65 us
    pallas_call x1, Pallas kernels, local(): pl.pallas_call(stage_kernel, out_shape=(pltpu.VMEM(queries.shape, BF16),)...  2.24 us
  transfers between devices with their start and end apart: 21, of which 9 were waited for; matrix products, arithmetic and copies ran while one was open for 2% of the time, Pallas kernels for 14%

profile of v3, /device:TPU:3, one launch (start us, length us, event | category | flops | bytes accessed | tf_op | source)
XLA Modules:
  0.0 61.0 jit_solution(1969698785247380752)
XLA Ops:
  0.6 1.2 %pack.1 = (bf16[256,256]{1,0:T(8,128)(2,1)S(1)}, bf16[256,256]{1,0:T(8,128)(2,1)S(1)}, bf16[256,256]{1,0:T(8,128)(2,1)S(1)}, bf16[256,256]{1,0:T(8,128)(2,1)S(1)...) custom-call(f32[16]{0:T(128)} %sink_hbm.1, ...), custom_call_target="tpu_custom_call" | custom-call | tf_op jit(solution)/shard_map/pack/pallas_call | solution.py:560
  1.8 1.9 %collective-permute-start = (bf16[256,256]{1,0:T(8,128)(2,1)S(1)}, bf16[256,256]{1,0:T(8,128)(2,1)S(1)}, u32[]{:S(2)}, u32[]{:S(2)}) collective-permute-start(bf16[256,256]{1,0:T(8,128)(2,1)S(1)} %get-tuple-element.54), channel_id=1, source_target_pairs={{0,1},{1,2},{2,3},{3,0},{4,5},{5,6},{6,7},{7,4},{8,9},{9,10},{10,1... | collective-permute-start | bytes 393224 | tf_op jit(solution)/shard_map/ppermute | solution.py:37
  4.1 3.4 %collective-permute-start.6 = (bf16[4,128,256]{2,1,0:T(8,128)(2,1)S(1)}, bf16[4,128,256]{2,1,0:T(8,128)(2,1)S(1)}, u32[]{:S(2)}, u32[]{:S(2)}) collective-permute-start(bf16[4,128,256]{2,1,0:T(8,128)(2,1)S(1)} %get-tuple-element.69), channel_id=1, source_target_pairs={{0,1},{1,2},{2,3},{4,5},{5,6},{6,7},{8,9},{9,10},{10,11},{12,13},{... | collective-permute-start | bytes 786440 | tf_op jit(solution)/shard_map/ppermute | solution.py:32
  7.5 0.8 %slice_bitcast_fusion.1 = (s32[16]{0:T(128)S(1)}, s32[16]{0:T(128)S(1)}) fusion(s32[16,2]{0,1:T(2,128)} %param.15), kind=kLoop, calls=%fused_computation.2 | loop fusion | bytes 256 | tf_op jit(solution)/shard_map/squeeze | solution.py:559
  11.0 2.3 %collective-permute-start.3 = (bf16[128,256]{1,0:T(8,128)(2,1)S(1)}, bf16[128,256]{1,0:T(8,128)(2,1)S(1)}, u32[]{:S(2)}, u32[]{:S(2)}) collective-permute-start(bf16[128,256]{1,0:T(8,128)(2,1)S(1)} %get-tuple-element.58), channel_id=1, source_target_pairs={{0,12},{4,16},{8,20},{12,24},{16,28},{20,0},{24,4},{28,8},{1,13},{... | collective-permute-start | bytes 196616 | tf_op jit(solution)/shard_map/ppermute | solution.py:37
  13.3 1.3 %collective-permute-start.4 = (bf16[128,256]{1,0:T(8,128)(2,1)S(1)}, bf16[128,256]{1,0:T(8,128)(2,1)S(1)}, u32[]{:S(2)}, u32[]{:S(2)}) collective-permute-start(bf16[128,256]{1,0:T(8,128)(2,1)S(1)} %get-tuple-element.59), channel_id=1, source_target_pairs={{0,8},{4,12},{8,16},{12,20},{16,24},{20,28},{24,0},{28,4},{1,9},{5... | collective-permute-start | bytes 196616 | tf_op jit(solution)/shard_map/ppermute | solution.py:37
  14.6 1.2 %collective-permute-start.5 = (bf16[128,256]{1,0:T(8,128)(2,1)S(1)}, bf16[128,256]{1,0:T(8,128)(2,1)S(1)}, u32[]{:S(2)}, u32[]{:S(2)}) collective-permute-start(bf16[128,256]{1,0:T(8,128)(2,1)S(1)} %get-tuple-element.60), channel_id=1, source_target_pairs={{0,4},{4,8},{8,12},{12,16},{16,20},{20,24},{24,28},{28,0},{1,5},{5... | collective-permute-start | bytes 196616 | tf_op jit(solution)/shard_map/ppermute | solution.py:37
  15.8 2.2 %stage.1 = (bf16[256,4096]{1,0:T(8,128)(2,1)S(1)}, bf16[256,4096]{1,0:T(8,128)(2,1)S(1)}) custom-call(bf16[256,4096]{1,0:T(8,128)(2,1)} %refs_0_, bf16[256,4096]{1,0:T(8,128)(2,1)} %refs_1_), custom_call_target="tpu_custom_call" | custom-call | tf_op jit(solution)/shard_map/stage/pallas_call | solution.py:595
  18.5 2.3 %collective-permute-start.9 = (bf16[128,256]{1,0:T(8,128)(2,1)S(1)}, bf16[128,256]{1,0:T(8,128)(2,1)S(1)}, u32[]{:S(2)}, u32[]{:S(2)}) collective-permute-start(bf16[128,256]{1,0:T(8,128)(2,1)S(1)} %arrive.1.refs_7_), channel_id=1, source_target_pairs={{0,3},{1,0},{2,1},{3,2},{4,7},{5,4},{6,5},{7,6},{8,11},{9,8},{10,9... | collective-permute-start | bytes 196616 | tf_op jit(solution)/shard_map/ppermute | solution.py:37
  21.3 1.9 %collective-permute-start.7 = (bf16[128,256]{1,0:T(8,128)(2,1)S(1)}, bf16[128,256]{1,0:T(8,128)(2,1)S(1)}, u32[]{:S(2)}, u32[]{:S(2)}) collective-permute-start(bf16[128,256]{1,0:T(8,128)(2,1)S(1)} %arrive.1.refs_7_), channel_id=1, source_target_pairs={{0,1},{1,2},{2,3},{3,0},{4,5},{5,6},{6,7},{7,4},{8,9},{9,10},{10,1... | collective-permute-start | bytes 196616 | tf_op jit(solution)/shard_map/ppermute | solution.py:37
  23.2 2.0 %attend.2 = (bf16[256,4096]{1,0:T(8,128)(2,1)S(1)}, bf16[256,4096]{1,0:T(8,128)(2,1)S(1)}, f32[256,512]{1,0:T(8,128)S(1)}, f32[256,512]{1,0:T(8,128)S(1)}, bf16[...) custom-call(s32[8,128]{1,0:T(8,128)S(1)} %plan.1.plan_ref.refs_0_, f32[64,128]{1,0:T(8,128)S(1)} %get-tuple-element.57.refs_1_, ...), custom_call_target="tpu_custom_call" | custom-call | tf_op jit(solution)/shard_map/attend/pallas_call | solution.py:629
  25.2 5.6 %attend.3 = (bf16[256,4096]{1,0:T(8,128)(2,1)S(1)}, bf16[256,4096]{1,0:T(8,128)(2,1)S(1)}, f32[256,512]{1,0:T(8,128)S(1)}, f32[256,512]{1,0:T(8,128)S(1)}, bf16[...) custom-call(s32[8,128]{1,0:T(8,128)S(1)} %plan.1.plan_ref.refs_0_, ...), custom_call_target="tpu_custom_call", output_to_operand_aliasing={{0}: (10, {}), {1}: (11, {}), {2}: (12, {}), {3}: (13, {}),... | custom-call | tf_op jit(solution)/shard_map/attend/pallas_call | solution.py:629
  30.9 6.4 %collective-permute-start.10 = (bf16[128,256]{1,0:T(8,128)(2,1)S(1)}, bf16[128,256]{1,0:T(8,128)(2,1)S(1)}, u32[]{:S(2)}, u32[]{:S(2)}) collective-permute-start(bf16[128,256]{1,0:T(8,128)(2,1)S(1)} %get-tuple-element.80), channel_id=1, source_target_pairs={{0,1},{1,2},{2,3},{3,0},{4,5},{5,6},{6,7},{7,4},{8,9},{9,10},{10,1... | collective-permute-start | bytes 196616 | tf_op jit(solution)/shard_map/ppermute | solution.py:37
  37.8 3.3 %collective-permute-start.16 = (bf16[4,128,256]{2,1,0:T(8,128)(2,1)S(1)}, bf16[4,128,256]{2,1,0:T(8,128)(2,1)S(1)}, u32[]{:S(2)}, u32[]{:S(2)}) collective-permute-start(bf16[4,128,256]{2,1,0:T(8,128)(2,1)S(1)} %get-tuple-element.93), channel_id=1, source_target_pairs={{1,0},{2,1},{3,2},{5,4},{6,5},{7,6},{9,8},{10,9},{11,10},{13,12},{... | collective-permute-start | bytes 786440 | tf_op jit(solution)/shard_map/ppermute | solution.py:32
  41.3 3.4 %collective-permute-start.15 = (bf16[128,256]{1,0:T(8,128)(2,1)S(1)}, bf16[128,256]{1,0:T(8,128)(2,1)S(1)}, u32[]{:S(2)}, u32[]{:S(2)}) collective-permute-start(bf16[128,256]{1,0:T(8,128)(2,1)S(1)} %gather.1.here_ref), channel_id=1, source_target_pairs={{0,20},{4,24},{8,28},{12,0},{16,4},{20,8},{24,12},{28,16},{1,21},{... | collective-permute-start | bytes 196616 | tf_op jit(solution)/shard_map/ppermute | solution.py:37
  44.7 1.2 %collective-permute-start.14 = (bf16[128,256]{1,0:T(8,128)(2,1)S(1)}, bf16[128,256]{1,0:T(8,128)(2,1)S(1)}, u32[]{:S(2)}, u32[]{:S(2)}) collective-permute-start(bf16[128,256]{1,0:T(8,128)(2,1)S(1)} %gather.1.here_ref), channel_id=1, source_target_pairs={{0,24},{4,28},{8,0},{12,4},{16,8},{20,12},{24,16},{28,20},{1,25},{... | collective-permute-start | bytes 196616 | tf_op jit(solution)/shard_map/ppermute | solution.py:37
  45.9 1.3 %flush.2 = bf16[256,4096]{1,0:T(8,128)(2,1)} custom-call(bf16[256,4096]{1,0:T(8,128)(2,1)S(1)} %get-tuple-element.83.refs_0_), custom_call_target="tpu_custom_call" | custom-call | tf_op jit(solution)/shard_map/flush/pallas_call | solution.py:679
  47.2 1.2 %collective-permute-done.15.refs_2_ = bf16[128,256]{1,0:T(8,128)(2,1)S(1)} collective-permute-done((bf16[128,256]{1,0:T(8,128)(2,1)S(1)}, bf16[128,256]{1,0:T(8,128)(2,1)S(1)}, u32[]{:S(2)}, u32[]{:S(2)}) %collective-permute-start.15) | collective-permute-done | bytes 65568 | tf_op jit(solution)/shard_map/ppermute | solution.py:37
  48.5 1.4 %collective-permute-done.13.refs_0_ = bf16[128,256]{1,0:T(8,128)(2,1)S(1)} collective-permute-done((bf16[128,256]{1,0:T(8,128)(2,1)S(1)}, bf16[128,256]{1,0:T(8,128)(2,1)S(1)}, u32[]{:S(2)}, u32[]{:S(2)}) %collective-permute-start.13) | collective-permute-done | bytes 65568 | tf_op jit(solution)/shard_map/ppermute | solution.py:37
  50.4 2.7 %collective-permute-start.18 = (bf16[256,256]{1,0:T(8,128)(2,1)S(1)}, bf16[256,256]{1,0:T(8,128)(2,1)S(1)}, u32[]{:S(2)}, u32[]{:S(2)}) collective-permute-start(bf16[256,256]{1,0:T(8,128)(2,1)S(1)} %get-tuple-element.95), channel_id=1, source_target_pairs={{0,1},{1,2},{2,3},{3,0},{4,5},{5,6},{6,7},{7,4},{8,9},{9,10},{10,1... | collective-permute-start | bytes 393224 | tf_op jit(solution)/shard_map/ppermute | solution.py:37
  53.6 1.3 %flush.3 = bf16[256,4096]{1,0:T(8,128)(2,1)} custom-call(bf16[256,4096]{1,0:T(8,128)(2,1)S(1)} %get-tuple-element.90.refs_0_), custom_call_target="tpu_custom_call" | custom-call | tf_op jit(solution)/shard_map/flush/pallas_call | solution.py:679
  54.9 2.0 %collective-permute-done.17.far_ref = f32[8,128]{1,0:T(8,128)S(1)} collective-permute-done((f32[8,128]{1,0:T(8,128)S(1)}, f32[8,128]{1,0:T(8,128)S(1)}, u32[]{:S(2)}, u32[]{:S(2)}) %collective-permute-start.17) | collective-permute-done | bytes 4128 | tf_op jit(solution)/shard_map/ppermute | solution.py:37
  56.9 2.6 %collective-permute-done.19.refs_2_ = bf16[256,256]{1,0:T(8,128)(2,1)S(1)} collective-permute-done((bf16[256,256]{1,0:T(8,128)(2,1)S(1)}, bf16[256,256]{1,0:T(8,128)(2,1)S(1)}, u32[]{:S(2)}, u32[]{:S(2)}) %collective-permute-start.19) | collective-permute-done | bytes 131104 | tf_op jit(solution)/shard_map/ppermute | solution.py:37
  60.0 1.0 %total.1 = (bf16[256,512]{1,0:T(8,128)(2,1)}, bf16[256,512]{1,0:T(8,128)(2,1)}, f32[16]{0:T(128)}) custom-call(f32[256,512]{1,0:T(8,128)S(1)} %get-tuple-element.91.dk_ref, f32[256,512]{1,0:T(8,128)S(1)} %get-tuple-element.92.dv_ref, bf16[4,128,256]{2,1,0:T(8,128)(2,1)S(1)} %collective-permute-done.16.halo_ref, f32[8,128]{1,0:T(8,128)S(1)} %get-tuple-element.89.sink_ref, ...), custom_call_target="tpu_custom_call" | custom-call | tf_op jit(solution)/shard_map/total/pallas_call | solution.py:710
  (32 shorter events, 6.4 us)
Async XLA Ops:
  1.8 7.9 %collective-permute-start = (bf16[256,256]{1,0:T(8,128)(2,1)S(1)}, bf16[256,256]{1,0:T(8,128)(2,1)S(1)}, u32[]{:S(2)}, u32[]{:S(2)}) collective-permute-start(bf16[256,256]{1,0:T(8,128)(2,1)S(1)} %get-tuple-element.54), channel_id=1, source_target_pairs={{0,1},{1,2},{2,3},{3,0},{4,5},{5,6},{6,7},{7,4},{8,9},{9,10},{10,1... | collective-permute-start | bytes 393224 | tf_op jit(solution)/shard_map/ppermute | solution.py:37
  3.7 6.2 %collective-permute-start.1 = (bf16[256,256]{1,0:T(8,128)(2,1)S(1)}, bf16[256,256]{1,0:T(8,128)(2,1)S(1)}, u32[]{:S(2)}, u32[]{:S(2)}) collective-permute-start(bf16[256,256]{1,0:T(8,128)(2,1)S(1)} %get-tuple-element.55), channel_id=1, source_target_pairs={{0,2},{1,3},{2,0},{3,1},{4,6},{5,7},{6,4},{7,5},{8,10},{9,11},{10,... | collective-permute-start | bytes 393224 | tf_op jit(solution)/shard_map/ppermute | solution.py:37
  3.9 6.6 %collective-permute-start.2 = (bf16[256,256]{1,0:T(8,128)(2,1)S(1)}, bf16[256,256]{1,0:T(8,128)(2,1)S(1)}, u32[]{:S(2)}, u32[]{:S(2)}) collective-permute-start(bf16[256,256]{1,0:T(8,128)(2,1)S(1)} %get-tuple-element.56), channel_id=1, source_target_pairs={{0,3},{1,0},{2,1},{3,2},{4,7},{5,4},{6,5},{7,6},{8,11},{9,8},{10,9... | collective-permute-start | bytes 393224 | tf_op jit(solution)/shard_map/ppermute | solution.py:37
  4.1 21.1 %collective-permute-start.6 = (bf16[4,128,256]{2,1,0:T(8,128)(2,1)S(1)}, bf16[4,128,256]{2,1,0:T(8,128)(2,1)S(1)}, u32[]{:S(2)}, u32[]{:S(2)}) collective-permute-start(bf16[4,128,256]{2,1,0:T(8,128)(2,1)S(1)} %get-tuple-element.69), channel_id=1, source_target_pairs={{0,1},{1,2},{2,3},{4,5},{5,6},{6,7},{8,9},{9,10},{10,11},{12,13},{... | collective-permute-start | bytes 786440 | tf_op jit(solution)/shard_map/ppermute | solution.py:32
  11.0 7.1 %collective-permute-start.3 = (bf16[128,256]{1,0:T(8,128)(2,1)S(1)}, bf16[128,256]{1,0:T(8,128)(2,1)S(1)}, u32[]{:S(2)}, u32[]{:S(2)}) collective-permute-start(bf16[128,256]{1,0:T(8,128)(2,1)S(1)} %get-tuple-element.58), channel_id=1, source_target_pairs={{0,12},{4,16},{8,20},{12,24},{16,28},{20,0},{24,4},{28,8},{1,13},{... | collective-permute-start | bytes 196616 | tf_op jit(solution)/shard_map/ppermute | solution.py:37
  13.3 4.9 %collective-permute-start.4 = (bf16[128,256]{1,0:T(8,128)(2,1)S(1)}, bf16[128,256]{1,0:T(8,128)(2,1)S(1)}, u32[]{:S(2)}, u32[]{:S(2)}) collective-permute-start(bf16[128,256]{1,0:T(8,128)(2,1)S(1)} %get-tuple-element.59), channel_id=1, source_target_pairs={{0,8},{4,12},{8,16},{12,20},{16,24},{20,28},{24,0},{28,4},{1,9},{5... | collective-permute-start | bytes 196616 | tf_op jit(solution)/shard_map/ppermute | solution.py:37
  14.6 3.7 %collective-permute-start.5 = (bf16[128,256]{1,0:T(8,128)(2,1)S(1)}, bf16[128,256]{1,0:T(8,128)(2,1)S(1)}, u32[]{:S(2)}, u32[]{:S(2)}) collective-permute-start(bf16[128,256]{1,0:T(8,128)(2,1)S(1)} %get-tuple-element.60), channel_id=1, source_target_pairs={{0,4},{4,8},{8,12},{12,16},{16,20},{20,24},{24,28},{28,0},{1,5},{5... | collective-permute-start | bytes 196616 | tf_op jit(solution)/shard_map/ppermute | solution.py:37
  18.5 6.7 %collective-permute-start.9 = (bf16[128,256]{1,0:T(8,128)(2,1)S(1)}, bf16[128,256]{1,0:T(8,128)(2,1)S(1)}, u32[]{:S(2)}, u32[]{:S(2)}) collective-permute-start(bf16[128,256]{1,0:T(8,128)(2,1)S(1)} %arrive.1.refs_7_), channel_id=1, source_target_pairs={{0,3},{1,0},{2,1},{3,2},{4,7},{5,4},{6,5},{7,6},{8,11},{9,8},{10,9... | collective-permute-start | bytes 196616 | tf_op jit(solution)/shard_map/ppermute | solution.py:37
  20.8 4.5 %collective-permute-start.8 = (bf16[128,256]{1,0:T(8,128)(2,1)S(1)}, bf16[128,256]{1,0:T(8,128)(2,1)S(1)}, u32[]{:S(2)}, u32[]{:S(2)}) collective-permute-start(bf16[128,256]{1,0:T(8,128)(2,1)S(1)} %arrive.1.refs_7_), channel_id=1, source_target_pairs={{0,2},{1,3},{2,0},{3,1},{4,6},{5,7},{6,4},{7,5},{8,10},{9,11},{10,... | collective-permute-start | bytes 196616 | tf_op jit(solution)/shard_map/ppermute | solution.py:37
  21.3 3.9 %collective-permute-start.7 = (bf16[128,256]{1,0:T(8,128)(2,1)S(1)}, bf16[128,256]{1,0:T(8,128)(2,1)S(1)}, u32[]{:S(2)}, u32[]{:S(2)}) collective-permute-start(bf16[128,256]{1,0:T(8,128)(2,1)S(1)} %arrive.1.refs_7_), channel_id=1, source_target_pairs={{0,1},{1,2},{2,3},{3,0},{4,5},{5,6},{6,7},{7,4},{8,9},{9,10},{10,1... | collective-permute-start | bytes 196616 | tf_op jit(solution)/shard_map/ppermute | solution.py:37
  30.9 10.2 %collective-permute-start.10 = (bf16[128,256]{1,0:T(8,128)(2,1)S(1)}, bf16[128,256]{1,0:T(8,128)(2,1)S(1)}, u32[]{:S(2)}, u32[]{:S(2)}) collective-permute-start(bf16[128,256]{1,0:T(8,128)(2,1)S(1)} %get-tuple-element.80), channel_id=1, source_target_pairs={{0,1},{1,2},{2,3},{3,0},{4,5},{5,6},{6,7},{7,4},{8,9},{9,10},{10,1... | collective-permute-start | bytes 196616 | tf_op jit(solution)/shard_map/ppermute | solution.py:37
  37.3 3.8 %collective-permute-start.11 = (bf16[128,256]{1,0:T(8,128)(2,1)S(1)}, bf16[128,256]{1,0:T(8,128)(2,1)S(1)}, u32[]{:S(2)}, u32[]{:S(2)}) collective-permute-start(bf16[128,256]{1,0:T(8,128)(2,1)S(1)} %get-tuple-element.81), channel_id=1, source_target_pairs={{0,2},{1,3},{2,0},{3,1},{4,6},{5,7},{6,4},{7,5},{8,10},{9,11},{10,... | collective-permute-start | bytes 196616 | tf_op jit(solution)/shard_map/ppermute | solution.py:37
  37.3 3.8 %collective-permute-start.12 = (bf16[128,256]{1,0:T(8,128)(2,1)S(1)}, bf16[128,256]{1,0:T(8,128)(2,1)S(1)}, u32[]{:S(2)}, u32[]{:S(2)}) collective-permute-start(bf16[128,256]{1,0:T(8,128)(2,1)S(1)} %get-tuple-element.82), channel_id=1, source_target_pairs={{0,3},{1,0},{2,1},{3,2},{4,7},{5,4},{6,5},{7,6},{8,11},{9,8},{10,9... | collective-permute-start | bytes 196616 | tf_op jit(solution)/shard_map/ppermute | solution.py:37
  37.8 19.1 %collective-permute-start.16 = (bf16[4,128,256]{2,1,0:T(8,128)(2,1)S(1)}, bf16[4,128,256]{2,1,0:T(8,128)(2,1)S(1)}, u32[]{:S(2)}, u32[]{:S(2)}) collective-permute-start(bf16[4,128,256]{2,1,0:T(8,128)(2,1)S(1)} %get-tuple-element.93), channel_id=1, source_target_pairs={{1,0},{2,1},{3,2},{5,4},{6,5},{7,6},{9,8},{10,9},{11,10},{13,12},{... | collective-permute-start | bytes 786440 | tf_op jit(solution)/shard_map/ppermute | solution.py:32
  41.3 7.2 %collective-permute-start.15 = (bf16[128,256]{1,0:T(8,128)(2,1)S(1)}, bf16[128,256]{1,0:T(8,128)(2,1)S(1)}, u32[]{:S(2)}, u32[]{:S(2)}) collective-permute-start(bf16[128,256]{1,0:T(8,128)(2,1)S(1)} %gather.1.here_ref), channel_id=1, source_target_pairs={{0,20},{4,24},{8,28},{12,0},{16,4},{20,8},{24,12},{28,16},{1,21},{... | collective-permute-start | bytes 196616 | tf_op jit(solution)/shard_map/ppermute | solution.py:37
  44.7 3.8 %collective-permute-start.14 = (bf16[128,256]{1,0:T(8,128)(2,1)S(1)}, bf16[128,256]{1,0:T(8,128)(2,1)S(1)}, u32[]{:S(2)}, u32[]{:S(2)}) collective-permute-start(bf16[128,256]{1,0:T(8,128)(2,1)S(1)} %gather.1.here_ref), channel_id=1, source_target_pairs={{0,24},{4,28},{8,0},{12,4},{16,8},{20,12},{24,16},{28,20},{1,25},{... | collective-permute-start | bytes 196616 | tf_op jit(solution)/shard_map/ppermute | solution.py:37
  45.9 4.0 %collective-permute-start.13 = (bf16[128,256]{1,0:T(8,128)(2,1)S(1)}, bf16[128,256]{1,0:T(8,128)(2,1)S(1)}, u32[]{:S(2)}, u32[]{:S(2)}) collective-permute-start(bf16[128,256]{1,0:T(8,128)(2,1)S(1)} %gather.1.here_ref), channel_id=1, source_target_pairs={{0,28},{4,0},{8,4},{12,8},{16,12},{20,16},{24,20},{28,24},{1,29},{... | collective-permute-start | bytes 196616 | tf_op jit(solution)/shard_map/ppermute | solution.py:37
  50.4 6.5 %collective-permute-start.18 = (bf16[256,256]{1,0:T(8,128)(2,1)S(1)}, bf16[256,256]{1,0:T(8,128)(2,1)S(1)}, u32[]{:S(2)}, u32[]{:S(2)}) collective-permute-start(bf16[256,256]{1,0:T(8,128)(2,1)S(1)} %get-tuple-element.95), channel_id=1, source_target_pairs={{0,1},{1,2},{2,3},{3,0},{4,5},{5,6},{6,7},{7,4},{8,9},{9,10},{10,1... | collective-permute-start | bytes 393224 | tf_op jit(solution)/shard_map/ppermute | solution.py:37
  53.0 6.4 %collective-permute-start.19 = (bf16[256,256]{1,0:T(8,128)(2,1)S(1)}, bf16[256,256]{1,0:T(8,128)(2,1)S(1)}, u32[]{:S(2)}, u32[]{:S(2)}) collective-permute-start(bf16[256,256]{1,0:T(8,128)(2,1)S(1)} %get-tuple-element.96), channel_id=1, source_target_pairs={{0,2},{1,3},{2,0},{3,1},{4,6},{5,7},{6,4},{7,5},{8,10},{9,11},{10,... | collective-permute-start | bytes 393224 | tf_op jit(solution)/shard_map/ppermute | solution.py:37
  53.5 6.6 %collective-permute-start.20 = (bf16[256,256]{1,0:T(8,128)(2,1)S(1)}, bf16[256,256]{1,0:T(8,128)(2,1)S(1)}, u32[]{:S(2)}, u32[]{:S(2)}) collective-permute-start(bf16[256,256]{1,0:T(8,128)(2,1)S(1)} %get-tuple-element.97), channel_id=1, source_target_pairs={{0,3},{1,0},{2,1},{3,2},{4,7},{5,4},{6,5},{7,6},{8,11},{9,8},{10,9... | collective-permute-start | bytes 393224 | tf_op jit(solution)/shard_map/ppermute | solution.py:37
  53.5 3.4 %collective-permute-start.17 = (f32[8,128]{1,0:T(8,128)S(1)}, f32[8,128]{1,0:T(8,128)S(1)}, u32[]{:S(2)}, u32[]{:S(2)}) collective-permute-start(f32[8,128]{1,0:T(8,128)S(1)} %get-tuple-element.89.sink_ref), channel_id=1, source_target_pairs={{0,16},{4,20},{8,24},{12,28},{16,0},{20,4},{24,8},{28,12},{1,17},{... | collective-permute-start | bytes 12296 | tf_op jit(solution)/shard_map/ppermute | solution.py:37

commit v4 on v3

--- a/solution.py
+++ b/solution.py
@@ -55,39 +55,37 @@
     return jnp.where(lax.broadcasted_iota(jnp.int32, (1, 128), 1) < 32, row, 0.0)
 
 
-def child_tail(table, tok, distance, tok_count, blocks):
-    branches = tok_count * BR_DEV
+def child_tail(starts, parents, tok, distance, tok_count, blocks):
     child = jnp.minimum(tok + distance, tok_count - 1) * BR_DEV
-    parent = table[2 * branches + child]
+    parent = parents[0, child]
     safe = jnp.maximum(parent, 0)
     valid = (tok + distance < tok_count) & (parent >= 0) & (safe // BR_DEV == tok)
-    place = (table[safe] + table[3 * branches + child]) // WINDOW - tok * blocks
+    place = (starts[safe] + parents[1, child]) // WINDOW - tok * blocks
     return valid, jnp.where(valid, place, 0)
 
 
-def block_state(table, tok, tok_count, block):
-    branches = tok_count * BR_DEV
+def block_state(starts, lengths, parents, tok, block):
     position = block * WINDOW
     alive, opening = jnp.bool_(False), jnp.bool_(False)
     for branch in range(BR_DEV):
-        start = table[tok * BR_DEV + branch]
-        length = table[branches + tok * BR_DEV + branch]
+        start = starts[tok * BR_DEV + branch]
+        length = lengths[tok * BR_DEV + branch]
         alive = alive | ((start <= position) & (position < start + length))
         opening = opening | (start == position)
-    has_tail = table[2 * branches + tok * BR_DEV] >= 0
+    has_tail = parents[0, tok * BR_DEV] >= 0
     return alive, opening, jnp.logical_not(opening) | has_tail
 
 
-def plan_kernel(tok_count, blocks, blocks_here, table, plan_ref):
+def plan_kernel(tok_count, blocks, blocks_here, starts, lengths, parents, plan_ref):
     tok, head = lax.axis_index("tok"), lax.axis_index("head")
     values = []
     for distance in range(1, LAG + 1):
-        values += child_tail(table, tok, distance, tok_count, blocks)
-    parent = table[2 * tok_count * BR_DEV + tok * BR_DEV]
+        values += child_tail(starts, parents, tok, distance, tok_count, blocks)
+    parent = parents[0, tok * BR_DEV]
     values.append(jnp.where(parent >= 0, tok - jnp.maximum(parent, 0) // BR_DEV, 1))
     for block in range(blocks_here):
         number = tok * blocks + head * blocks_here + block
-        values += block_state(table, tok, tok_count, number)
+        values += block_state(starts, lengths, parents, tok, number)
     lane = lax.broadcasted_iota(jnp.int32, plan_ref.shape, 1)
     plan = jnp.zeros(plan_ref.shape, jnp.int32)
     for place, value in enumerate(values):
@@ -206,273 +204,312 @@
         tails[lax.rem(head - step + slots, slots)] = tail_ref[...]
 
     def step(place, carry):
-        pair = place // blocks_here
-        if offset is not None:
-            pair = lax.rem(head + pair + offset, PAIRS)
-        block = place % blocks_here
-        state = states[0]
-        for other in range(1, blocks_here):
-            state = [jnp.where(block == other, *two) for two in zip(states[other], state)]
-        attend_block(
-            blocks_here,
-            slots,
-            pair,
-            block,
-            [value != 0 for value in state],
-            inputs,
-            outputs,
-            tails,
-            tuple(zip(steps, dtail_refs)),
-            scratch,
+        pair = place if offset is None else lax.rem(head + place + offset, PAIRS)
+        attend_pair(
+            slots, pair, states, inputs, outputs, tails, tuple(zip(steps, dtail_refs)), scratch
         )
         return carry
 
-    lax.fori_loop(0, pairs * blocks_here, step, 0)
-
-
-def attend_block(
-    blocks_here, slots, pair, block, state, inputs, outputs, tails, dtails, scratch
-):
+    lax.fori_loop(0, pairs, step, 0)
+
+
+def attend_pair(slots, pair, states, inputs, outputs, tails, dtails, scratch):
     _, sink_ref, q_ref, g_ref, k_ref, v_ref, halo_ref = inputs
     o_ref, dq_ref, dk_ref, dv_ref, dhalo_ref = outputs
     tail_sum, sink_rows, prob2, slope2 = scratch
     per_slot = KV_HEADS // slots
     head = lax.axis_index("head")
-    alive, opening, prev_ok = state
-    here = pl.ds(pl.multiple_of(block * WINDOW, WINDOW), WINDOW)
-    before = pl.ds(pl.multiple_of(jnp.maximum(block - 1, 0) * WINDOW, WINDOW), WINDOW)
-    first = block == 0
     near = pl.ds(pl.multiple_of(pair * 128, 128), 128)
     big = pl.ds(pl.multiple_of(pair * 1024, 1024), 1024)
-    q_ref, g_ref, o_ref, dq_ref = (ref.at[here, big] for ref in (q_ref, g_ref, o_ref, dq_ref))
-    k_ref, v_ref, dk_ref, dv_ref = (ref.at[:, near] for ref in (k_ref, v_ref, dk_ref, dv_ref))
-    sink_ref = sink_ref.at[pl.ds(pl.multiple_of(pair * 16, 16), 16)]
     dhalo_ref = dhalo_ref.at[pair]
-
-    @pl.when(first)
+    tail_sum[...] = jnp.zeros_like(tail_sum)
+    dhalo_ref[...] = jnp.zeros((WINDOW, 256), BF16)
+    sink_rows[...] = jnp.zeros_like(sink_rows)
+    if len(halo_ref.shape) == 2:
+        halo_ref = halo_ref.at[halo_ref.shape[0] - WINDOW :]
+    else:
+        halo_ref = halo_ref.at[pair]
+    if per_slot == 2:
+        tail_refs = (tails.at[pair],)
+    else:
+        tail_refs = (tails.at[2 * pair], tails.at[2 * pair + 1])
+
+    def attend(blocks, blocks_state):
+        attend_blocks(
+            blocks,
+            blocks_state,
+            [ref.at[:, big] for ref in (q_ref, g_ref, o_ref, dq_ref)],
+            [ref.at[:, near] for ref in (k_ref, v_ref, dk_ref, dv_ref)],
+            sink_ref.at[pl.ds(pl.multiple_of(pair * 16, 16), 16)],
+            halo_ref,
+            tail_refs,
+            dhalo_ref,
+            scratch,
+        )
+
+    for block, (alive, _, _) in enumerate(states):
+        here = slice(block * WINDOW, (block + 1) * WINDOW)
+
+        @pl.when(alive == 0)
+        def _(here=here):
+            o_ref[here, big] = jnp.zeros((WINDOW, 1024), BF16)
+            dq_ref[here, big] = jnp.zeros((WINDOW, 1024), BF16)
+            dk_ref[here, near] = jnp.zeros((WINDOW, 128), F32)
+            dv_ref[here, near] = jnp.zeros((WINDOW, 128), F32)
+
+    count = len(states)
+    living = sum(alive for alive, _, _ in states)
+    if count > 1:
+
+        @pl.when(living == count)
+        def _():
+            attend(tuple(range(count)), states)
+
+    @pl.when((living > 0) & ((living < count) | (count == 1)))
     def _():
-        tail_sum[...] = jnp.zeros_like(tail_sum)
-        dhalo_ref[...] = jnp.zeros((WINDOW, 256), BF16)
-        sink_rows[...] = jnp.zeros_like(sink_rows)
-
-    @pl.when(jnp.logical_not(alive))
-    def _():
-        o_ref[...] = jnp.zeros((WINDOW, 1024), BF16)
-        dq_ref[...] = jnp.zeros((WINDOW, 1024), BF16)
-        dk_ref[here, :] = jnp.zeros((WINDOW, 128), F32)
-        dv_ref[here, :] = jnp.zeros((WINDOW, 128), F32)
-
-    @pl.when(alive)
-    def _():
-        if len(halo_ref.shape) == 2:
-            halo = halo_ref[halo_ref.shape[0] - WINDOW :]
-        else:
-            halo = halo_ref[pair]
-        if per_slot == 2:
-            tail = tails[pair]
+        def single(block, carry):
+            state = states[0]
+            for other in range(1, count):
+                state = [jnp.where(block == other, *two) for two in zip(states[other], state)]
+
+            @pl.when(state[0] != 0)
+            def _():
+                attend((block,), (state,))
+
+            return carry
+
+        lax.fori_loop(0, count, single, 0)
+
+    width = 2 * per_slot * HEAD_DIM
+    heads = per_slot * GROUP
+    total = tail_sum[...].astype(BF16)
+    for part in range(2 // per_slot):
+        feats = slice(part * width // 2, (part + 1) * width // 2)
+        tail = jnp.concatenate([total[:, :128][:, feats], total[:, 128:][:, feats]], axis=1)
+        rows = sink_rows[part * heads : (part + 1) * heads]
+        rows = jnp.concatenate([rows, jnp.zeros((128 - heads, WINDOW), F32)], axis=0)
+        sink_row = jnp.sum(rows.T, axis=0, keepdims=True)
+        tail = with_row(tail, sink_row)
+        wanted = lax.rem(pair * (2 // per_slot) + part - head + slots, slots)
+        for step, dtail_ref in dtails:
+
+            @pl.when(wanted == step)
+            def _(dtail_ref=dtail_ref, tail=tail):
+                dtail_ref[...] = tail
+
+
+def attend_blocks(
+    blocks, states, bigs, smalls, sink_ref, halo_ref, tail_refs, dhalo_ref, scratch
+):
+    q_ref, g_ref, o_ref, dq_ref = bigs
+    k_ref, v_ref, dk_ref, dv_ref = smalls
+    tail_sum, sink_rows, prob2, slope2 = scratch
+    left = lax.broadcasted_iota(jnp.int32, (1, 128), 1) < HALF
+    low16 = left.astype(F32).astype(BF16)
+    high16 = BF16(1) - low16
+    key_place = lax.broadcasted_iota(jnp.int32, (HALF, 4 * HALF), 0)
+    query_place = lax.broadcasted_iota(jnp.int32, (HALF, 4 * HALF), 1) & (HALF - 1)
+    own = key_place <= query_place
+    own16 = own.astype(F32).astype(BF16)
+    turn = (((1,), (1,)), ((), ()))
+    seen = 3 * HALF
+
+    def at(block, begin=0, count=WINDOW):
+        start = block * WINDOW + begin
+        if isinstance(start, int):
+            return pl.ds(start, count)
+        return pl.ds(pl.multiple_of(start, HALF), count)
+
+    def before(block):
+        return at(max(block - 1, 0) if isinstance(block, int) else jnp.maximum(block - 1, 0))
+
+    def halves(own, prev):
+        return (
+            jnp.concatenate([own[:HALF], prev[:HALF], prev[HALF:]], axis=0),
+            jnp.concatenate([own[HALF:], prev[HALF:], own[:HALF]], axis=0),
+        )
+
+    def padded(rows):
+        swapped = jnp.concatenate([rows[:, 64:], rows[:, :64]], axis=1)
+        return (
+            jnp.concatenate([rows * low16, swapped * high16], axis=0),
+            jnp.concatenate([swapped * low16, rows * high16], axis=0),
+        )
+
+    def prepare(block, opening):
+        halo = halo_ref[...]
+        if len(tail_refs) == 1:
+            tail = tail_refs[0][...]
             tail_k, tail_v = tail[:, :128], tail[:, 128:]
         else:
-            tail_a, tail_b = tails[2 * pair], tails[2 * pair + 1]
+            tail_a, tail_b = (ref[...] for ref in tail_refs)
             tail_k = jnp.concatenate([tail_a[:, :64], tail_b[:, :64]], axis=1)
             tail_v = jnp.concatenate([tail_a[:, 64:], tail_b[:, 64:]], axis=1)
-        near_k = jnp.where(first, halo[:, :128], k_ref[before, :])
-        near_v = jnp.where(first, halo[:, 128:], v_ref[before, :])
-        prev_k = jnp.where(opening, tail_k, near_k)
-        prev_v = jnp.where(opening, tail_v, near_v)
-        own_k, own_v = k_ref[here, :], v_ref[here, :]
-
-        def halves(own, prev):
-            return (
-                jnp.concatenate([own[:HALF], prev[:HALF], prev[HALF:]], axis=0),
-                jnp.concatenate([own[HALF:], prev[HALF:], own[:HALF]], axis=0),
+        near_k = jnp.where(block == 0, halo[:, :128], k_ref[before(block), :])
+        near_v = jnp.where(block == 0, halo[:, 128:], v_ref[before(block), :])
+        prev_k = jnp.where(opening != 0, tail_k, near_k)
+        prev_v = jnp.where(opening != 0, tail_v, near_v)
+        seen_k = halves(k_ref[at(block), :] * BF16(FACTOR), prev_k * BF16(FACTOR))
+        seen_v = halves(v_ref[at(block), :], prev_v)
+        return (
+            tuple(padded(value) for value in seen_k),
+            tuple(padded(value) for value in seen_v),
+            tuple(value.T for value in seen_k),
+            tuple(value.T for value in seen_v),
+        )
+
+    keys = [prepare(block, opening) for block, (_, opening, _) in zip(blocks, states)]
+    biases = [jnp.where(prev_ok != 0, 0.0, LOW) for _, _, prev_ok in states]
+    items = [
+        (place, unit, half)
+        for place in range(len(blocks))
+        for unit in range(2)
+        for half in range(2)
+    ]
+
+    def wide(index):
+        return slice(index * 256, (index + 1) * 256)
+
+    def feats(index):
+        unit = items[index][1]
+        return slice(unit * HEAD_DIM, (unit + 1) * HEAD_DIM)
+
+    def corners(index):
+        place, unit, half = items[index]
+        rows = at(blocks[place], half * HALF, HALF)
+        return [(rows, slice(unit * 512 + by * 128, unit * 512 + (by + 1) * 128)) for by in range(4)]
+
+    def stacked(ref, index):
+        return jnp.concatenate([ref[corner] for corner in corners(index)], axis=0)
+
+    def products(index):
+        place, unit, half = items[index]
+        padded_k, padded_v, _, _ = keys[place]
+        bias = biases[place]
+        score, dp = (
+            lax.dot_general(
+                rows[half][unit], stacked(ref, index), turn, preferred_element_type=F32
             )
-
-        left = lax.broadcasted_iota(jnp.int32, (1, 128), 1) < HALF
-        low16 = left.astype(F32).astype(BF16)
-        high16 = BF16(1) - low16
-
-        def padded(seen):
-            swapped = jnp.concatenate([seen[:, 64:], seen[:, :64]], axis=1)
-            return (
-                jnp.concatenate([seen * low16, swapped * high16], axis=0),
-                jnp.concatenate([swapped * low16, seen * high16], axis=0),
+            for rows, ref in ((padded_k, q_ref), (padded_v, g_ref))
+        )
+        parts = []
+        for base in (0, seen):
+            near, far = slice(base, base + HALF), slice(base + HALF, base + 2 * HALF)
+            rest = slice(base + 2 * HALF, base + 3 * HALF)
+            edge = jnp.where(own, score[near], score[far] + bias)
+            whole = score[rest] + bias if half == 0 else score[rest]
+            parts.append((edge, whole, jnp.where(own, dp[near], dp[far]), dp[rest]))
+        return parts
+
+    def weigh(index, odd, edge, whole, dp_edge, dp_whole):
+        unit = items[index][1]
+        base = odd * seen
+        row = unit * GROUP + odd
+        sink = jnp.concatenate(
+            [
+                jnp.where(left, sink_ref[by : by + 1], sink_ref[by + 2 : by + 3])
+                for by in (row, row + 4)
+            ],
+            axis=1,
+        )
+        peak = jnp.max(jnp.maximum(edge, whole), axis=0, keepdims=True)
+        peak = jnp.maximum(peak, sink)
+        edge, whole = jnp.exp(edge - peak), jnp.exp(whole - peak)
+        sink_weight = jnp.exp(sink - peak)
+        inverse = 1.0 / (jnp.sum(edge + whole, axis=0, keepdims=True) + sink_weight)
+        edge, whole = edge * inverse, whole * inverse
+        term_edge, term_whole = edge * dp_edge, whole * dp_whole
+        delta = jnp.sum(term_edge + term_whole, axis=0, keepdims=True)
+        for target, at_edge, at_whole in (
+            (prob2, edge, whole),
+            (slope2, term_edge - edge * delta, term_whole - whole * delta),
+        ):
+            edge16 = at_edge.astype(BF16)
+            edge_own = edge16 * own16
+            target[base : base + HALF, wide(index)] = edge_own
+            target[base + HALF : base + 2 * HALF, wide(index)] = edge16 - edge_own
+            target[base + 2 * HALF : base + seen, wide(index)] = at_whole.astype(BF16)
+        sink_term = sink_weight * inverse * delta
+        for by, lanes in ((row, slice(0, 128)), (row + 4, slice(128, 256))):
+            part = sink_term[:, lanes]
+            sink_rows[by : by + 1] += jnp.where(left, part, 0.0)
+            sink_rows[by + 2 : by + 3] += jnp.where(left, 0.0, part)
+
+    def finish(index):
+        place, _, half = items[index]
+        _, _, turned_k, turned_v = keys[place]
+        for source, across, out_ref in ((prob2, turned_v, o_ref), (slope2, turned_k, dq_ref)):
+            out_t = [
+                jnp.dot(
+                    across[half][feats(index)],
+                    source[base : base + seen, wide(index)],
+                    preferred_element_type=F32,
+                ).astype(BF16)
+                for base in (0, seen)
+            ]
+            out = jnp.concatenate(out_t, axis=0).T
+            for by, corner in enumerate(corners(index)):
+                out_ref[corner] = out[by * HALF : (by + 1) * HALF]
+
+    def reduce(index):
+        parts = []
+        for weights, ref in ((slope2, q_ref), (prob2, g_ref)):
+            part = jnp.dot(
+                weights[:, wide(index)], stacked(ref, index), preferred_element_type=F32
             )
-
-        seen_k = halves(own_k * BF16(FACTOR), prev_k * BF16(FACTOR))
-        seen_v = halves(own_v, prev_v)
-        padded_k = tuple(padded(value) for value in seen_k)
-        padded_v = tuple(padded(value) for value in seen_v)
-        turned_k = tuple(value.T for value in seen_k)
-        turned_v = tuple(value.T for value in seen_v)
-        bias = jnp.where(prev_ok, 0.0, LOW)
-        key_place = lax.broadcasted_iota(jnp.int32, (HALF, 4 * HALF), 0)
-        query_place = lax.broadcasted_iota(jnp.int32, (HALF, 4 * HALF), 1) & (HALF - 1)
-        own = key_place <= query_place
-        own16 = own.astype(F32).astype(BF16)
-        turn = (((1,), (1,)), ((), ()))
-        items = [(unit, half) for unit in range(2) for half in range(2)]
-        seen = 3 * HALF
-
-        def wide(index):
-            return slice(index * 256, (index + 1) * 256)
-
-        def feats(index):
-            unit = items[index][0]
-            return slice(unit * HEAD_DIM, (unit + 1) * HEAD_DIM)
-
-        def corners(unit, half):
-            rows = slice(half * HALF, (half + 1) * HALF)
-            return [
-                (rows, slice(unit * 512 + at * 128, unit * 512 + (at + 1) * 128)) for at in range(4)
+            parts.append(jnp.where(left, part[:seen], part[seen:]))
+        return parts
+
+    def join(first_half, second_half):
+        total = jnp.concatenate(
+            [
+                first_half[:HALF] + second_half[2 * HALF :],
+                second_half[:HALF],
+                first_half[HALF : 2 * HALF],
+                first_half[2 * HALF :] + second_half[HALF : 2 * HALF],
+            ],
+            axis=0,
+        )
+        return total + pltpu.roll(total, HEAD_DIM, 1)
+
+    ahead, parts, grads = products(0), [], []
+    for index in range(len(items)):
+        now = ahead
+        weigh(index, 0, *now[0])
+        if index + 1 < len(items):
+            ahead = products(index + 1)
+        weigh(index, 1, *now[1])
+        if index >= 1:
+            finish(index - 1)
+        parts.append(reduce(index))
+        if len(parts) == 4:
+            joined = [
+                [join(parts[2 * unit][which], parts[2 * unit + 1][which]) for unit in range(2)]
+                for which in range(2)
             ]
-
-        def stacked(ref, unit, half):
-            return jnp.concatenate([ref[corner] for corner in corners(unit, half)], axis=0)
-
-        def products(index):
-            unit, half = items[index]
-            score, dp = (
-                lax.dot_general(
-                    padded[half][unit],
-                    stacked(ref, unit, half),
-                    turn,
-                    preferred_element_type=F32,
-                )
-                for padded, ref in ((padded_k, q_ref), (padded_v, g_ref))
-            )
+            dk, dv = (jnp.where(left, *both) for both in joined)
+            grads.append((dk * FACTOR, dv))
             parts = []
-            for base in (0, seen):
-                near, far = slice(base, base + HALF), slice(base + HALF, base + 2 * HALF)
-                rest = slice(base + 2 * HALF, base + 3 * HALF)
-                edge = jnp.where(own, score[near], score[far] + bias)
-                whole = score[rest] + bias if half == 0 else score[rest]
-                parts.append((edge, whole, jnp.where(own, dp[near], dp[far]), dp[rest]))
-            return parts
-
-        def weigh(index, odd, edge, whole, dp_edge, dp_whole):
-            unit, half = items[index]
-            base = odd * seen
-            row = unit * GROUP + odd
-            sink = jnp.concatenate(
-                [
-                    jnp.where(left, sink_ref[at : at + 1], sink_ref[at + 2 : at + 3])
-                    for at in (row, row + 4)
-                ],
-                axis=1,
-            )
-            peak = jnp.max(jnp.maximum(edge, whole), axis=0, keepdims=True)
-            peak = jnp.maximum(peak, sink)
-            edge, whole = jnp.exp(edge - peak), jnp.exp(whole - peak)
-            sink_weight = jnp.exp(sink - peak)
-            inverse = 1.0 / (jnp.sum(edge + whole, axis=0, keepdims=True) + sink_weight)
-            edge, whole = edge * inverse, whole * inverse
-            term_edge, term_whole = edge * dp_edge, whole * dp_whole
-            delta = jnp.sum(term_edge + term_whole, axis=0, keepdims=True)
-            for target, at_edge, at_whole in (
-                (prob2, edge, whole),
-                (slope2, term_edge - edge * delta, term_whole - whole * delta),
-            ):
-                edge16 = at_edge.astype(BF16)
-                edge_own = edge16 * own16
-                target[base : base + HALF, wide(index)] = edge_own
-                target[base + HALF : base + 2 * HALF, wide(index)] = edge16 - edge_own
-                target[base + 2 * HALF : base + seen, wide(index)] = at_whole.astype(BF16)
-            sink_term = sink_weight * inverse * delta
-            for at, lanes in ((row, slice(0, 128)), (row + 4, slice(128, 256))):
-                part = sink_term[:, lanes]
-                sink_rows[at : at + 1] += jnp.where(left, part, 0.0)
-                sink_rows[at + 2 : at + 3] += jnp.where(left, 0.0, part)
-
-        def finish(index):
-            unit, half = items[index]
-            for source, across, out_ref in ((prob2, turned_v, o_ref), (slope2, turned_k, dq_ref)):
-                out_t = [
-                    jnp.dot(
-                        across[half][feats(index)],
-                        source[base : base + seen, wide(index)],
-                        preferred_element_type=F32,
-                    ).astype(BF16)
-                    for base in (0, seen)
-                ]
-                out = jnp.concatenate(out_t, axis=0).T
-                for at, corner in enumerate(corners(unit, half)):
-                    out_ref[corner] = out[at * HALF : (at + 1) * HALF]
-
-        def reduce(index):
-            unit, half = items[index]
-            parts = []
-            for weights, ref in ((slope2, q_ref), (prob2, g_ref)):
-                part = jnp.dot(
-                    weights[:, wide(index)], stacked(ref, unit, half), preferred_element_type=F32
-                )
-                parts.append(jnp.where(left, part[:seen], part[seen:]))
-            return parts
-
-        def join(first_half, second_half):
-            total = jnp.concatenate(
-                [
-                    first_half[:HALF] + second_half[2 * HALF :],
-                    second_half[:HALF],
-                    first_half[HALF : 2 * HALF],
-                    first_half[2 * HALF :] + second_half[HALF : 2 * HALF],
-                ],
-                axis=0,
-            )
-            return total + pltpu.roll(total, HEAD_DIM, 1)
-
-        ahead, parts = products(0), []
-        for index in range(len(items)):
-            now = ahead
-            weigh(index, 0, *now[0])
-            if index + 1 < len(items):
-                ahead = products(index + 1)
-            weigh(index, 1, *now[1])
-            if index >= 1:
-                finish(index - 1)
-            parts.append(reduce(index))
-        finish(len(items) - 1)
-        grads = [
-            [join(parts[2 * unit][place], parts[2 * unit + 1][place]) for place in range(2)]
-            for unit in range(2)
-        ]
-        dk = jnp.where(left, grads[0][0], grads[1][0]) * FACTOR
-        dv = jnp.where(left, grads[0][1], grads[1][1])
-        dk_ref[here, :] = dk[:WINDOW]
-        dv_ref[here, :] = dv[:WINDOW]
-
-        @pl.when(opening & prev_ok)
-        def _():
+    finish(len(items) - 1)
+    for block, (dk, dv) in zip(blocks, grads):
+        dk_ref[at(block), :] = dk[:WINDOW]
+        dv_ref[at(block), :] = dv[:WINDOW]
+    for block, (_, opening, prev_ok), (dk, dv) in zip(blocks, states, grads):
+
+        @pl.when((opening != 0) & (prev_ok != 0))
+        def _(dk=dk, dv=dv):
             tail_sum[:, :128] += dk[WINDOW:]
             tail_sum[:, 128:] += dv[WINDOW:]
 
-        @pl.when(jnp.logical_not(opening) & first)
-        def _():
+        @pl.when((opening == 0) & (block == 0))
+        def _(dk=dk, dv=dv):
             dhalo_ref[:, :128] = dk[WINDOW:].astype(BF16)
             dhalo_ref[:, 128:] = dv[WINDOW:].astype(BF16)
 
-        @pl.when(jnp.logical_not(opening) & jnp.logical_not(first))
-        def _():
-            dk_ref[before, :] += dk[WINDOW:]
-            dv_ref[before, :] += dv[WINDOW:]
-
-    @pl.when(block == blocks_here - 1)
-    def _():
-        width = 2 * per_slot * HEAD_DIM
-        heads = per_slot * GROUP
-        total = tail_sum[...].astype(BF16)
-        for part in range(2 // per_slot):
-            feats = slice(part * width // 2, (part + 1) * width // 2)
-            tail = jnp.concatenate([total[:, :128][:, feats], total[:, 128:][:, feats]], axis=1)
-            rows = sink_rows[part * heads : (part + 1) * heads]
-            rows = jnp.concatenate([rows, jnp.zeros((128 - heads, WINDOW), F32)], axis=0)
-            sink_row = jnp.sum(rows.T, axis=0, keepdims=True)
-            tail = with_row(tail, sink_row)
-            wanted = lax.rem(pair * (2 // per_slot) + part - head + slots, slots)
-            for step, dtail_ref in dtails:
-
-                @pl.when(wanted == step)
-                def _(dtail_ref=dtail_ref, tail=tail):
-                    dtail_ref[...] = tail
+        @pl.when((opening == 0) & (block != 0))
+        def _(dk=dk, dv=dv, block=block):
+            dk_ref[before(block), :] += dk[WINDOW:]
+            dv_ref[before(block), :] += dv[WINDOW:]
 
 
 def gather_kernel(*refs):
@@ -556,7 +593,6 @@
     def close(value):
         return pltpu.with_memory_space_constraint(value, pltpu.VMEM)
 
-    table = jnp.concatenate([branch_start, branch_len, parent_list[:, 0], parent_list[:, 1]])
     *slots, halo_out, keys, values = pl.pallas_call(
         pack_kernel,
         out_shape=(shape((rows, width)),) * head_count
@@ -576,11 +612,11 @@
     plan = pl.pallas_call(
         functools.partial(plan_kernel, tok_count, blocks, blocks_here),
         out_shape=pltpu.VMEM((8, 128), jnp.int32),
-        in_specs=[SMEM],
+        in_specs=[SMEM] * 3,
         out_specs=VMEM,
         compiler_params=PARAMS,
         name="plan",
-    )(table)
+    )(far(branch_start), far(branch_len), far(parent_list.T))
     plan = close(plan)
     *chosen, sinks = pl.pallas_call(
         choose_kernel,
@@ -650,8 +686,8 @@
                 pltpu.VMEM((head_count, WINDOW, width), BF16),
                 pltpu.VMEM((WINDOW, 256), F32),
                 pltpu.VMEM((2 * GROUP, WINDOW), F32),
-                pltpu.VMEM((6 * HALF, 1024), BF16),
-                pltpu.VMEM((6 * HALF, 1024), BF16),
+                pltpu.VMEM((6 * HALF, 1024 * blocks_here), BF16),
+                pltpu.VMEM((6 * HALF, 1024 * blocks_here), BF16),
             ],
             input_output_aliases={base + place: place for place in range(len(joined))},
             compiler_params=PARAMS,

time: 61.1 us -> 61.9 us (1.013)
  waiting for transfers between devices: 8.89 us -> 10.6 us
  Pallas kernels: 16.5 us -> 17.5 us
  local copies, waits for them, and re-layouts: 0.76 us -> 0 us
  other arithmetic: 0.75 us -> 0 us
    ppermute x19, waiting for transfers between devices: 8.88 us -> 10.6 us  [ring(): lax.ppermute(value, axis, [(source, (source + steps) % count) for source...]
    pallas_call x2, Pallas kernels: 7.61 us -> 8.45 us  [attend(): pl.pallas_call(functools.partial(attend_kernel, blocks_here, head_count,...]
    squeeze x1 -> x0, local copies, waits for them, and re-layouts: 0.76 us -> none  [local(): parent_list[:, 0]]
    concatenate x1 -> x0, other arithmetic: 0.75 us -> none  [local(): jnp.concatenate([branch_start, branch_len, parent_list[:, 0], parent_list...]
  transfers between devices with their start and end apart: 21 -> 21, of which waited for: 9 -> 10; matrix products, arithmetic and copies ran while one was open for 2% -> 0% of each run, Pallas kernels for 14% -> 15%
where the time goes in v4:
time: 61.9 us; the launch traced here: 62 us
  starting transfers between devices  33.1 us (53%)
  Pallas kernels  17.5 us (28%)
  waiting for transfers between devices  10.6 us (17%)
  between operations  0.77 us (1%)
    ppermute x19, starting transfers between devices, ring(): lax.ppermute(value, axis, [(source, (source + steps) % count) for source...  26.4 us
    ppermute x19, waiting for transfers between devices, ring(): lax.ppermute(value, axis, [(source, (source + steps) % count) for source...  10.6 us
    pallas_call x2, Pallas kernels, attend(): pl.pallas_call(functools.partial(attend_kernel, blocks_here, head_count,...  8.45 us
    ppermute x2, starting transfers between devices, shift(): lax.ppermute(value, axis, [(source, source + steps) for source in range(l...  6.68 us
    pallas_call x2, Pallas kernels, flush(): pl.pallas_call(stage_kernel, out_shape=pltpu.HBM(value.shape, BF16), in_s...  2.65 us
    pallas_call x1, Pallas kernels, local(): pl.pallas_call(stage_kernel, out_shape=(pltpu.VMEM(queries.shape, BF16),)...  2.24 us
  transfers between devices with their start and end apart: 21, of which 10 were waited for; matrix products, arithmetic and copies ran while one was open for 0% of the time, Pallas kernels for 15%

profile of v4, /device:TPU:3, one launch (start us, length us, event | category | flops | bytes accessed | tf_op | source)
XLA Modules:
  0.0 62.0 jit_solution(13140698424527077485)
XLA Ops:
  0.6 1.2 %pack.1 = (bf16[256,256]{1,0:T(8,128)(2,1)S(1)}, bf16[256,256]{1,0:T(8,128)(2,1)S(1)}, bf16[256,256]{1,0:T(8,128)(2,1)S(1)}, bf16[256,256]{1,0:T(8,128)(2,1)S(1)...) custom-call(f32[16]{0:T(128)} %sink_hbm.1, ...), custom_call_target="tpu_custom_call" | custom-call | tf_op jit(solution)/shard_map/pack/pallas_call | solution.py:596
  1.8 1.9 %collective-permute-start = (bf16[256,256]{1,0:T(8,128)(2,1)S(1)}, bf16[256,256]{1,0:T(8,128)(2,1)S(1)}, u32[]{:S(2)}, u32[]{:S(2)}) collective-permute-start(bf16[256,256]{1,0:T(8,128)(2,1)S(1)} %get-tuple-element.54), channel_id=1, source_target_pairs={{0,1},{1,2},{2,3},{3,0},{4,5},{5,6},{6,7},{7,4},{8,9},{9,10},{10,1... | collective-permute-start | bytes 393224 | tf_op jit(solution)/shard_map/ppermute | solution.py:37
  4.1 3.4 %collective-permute-start.6 = (bf16[4,128,256]{2,1,0:T(8,128)(2,1)S(1)}, bf16[4,128,256]{2,1,0:T(8,128)(2,1)S(1)}, u32[]{:S(2)}, u32[]{:S(2)}) collective-permute-start(bf16[4,128,256]{2,1,0:T(8,128)(2,1)S(1)} %get-tuple-element.69), channel_id=1, source_target_pairs={{0,1},{1,2},{2,3},{4,5},{5,6},{6,7},{8,9},{9,10},{10,11},{12,13},{... | collective-permute-start | bytes 786440 | tf_op jit(solution)/shard_map/ppermute | solution.py:32
  8.3 1.5 %collective-permute-done.1.refs_2_ = bf16[256,256]{1,0:T(8,128)(2,1)S(1)} collective-permute-done((bf16[256,256]{1,0:T(8,128)(2,1)S(1)}, bf16[256,256]{1,0:T(8,128)(2,1)S(1)}, u32[]{:S(2)}, u32[]{:S(2)}) %collective-permute-start.1) | collective-permute-done | bytes 131104 | tf_op jit(solution)/shard_map/ppermute | solution.py:37
  11.0 2.3 %collective-permute-start.3 = (bf16[128,256]{1,0:T(8,128)(2,1)S(1)}, bf16[128,256]{1,0:T(8,128)(2,1)S(1)}, u32[]{:S(2)}, u32[]{:S(2)}) collective-permute-start(bf16[128,256]{1,0:T(8,128)(2,1)S(1)} %get-tuple-element.58), channel_id=1, source_target_pairs={{0,12},{4,16},{8,20},{12,24},{16,28},{20,0},{24,4},{28,8},{1,13},{... | collective-permute-start | bytes 196616 | tf_op jit(solution)/shard_map/ppermute | solution.py:37
  13.3 1.3 %collective-permute-start.4 = (bf16[128,256]{1,0:T(8,128)(2,1)S(1)}, bf16[128,256]{1,0:T(8,128)(2,1)S(1)}, u32[]{:S(2)}, u32[]{:S(2)}) collective-permute-start(bf16[128,256]{1,0:T(8,128)(2,1)S(1)} %get-tuple-element.59), channel_id=1, source_target_pairs={{0,8},{4,12},{8,16},{12,20},{16,24},{20,28},{24,0},{28,4},{1,9},{5... | collective-permute-start | bytes 196616 | tf_op jit(solution)/shard_map/ppermute | solution.py:37
  14.6 1.2 %collective-permute-start.5 = (bf16[128,256]{1,0:T(8,128)(2,1)S(1)}, bf16[128,256]{1,0:T(8,128)(2,1)S(1)}, u32[]{:S(2)}, u32[]{:S(2)}) collective-permute-start(bf16[128,256]{1,0:T(8,128)(2,1)S(1)} %get-tuple-element.60), channel_id=1, source_target_pairs={{0,4},{4,8},{8,12},{12,16},{16,20},{20,24},{24,28},{28,0},{1,5},{5... | collective-permute-start | bytes 196616 | tf_op jit(solution)/shard_map/ppermute | solution.py:37
  15.8 2.2 %stage.1 = (bf16[256,4096]{1,0:T(8,128)(2,1)S(1)}, bf16[256,4096]{1,0:T(8,128)(2,1)S(1)}) custom-call(bf16[256,4096]{1,0:T(8,128)(2,1)} %refs_0_, bf16[256,4096]{1,0:T(8,128)(2,1)} %refs_1_), custom_call_target="tpu_custom_call" | custom-call | tf_op jit(solution)/shard_map/stage/pallas_call | solution.py:631
  18.5 2.3 %collective-permute-start.9 = (bf16[128,256]{1,0:T(8,128)(2,1)S(1)}, bf16[128,256]{1,0:T(8,128)(2,1)S(1)}, u32[]{:S(2)}, u32[]{:S(2)}) collective-permute-start(bf16[128,256]{1,0:T(8,128)(2,1)S(1)} %arrive.1.refs_7_), channel_id=1, source_target_pairs={{0,3},{1,0},{2,1},{3,2},{4,7},{5,4},{6,5},{7,6},{8,11},{9,8},{10,9... | collective-permute-start | bytes 196616 | tf_op jit(solution)/shard_map/ppermute | solution.py:37
  21.3 1.9 %collective-permute-start.7 = (bf16[128,256]{1,0:T(8,128)(2,1)S(1)}, bf16[128,256]{1,0:T(8,128)(2,1)S(1)}, u32[]{:S(2)}, u32[]{:S(2)}) collective-permute-start(bf16[128,256]{1,0:T(8,128)(2,1)S(1)} %arrive.1.refs_7_), channel_id=1, source_target_pairs={{0,1},{1,2},{2,3},{3,0},{4,5},{5,6},{6,7},{7,4},{8,9},{9,10},{10,1... | collective-permute-start | bytes 196616 | tf_op jit(solution)/shard_map/ppermute | solution.py:37
  23.2 2.2 %attend.2 = (bf16[256,4096]{1,0:T(8,128)(2,1)S(1)}, bf16[256,4096]{1,0:T(8,128)(2,1)S(1)}, f32[256,512]{1,0:T(8,128)S(1)}, f32[256,512]{1,0:T(8,128)S(1)}, bf16[...) custom-call(s32[8,128]{1,0:T(8,128)S(1)} %plan.1.plan_ref.refs_0_, f32[64,128]{1,0:T(8,128)S(1)} %get-tuple-element.57.refs_1_, ...), custom_call_target="tpu_custom_call" | custom-call | tf_op jit(solution)/shard_map/attend/pallas_call | solution.py:665
  25.4 6.3 %attend.3 = (bf16[256,4096]{1,0:T(8,128)(2,1)S(1)}, bf16[256,4096]{1,0:T(8,128)(2,1)S(1)}, f32[256,512]{1,0:T(8,128)S(1)}, f32[256,512]{1,0:T(8,128)S(1)}, bf16[...) custom-call(s32[8,128]{1,0:T(8,128)S(1)} %plan.1.plan_ref.refs_0_, ...), custom_call_target="tpu_custom_call", output_to_operand_aliasing={{0}: (10, {}), {1}: (11, {}), {2}: (12, {}), {3}: (13, {}),... | custom-call | tf_op jit(solution)/shard_map/attend/pallas_call | solution.py:665
  31.7 5.9 %collective-permute-start.10 = (bf16[128,256]{1,0:T(8,128)(2,1)S(1)}, bf16[128,256]{1,0:T(8,128)(2,1)S(1)}, u32[]{:S(2)}, u32[]{:S(2)}) collective-permute-start(bf16[128,256]{1,0:T(8,128)(2,1)S(1)} %get-tuple-element.80), channel_id=1, source_target_pairs={{0,1},{1,2},{2,3},{3,0},{4,5},{5,6},{6,7},{7,4},{8,9},{9,10},{10,1... | collective-permute-start | bytes 196616 | tf_op jit(solution)/shard_map/ppermute | solution.py:37
  38.2 3.3 %collective-permute-start.16 = (bf16[4,128,256]{2,1,0:T(8,128)(2,1)S(1)}, bf16[4,128,256]{2,1,0:T(8,128)(2,1)S(1)}, u32[]{:S(2)}, u32[]{:S(2)}) collective-permute-start(bf16[4,128,256]{2,1,0:T(8,128)(2,1)S(1)} %get-tuple-element.93), channel_id=1, source_target_pairs={{1,0},{2,1},{3,2},{5,4},{6,5},{7,6},{9,8},{10,9},{11,10},{13,12},{... | collective-permute-start | bytes 786440 | tf_op jit(solution)/shard_map/ppermute | solution.py:32
  41.9 3.2 %collective-permute-start.15 = (bf16[128,256]{1,0:T(8,128)(2,1)S(1)}, bf16[128,256]{1,0:T(8,128)(2,1)S(1)}, u32[]{:S(2)}, u32[]{:S(2)}) collective-permute-start(bf16[128,256]{1,0:T(8,128)(2,1)S(1)} %gather.1.here_ref), channel_id=1, source_target_pairs={{0,20},{4,24},{8,28},{12,0},{16,4},{20,8},{24,12},{28,16},{1,21},{... | collective-permute-start | bytes 196616 | tf_op jit(solution)/shard_map/ppermute | solution.py:37
  45.1 1.9 %collective-permute-start.14 = (bf16[128,256]{1,0:T(8,128)(2,1)S(1)}, bf16[128,256]{1,0:T(8,128)(2,1)S(1)}, u32[]{:S(2)}, u32[]{:S(2)}) collective-permute-start(bf16[128,256]{1,0:T(8,128)(2,1)S(1)} %gather.1.here_ref), channel_id=1, source_target_pairs={{0,24},{4,28},{8,0},{12,4},{16,8},{20,12},{24,16},{28,20},{1,25},{... | collective-permute-start | bytes 196616 | tf_op jit(solution)/shard_map/ppermute | solution.py:37
  47.0 1.3 %flush.2 = bf16[256,4096]{1,0:T(8,128)(2,1)} custom-call(bf16[256,4096]{1,0:T(8,128)(2,1)S(1)} %get-tuple-element.83.refs_0_), custom_call_target="tpu_custom_call" | custom-call | tf_op jit(solution)/shard_map/flush/pallas_call | solution.py:715
  48.3 1.5 %collective-permute-done.15.refs_2_ = bf16[128,256]{1,0:T(8,128)(2,1)S(1)} collective-permute-done((bf16[128,256]{1,0:T(8,128)(2,1)S(1)}, bf16[128,256]{1,0:T(8,128)(2,1)S(1)}, u32[]{:S(2)}, u32[]{:S(2)}) %collective-permute-start.15) | collective-permute-done | bytes 65568 | tf_op jit(solution)/shard_map/ppermute | solution.py:37
  49.8 1.2 %collective-permute-done.13.refs_0_ = bf16[128,256]{1,0:T(8,128)(2,1)S(1)} collective-permute-done((bf16[128,256]{1,0:T(8,128)(2,1)S(1)}, bf16[128,256]{1,0:T(8,128)(2,1)S(1)}, u32[]{:S(2)}, u32[]{:S(2)}) %collective-permute-start.13) | collective-permute-done | bytes 65568 | tf_op jit(solution)/shard_map/ppermute | solution.py:37
  51.4 1.7 %collective-permute-start.18 = (bf16[256,256]{1,0:T(8,128)(2,1)S(1)}, bf16[256,256]{1,0:T(8,128)(2,1)S(1)}, u32[]{:S(2)}, u32[]{:S(2)}) collective-permute-start(bf16[256,256]{1,0:T(8,128)(2,1)S(1)} %get-tuple-element.95), channel_id=1, source_target_pairs={{0,1},{1,2},{2,3},{3,0},{4,5},{5,6},{6,7},{7,4},{8,9},{9,10},{10,1... | collective-permute-start | bytes 393224 | tf_op jit(solution)/shard_map/ppermute | solution.py:37
  53.1 1.3 %collective-permute-start.19 = (bf16[256,256]{1,0:T(8,128)(2,1)S(1)}, bf16[256,256]{1,0:T(8,128)(2,1)S(1)}, u32[]{:S(2)}, u32[]{:S(2)}) collective-permute-start(bf16[256,256]{1,0:T(8,128)(2,1)S(1)} %get-tuple-element.96), channel_id=1, source_target_pairs={{0,2},{1,3},{2,0},{3,1},{4,6},{5,7},{6,4},{7,5},{8,10},{9,11},{10,... | collective-permute-start | bytes 393224 | tf_op jit(solution)/shard_map/ppermute | solution.py:37
  54.5 1.3 %flush.3 = bf16[256,4096]{1,0:T(8,128)(2,1)} custom-call(bf16[256,4096]{1,0:T(8,128)(2,1)S(1)} %get-tuple-element.90.refs_0_), custom_call_target="tpu_custom_call" | custom-call | tf_op jit(solution)/shard_map/flush/pallas_call | solution.py:715
  55.8 2.0 %collective-permute-done.17.far_ref = f32[8,128]{1,0:T(8,128)S(1)} collective-permute-done((f32[8,128]{1,0:T(8,128)S(1)}, f32[8,128]{1,0:T(8,128)S(1)}, u32[]{:S(2)}, u32[]{:S(2)}) %collective-permute-start.17) | collective-permute-done | bytes 4128 | tf_op jit(solution)/shard_map/ppermute | solution.py:37
  57.8 2.6 %collective-permute-done.19.refs_2_ = bf16[256,256]{1,0:T(8,128)(2,1)S(1)} collective-permute-done((bf16[256,256]{1,0:T(8,128)(2,1)S(1)}, bf16[256,256]{1,0:T(8,128)(2,1)S(1)}, u32[]{:S(2)}, u32[]{:S(2)}) %collective-permute-start.19) | collective-permute-done | bytes 131104 | tf_op jit(solution)/shard_map/ppermute | solution.py:37
  (30 shorter events, 6.3 us)
Async XLA Ops:
  1.8 6.5 %collective-permute-start = (bf16[256,256]{1,0:T(8,128)(2,1)S(1)}, bf16[256,256]{1,0:T(8,128)(2,1)S(1)}, u32[]{:S(2)}, u32[]{:S(2)}) collective-permute-start(bf16[256,256]{1,0:T(8,128)(2,1)S(1)} %get-tuple-element.54), channel_id=1, source_target_pairs={{0,1},{1,2},{2,3},{3,0},{4,5},{5,6},{6,7},{7,4},{8,9},{9,10},{10,1... | collective-permute-start | bytes 393224 | tf_op jit(solution)/shard_map/ppermute | solution.py:37
  3.7 6.2 %collective-permute-start.1 = (bf16[256,256]{1,0:T(8,128)(2,1)S(1)}, bf16[256,256]{1,0:T(8,128)(2,1)S(1)}, u32[]{:S(2)}, u32[]{:S(2)}) collective-permute-start(bf16[256,256]{1,0:T(8,128)(2,1)S(1)} %get-tuple-element.55), channel_id=1, source_target_pairs={{0,2},{1,3},{2,0},{3,1},{4,6},{5,7},{6,4},{7,5},{8,10},{9,11},{10,... | collective-permute-start | bytes 393224 | tf_op jit(solution)/shard_map/ppermute | solution.py:37
  3.9 6.6 %collective-permute-start.2 = (bf16[256,256]{1,0:T(8,128)(2,1)S(1)}, bf16[256,256]{1,0:T(8,128)(2,1)S(1)}, u32[]{:S(2)}, u32[]{:S(2)}) collective-permute-start(bf16[256,256]{1,0:T(8,128)(2,1)S(1)} %get-tuple-element.56), channel_id=1, source_target_pairs={{0,3},{1,0},{2,1},{3,2},{4,7},{5,4},{6,5},{7,6},{8,11},{9,8},{10,9... | collective-permute-start | bytes 393224 | tf_op jit(solution)/shard_map/ppermute | solution.py:37
  4.1 21.3 %collective-permute-start.6 = (bf16[4,128,256]{2,1,0:T(8,128)(2,1)S(1)}, bf16[4,128,256]{2,1,0:T(8,128)(2,1)S(1)}, u32[]{:S(2)}, u32[]{:S(2)}) collective-permute-start(bf16[4,128,256]{2,1,0:T(8,128)(2,1)S(1)} %get-tuple-element.69), channel_id=1, source_target_pairs={{0,1},{1,2},{2,3},{4,5},{5,6},{6,7},{8,9},{9,10},{10,11},{12,13},{... | collective-permute-start | bytes 786440 | tf_op jit(solution)/shard_map/ppermute | solution.py:32
  11.0 7.1 %collective-permute-start.3 = (bf16[128,256]{1,0:T(8,128)(2,1)S(1)}, bf16[128,256]{1,0:T(8,128)(2,1)S(1)}, u32[]{:S(2)}, u32[]{:S(2)}) collective-permute-start(bf16[128,256]{1,0:T(8,128)(2,1)S(1)} %get-tuple-element.58), channel_id=1, source_target_pairs={{0,12},{4,16},{8,20},{12,24},{16,28},{20,0},{24,4},{28,8},{1,13},{... | collective-permute-start | bytes 196616 | tf_op jit(solution)/shard_map/ppermute | solution.py:37
  13.3 4.9 %collective-permute-start.4 = (bf16[128,256]{1,0:T(8,128)(2,1)S(1)}, bf16[128,256]{1,0:T(8,128)(2,1)S(1)}, u32[]{:S(2)}, u32[]{:S(2)}) collective-permute-start(bf16[128,256]{1,0:T(8,128)(2,1)S(1)} %get-tuple-element.59), channel_id=1, source_target_pairs={{0,8},{4,12},{8,16},{12,20},{16,24},{20,28},{24,0},{28,4},{1,9},{5... | collective-permute-start | bytes 196616 | tf_op jit(solution)/shard_map/ppermute | solution.py:37
  14.6 3.7 %collective-permute-start.5 = (bf16[128,256]{1,0:T(8,128)(2,1)S(1)}, bf16[128,256]{1,0:T(8,128)(2,1)S(1)}, u32[]{:S(2)}, u32[]{:S(2)}) collective-permute-start(bf16[128,256]{1,0:T(8,128)(2,1)S(1)} %get-tuple-element.60), channel_id=1, source_target_pairs={{0,4},{4,8},{8,12},{12,16},{16,20},{20,24},{24,28},{28,0},{1,5},{5... | collective-permute-start | bytes 196616 | tf_op jit(solution)/shard_map/ppermute | solution.py:37
  18.5 6.9 %collective-permute-start.9 = (bf16[128,256]{1,0:T(8,128)(2,1)S(1)}, bf16[128,256]{1,0:T(8,128)(2,1)S(1)}, u32[]{:S(2)}, u32[]{:S(2)}) collective-permute-start(bf16[128,256]{1,0:T(8,128)(2,1)S(1)} %arrive.1.refs_7_), channel_id=1, source_target_pairs={{0,3},{1,0},{2,1},{3,2},{4,7},{5,4},{6,5},{7,6},{8,11},{9,8},{10,9... | collective-permute-start | bytes 196616 | tf_op jit(solution)/shard_map/ppermute | solution.py:37
  20.8 4.7 %collective-permute-start.8 = (bf16[128,256]{1,0:T(8,128)(2,1)S(1)}, bf16[128,256]{1,0:T(8,128)(2,1)S(1)}, u32[]{:S(2)}, u32[]{:S(2)}) collective-permute-start(bf16[128,256]{1,0:T(8,128)(2,1)S(1)} %arrive.1.refs_7_), channel_id=1, source_target_pairs={{0,2},{1,3},{2,0},{3,1},{4,6},{5,7},{6,4},{7,5},{8,10},{9,11},{10,... | collective-permute-start | bytes 196616 | tf_op jit(solution)/shard_map/ppermute | solution.py:37
  21.3 4.1 %collective-permute-start.7 = (bf16[128,256]{1,0:T(8,128)(2,1)S(1)}, bf16[128,256]{1,0:T(8,128)(2,1)S(1)}, u32[]{:S(2)}, u32[]{:S(2)}) collective-permute-start(bf16[128,256]{1,0:T(8,128)(2,1)S(1)} %arrive.1.refs_7_), channel_id=1, source_target_pairs={{0,1},{1,2},{2,3},{3,0},{4,5},{5,6},{6,7},{7,4},{8,9},{9,10},{10,1... | collective-permute-start | bytes 196616 | tf_op jit(solution)/shard_map/ppermute | solution.py:37
  31.7 9.7 %collective-permute-start.10 = (bf16[128,256]{1,0:T(8,128)(2,1)S(1)}, bf16[128,256]{1,0:T(8,128)(2,1)S(1)}, u32[]{:S(2)}, u32[]{:S(2)}) collective-permute-start(bf16[128,256]{1,0:T(8,128)(2,1)S(1)} %get-tuple-element.80), channel_id=1, source_target_pairs={{0,1},{1,2},{2,3},{3,0},{4,5},{5,6},{6,7},{7,4},{8,9},{9,10},{10,1... | collective-permute-start | bytes 196616 | tf_op jit(solution)/shard_map/ppermute | solution.py:37
  37.7 3.8 %collective-permute-start.11 = (bf16[128,256]{1,0:T(8,128)(2,1)S(1)}, bf16[128,256]{1,0:T(8,128)(2,1)S(1)}, u32[]{:S(2)}, u32[]{:S(2)}) collective-permute-start(bf16[128,256]{1,0:T(8,128)(2,1)S(1)} %get-tuple-element.81), channel_id=1, source_target_pairs={{0,2},{1,3},{2,0},{3,1},{4,6},{5,7},{6,4},{7,5},{8,10},{9,11},{10,... | collective-permute-start | bytes 196616 | tf_op jit(solution)/shard_map/ppermute | solution.py:37
  38.0 3.8 %collective-permute-start.12 = (bf16[128,256]{1,0:T(8,128)(2,1)S(1)}, bf16[128,256]{1,0:T(8,128)(2,1)S(1)}, u32[]{:S(2)}, u32[]{:S(2)}) collective-permute-start(bf16[128,256]{1,0:T(8,128)(2,1)S(1)} %get-tuple-element.82), channel_id=1, source_target_pairs={{0,3},{1,0},{2,1},{3,2},{4,7},{5,4},{6,5},{7,6},{8,11},{9,8},{10,9... | collective-permute-start | bytes 196616 | tf_op jit(solution)/shard_map/ppermute | solution.py:37
  38.2 19.7 %collective-permute-start.16 = (bf16[4,128,256]{2,1,0:T(8,128)(2,1)S(1)}, bf16[4,128,256]{2,1,0:T(8,128)(2,1)S(1)}, u32[]{:S(2)}, u32[]{:S(2)}) collective-permute-start(bf16[4,128,256]{2,1,0:T(8,128)(2,1)S(1)} %get-tuple-element.93), channel_id=1, source_target_pairs={{1,0},{2,1},{3,2},{5,4},{6,5},{7,6},{9,8},{10,9},{11,10},{13,12},{... | collective-permute-start | bytes 786440 | tf_op jit(solution)/shard_map/ppermute | solution.py:32
  41.9 7.9 %collective-permute-start.15 = (bf16[128,256]{1,0:T(8,128)(2,1)S(1)}, bf16[128,256]{1,0:T(8,128)(2,1)S(1)}, u32[]{:S(2)}, u32[]{:S(2)}) collective-permute-start(bf16[128,256]{1,0:T(8,128)(2,1)S(1)} %gather.1.here_ref), channel_id=1, source_target_pairs={{0,20},{4,24},{8,28},{12,0},{16,4},{20,8},{24,12},{28,16},{1,21},{... | collective-permute-start | bytes 196616 | tf_op jit(solution)/shard_map/ppermute | solution.py:37
  45.1 4.7 %collective-permute-start.14 = (bf16[128,256]{1,0:T(8,128)(2,1)S(1)}, bf16[128,256]{1,0:T(8,128)(2,1)S(1)}, u32[]{:S(2)}, u32[]{:S(2)}) collective-permute-start(bf16[128,256]{1,0:T(8,128)(2,1)S(1)} %gather.1.here_ref), channel_id=1, source_target_pairs={{0,24},{4,28},{8,0},{12,4},{16,8},{20,12},{24,16},{28,20},{1,25},{... | collective-permute-start | bytes 196616 | tf_op jit(solution)/shard_map/ppermute | solution.py:37
  47.0 4.0 %collective-permute-start.13 = (bf16[128,256]{1,0:T(8,128)(2,1)S(1)}, bf16[128,256]{1,0:T(8,128)(2,1)S(1)}, u32[]{:S(2)}, u32[]{:S(2)}) collective-permute-start(bf16[128,256]{1,0:T(8,128)(2,1)S(1)} %gather.1.here_ref), channel_id=1, source_target_pairs={{0,28},{4,0},{8,4},{12,8},{16,12},{20,16},{24,20},{28,24},{1,29},{... | collective-permute-start | bytes 196616 | tf_op jit(solution)/shard_map/ppermute | solution.py:37
  51.4 6.4 %collective-permute-start.18 = (bf16[256,256]{1,0:T(8,128)(2,1)S(1)}, bf16[256,256]{1,0:T(8,128)(2,1)S(1)}, u32[]{:S(2)}, u32[]{:S(2)}) collective-permute-start(bf16[256,256]{1,0:T(8,128)(2,1)S(1)} %get-tuple-element.95), channel_id=1, source_target_pairs={{0,1},{1,2},{2,3},{3,0},{4,5},{5,6},{6,7},{7,4},{8,9},{9,10},{10,1... | collective-permute-start | bytes 393224 | tf_op jit(solution)/shard_map/ppermute | solution.py:37
  53.1 7.3 %collective-permute-start.19 = (bf16[256,256]{1,0:T(8,128)(2,1)S(1)}, bf16[256,256]{1,0:T(8,128)(2,1)S(1)}, u32[]{:S(2)}, u32[]{:S(2)}) collective-permute-start(bf16[256,256]{1,0:T(8,128)(2,1)S(1)} %get-tuple-element.96), channel_id=1, source_target_pairs={{0,2},{1,3},{2,0},{3,1},{4,6},{5,7},{6,4},{7,5},{8,10},{9,11},{10,... | collective-permute-start | bytes 393224 | tf_op jit(solution)/shard_map/ppermute | solution.py:37
  54.4 6.6 %collective-permute-start.20 = (bf16[256,256]{1,0:T(8,128)(2,1)S(1)}, bf16[256,256]{1,0:T(8,128)(2,1)S(1)}, u32[]{:S(2)}, u32[]{:S(2)}) collective-permute-start(bf16[256,256]{1,0:T(8,128)(2,1)S(1)} %get-tuple-element.97), channel_id=1, source_target_pairs={{0,3},{1,0},{2,1},{3,2},{4,7},{5,4},{6,5},{7,6},{8,11},{9,8},{10,9... | collective-permute-start | bytes 393224 | tf_op jit(solution)/shard_map/ppermute | solution.py:37
  54.5 3.4 %collective-permute-start.17 = (f32[8,128]{1,0:T(8,128)S(1)}, f32[8,128]{1,0:T(8,128)S(1)}, u32[]{:S(2)}, u32[]{:S(2)}) collective-permute-start(f32[8,128]{1,0:T(8,128)S(1)} %get-tuple-element.89.sink_ref), channel_id=1, source_target_pairs={{0,16},{4,20},{8,24},{12,28},{16,0},{20,4},{24,8},{28,12},{1,17},{... | collective-permute-start | bytes 12296 | tf_op jit(solution)/shard_map/ppermute | solution.py:37

commit v5 on v3

--- a/solution.py
+++ b/solution.py
@@ -55,39 +55,37 @@
     return jnp.where(lax.broadcasted_iota(jnp.int32, (1, 128), 1) < 32, row, 0.0)
 
 
-def child_tail(table, tok, distance, tok_count, blocks):
-    branches = tok_count * BR_DEV
+def child_tail(starts, parents, tok, distance, tok_count, blocks):
     child = jnp.minimum(tok + distance, tok_count - 1) * BR_DEV
-    parent = table[2 * branches + child]
+    parent = parents[0, child]
     safe = jnp.maximum(parent, 0)
     valid = (tok + distance < tok_count) & (parent >= 0) & (safe // BR_DEV == tok)
-    place = (table[safe] + table[3 * branches + child]) // WINDOW - tok * blocks
+    place = (starts[safe] + parents[1, child]) // WINDOW - tok * blocks
     return valid, jnp.where(valid, place, 0)
 
 
-def block_state(table, tok, tok_count, block):
-    branches = tok_count * BR_DEV
+def block_state(starts, lengths, parents, tok, block):
     position = block * WINDOW
     alive, opening = jnp.bool_(False), jnp.bool_(False)
     for branch in range(BR_DEV):
-        start = table[tok * BR_DEV + branch]
-        length = table[branches + tok * BR_DEV + branch]
+        start = starts[tok * BR_DEV + branch]
+        length = lengths[tok * BR_DEV + branch]
         alive = alive | ((start <= position) & (position < start + length))
         opening = opening | (start == position)
-    has_tail = table[2 * branches + tok * BR_DEV] >= 0
+    has_tail = parents[0, tok * BR_DEV] >= 0
     return alive, opening, jnp.logical_not(opening) | has_tail
 
 
-def plan_kernel(tok_count, blocks, blocks_here, table, plan_ref):
+def plan_kernel(tok_count, blocks, blocks_here, starts, lengths, parents, plan_ref):
     tok, head = lax.axis_index("tok"), lax.axis_index("head")
     values = []
     for distance in range(1, LAG + 1):
-        values += child_tail(table, tok, distance, tok_count, blocks)
-    parent = table[2 * tok_count * BR_DEV + tok * BR_DEV]
+        values += child_tail(starts, parents, tok, distance, tok_count, blocks)
+    parent = parents[0, tok * BR_DEV]
     values.append(jnp.where(parent >= 0, tok - jnp.maximum(parent, 0) // BR_DEV, 1))
     for block in range(blocks_here):
         number = tok * blocks + head * blocks_here + block
-        values += block_state(table, tok, tok_count, number)
+        values += block_state(starts, lengths, parents, tok, number)
     lane = lax.broadcasted_iota(jnp.int32, plan_ref.shape, 1)
     plan = jnp.zeros(plan_ref.shape, jnp.int32)
     for place, value in enumerate(values):
@@ -292,6 +290,15 @@
         high16 = BF16(1) - low16
 
         def padded(seen):
+            seen = jnp.concatenate(
+                [
+                    seen[start + by : start + by + 16]
+                    for by in range(0, HALF, 16)
+                    for start in (0, HALF)
+                ]
+                + [seen[2 * HALF :]],
+                axis=0,
+            )
             swapped = jnp.concatenate([seen[:, 64:], seen[:, :64]], axis=1)
             return (
                 jnp.concatenate([seen * low16, swapped * high16], axis=0),
@@ -342,11 +349,16 @@
             )
             parts = []
             for base in (0, seen):
-                near, far = slice(base, base + HALF), slice(base + HALF, base + 2 * HALF)
+                edge, dp_edge = [], []
+                for by in range(0, HALF, 16):
+                    start = base + 2 * by
+                    near, far = slice(start, start + 16), slice(start + 16, start + 32)
+                    edge.append(jnp.where(own[by : by + 16], score[near], score[far] + bias))
+                    dp_edge.append(jnp.where(own[by : by + 16], dp[near], dp[far]))
+                edge, dp_edge = (jnp.concatenate(value, axis=0) for value in (edge, dp_edge))
                 rest = slice(base + 2 * HALF, base + 3 * HALF)
-                edge = jnp.where(own, score[near], score[far] + bias)
                 whole = score[rest] + bias if half == 0 else score[rest]
-                parts.append((edge, whole, jnp.where(own, dp[near], dp[far]), dp[rest]))
+                parts.append((edge, whole, dp_edge, dp[rest]))
             return parts
 
         def weigh(index, odd, edge, whole, dp_edge, dp_whole):
@@ -420,17 +432,16 @@
             )
             return total + pltpu.roll(total, HEAD_DIM, 1)
 
-        ahead, parts = products(0), []
+        parts = []
         for index in range(len(items)):
-            now = ahead
-            weigh(index, 0, *now[0])
-            if index + 1 < len(items):
-                ahead = products(index + 1)
-            weigh(index, 1, *now[1])
+            now = products(index)
             if index >= 1:
                 finish(index - 1)
-            parts.append(reduce(index))
+                parts.append(reduce(index - 1))
+            weigh(index, 0, *now[0])
+            weigh(index, 1, *now[1])
         finish(len(items) - 1)
+        parts.append(reduce(len(items) - 1))
         grads = [
             [join(parts[2 * unit][place], parts[2 * unit + 1][place]) for place in range(2)]
             for unit in range(2)
@@ -556,7 +567,6 @@
     def close(value):
         return pltpu.with_memory_space_constraint(value, pltpu.VMEM)
 
-    table = jnp.concatenate([branch_start, branch_len, parent_list[:, 0], parent_list[:, 1]])
     *slots, halo_out, keys, values = pl.pallas_call(
         pack_kernel,
         out_shape=(shape((rows, width)),) * head_count
@@ -576,11 +586,11 @@
     plan = pl.pallas_call(
         functools.partial(plan_kernel, tok_count, blocks, blocks_here),
         out_shape=pltpu.VMEM((8, 128), jnp.int32),
-        in_specs=[SMEM],
+        in_specs=[SMEM] * 3,
         out_specs=VMEM,
         compiler_params=PARAMS,
         name="plan",
-    )(table)
+    )(far(branch_start), far(branch_len), far(parent_list.T))
     plan = close(plan)
     *chosen, sinks = pl.pallas_call(
         choose_kernel,

time: 61.1 us -> 62 us (1.015)
  local copies, waits for them, and re-layouts: 0.76 us -> 0 us
  other arithmetic: 0.75 us -> 0 us
  starting transfers between devices: 33.3 us -> 34 us
    squeeze x1 -> x0, local copies, waits for them, and re-layouts: 0.76 us -> none  [local(): parent_list[:, 0]]
    concatenate x1 -> x0, other arithmetic: 0.75 us -> none  [local(): jnp.concatenate([branch_start, branch_len, parent_list[:, 0], parent_list...]
    ppermute x19, starting transfers between devices: 26.6 us -> 27.4 us  [ring(): lax.ppermute(value, axis, [(source, (source + steps) % count) for source...]
  transfers between devices with their start and end apart: 21 -> 21, of which waited for: 9 -> 11; matrix products, arithmetic and copies ran while one was open for 2% -> 0% of each run, Pallas kernels for 14% -> 15%
where the time goes in v5:
time: 62 us; the launch traced here: 61.3 us
  starting transfers between devices  34 us (55%)
  Pallas kernels  17.1 us (28%)
  waiting for transfers between devices  9.41 us (15%)
  between operations  0.77 us (1%)
    ppermute x19, starting transfers between devices, ring(): lax.ppermute(value, axis, [(source, (source + steps) % count) for source...  27.4 us
    ppermute x19, waiting for transfers between devices, ring(): lax.ppermute(value, axis, [(source, (source + steps) % count) for source...  9.4 us
    pallas_call x2, Pallas kernels, attend(): pl.pallas_call(functools.partial(attend_kernel, blocks_here, head_count,...  8.02 us
    ppermute x2, starting transfers between devices, shift(): lax.ppermute(value, axis, [(source, source + steps) for source in range(l...  6.68 us
    pallas_call x2, Pallas kernels, flush(): pl.pallas_call(stage_kernel, out_shape=pltpu.HBM(value.shape, BF16), in_s...  2.65 us
    pallas_call x1, Pallas kernels, local(): pl.pallas_call(stage_kernel, out_shape=(pltpu.VMEM(queries.shape, BF16),)...  2.24 us
  transfers between devices with their start and end apart: 21, of which 11 were waited for; matrix products, arithmetic and copies ran while one was open for 0% of the time, Pallas kernels for 15%

profile of v5, /device:TPU:3, one launch (start us, length us, event | category | flops | bytes accessed | tf_op | source)
XLA Modules:
  0.0 61.3 jit_solution(13061032856156548449)
XLA Ops:
  0.6 1.2 %pack.1 = (bf16[256,256]{1,0:T(8,128)(2,1)S(1)}, bf16[256,256]{1,0:T(8,128)(2,1)S(1)}, bf16[256,256]{1,0:T(8,128)(2,1)S(1)}, bf16[256,256]{1,0:T(8,128)(2,1)S(1)...) custom-call(f32[16]{0:T(128)} %sink_hbm.1, ...), custom_call_target="tpu_custom_call" | custom-call | tf_op jit(solution)/shard_map/pack/pallas_call | solution.py:570
  1.8 1.9 %collective-permute-start = (bf16[256,256]{1,0:T(8,128)(2,1)S(1)}, bf16[256,256]{1,0:T(8,128)(2,1)S(1)}, u32[]{:S(2)}, u32[]{:S(2)}) collective-permute-start(bf16[256,256]{1,0:T(8,128)(2,1)S(1)} %get-tuple-element.54), channel_id=1, source_target_pairs={{0,1},{1,2},{2,3},{3,0},{4,5},{5,6},{6,7},{7,4},{8,9},{9,10},{10,1... | collective-permute-start | bytes 393224 | tf_op jit(solution)/shard_map/ppermute | solution.py:37
  4.1 3.4 %collective-permute-start.6 = (bf16[4,128,256]{2,1,0:T(8,128)(2,1)S(1)}, bf16[4,128,256]{2,1,0:T(8,128)(2,1)S(1)}, u32[]{:S(2)}, u32[]{:S(2)}) collective-permute-start(bf16[4,128,256]{2,1,0:T(8,128)(2,1)S(1)} %get-tuple-element.69), channel_id=1, source_target_pairs={{0,1},{1,2},{2,3},{4,5},{5,6},{6,7},{8,9},{9,10},{10,11},{12,13},{... | collective-permute-start | bytes 786440 | tf_op jit(solution)/shard_map/ppermute | solution.py:32
  7.5 0.8 %plan.1.plan_ref.refs_0_ = s32[8,128]{1,0:T(8,128)S(1)} custom-call(s32[16]{0:T(128)} %starts.1, s32[16]{0:T(128)} %lengths.1, s32[2,16]{1,0:T(2,128)} %bitcast.1), custom_call_target="tpu_custom_call" | custom-call | tf_op jit(solution)/shard_map/plan/pallas_call | solution.py:586
  8.3 1.5 %collective-permute-done.1.refs_2_ = bf16[256,256]{1,0:T(8,128)(2,1)S(1)} collective-permute-done((bf16[256,256]{1,0:T(8,128)(2,1)S(1)}, bf16[256,256]{1,0:T(8,128)(2,1)S(1)}, u32[]{:S(2)}, u32[]{:S(2)}) %collective-permute-start.1) | collective-permute-done | bytes 131104 | tf_op jit(solution)/shard_map/ppermute | solution.py:37
  11.0 2.3 %collective-permute-start.3 = (bf16[128,256]{1,0:T(8,128)(2,1)S(1)}, bf16[128,256]{1,0:T(8,128)(2,1)S(1)}, u32[]{:S(2)}, u32[]{:S(2)}) collective-permute-start(bf16[128,256]{1,0:T(8,128)(2,1)S(1)} %get-tuple-element.58), channel_id=1, source_target_pairs={{0,12},{4,16},{8,20},{12,24},{16,28},{20,0},{24,4},{28,8},{1,13},{... | collective-permute-start | bytes 196616 | tf_op jit(solution)/shard_map/ppermute | solution.py:37
  13.3 1.3 %collective-permute-start.4 = (bf16[128,256]{1,0:T(8,128)(2,1)S(1)}, bf16[128,256]{1,0:T(8,128)(2,1)S(1)}, u32[]{:S(2)}, u32[]{:S(2)}) collective-permute-start(bf16[128,256]{1,0:T(8,128)(2,1)S(1)} %get-tuple-element.59), channel_id=1, source_target_pairs={{0,8},{4,12},{8,16},{12,20},{16,24},{20,28},{24,0},{28,4},{1,9},{5... | collective-permute-start | bytes 196616 | tf_op jit(solution)/shard_map/ppermute | solution.py:37
  14.6 1.2 %collective-permute-start.5 = (bf16[128,256]{1,0:T(8,128)(2,1)S(1)}, bf16[128,256]{1,0:T(8,128)(2,1)S(1)}, u32[]{:S(2)}, u32[]{:S(2)}) collective-permute-start(bf16[128,256]{1,0:T(8,128)(2,1)S(1)} %get-tuple-element.60), channel_id=1, source_target_pairs={{0,4},{4,8},{8,12},{12,16},{16,20},{20,24},{24,28},{28,0},{1,5},{5... | collective-permute-start | bytes 196616 | tf_op jit(solution)/shard_map/ppermute | solution.py:37
  15.8 2.2 %stage.1 = (bf16[256,4096]{1,0:T(8,128)(2,1)S(1)}, bf16[256,4096]{1,0:T(8,128)(2,1)S(1)}) custom-call(bf16[256,4096]{1,0:T(8,128)(2,1)} %refs_0_, bf16[256,4096]{1,0:T(8,128)(2,1)} %refs_1_), custom_call_target="tpu_custom_call" | custom-call | tf_op jit(solution)/shard_map/stage/pallas_call | solution.py:605
  18.5 2.3 %collective-permute-start.9 = (bf16[128,256]{1,0:T(8,128)(2,1)S(1)}, bf16[128,256]{1,0:T(8,128)(2,1)S(1)}, u32[]{:S(2)}, u32[]{:S(2)}) collective-permute-start(bf16[128,256]{1,0:T(8,128)(2,1)S(1)} %arrive.1.refs_7_), channel_id=1, source_target_pairs={{0,3},{1,0},{2,1},{3,2},{4,7},{5,4},{6,5},{7,6},{8,11},{9,8},{10,9... | collective-permute-start | bytes 196616 | tf_op jit(solution)/shard_map/ppermute | solution.py:37
  21.3 1.9 %collective-permute-start.7 = (bf16[128,256]{1,0:T(8,128)(2,1)S(1)}, bf16[128,256]{1,0:T(8,128)(2,1)S(1)}, u32[]{:S(2)}, u32[]{:S(2)}) collective-permute-start(bf16[128,256]{1,0:T(8,128)(2,1)S(1)} %arrive.1.refs_7_), channel_id=1, source_target_pairs={{0,1},{1,2},{2,3},{3,0},{4,5},{5,6},{6,7},{7,4},{8,9},{9,10},{10,1... | collective-permute-start | bytes 196616 | tf_op jit(solution)/shard_map/ppermute | solution.py:37
  23.2 2.1 %attend.2 = (bf16[256,4096]{1,0:T(8,128)(2,1)S(1)}, bf16[256,4096]{1,0:T(8,128)(2,1)S(1)}, f32[256,512]{1,0:T(8,128)S(1)}, f32[256,512]{1,0:T(8,128)S(1)}, bf16[...) custom-call(s32[8,128]{1,0:T(8,128)S(1)} %plan.1.plan_ref.refs_0_, f32[64,128]{1,0:T(8,128)S(1)} %get-tuple-element.57.refs_1_, ...), custom_call_target="tpu_custom_call" | custom-call | tf_op jit(solution)/shard_map/attend/pallas_call | solution.py:639
  25.3 6.0 %attend.3 = (bf16[256,4096]{1,0:T(8,128)(2,1)S(1)}, bf16[256,4096]{1,0:T(8,128)(2,1)S(1)}, f32[256,512]{1,0:T(8,128)S(1)}, f32[256,512]{1,0:T(8,128)S(1)}, bf16[...) custom-call(s32[8,128]{1,0:T(8,128)S(1)} %plan.1.plan_ref.refs_0_, ...), custom_call_target="tpu_custom_call", output_to_operand_aliasing={{0}: (10, {}), {1}: (11, {}), {2}: (12, {}), {3}: (13, {}),... | custom-call | tf_op jit(solution)/shard_map/attend/pallas_call | solution.py:639
  31.3 6.7 %collective-permute-start.10 = (bf16[128,256]{1,0:T(8,128)(2,1)S(1)}, bf16[128,256]{1,0:T(8,128)(2,1)S(1)}, u32[]{:S(2)}, u32[]{:S(2)}) collective-permute-start(bf16[128,256]{1,0:T(8,128)(2,1)S(1)} %get-tuple-element.80), channel_id=1, source_target_pairs={{0,1},{1,2},{2,3},{3,0},{4,5},{5,6},{6,7},{7,4},{8,9},{9,10},{10,1... | collective-permute-start | bytes 196616 | tf_op jit(solution)/shard_map/ppermute | solution.py:37
  38.5 3.3 %collective-permute-start.16 = (bf16[4,128,256]{2,1,0:T(8,128)(2,1)S(1)}, bf16[4,128,256]{2,1,0:T(8,128)(2,1)S(1)}, u32[]{:S(2)}, u32[]{:S(2)}) collective-permute-start(bf16[4,128,256]{2,1,0:T(8,128)(2,1)S(1)} %get-tuple-element.93), channel_id=1, source_target_pairs={{1,0},{2,1},{3,2},{5,4},{6,5},{7,6},{9,8},{10,9},{11,10},{13,12},{... | collective-permute-start | bytes 786440 | tf_op jit(solution)/shard_map/ppermute | solution.py:32
  42.2 2.7 %collective-permute-start.15 = (bf16[128,256]{1,0:T(8,128)(2,1)S(1)}, bf16[128,256]{1,0:T(8,128)(2,1)S(1)}, u32[]{:S(2)}, u32[]{:S(2)}) collective-permute-start(bf16[128,256]{1,0:T(8,128)(2,1)S(1)} %gather.1.here_ref), channel_id=1, source_target_pairs={{0,20},{4,24},{8,28},{12,0},{16,4},{20,8},{24,12},{28,16},{1,21},{... | collective-permute-start | bytes 196616 | tf_op jit(solution)/shard_map/ppermute | solution.py:37
  44.8 1.4 %collective-permute-start.14 = (bf16[128,256]{1,0:T(8,128)(2,1)S(1)}, bf16[128,256]{1,0:T(8,128)(2,1)S(1)}, u32[]{:S(2)}, u32[]{:S(2)}) collective-permute-start(bf16[128,256]{1,0:T(8,128)(2,1)S(1)} %gather.1.here_ref), channel_id=1, source_target_pairs={{0,24},{4,28},{8,0},{12,4},{16,8},{20,12},{24,16},{28,20},{1,25},{... | collective-permute-start | bytes 196616 | tf_op jit(solution)/shard_map/ppermute | solution.py:37
  46.6 1.3 %flush.2 = bf16[256,4096]{1,0:T(8,128)(2,1)} custom-call(bf16[256,4096]{1,0:T(8,128)(2,1)S(1)} %get-tuple-element.83.refs_0_), custom_call_target="tpu_custom_call" | custom-call | tf_op jit(solution)/shard_map/flush/pallas_call | solution.py:689
  47.9 1.5 %collective-permute-done.15.refs_2_ = bf16[128,256]{1,0:T(8,128)(2,1)S(1)} collective-permute-done((bf16[128,256]{1,0:T(8,128)(2,1)S(1)}, bf16[128,256]{1,0:T(8,128)(2,1)S(1)}, u32[]{:S(2)}, u32[]{:S(2)}) %collective-permute-start.15) | collective-permute-done | bytes 65568 | tf_op jit(solution)/shard_map/ppermute | solution.py:37
  50.7 2.9 %collective-permute-start.18 = (bf16[256,256]{1,0:T(8,128)(2,1)S(1)}, bf16[256,256]{1,0:T(8,128)(2,1)S(1)}, u32[]{:S(2)}, u32[]{:S(2)}) collective-permute-start(bf16[256,256]{1,0:T(8,128)(2,1)S(1)} %get-tuple-element.95), channel_id=1, source_target_pairs={{0,1},{1,2},{2,3},{3,0},{4,5},{5,6},{6,7},{7,4},{8,9},{9,10},{10,1... | collective-permute-start | bytes 393224 | tf_op jit(solution)/shard_map/ppermute | solution.py:37
  54.6 1.3 %flush.3 = bf16[256,4096]{1,0:T(8,128)(2,1)} custom-call(bf16[256,4096]{1,0:T(8,128)(2,1)S(1)} %get-tuple-element.90.refs_0_), custom_call_target="tpu_custom_call" | custom-call | tf_op jit(solution)/shard_map/flush/pallas_call | solution.py:689
  56.0 1.5 %collective-permute-done.17.far_ref = f32[8,128]{1,0:T(8,128)S(1)} collective-permute-done((f32[8,128]{1,0:T(8,128)S(1)}, f32[8,128]{1,0:T(8,128)S(1)}, u32[]{:S(2)}, u32[]{:S(2)}) %collective-permute-start.17) | collective-permute-done | bytes 4128 | tf_op jit(solution)/shard_map/ppermute | solution.py:37
  57.5 2.2 %collective-permute-done.19.refs_2_ = bf16[256,256]{1,0:T(8,128)(2,1)S(1)} collective-permute-done((bf16[256,256]{1,0:T(8,128)(2,1)S(1)}, bf16[256,256]{1,0:T(8,128)(2,1)S(1)}, u32[]{:S(2)}, u32[]{:S(2)}) %collective-permute-start.19) | collective-permute-done | bytes 131104 | tf_op jit(solution)/shard_map/ppermute | solution.py:37
  60.3 1.0 %total.1 = (bf16[256,512]{1,0:T(8,128)(2,1)}, bf16[256,512]{1,0:T(8,128)(2,1)}, f32[16]{0:T(128)}) custom-call(f32[256,512]{1,0:T(8,128)S(1)} %get-tuple-element.91.dk_ref, f32[256,512]{1,0:T(8,128)S(1)} %get-tuple-element.92.dv_ref, bf16[4,128,256]{2,1,0:T(8,128)(2,1)S(1)} %collective-permute-done.16.halo_ref, f32[8,128]{1,0:T(8,128)S(1)} %get-tuple-element.89.sink_ref, ...), custom_call_target="tpu_custom_call" | custom-call | tf_op jit(solution)/shard_map/total/pallas_call | solution.py:720
  (30 shorter events, 6.7 us)
Async XLA Ops:
  1.8 6.5 %collective-permute-start = (bf16[256,256]{1,0:T(8,128)(2,1)S(1)}, bf16[256,256]{1,0:T(8,128)(2,1)S(1)}, u32[]{:S(2)}, u32[]{:S(2)}) collective-permute-start(bf16[256,256]{1,0:T(8,128)(2,1)S(1)} %get-tuple-element.54), channel_id=1, source_target_pairs={{0,1},{1,2},{2,3},{3,0},{4,5},{5,6},{6,7},{7,4},{8,9},{9,10},{10,1... | collective-permute-start | bytes 393224 | tf_op jit(solution)/shard_map/ppermute | solution.py:37
  3.7 6.2 %collective-permute-start.1 = (bf16[256,256]{1,0:T(8,128)(2,1)S(1)}, bf16[256,256]{1,0:T(8,128)(2,1)S(1)}, u32[]{:S(2)}, u32[]{:S(2)}) collective-permute-start(bf16[256,256]{1,0:T(8,128)(2,1)S(1)} %get-tuple-element.55), channel_id=1, source_target_pairs={{0,2},{1,3},{2,0},{3,1},{4,6},{5,7},{6,4},{7,5},{8,10},{9,11},{10,... | collective-permute-start | bytes 393224 | tf_op jit(solution)/shard_map/ppermute | solution.py:37
  3.9 6.6 %collective-permute-start.2 = (bf16[256,256]{1,0:T(8,128)(2,1)S(1)}, bf16[256,256]{1,0:T(8,128)(2,1)S(1)}, u32[]{:S(2)}, u32[]{:S(2)}) collective-permute-start(bf16[256,256]{1,0:T(8,128)(2,1)S(1)} %get-tuple-element.56), channel_id=1, source_target_pairs={{0,3},{1,0},{2,1},{3,2},{4,7},{5,4},{6,5},{7,6},{8,11},{9,8},{10,9... | collective-permute-start | bytes 393224 | tf_op jit(solution)/shard_map/ppermute | solution.py:37
  4.1 21.2 %collective-permute-start.6 = (bf16[4,128,256]{2,1,0:T(8,128)(2,1)S(1)}, bf16[4,128,256]{2,1,0:T(8,128)(2,1)S(1)}, u32[]{:S(2)}, u32[]{:S(2)}) collective-permute-start(bf16[4,128,256]{2,1,0:T(8,128)(2,1)S(1)} %get-tuple-element.69), channel_id=1, source_target_pairs={{0,1},{1,2},{2,3},{4,5},{5,6},{6,7},{8,9},{9,10},{10,11},{12,13},{... | collective-permute-start | bytes 786440 | tf_op jit(solution)/shard_map/ppermute | solution.py:32
  11.0 7.1 %collective-permute-start.3 = (bf16[128,256]{1,0:T(8,128)(2,1)S(1)}, bf16[128,256]{1,0:T(8,128)(2,1)S(1)}, u32[]{:S(2)}, u32[]{:S(2)}) collective-permute-start(bf16[128,256]{1,0:T(8,128)(2,1)S(1)} %get-tuple-element.58), channel_id=1, source_target_pairs={{0,12},{4,16},{8,20},{12,24},{16,28},{20,0},{24,4},{28,8},{1,13},{... | collective-permute-start | bytes 196616 | tf_op jit(solution)/shard_map/ppermute | solution.py:37
  13.3 4.9 %collective-permute-start.4 = (bf16[128,256]{1,0:T(8,128)(2,1)S(1)}, bf16[128,256]{1,0:T(8,128)(2,1)S(1)}, u32[]{:S(2)}, u32[]{:S(2)}) collective-permute-start(bf16[128,256]{1,0:T(8,128)(2,1)S(1)} %get-tuple-element.59), channel_id=1, source_target_pairs={{0,8},{4,12},{8,16},{12,20},{16,24},{20,28},{24,0},{28,4},{1,9},{5... | collective-permute-start | bytes 196616 | tf_op jit(solution)/shard_map/ppermute | solution.py:37
  14.6 3.7 %collective-permute-start.5 = (bf16[128,256]{1,0:T(8,128)(2,1)S(1)}, bf16[128,256]{1,0:T(8,128)(2,1)S(1)}, u32[]{:S(2)}, u32[]{:S(2)}) collective-permute-start(bf16[128,256]{1,0:T(8,128)(2,1)S(1)} %get-tuple-element.60), channel_id=1, source_target_pairs={{0,4},{4,8},{8,12},{12,16},{16,20},{20,24},{24,28},{28,0},{1,5},{5... | collective-permute-start | bytes 196616 | tf_op jit(solution)/shard_map/ppermute | solution.py:37
  18.5 6.8 %collective-permute-start.9 = (bf16[128,256]{1,0:T(8,128)(2,1)S(1)}, bf16[128,256]{1,0:T(8,128)(2,1)S(1)}, u32[]{:S(2)}, u32[]{:S(2)}) collective-permute-start(bf16[128,256]{1,0:T(8,128)(2,1)S(1)} %arrive.1.refs_7_), channel_id=1, source_target_pairs={{0,3},{1,0},{2,1},{3,2},{4,7},{5,4},{6,5},{7,6},{8,11},{9,8},{10,9... | collective-permute-start | bytes 196616 | tf_op jit(solution)/shard_map/ppermute | solution.py:37
  20.8 4.6 %collective-permute-start.8 = (bf16[128,256]{1,0:T(8,128)(2,1)S(1)}, bf16[128,256]{1,0:T(8,128)(2,1)S(1)}, u32[]{:S(2)}, u32[]{:S(2)}) collective-permute-start(bf16[128,256]{1,0:T(8,128)(2,1)S(1)} %arrive.1.refs_7_), channel_id=1, source_target_pairs={{0,2},{1,3},{2,0},{3,1},{4,6},{5,7},{6,4},{7,5},{8,10},{9,11},{10,... | collective-permute-start | bytes 196616 | tf_op jit(solution)/shard_map/ppermute | solution.py:37
  21.3 4.0 %collective-permute-start.7 = (bf16[128,256]{1,0:T(8,128)(2,1)S(1)}, bf16[128,256]{1,0:T(8,128)(2,1)S(1)}, u32[]{:S(2)}, u32[]{:S(2)}) collective-permute-start(bf16[128,256]{1,0:T(8,128)(2,1)S(1)} %arrive.1.refs_7_), channel_id=1, source_target_pairs={{0,1},{1,2},{2,3},{3,0},{4,5},{5,6},{6,7},{7,4},{8,9},{9,10},{10,1... | collective-permute-start | bytes 196616 | tf_op jit(solution)/shard_map/ppermute | solution.py:37
  31.3 10.5 %collective-permute-start.10 = (bf16[128,256]{1,0:T(8,128)(2,1)S(1)}, bf16[128,256]{1,0:T(8,128)(2,1)S(1)}, u32[]{:S(2)}, u32[]{:S(2)}) collective-permute-start(bf16[128,256]{1,0:T(8,128)(2,1)S(1)} %get-tuple-element.80), channel_id=1, source_target_pairs={{0,1},{1,2},{2,3},{3,0},{4,5},{5,6},{6,7},{7,4},{8,9},{9,10},{10,1... | collective-permute-start | bytes 196616 | tf_op jit(solution)/shard_map/ppermute | solution.py:37
  38.0 3.8 %collective-permute-start.11 = (bf16[128,256]{1,0:T(8,128)(2,1)S(1)}, bf16[128,256]{1,0:T(8,128)(2,1)S(1)}, u32[]{:S(2)}, u32[]{:S(2)}) collective-permute-start(bf16[128,256]{1,0:T(8,128)(2,1)S(1)} %get-tuple-element.81), channel_id=1, source_target_pairs={{0,2},{1,3},{2,0},{3,1},{4,6},{5,7},{6,4},{7,5},{8,10},{9,11},{10,... | collective-permute-start | bytes 196616 | tf_op jit(solution)/shard_map/ppermute | solution.py:37
  38.3 3.8 %collective-permute-start.12 = (bf16[128,256]{1,0:T(8,128)(2,1)S(1)}, bf16[128,256]{1,0:T(8,128)(2,1)S(1)}, u32[]{:S(2)}, u32[]{:S(2)}) collective-permute-start(bf16[128,256]{1,0:T(8,128)(2,1)S(1)} %get-tuple-element.82), channel_id=1, source_target_pairs={{0,3},{1,0},{2,1},{3,2},{4,7},{5,4},{6,5},{7,6},{8,11},{9,8},{10,9... | collective-permute-start | bytes 196616 | tf_op jit(solution)/shard_map/ppermute | solution.py:37
  38.5 19.0 %collective-permute-start.16 = (bf16[4,128,256]{2,1,0:T(8,128)(2,1)S(1)}, bf16[4,128,256]{2,1,0:T(8,128)(2,1)S(1)}, u32[]{:S(2)}, u32[]{:S(2)}) collective-permute-start(bf16[4,128,256]{2,1,0:T(8,128)(2,1)S(1)} %get-tuple-element.93), channel_id=1, source_target_pairs={{1,0},{2,1},{3,2},{5,4},{6,5},{7,6},{9,8},{10,9},{11,10},{13,12},{... | collective-permute-start | bytes 786440 | tf_op jit(solution)/shard_map/ppermute | solution.py:32
  42.2 7.2 %collective-permute-start.15 = (bf16[128,256]{1,0:T(8,128)(2,1)S(1)}, bf16[128,256]{1,0:T(8,128)(2,1)S(1)}, u32[]{:S(2)}, u32[]{:S(2)}) collective-permute-start(bf16[128,256]{1,0:T(8,128)(2,1)S(1)} %gather.1.here_ref), channel_id=1, source_target_pairs={{0,20},{4,24},{8,28},{12,0},{16,4},{20,8},{24,12},{28,16},{1,21},{... | collective-permute-start | bytes 196616 | tf_op jit(solution)/shard_map/ppermute | solution.py:37
  44.8 4.7 %collective-permute-start.14 = (bf16[128,256]{1,0:T(8,128)(2,1)S(1)}, bf16[128,256]{1,0:T(8,128)(2,1)S(1)}, u32[]{:S(2)}, u32[]{:S(2)}) collective-permute-start(bf16[128,256]{1,0:T(8,128)(2,1)S(1)} %gather.1.here_ref), channel_id=1, source_target_pairs={{0,24},{4,28},{8,0},{12,4},{16,8},{20,12},{24,16},{28,20},{1,25},{... | collective-permute-start | bytes 196616 | tf_op jit(solution)/shard_map/ppermute | solution.py:37
  46.3 4.0 %collective-permute-start.13 = (bf16[128,256]{1,0:T(8,128)(2,1)S(1)}, bf16[128,256]{1,0:T(8,128)(2,1)S(1)}, u32[]{:S(2)}, u32[]{:S(2)}) collective-permute-start(bf16[128,256]{1,0:T(8,128)(2,1)S(1)} %gather.1.here_ref), channel_id=1, source_target_pairs={{0,28},{4,0},{8,4},{12,8},{16,12},{20,16},{24,20},{28,24},{1,29},{... | collective-permute-start | bytes 196616 | tf_op jit(solution)/shard_map/ppermute | solution.py:37
  50.7 6.8 %collective-permute-start.18 = (bf16[256,256]{1,0:T(8,128)(2,1)S(1)}, bf16[256,256]{1,0:T(8,128)(2,1)S(1)}, u32[]{:S(2)}, u32[]{:S(2)}) collective-permute-start(bf16[256,256]{1,0:T(8,128)(2,1)S(1)} %get-tuple-element.95), channel_id=1, source_target_pairs={{0,1},{1,2},{2,3},{3,0},{4,5},{5,6},{6,7},{7,4},{8,9},{9,10},{10,1... | collective-permute-start | bytes 393224 | tf_op jit(solution)/shard_map/ppermute | solution.py:37
  53.7 6.1 %collective-permute-start.19 = (bf16[256,256]{1,0:T(8,128)(2,1)S(1)}, bf16[256,256]{1,0:T(8,128)(2,1)S(1)}, u32[]{:S(2)}, u32[]{:S(2)}) collective-permute-start(bf16[256,256]{1,0:T(8,128)(2,1)S(1)} %get-tuple-element.96), channel_id=1, source_target_pairs={{0,2},{1,3},{2,0},{3,1},{4,6},{5,7},{6,4},{7,5},{8,10},{9,11},{10,... | collective-permute-start | bytes 393224 | tf_op jit(solution)/shard_map/ppermute | solution.py:37
  53.8 6.6 %collective-permute-start.20 = (bf16[256,256]{1,0:T(8,128)(2,1)S(1)}, bf16[256,256]{1,0:T(8,128)(2,1)S(1)}, u32[]{:S(2)}, u32[]{:S(2)}) collective-permute-start(bf16[256,256]{1,0:T(8,128)(2,1)S(1)} %get-tuple-element.97), channel_id=1, source_target_pairs={{0,3},{1,0},{2,1},{3,2},{4,7},{5,4},{6,5},{7,6},{8,11},{9,8},{10,9... | collective-permute-start | bytes 393224 | tf_op jit(solution)/shard_map/ppermute | solution.py:37
  54.1 3.4 %collective-permute-start.17 = (f32[8,128]{1,0:T(8,128)S(1)}, f32[8,128]{1,0:T(8,128)S(1)}, u32[]{:S(2)}, u32[]{:S(2)}) collective-permute-start(f32[8,128]{1,0:T(8,128)S(1)} %get-tuple-element.89.sink_ref), channel_id=1, source_target_pairs={{0,16},{4,20},{8,24},{12,28},{16,0},{20,4},{24,8},{28,12},{1,17},{... | collective-permute-start | bytes 12296 | tf_op jit(solution)/shard_map/ppermute | solution.py:37

commit v6 on v5

--- a/solution.py
+++ b/solution.py
@@ -290,15 +290,6 @@
         high16 = BF16(1) - low16
 
         def padded(seen):
-            seen = jnp.concatenate(
-                [
-                    seen[start + by : start + by + 16]
-                    for by in range(0, HALF, 16)
-                    for start in (0, HALF)
-                ]
-                + [seen[2 * HALF :]],
-                axis=0,
-            )
             swapped = jnp.concatenate([seen[:, 64:], seen[:, :64]], axis=1)
             return (
                 jnp.concatenate([seen * low16, swapped * high16], axis=0),
@@ -349,16 +340,11 @@
             )
             parts = []
             for base in (0, seen):
-                edge, dp_edge = [], []
-                for by in range(0, HALF, 16):
-                    start = base + 2 * by
-                    near, far = slice(start, start + 16), slice(start + 16, start + 32)
-                    edge.append(jnp.where(own[by : by + 16], score[near], score[far] + bias))
-                    dp_edge.append(jnp.where(own[by : by + 16], dp[near], dp[far]))
-                edge, dp_edge = (jnp.concatenate(value, axis=0) for value in (edge, dp_edge))
+                near, far = slice(base, base + HALF), slice(base + HALF, base + 2 * HALF)
                 rest = slice(base + 2 * HALF, base + 3 * HALF)
+                edge = jnp.where(own, score[near], score[far] + bias)
                 whole = score[rest] + bias if half == 0 else score[rest]
-                parts.append((edge, whole, dp_edge, dp[rest]))
+                parts.append((edge, whole, jnp.where(own, dp[near], dp[far]), dp[rest]))
             return parts
 
         def weigh(index, odd, edge, whole, dp_edge, dp_whole):
@@ -432,16 +418,17 @@
             )
             return total + pltpu.roll(total, HEAD_DIM, 1)
 
-        parts = []
+        ahead, parts = products(0), []
         for index in range(len(items)):
-            now = products(index)
+            now = ahead
+            if index + 1 < len(items):
+                ahead = products(index + 1)
+            weigh(index, 0, *now[0])
             if index >= 1:
                 finish(index - 1)
-                parts.append(reduce(index - 1))
-            weigh(index, 0, *now[0])
             weigh(index, 1, *now[1])
+            parts.append(reduce(index))
         finish(len(items) - 1)
-        parts.append(reduce(len(items) - 1))
         grads = [
             [join(parts[2 * unit][place], parts[2 * unit + 1][place]) for place in range(2)]
             for unit in range(2)
@@ -540,8 +527,7 @@
                 total = total + halo.astype(F32)
             out_ref[here, :] = total.astype(BF16)
     sink_row = -(sink_ref[0:1] + far_ref[0:1])
-    for place in range(sink_grad.shape[0]):
-        sink_grad[place] = sink_row[0, place]
+    sink_grad[...] = sink_row[0, : sink_grad.shape[0]]
 
 
 def swap(values, axis):
@@ -725,7 +711,7 @@
             shape(sink_logits.shape, F32),
         ),
         in_specs=[VMEM] * (5 + head_count),
-        out_specs=(VMEM, VMEM, SMEM),
+        out_specs=(VMEM,) * 3,
         scratch_shapes=[pltpu.VMEM((head_count, rows, width), BF16)],
         compiler_params=PARAMS,
         name="total",

time: 62 us -> 61 us (0.984)
  starting transfers between devices: 34 us -> 33.1 us
  waiting for transfers between devices: 9.41 us -> 10.2 us
    ppermute x19, starting transfers between devices: 27.4 us -> 26.4 us  [ring(): lax.ppermute(value, axis, [(source, (source + steps) % count) for source...]
    ppermute x19, waiting for transfers between devices: 9.4 us -> 10.2 us  [ring(): lax.ppermute(value, axis, [(source, (source + steps) % count) for source...]
where the time goes in v6:
time: 61 us; the launch traced here: 60.7 us
  starting transfers between devices  33.1 us (54%)
  Pallas kernels  16.6 us (27%)
  waiting for transfers between devices  10.2 us (17%)
  between operations  0.77 us (1%)
    ppermute x19, starting transfers between devices, ring(): lax.ppermute(value, axis, [(source, (source + steps) % count) for source...  26.4 us
    ppermute x19, waiting for transfers between devices, ring(): lax.ppermute(value, axis, [(source, (source + steps) % count) for source...  10.2 us
    pallas_call x2, Pallas kernels, attend(): pl.pallas_call(functools.partial(attend_kernel, blocks_here, head_count,...  7.61 us
    ppermute x2, starting transfers between devices, shift(): lax.ppermute(value, axis, [(source, source + steps) for source in range(l...  6.68 us
    pallas_call x2, Pallas kernels, flush(): pl.pallas_call(stage_kernel, out_shape=pltpu.HBM(value.shape, BF16), in_s...  2.65 us
    pallas_call x1, Pallas kernels, local(): pl.pallas_call(stage_kernel, out_shape=(pltpu.VMEM(queries.shape, BF16),)...  2.24 us
  transfers between devices with their start and end apart: 21, of which 11 were waited for; matrix products, arithmetic and copies ran while one was open for 0% of the time, Pallas kernels for 15%

profile of v6, /device:TPU:3, one launch (start us, length us, event | category | flops | bytes accessed | tf_op | source)
XLA Modules:
  0.0 60.7 jit_solution(5741330430603722473)
XLA Ops:
  0.6 1.2 %pack.1 = (bf16[256,256]{1,0:T(8,128)(2,1)S(1)}, bf16[256,256]{1,0:T(8,128)(2,1)S(1)}, bf16[256,256]{1,0:T(8,128)(2,1)S(1)}, bf16[256,256]{1,0:T(8,128)(2,1)S(1)...) custom-call(f32[16]{0:T(128)} %sink_hbm.1, ...), custom_call_target="tpu_custom_call" | custom-call | tf_op jit(solution)/shard_map/pack/pallas_call | solution.py:556
  1.8 1.9 %collective-permute-start = (bf16[256,256]{1,0:T(8,128)(2,1)S(1)}, bf16[256,256]{1,0:T(8,128)(2,1)S(1)}, u32[]{:S(2)}, u32[]{:S(2)}) collective-permute-start(bf16[256,256]{1,0:T(8,128)(2,1)S(1)} %get-tuple-element.54), channel_id=1, source_target_pairs={{0,1},{1,2},{2,3},{3,0},{4,5},{5,6},{6,7},{7,4},{8,9},{9,10},{10,1... | collective-permute-start | bytes 393224 | tf_op jit(solution)/shard_map/ppermute | solution.py:37
  4.1 3.4 %collective-permute-start.6 = (bf16[4,128,256]{2,1,0:T(8,128)(2,1)S(1)}, bf16[4,128,256]{2,1,0:T(8,128)(2,1)S(1)}, u32[]{:S(2)}, u32[]{:S(2)}) collective-permute-start(bf16[4,128,256]{2,1,0:T(8,128)(2,1)S(1)} %get-tuple-element.69), channel_id=1, source_target_pairs={{0,1},{1,2},{2,3},{4,5},{5,6},{6,7},{8,9},{9,10},{10,11},{12,13},{... | collective-permute-start | bytes 786440 | tf_op jit(solution)/shard_map/ppermute | solution.py:32
  8.3 1.5 %collective-permute-done.1.refs_2_ = bf16[256,256]{1,0:T(8,128)(2,1)S(1)} collective-permute-done((bf16[256,256]{1,0:T(8,128)(2,1)S(1)}, bf16[256,256]{1,0:T(8,128)(2,1)S(1)}, u32[]{:S(2)}, u32[]{:S(2)}) %collective-permute-start.1) | collective-permute-done | bytes 131104 | tf_op jit(solution)/shard_map/ppermute | solution.py:37
  11.0 2.3 %collective-permute-start.3 = (bf16[128,256]{1,0:T(8,128)(2,1)S(1)}, bf16[128,256]{1,0:T(8,128)(2,1)S(1)}, u32[]{:S(2)}, u32[]{:S(2)}) collective-permute-start(bf16[128,256]{1,0:T(8,128)(2,1)S(1)} %get-tuple-element.58), channel_id=1, source_target_pairs={{0,12},{4,16},{8,20},{12,24},{16,28},{20,0},{24,4},{28,8},{1,13},{... | collective-permute-start | bytes 196616 | tf_op jit(solution)/shard_map/ppermute | solution.py:37
  13.3 1.3 %collective-permute-start.4 = (bf16[128,256]{1,0:T(8,128)(2,1)S(1)}, bf16[128,256]{1,0:T(8,128)(2,1)S(1)}, u32[]{:S(2)}, u32[]{:S(2)}) collective-permute-start(bf16[128,256]{1,0:T(8,128)(2,1)S(1)} %get-tuple-element.59), channel_id=1, source_target_pairs={{0,8},{4,12},{8,16},{12,20},{16,24},{20,28},{24,0},{28,4},{1,9},{5... | collective-permute-start | bytes 196616 | tf_op jit(solution)/shard_map/ppermute | solution.py:37
  14.6 1.2 %collective-permute-start.5 = (bf16[128,256]{1,0:T(8,128)(2,1)S(1)}, bf16[128,256]{1,0:T(8,128)(2,1)S(1)}, u32[]{:S(2)}, u32[]{:S(2)}) collective-permute-start(bf16[128,256]{1,0:T(8,128)(2,1)S(1)} %get-tuple-element.60), channel_id=1, source_target_pairs={{0,4},{4,8},{8,12},{12,16},{16,20},{20,24},{24,28},{28,0},{1,5},{5... | collective-permute-start | bytes 196616 | tf_op jit(solution)/shard_map/ppermute | solution.py:37
  15.8 2.2 %stage.1 = (bf16[256,4096]{1,0:T(8,128)(2,1)S(1)}, bf16[256,4096]{1,0:T(8,128)(2,1)S(1)}) custom-call(bf16[256,4096]{1,0:T(8,128)(2,1)} %refs_0_, bf16[256,4096]{1,0:T(8,128)(2,1)} %refs_1_), custom_call_target="tpu_custom_call" | custom-call | tf_op jit(solution)/shard_map/stage/pallas_call | solution.py:591
  18.5 2.3 %collective-permute-start.9 = (bf16[128,256]{1,0:T(8,128)(2,1)S(1)}, bf16[128,256]{1,0:T(8,128)(2,1)S(1)}, u32[]{:S(2)}, u32[]{:S(2)}) collective-permute-start(bf16[128,256]{1,0:T(8,128)(2,1)S(1)} %arrive.1.refs_7_), channel_id=1, source_target_pairs={{0,3},{1,0},{2,1},{3,2},{4,7},{5,4},{6,5},{7,6},{8,11},{9,8},{10,9... | collective-permute-start | bytes 196616 | tf_op jit(solution)/shard_map/ppermute | solution.py:37
  21.3 1.9 %collective-permute-start.7 = (bf16[128,256]{1,0:T(8,128)(2,1)S(1)}, bf16[128,256]{1,0:T(8,128)(2,1)S(1)}, u32[]{:S(2)}, u32[]{:S(2)}) collective-permute-start(bf16[128,256]{1,0:T(8,128)(2,1)S(1)} %arrive.1.refs_7_), channel_id=1, source_target_pairs={{0,1},{1,2},{2,3},{3,0},{4,5},{5,6},{6,7},{7,4},{8,9},{9,10},{10,1... | collective-permute-start | bytes 196616 | tf_op jit(solution)/shard_map/ppermute | solution.py:37
  23.2 2.0 %attend.2 = (bf16[256,4096]{1,0:T(8,128)(2,1)S(1)}, bf16[256,4096]{1,0:T(8,128)(2,1)S(1)}, f32[256,512]{1,0:T(8,128)S(1)}, f32[256,512]{1,0:T(8,128)S(1)}, bf16[...) custom-call(s32[8,128]{1,0:T(8,128)S(1)} %plan.1.plan_ref.refs_0_, f32[64,128]{1,0:T(8,128)S(1)} %get-tuple-element.57.refs_1_, ...), custom_call_target="tpu_custom_call" | custom-call | tf_op jit(solution)/shard_map/attend/pallas_call | solution.py:625
  25.2 5.6 %attend.3 = (bf16[256,4096]{1,0:T(8,128)(2,1)S(1)}, bf16[256,4096]{1,0:T(8,128)(2,1)S(1)}, f32[256,512]{1,0:T(8,128)S(1)}, f32[256,512]{1,0:T(8,128)S(1)}, bf16[...) custom-call(s32[8,128]{1,0:T(8,128)S(1)} %plan.1.plan_ref.refs_0_, ...), custom_call_target="tpu_custom_call", output_to_operand_aliasing={{0}: (10, {}), {1}: (11, {}), {2}: (12, {}), {3}: (13, {}),... | custom-call | tf_op jit(solution)/shard_map/attend/pallas_call | solution.py:625
  30.9 6.4 %collective-permute-start.10 = (bf16[128,256]{1,0:T(8,128)(2,1)S(1)}, bf16[128,256]{1,0:T(8,128)(2,1)S(1)}, u32[]{:S(2)}, u32[]{:S(2)}) collective-permute-start(bf16[128,256]{1,0:T(8,128)(2,1)S(1)} %get-tuple-element.80), channel_id=1, source_target_pairs={{0,1},{1,2},{2,3},{3,0},{4,5},{5,6},{6,7},{7,4},{8,9},{9,10},{10,1... | collective-permute-start | bytes 196616 | tf_op jit(solution)/shard_map/ppermute | solution.py:37
  37.8 3.3 %collective-permute-start.16 = (bf16[4,128,256]{2,1,0:T(8,128)(2,1)S(1)}, bf16[4,128,256]{2,1,0:T(8,128)(2,1)S(1)}, u32[]{:S(2)}, u32[]{:S(2)}) collective-permute-start(bf16[4,128,256]{2,1,0:T(8,128)(2,1)S(1)} %get-tuple-element.93), channel_id=1, source_target_pairs={{1,0},{2,1},{3,2},{5,4},{6,5},{7,6},{9,8},{10,9},{11,10},{13,12},{... | collective-permute-start | bytes 786440 | tf_op jit(solution)/shard_map/ppermute | solution.py:32
  41.5 2.5 %collective-permute-start.15 = (bf16[128,256]{1,0:T(8,128)(2,1)S(1)}, bf16[128,256]{1,0:T(8,128)(2,1)S(1)}, u32[]{:S(2)}, u32[]{:S(2)}) collective-permute-start(bf16[128,256]{1,0:T(8,128)(2,1)S(1)} %gather.1.here_ref), channel_id=1, source_target_pairs={{0,20},{4,24},{8,28},{12,0},{16,4},{20,8},{24,12},{28,16},{1,21},{... | collective-permute-start | bytes 196616 | tf_op jit(solution)/shard_map/ppermute | solution.py:37
  44.0 1.6 %collective-permute-start.14 = (bf16[128,256]{1,0:T(8,128)(2,1)S(1)}, bf16[128,256]{1,0:T(8,128)(2,1)S(1)}, u32[]{:S(2)}, u32[]{:S(2)}) collective-permute-start(bf16[128,256]{1,0:T(8,128)(2,1)S(1)} %gather.1.here_ref), channel_id=1, source_target_pairs={{0,24},{4,28},{8,0},{12,4},{16,8},{20,12},{24,16},{28,20},{1,25},{... | collective-permute-start | bytes 196616 | tf_op jit(solution)/shard_map/ppermute | solution.py:37
  45.7 1.3 %flush.2 = bf16[256,4096]{1,0:T(8,128)(2,1)} custom-call(bf16[256,4096]{1,0:T(8,128)(2,1)S(1)} %get-tuple-element.83.refs_0_), custom_call_target="tpu_custom_call" | custom-call | tf_op jit(solution)/shard_map/flush/pallas_call | solution.py:675
  47.0 1.7 %collective-permute-done.15.refs_2_ = bf16[128,256]{1,0:T(8,128)(2,1)S(1)} collective-permute-done((bf16[128,256]{1,0:T(8,128)(2,1)S(1)}, bf16[128,256]{1,0:T(8,128)(2,1)S(1)}, u32[]{:S(2)}, u32[]{:S(2)}) %collective-permute-start.15) | collective-permute-done | bytes 65568 | tf_op jit(solution)/shard_map/ppermute | solution.py:37
  48.8 1.1 %collective-permute-done.13.refs_0_ = bf16[128,256]{1,0:T(8,128)(2,1)S(1)} collective-permute-done((bf16[128,256]{1,0:T(8,128)(2,1)S(1)}, bf16[128,256]{1,0:T(8,128)(2,1)S(1)}, u32[]{:S(2)}, u32[]{:S(2)}) %collective-permute-start.13) | collective-permute-done | bytes 65568 | tf_op jit(solution)/shard_map/ppermute | solution.py:37
  50.4 1.8 %collective-permute-start.18 = (bf16[256,256]{1,0:T(8,128)(2,1)S(1)}, bf16[256,256]{1,0:T(8,128)(2,1)S(1)}, u32[]{:S(2)}, u32[]{:S(2)}) collective-permute-start(bf16[256,256]{1,0:T(8,128)(2,1)S(1)} %get-tuple-element.95), channel_id=1, source_target_pairs={{0,1},{1,2},{2,3},{3,0},{4,5},{5,6},{6,7},{7,4},{8,9},{9,10},{10,1... | collective-permute-start | bytes 393224 | tf_op jit(solution)/shard_map/ppermute | solution.py:37
  52.2 1.0 %collective-permute-start.19 = (bf16[256,256]{1,0:T(8,128)(2,1)S(1)}, bf16[256,256]{1,0:T(8,128)(2,1)S(1)}, u32[]{:S(2)}, u32[]{:S(2)}) collective-permute-start(bf16[256,256]{1,0:T(8,128)(2,1)S(1)} %get-tuple-element.96), channel_id=1, source_target_pairs={{0,2},{1,3},{2,0},{3,1},{4,6},{5,7},{6,4},{7,5},{8,10},{9,11},{10,... | collective-permute-start | bytes 393224 | tf_op jit(solution)/shard_map/ppermute | solution.py:37
  53.9 1.3 %flush.3 = bf16[256,4096]{1,0:T(8,128)(2,1)} custom-call(bf16[256,4096]{1,0:T(8,128)(2,1)S(1)} %get-tuple-element.90.refs_0_), custom_call_target="tpu_custom_call" | custom-call | tf_op jit(solution)/shard_map/flush/pallas_call | solution.py:675
  55.2 1.4 %collective-permute-done.17.far_ref = f32[8,128]{1,0:T(8,128)S(1)} collective-permute-done((f32[8,128]{1,0:T(8,128)S(1)}, f32[8,128]{1,0:T(8,128)S(1)}, u32[]{:S(2)}, u32[]{:S(2)}) %collective-permute-start.17) | collective-permute-done | bytes 4128 | tf_op jit(solution)/shard_map/ppermute | solution.py:37
  56.6 2.6 %collective-permute-done.19.refs_2_ = bf16[256,256]{1,0:T(8,128)(2,1)S(1)} collective-permute-done((bf16[256,256]{1,0:T(8,128)(2,1)S(1)}, bf16[256,256]{1,0:T(8,128)(2,1)S(1)}, u32[]{:S(2)}, u32[]{:S(2)}) %collective-permute-start.19) | collective-permute-done | bytes 131104 | tf_op jit(solution)/shard_map/ppermute | solution.py:37
  (30 shorter events, 7.0 us)
Async XLA Ops:
  1.8 6.5 %collective-permute-start = (bf16[256,256]{1,0:T(8,128)(2,1)S(1)}, bf16[256,256]{1,0:T(8,128)(2,1)S(1)}, u32[]{:S(2)}, u32[]{:S(2)}) collective-permute-start(bf16[256,256]{1,0:T(8,128)(2,1)S(1)} %get-tuple-element.54), channel_id=1, source_target_pairs={{0,1},{1,2},{2,3},{3,0},{4,5},{5,6},{6,7},{7,4},{8,9},{9,10},{10,1... | collective-permute-start | bytes 393224 | tf_op jit(solution)/shard_map/ppermute | solution.py:37
  3.7 6.2 %collective-permute-start.1 = (bf16[256,256]{1,0:T(8,128)(2,1)S(1)}, bf16[256,256]{1,0:T(8,128)(2,1)S(1)}, u32[]{:S(2)}, u32[]{:S(2)}) collective-permute-start(bf16[256,256]{1,0:T(8,128)(2,1)S(1)} %get-tuple-element.55), channel_id=1, source_target_pairs={{0,2},{1,3},{2,0},{3,1},{4,6},{5,7},{6,4},{7,5},{8,10},{9,11},{10,... | collective-permute-start | bytes 393224 | tf_op jit(solution)/shard_map/ppermute | solution.py:37
  3.9 6.6 %collective-permute-start.2 = (bf16[256,256]{1,0:T(8,128)(2,1)S(1)}, bf16[256,256]{1,0:T(8,128)(2,1)S(1)}, u32[]{:S(2)}, u32[]{:S(2)}) collective-permute-start(bf16[256,256]{1,0:T(8,128)(2,1)S(1)} %get-tuple-element.56), channel_id=1, source_target_pairs={{0,3},{1,0},{2,1},{3,2},{4,7},{5,4},{6,5},{7,6},{8,11},{9,8},{10,9... | collective-permute-start | bytes 393224 | tf_op jit(solution)/shard_map/ppermute | solution.py:37
  4.1 21.1 %collective-permute-start.6 = (bf16[4,128,256]{2,1,0:T(8,128)(2,1)S(1)}, bf16[4,128,256]{2,1,0:T(8,128)(2,1)S(1)}, u32[]{:S(2)}, u32[]{:S(2)}) collective-permute-start(bf16[4,128,256]{2,1,0:T(8,128)(2,1)S(1)} %get-tuple-element.69), channel_id=1, source_target_pairs={{0,1},{1,2},{2,3},{4,5},{5,6},{6,7},{8,9},{9,10},{10,11},{12,13},{... | collective-permute-start | bytes 786440 | tf_op jit(solution)/shard_map/ppermute | solution.py:32
  11.0 7.1 %collective-permute-start.3 = (bf16[128,256]{1,0:T(8,128)(2,1)S(1)}, bf16[128,256]{1,0:T(8,128)(2,1)S(1)}, u32[]{:S(2)}, u32[]{:S(2)}) collective-permute-start(bf16[128,256]{1,0:T(8,128)(2,1)S(1)} %get-tuple-element.58), channel_id=1, source_target_pairs={{0,12},{4,16},{8,20},{12,24},{16,28},{20,0},{24,4},{28,8},{1,13},{... | collective-permute-start | bytes 196616 | tf_op jit(solution)/shard_map/ppermute | solution.py:37
  13.3 4.9 %collective-permute-start.4 = (bf16[128,256]{1,0:T(8,128)(2,1)S(1)}, bf16[128,256]{1,0:T(8,128)(2,1)S(1)}, u32[]{:S(2)}, u32[]{:S(2)}) collective-permute-start(bf16[128,256]{1,0:T(8,128)(2,1)S(1)} %get-tuple-element.59), channel_id=1, source_target_pairs={{0,8},{4,12},{8,16},{12,20},{16,24},{20,28},{24,0},{28,4},{1,9},{5... | collective-permute-start | bytes 196616 | tf_op jit(solution)/shard_map/ppermute | solution.py:37
  14.6 3.7 %collective-permute-start.5 = (bf16[128,256]{1,0:T(8,128)(2,1)S(1)}, bf16[128,256]{1,0:T(8,128)(2,1)S(1)}, u32[]{:S(2)}, u32[]{:S(2)}) collective-permute-start(bf16[128,256]{1,0:T(8,128)(2,1)S(1)} %get-tuple-element.60), channel_id=1, source_target_pairs={{0,4},{4,8},{8,12},{12,16},{16,20},{20,24},{24,28},{28,0},{1,5},{5... | collective-permute-start | bytes 196616 | tf_op jit(solution)/shard_map/ppermute | solution.py:37
  18.5 6.7 %collective-permute-start.9 = (bf16[128,256]{1,0:T(8,128)(2,1)S(1)}, bf16[128,256]{1,0:T(8,128)(2,1)S(1)}, u32[]{:S(2)}, u32[]{:S(2)}) collective-permute-start(bf16[128,256]{1,0:T(8,128)(2,1)S(1)} %arrive.1.refs_7_), channel_id=1, source_target_pairs={{0,3},{1,0},{2,1},{3,2},{4,7},{5,4},{6,5},{7,6},{8,11},{9,8},{10,9... | collective-permute-start | bytes 196616 | tf_op jit(solution)/shard_map/ppermute | solution.py:37
  20.8 4.5 %collective-permute-start.8 = (bf16[128,256]{1,0:T(8,128)(2,1)S(1)}, bf16[128,256]{1,0:T(8,128)(2,1)S(1)}, u32[]{:S(2)}, u32[]{:S(2)}) collective-permute-start(bf16[128,256]{1,0:T(8,128)(2,1)S(1)} %arrive.1.refs_7_), channel_id=1, source_target_pairs={{0,2},{1,3},{2,0},{3,1},{4,6},{5,7},{6,4},{7,5},{8,10},{9,11},{10,... | collective-permute-start | bytes 196616 | tf_op jit(solution)/shard_map/ppermute | solution.py:37
  21.3 3.9 %collective-permute-start.7 = (bf16[128,256]{1,0:T(8,128)(2,1)S(1)}, bf16[128,256]{1,0:T(8,128)(2,1)S(1)}, u32[]{:S(2)}, u32[]{:S(2)}) collective-permute-start(bf16[128,256]{1,0:T(8,128)(2,1)S(1)} %arrive.1.refs_7_), channel_id=1, source_target_pairs={{0,1},{1,2},{2,3},{3,0},{4,5},{5,6},{6,7},{7,4},{8,9},{9,10},{10,1... | collective-permute-start | bytes 196616 | tf_op jit(solution)/shard_map/ppermute | solution.py:37
  30.9 10.2 %collective-permute-start.10 = (bf16[128,256]{1,0:T(8,128)(2,1)S(1)}, bf16[128,256]{1,0:T(8,128)(2,1)S(1)}, u32[]{:S(2)}, u32[]{:S(2)}) collective-permute-start(bf16[128,256]{1,0:T(8,128)(2,1)S(1)} %get-tuple-element.80), channel_id=1, source_target_pairs={{0,1},{1,2},{2,3},{3,0},{4,5},{5,6},{6,7},{7,4},{8,9},{9,10},{10,1... | collective-permute-start | bytes 196616 | tf_op jit(solution)/shard_map/ppermute | solution.py:37
  37.3 3.8 %collective-permute-start.11 = (bf16[128,256]{1,0:T(8,128)(2,1)S(1)}, bf16[128,256]{1,0:T(8,128)(2,1)S(1)}, u32[]{:S(2)}, u32[]{:S(2)}) collective-permute-start(bf16[128,256]{1,0:T(8,128)(2,1)S(1)} %get-tuple-element.81), channel_id=1, source_target_pairs={{0,2},{1,3},{2,0},{3,1},{4,6},{5,7},{6,4},{7,5},{8,10},{9,11},{10,... | collective-permute-start | bytes 196616 | tf_op jit(solution)/shard_map/ppermute | solution.py:37
  37.6 3.8 %collective-permute-start.12 = (bf16[128,256]{1,0:T(8,128)(2,1)S(1)}, bf16[128,256]{1,0:T(8,128)(2,1)S(1)}, u32[]{:S(2)}, u32[]{:S(2)}) collective-permute-start(bf16[128,256]{1,0:T(8,128)(2,1)S(1)} %get-tuple-element.82), channel_id=1, source_target_pairs={{0,3},{1,0},{2,1},{3,2},{4,7},{5,4},{6,5},{7,6},{8,11},{9,8},{10,9... | collective-permute-start | bytes 196616 | tf_op jit(solution)/shard_map/ppermute | solution.py:37
  37.8 18.8 %collective-permute-start.16 = (bf16[4,128,256]{2,1,0:T(8,128)(2,1)S(1)}, bf16[4,128,256]{2,1,0:T(8,128)(2,1)S(1)}, u32[]{:S(2)}, u32[]{:S(2)}) collective-permute-start(bf16[4,128,256]{2,1,0:T(8,128)(2,1)S(1)} %get-tuple-element.93), channel_id=1, source_target_pairs={{1,0},{2,1},{3,2},{5,4},{6,5},{7,6},{9,8},{10,9},{11,10},{13,12},{... | collective-permute-start | bytes 786440 | tf_op jit(solution)/shard_map/ppermute | solution.py:32
  41.5 7.2 %collective-permute-start.15 = (bf16[128,256]{1,0:T(8,128)(2,1)S(1)}, bf16[128,256]{1,0:T(8,128)(2,1)S(1)}, u32[]{:S(2)}, u32[]{:S(2)}) collective-permute-start(bf16[128,256]{1,0:T(8,128)(2,1)S(1)} %gather.1.here_ref), channel_id=1, source_target_pairs={{0,20},{4,24},{8,28},{12,0},{16,4},{20,8},{24,12},{28,16},{1,21},{... | collective-permute-start | bytes 196616 | tf_op jit(solution)/shard_map/ppermute | solution.py:37
  44.0 4.8 %collective-permute-start.14 = (bf16[128,256]{1,0:T(8,128)(2,1)S(1)}, bf16[128,256]{1,0:T(8,128)(2,1)S(1)}, u32[]{:S(2)}, u32[]{:S(2)}) collective-permute-start(bf16[128,256]{1,0:T(8,128)(2,1)S(1)} %gather.1.here_ref), channel_id=1, source_target_pairs={{0,24},{4,28},{8,0},{12,4},{16,8},{20,12},{24,16},{28,20},{1,25},{... | collective-permute-start | bytes 196616 | tf_op jit(solution)/shard_map/ppermute | solution.py:37
  45.7 4.3 %collective-permute-start.13 = (bf16[128,256]{1,0:T(8,128)(2,1)S(1)}, bf16[128,256]{1,0:T(8,128)(2,1)S(1)}, u32[]{:S(2)}, u32[]{:S(2)}) collective-permute-start(bf16[128,256]{1,0:T(8,128)(2,1)S(1)} %gather.1.here_ref), channel_id=1, source_target_pairs={{0,28},{4,0},{8,4},{12,8},{16,12},{20,16},{24,20},{28,24},{1,29},{... | collective-permute-start | bytes 196616 | tf_op jit(solution)/shard_map/ppermute | solution.py:37
  50.4 6.2 %collective-permute-start.18 = (bf16[256,256]{1,0:T(8,128)(2,1)S(1)}, bf16[256,256]{1,0:T(8,128)(2,1)S(1)}, u32[]{:S(2)}, u32[]{:S(2)}) collective-permute-start(bf16[256,256]{1,0:T(8,128)(2,1)S(1)} %get-tuple-element.95), channel_id=1, source_target_pairs={{0,1},{1,2},{2,3},{3,0},{4,5},{5,6},{6,7},{7,4},{8,9},{9,10},{10,1... | collective-permute-start | bytes 393224 | tf_op jit(solution)/shard_map/ppermute | solution.py:37
  52.2 7.0 %collective-permute-start.19 = (bf16[256,256]{1,0:T(8,128)(2,1)S(1)}, bf16[256,256]{1,0:T(8,128)(2,1)S(1)}, u32[]{:S(2)}, u32[]{:S(2)}) collective-permute-start(bf16[256,256]{1,0:T(8,128)(2,1)S(1)} %get-tuple-element.96), channel_id=1, source_target_pairs={{0,2},{1,3},{2,0},{3,1},{4,6},{5,7},{6,4},{7,5},{8,10},{9,11},{10,... | collective-permute-start | bytes 393224 | tf_op jit(solution)/shard_map/ppermute | solution.py:37
  53.2 6.6 %collective-permute-start.20 = (bf16[256,256]{1,0:T(8,128)(2,1)S(1)}, bf16[256,256]{1,0:T(8,128)(2,1)S(1)}, u32[]{:S(2)}, u32[]{:S(2)}) collective-permute-start(bf16[256,256]{1,0:T(8,128)(2,1)S(1)} %get-tuple-element.97), channel_id=1, source_target_pairs={{0,3},{1,0},{2,1},{3,2},{4,7},{5,4},{6,5},{7,6},{8,11},{9,8},{10,9... | collective-permute-start | bytes 393224 | tf_op jit(solution)/shard_map/ppermute | solution.py:37
  53.2 3.4 %collective-permute-start.17 = (f32[8,128]{1,0:T(8,128)S(1)}, f32[8,128]{1,0:T(8,128)S(1)}, u32[]{:S(2)}, u32[]{:S(2)}) collective-permute-start(f32[8,128]{1,0:T(8,128)S(1)} %get-tuple-element.89.sink_ref), channel_id=1, source_target_pairs={{0,16},{4,20},{8,24},{12,28},{16,0},{20,4},{24,8},{28,12},{1,17},{... | collective-permute-start | bytes 12296 | tf_op jit(solution)/shard_map/ppermute | solution.py:37

commit v7 on v6

--- a/solution.py
+++ b/solution.py
@@ -146,12 +146,11 @@
 
 
 def choose_kernel(plan_ref, *refs):
-    slots = len(refs) - LAG - 1
-    slot_refs, out_refs, sink_ref = refs[:slots], refs[slots:-1], refs[-1]
+    slots = len(refs) - LAG
+    slot_refs, out_refs = refs[:slots], refs[slots:]
     head = lax.axis_index("head")
     rows = slot_refs[0].shape[0]
     blocks_here = rows // WINDOW
-    heads = sink_ref.shape[0] // slots
     for distance, out_ref in zip(range(LAG, 0, -1), out_refs):
         _, place = planned_tail(plan_ref, distance)
         begin = pl.multiple_of(place % blocks_here * WINDOW, WINDOW)
@@ -162,6 +161,12 @@
             def _(out_ref=out_ref, slot_ref=slot_ref, begin=begin):
                 out_ref[...] = slot_ref[pl.ds(begin, WINDOW), :]
 
+
+def sinks_kernel(*refs):
+    *slot_refs, sink_ref = refs
+    slots = len(slot_refs)
+    head = lax.axis_index("head")
+    heads = sink_ref.shape[0] // slots
     for step, slot_ref in enumerate(slot_refs):
         source = lax.rem(head - step + slots, slots)
         sink_row = row_join(slot_ref[:16])
@@ -421,12 +426,12 @@
         ahead, parts = products(0), []
         for index in range(len(items)):
             now = ahead
+            weigh(index, 0, *now[0])
             if index + 1 < len(items):
                 ahead = products(index + 1)
-            weigh(index, 0, *now[0])
+            weigh(index, 1, *now[1])
             if index >= 1:
                 finish(index - 1)
-            weigh(index, 1, *now[1])
             parts.append(reduce(index))
         finish(len(items) - 1)
         grads = [
@@ -506,7 +511,7 @@
     sink_ref[...] = jnp.broadcast_to(sink_row, sink_ref.shape)
 
 
-def total_kernel(dk_ref, dv_ref, halo_ref, sink_ref, far_ref, *refs):
+def total_kernel(halo_ref, dk_ref, dv_ref, sink_ref, far_ref, *refs):
     *tail_refs, key_ref, value_ref, sink_grad, tails = refs
     slots, rows = len(tail_refs), dk_ref.shape[0]
     width = tails.shape[2] // 2
@@ -578,14 +583,24 @@
         name="plan",
     )(far(branch_start), far(branch_len), far(parent_list.T))
     plan = close(plan)
-    *chosen, sinks = pl.pallas_call(
+    chosen = pl.pallas_call(
         choose_kernel,
-        out_shape=(shape((WINDOW, width)),) * LAG + (shape((KV_HEADS * GROUP, 128), F32),),
+        out_shape=(shape((WINDOW, width)),) * LAG,
         in_specs=[VMEM] * (1 + head_count),
-        out_specs=(VMEM,) * (LAG + 1),
+        out_specs=(VMEM,) * LAG,
         compiler_params=PARAMS,
         name="choose",
     )(plan, *spread)
+    late_slots = lax.optimization_barrier((*spread, *chosen))
+    late_slots, chosen = late_slots[:head_count], late_slots[head_count:]
+    sinks = pl.pallas_call(
+        sinks_kernel,
+        out_shape=shape((KV_HEADS * GROUP, 128), F32),
+        in_specs=[VMEM] * head_count,
+        out_specs=VMEM,
+        compiler_params=PARAMS,
+        name="sinks",
+    )(*late_slots)
     arrived = [ring(chosen[LAG - s], "tok", s) for s in range(LAG, 0, -1)]
     queries, out_grad, _ = lax.optimization_barrier((queries, out_grad, sinks))
     near_queries, near_grad = pl.pallas_call(
@@ -686,6 +701,7 @@
     attended, _ = lax.optimization_barrier((attended, quarter_grad))
     attended = flush(attended)
     attended, *returned = lax.optimization_barrier((attended, *returned))
+    dhalo, _ = lax.optimization_barrier((dhalo, quarter_grad))
     halo_back = shift(dhalo, "head", -1)
     *landed, sink_near = pl.pallas_call(
         functools.partial(land_kernel, blocks),
@@ -715,7 +731,7 @@
         scratch_shapes=[pltpu.VMEM((head_count, rows, width), BF16)],
         compiler_params=PARAMS,
         name="total",
-    )(dk, dv, halo_back, sink_near, sink_far, *tails_back)
+    )(halo_back, dk, dv, sink_near, sink_far, *tails_back)
     return attended, query_grad, key_grad, value_grad, sink_grad
 
 

time: 61 us -> 63.8 us (1.046)
  the two profiles are of different devices: /device:TPU:3 before, /device:TPU:7 now
where the time goes in v7:
time: 63.8 us; the launch traced here: 63.1 us
  starting transfers between devices  33.6 us (53%)
  waiting for transfers between devices  18 us (28%)
  Pallas kernels  10.6 us (17%)
  between operations  0.77 us (1%)
    ppermute x19, starting transfers between devices, ring(): lax.ppermute(value, axis, [(source, (source + steps) % count) for source...  30.5 us
    ppermute x19, waiting for transfers between devices, ring(): lax.ppermute(value, axis, [(source, (source + steps) % count) for source...  18 us
    ppermute x2, starting transfers between devices, shift(): lax.ppermute(value, axis, [(source, source + steps) for source in range(l...  3.11 us
    pallas_call x2, Pallas kernels, flush(): pl.pallas_call(stage_kernel, out_shape=pltpu.HBM(value.shape, BF16), in_s...  2.65 us
    pallas_call x1, Pallas kernels, local(): pl.pallas_call(stage_kernel, out_shape=(pltpu.VMEM(queries.shape, BF16),)...  2.26 us
    pallas_call x2, Pallas kernels, attend(): pl.pallas_call(functools.partial(attend_kernel, blocks_here, head_count,...  1.57 us
  transfers between devices with their start and end apart: 21, of which 10 were waited for; matrix products, arithmetic and copies ran while one was open for 0% of the time, Pallas kernels for 11%

profile of v7, /device:TPU:7, one launch (start us, length us, event | category | flops | bytes accessed | tf_op | source)
XLA Modules:
  0.0 63.1 jit_solution(12886938091614313575)
XLA Ops:
  0.6 1.2 %pack.1 = (bf16[256,256]{1,0:T(8,128)(2,1)S(1)}, bf16[256,256]{1,0:T(8,128)(2,1)S(1)}, bf16[256,256]{1,0:T(8,128)(2,1)S(1)}, bf16[256,256]{1,0:T(8,128)(2,1)S(1)...) custom-call(f32[16]{0:T(128)} %sink_hbm.1, ...), custom_call_target="tpu_custom_call" | custom-call | tf_op jit(solution)/shard_map/pack/pallas_call | solution.py:561
  2.7 1.2 %collective-permute-start.1 = (bf16[256,256]{1,0:T(8,128)(2,1)S(1)}, bf16[256,256]{1,0:T(8,128)(2,1)S(1)}, u32[]{:S(2)}, u32[]{:S(2)}) collective-permute-start(bf16[256,256]{1,0:T(8,128)(2,1)S(1)} %get-tuple-element.62), channel_id=1, source_target_pairs={{0,2},{1,3},{2,0},{3,1},{4,6},{5,7},{6,4},{7,5},{8,10},{9,11},{10,... | collective-permute-start | bytes 393224 | tf_op jit(solution)/shard_map/ppermute | solution.py:37
  3.9 1.3 %collective-permute-start.6 = (bf16[4,128,256]{2,1,0:T(8,128)(2,1)S(1)}, bf16[4,128,256]{2,1,0:T(8,128)(2,1)S(1)}, u32[]{:S(2)}, u32[]{:S(2)}) collective-permute-start(bf16[4,128,256]{2,1,0:T(8,128)(2,1)S(1)} %get-tuple-element.82), channel_id=1, source_target_pairs={{0,1},{1,2},{2,3},{4,5},{5,6},{6,7},{8,9},{9,10},{10,11},{12,13},{... | collective-permute-start | bytes 786440 | tf_op jit(solution)/shard_map/ppermute | solution.py:32
  6.0 3.9 %collective-permute-done.1.refs_2_ = bf16[256,256]{1,0:T(8,128)(2,1)S(1)} collective-permute-done((bf16[256,256]{1,0:T(8,128)(2,1)S(1)}, bf16[256,256]{1,0:T(8,128)(2,1)S(1)}, u32[]{:S(2)}, u32[]{:S(2)}) %collective-permute-start.1) | collective-permute-done | bytes 131104 | tf_op jit(solution)/shard_map/ppermute | solution.py:37
  9.8 1.5 %collective-permute-done.2.refs_3_ = bf16[256,256]{1,0:T(8,128)(2,1)S(1)} collective-permute-done((bf16[256,256]{1,0:T(8,128)(2,1)S(1)}, bf16[256,256]{1,0:T(8,128)(2,1)S(1)}, u32[]{:S(2)}, u32[]{:S(2)}) %collective-permute-start.2) | collective-permute-done | bytes 131104 | tf_op jit(solution)/shard_map/ppermute | solution.py:37
  11.8 2.3 %collective-permute-start.3 = (bf16[128,256]{1,0:T(8,128)(2,1)S(1)}, bf16[128,256]{1,0:T(8,128)(2,1)S(1)}, u32[]{:S(2)}, u32[]{:S(2)}) collective-permute-start(bf16[128,256]{1,0:T(8,128)(2,1)S(1)} %get-tuple-element.71), channel_id=1, source_target_pairs={{0,12},{4,16},{8,20},{12,24},{16,28},{20,0},{24,4},{28,8},{1,13},{... | collective-permute-start | bytes 196616 | tf_op jit(solution)/shard_map/ppermute | solution.py:37
  14.1 1.3 %collective-permute-start.4 = (bf16[128,256]{1,0:T(8,128)(2,1)S(1)}, bf16[128,256]{1,0:T(8,128)(2,1)S(1)}, u32[]{:S(2)}, u32[]{:S(2)}) collective-permute-start(bf16[128,256]{1,0:T(8,128)(2,1)S(1)} %get-tuple-element.72), channel_id=1, source_target_pairs={{0,8},{4,12},{8,16},{12,20},{16,24},{20,28},{24,0},{28,4},{1,9},{5... | collective-permute-start | bytes 196616 | tf_op jit(solution)/shard_map/ppermute | solution.py:37
  15.4 1.2 %collective-permute-start.5 = (bf16[128,256]{1,0:T(8,128)(2,1)S(1)}, bf16[128,256]{1,0:T(8,128)(2,1)S(1)}, u32[]{:S(2)}, u32[]{:S(2)}) collective-permute-start(bf16[128,256]{1,0:T(8,128)(2,1)S(1)} %get-tuple-element.73), channel_id=1, source_target_pairs={{0,4},{4,8},{8,12},{12,16},{16,20},{20,24},{24,28},{28,0},{1,5},{5... | collective-permute-start | bytes 196616 | tf_op jit(solution)/shard_map/ppermute | solution.py:37
  16.8 2.3 %stage.1 = (bf16[256,4096]{1,0:T(8,128)(2,1)S(1)}, bf16[256,4096]{1,0:T(8,128)(2,1)S(1)}) custom-call(bf16[256,4096]{1,0:T(8,128)(2,1)} %refs_0_, bf16[256,4096]{1,0:T(8,128)(2,1)} %refs_1_), custom_call_target="tpu_custom_call" | custom-call | tf_op jit(solution)/shard_map/stage/pallas_call | solution.py:606
  22.1 1.7 %collective-permute-done.9.refs_9_ = bf16[128,256]{1,0:T(8,128)(2,1)S(1)} collective-permute-done((bf16[128,256]{1,0:T(8,128)(2,1)S(1)}, bf16[128,256]{1,0:T(8,128)(2,1)S(1)}, u32[]{:S(2)}, u32[]{:S(2)}) %collective-permute-start.9) | collective-permute-done | bytes 65568 | tf_op jit(solution)/shard_map/ppermute | solution.py:37
  23.8 1.1 %attend.3 = (bf16[256,4096]{1,0:T(8,128)(2,1)S(1)}, bf16[256,4096]{1,0:T(8,128)(2,1)S(1)}, f32[256,512]{1,0:T(8,128)S(1)}, f32[256,512]{1,0:T(8,128)S(1)}, bf16[...) custom-call(s32[8,128]{1,0:T(8,128)S(1)} %plan.1.plan_ref.refs_0_, ...), custom_call_target="tpu_custom_call", output_to_operand_aliasing={{0}: (10, {}), {1}: (11, {}), {2}: (12, {}), {3}: (13, {}),... | custom-call | tf_op jit(solution)/shard_map/attend/pallas_call | solution.py:640
  24.9 6.8 %collective-permute-start.10 = (bf16[128,256]{1,0:T(8,128)(2,1)S(1)}, bf16[128,256]{1,0:T(8,128)(2,1)S(1)}, u32[]{:S(2)}, u32[]{:S(2)}) collective-permute-start(bf16[128,256]{1,0:T(8,128)(2,1)S(1)} %get-tuple-element.93), channel_id=1, source_target_pairs={{0,1},{1,2},{2,3},{3,0},{4,5},{5,6},{6,7},{7,4},{8,9},{9,10},{10,1... | collective-permute-start | bytes 196616 | tf_op jit(solution)/shard_map/ppermute | solution.py:37
  31.7 5.4 %collective-permute-start.11 = (bf16[128,256]{1,0:T(8,128)(2,1)S(1)}, bf16[128,256]{1,0:T(8,128)(2,1)S(1)}, u32[]{:S(2)}, u32[]{:S(2)}) collective-permute-start(bf16[128,256]{1,0:T(8,128)(2,1)S(1)} %get-tuple-element.94), channel_id=1, source_target_pairs={{0,2},{1,3},{2,0},{3,1},{4,6},{5,7},{6,4},{7,5},{8,10},{9,11},{10,... | collective-permute-start | bytes 196616 | tf_op jit(solution)/shard_map/ppermute | solution.py:37
  37.8 2.5 %collective-permute-done.11.refs_2_ = bf16[128,256]{1,0:T(8,128)(2,1)S(1)} collective-permute-done((bf16[128,256]{1,0:T(8,128)(2,1)S(1)}, bf16[128,256]{1,0:T(8,128)(2,1)S(1)}, u32[]{:S(2)}, u32[]{:S(2)}) %collective-permute-start.11) | collective-permute-done | bytes 65568 | tf_op jit(solution)/shard_map/ppermute | solution.py:37
  40.9 1.8 %collective-permute-start.16 = (bf16[4,128,256]{2,1,0:T(8,128)(2,1)S(1)}, bf16[4,128,256]{2,1,0:T(8,128)(2,1)S(1)}, u32[]{:S(2)}, u32[]{:S(2)}) collective-permute-start(bf16[4,128,256]{2,1,0:T(8,128)(2,1)S(1)} %get-tuple-element.105), channel_id=1, source_target_pairs={{1,0},{2,1},{3,2},{5,4},{6,5},{7,6},{9,8},{10,9},{11,10},{13,12},{... | collective-permute-start | bytes 786440 | tf_op jit(solution)/shard_map/ppermute | solution.py:32
  42.8 2.1 %collective-permute-start.15 = (bf16[128,256]{1,0:T(8,128)(2,1)S(1)}, bf16[128,256]{1,0:T(8,128)(2,1)S(1)}, u32[]{:S(2)}, u32[]{:S(2)}) collective-permute-start(bf16[128,256]{1,0:T(8,128)(2,1)S(1)} %gather.1.here_ref), channel_id=1, source_target_pairs={{0,20},{4,24},{8,28},{12,0},{16,4},{20,8},{24,12},{28,16},{1,21},{... | collective-permute-start | bytes 196616 | tf_op jit(solution)/shard_map/ppermute | solution.py:37
  44.9 2.6 %collective-permute-start.14 = (bf16[128,256]{1,0:T(8,128)(2,1)S(1)}, bf16[128,256]{1,0:T(8,128)(2,1)S(1)}, u32[]{:S(2)}, u32[]{:S(2)}) collective-permute-start(bf16[128,256]{1,0:T(8,128)(2,1)S(1)} %gather.1.here_ref), channel_id=1, source_target_pairs={{0,24},{4,28},{8,0},{12,4},{16,8},{20,12},{24,16},{28,20},{1,25},{... | collective-permute-start | bytes 196616 | tf_op jit(solution)/shard_map/ppermute | solution.py:37
  47.5 1.3 %flush.2 = bf16[256,4096]{1,0:T(8,128)(2,1)} custom-call(bf16[256,4096]{1,0:T(8,128)(2,1)S(1)} %get-tuple-element.96.refs_0_), custom_call_target="tpu_custom_call" | custom-call | tf_op jit(solution)/shard_map/flush/pallas_call | solution.py:690
  48.8 2.9 %collective-permute-done.13.refs_0_ = bf16[128,256]{1,0:T(8,128)(2,1)S(1)} collective-permute-done((bf16[128,256]{1,0:T(8,128)(2,1)S(1)}, bf16[128,256]{1,0:T(8,128)(2,1)S(1)}, u32[]{:S(2)}, u32[]{:S(2)}) %collective-permute-start.13) | collective-permute-done | bytes 65568 | tf_op jit(solution)/shard_map/ppermute | solution.py:37
  52.1 1.4 %collective-permute-start.18 = (bf16[256,256]{1,0:T(8,128)(2,1)S(1)}, bf16[256,256]{1,0:T(8,128)(2,1)S(1)}, u32[]{:S(2)}, u32[]{:S(2)}) collective-permute-start(bf16[256,256]{1,0:T(8,128)(2,1)S(1)} %get-tuple-element.109), channel_id=1, source_target_pairs={{0,1},{1,2},{2,3},{3,0},{4,5},{5,6},{6,7},{7,4},{8,9},{9,10},{10,1... | collective-permute-start | bytes 393224 | tf_op jit(solution)/shard_map/ppermute | solution.py:37
  53.5 2.1 %collective-permute-start.19 = (bf16[256,256]{1,0:T(8,128)(2,1)S(1)}, bf16[256,256]{1,0:T(8,128)(2,1)S(1)}, u32[]{:S(2)}, u32[]{:S(2)}) collective-permute-start(bf16[256,256]{1,0:T(8,128)(2,1)S(1)} %get-tuple-element.110), channel_id=1, source_target_pairs={{0,2},{1,3},{2,0},{3,1},{4,6},{5,7},{6,4},{7,5},{8,10},{9,11},{10,... | collective-permute-start | bytes 393224 | tf_op jit(solution)/shard_map/ppermute | solution.py:37
  56.3 1.3 %flush.3 = bf16[256,4096]{1,0:T(8,128)(2,1)} custom-call(bf16[256,4096]{1,0:T(8,128)(2,1)S(1)} %get-tuple-element.103.refs_0_), custom_call_target="tpu_custom_call" | custom-call | tf_op jit(solution)/shard_map/flush/pallas_call | solution.py:690
  57.6 1.3 %collective-permute-done.17.far_ref = f32[8,128]{1,0:T(8,128)S(1)} collective-permute-done((f32[8,128]{1,0:T(8,128)S(1)}, f32[8,128]{1,0:T(8,128)S(1)}, u32[]{:S(2)}, u32[]{:S(2)}) %collective-permute-start.17) | collective-permute-done | bytes 4128 | tf_op jit(solution)/shard_map/ppermute | solution.py:37
  58.9 2.6 %collective-permute-done.19.refs_2_ = bf16[256,256]{1,0:T(8,128)(2,1)S(1)} collective-permute-done((bf16[256,256]{1,0:T(8,128)(2,1)S(1)}, bf16[256,256]{1,0:T(8,128)(2,1)S(1)}, u32[]{:S(2)}, u32[]{:S(2)}) %collective-permute-start.19) | collective-permute-done | bytes 131104 | tf_op jit(solution)/shard_map/ppermute | solution.py:37
  (31 shorter events, 9.2 us)
Async XLA Ops:
  1.8 4.2 %collective-permute-start = (bf16[256,256]{1,0:T(8,128)(2,1)S(1)}, bf16[256,256]{1,0:T(8,128)(2,1)S(1)}, u32[]{:S(2)}, u32[]{:S(2)}) collective-permute-start(bf16[256,256]{1,0:T(8,128)(2,1)S(1)} %get-tuple-element.61), channel_id=1, source_target_pairs={{0,1},{1,2},{2,3},{3,0},{4,5},{5,6},{6,7},{7,4},{8,9},{9,10},{10,1... | collective-permute-start | bytes 393224 | tf_op jit(solution)/shard_map/ppermute | solution.py:37
  2.7 7.2 %collective-permute-start.1 = (bf16[256,256]{1,0:T(8,128)(2,1)S(1)}, bf16[256,256]{1,0:T(8,128)(2,1)S(1)}, u32[]{:S(2)}, u32[]{:S(2)}) collective-permute-start(bf16[256,256]{1,0:T(8,128)(2,1)S(1)} %get-tuple-element.62), channel_id=1, source_target_pairs={{0,2},{1,3},{2,0},{3,1},{4,6},{5,7},{6,4},{7,5},{8,10},{9,11},{10,... | collective-permute-start | bytes 393224 | tf_op jit(solution)/shard_map/ppermute | solution.py:37
  3.9 7.5 %collective-permute-start.2 = (bf16[256,256]{1,0:T(8,128)(2,1)S(1)}, bf16[256,256]{1,0:T(8,128)(2,1)S(1)}, u32[]{:S(2)}, u32[]{:S(2)}) collective-permute-start(bf16[256,256]{1,0:T(8,128)(2,1)S(1)} %get-tuple-element.63), channel_id=1, source_target_pairs={{0,3},{1,0},{2,1},{3,2},{4,7},{5,4},{6,5},{7,6},{8,11},{9,8},{10,9... | collective-permute-start | bytes 393224 | tf_op jit(solution)/shard_map/ppermute | solution.py:37
  3.9 18.2 %collective-permute-start.6 = (bf16[4,128,256]{2,1,0:T(8,128)(2,1)S(1)}, bf16[4,128,256]{2,1,0:T(8,128)(2,1)S(1)}, u32[]{:S(2)}, u32[]{:S(2)}) collective-permute-start(bf16[4,128,256]{2,1,0:T(8,128)(2,1)S(1)} %get-tuple-element.82), channel_id=1, source_target_pairs={{0,1},{1,2},{2,3},{4,5},{5,6},{6,7},{8,9},{9,10},{10,11},{12,13},{... | collective-permute-start | bytes 786440 | tf_op jit(solution)/shard_map/ppermute | solution.py:32
  11.8 7.3 %collective-permute-start.3 = (bf16[128,256]{1,0:T(8,128)(2,1)S(1)}, bf16[128,256]{1,0:T(8,128)(2,1)S(1)}, u32[]{:S(2)}, u32[]{:S(2)}) collective-permute-start(bf16[128,256]{1,0:T(8,128)(2,1)S(1)} %get-tuple-element.71), channel_id=1, source_target_pairs={{0,12},{4,16},{8,20},{12,24},{16,28},{20,0},{24,4},{28,8},{1,13},{... | collective-permute-start | bytes 196616 | tf_op jit(solution)/shard_map/ppermute | solution.py:37
  14.1 5.6 %collective-permute-start.4 = (bf16[128,256]{1,0:T(8,128)(2,1)S(1)}, bf16[128,256]{1,0:T(8,128)(2,1)S(1)}, u32[]{:S(2)}, u32[]{:S(2)}) collective-permute-start(bf16[128,256]{1,0:T(8,128)(2,1)S(1)} %get-tuple-element.72), channel_id=1, source_target_pairs={{0,8},{4,12},{8,16},{12,20},{16,24},{20,28},{24,0},{28,4},{1,9},{5... | collective-permute-start | bytes 196616 | tf_op jit(solution)/shard_map/ppermute | solution.py:37
  15.4 4.3 %collective-permute-start.5 = (bf16[128,256]{1,0:T(8,128)(2,1)S(1)}, bf16[128,256]{1,0:T(8,128)(2,1)S(1)}, u32[]{:S(2)}, u32[]{:S(2)}) collective-permute-start(bf16[128,256]{1,0:T(8,128)(2,1)S(1)} %get-tuple-element.73), channel_id=1, source_target_pairs={{0,4},{4,8},{8,12},{12,16},{16,20},{20,24},{24,28},{28,0},{1,5},{5... | collective-permute-start | bytes 196616 | tf_op jit(solution)/shard_map/ppermute | solution.py:37
  19.8 3.9 %collective-permute-start.9 = (bf16[128,256]{1,0:T(8,128)(2,1)S(1)}, bf16[128,256]{1,0:T(8,128)(2,1)S(1)}, u32[]{:S(2)}, u32[]{:S(2)}) collective-permute-start(bf16[128,256]{1,0:T(8,128)(2,1)S(1)} %arrive.1.refs_7_), channel_id=1, source_target_pairs={{0,3},{1,0},{2,1},{3,2},{4,7},{5,4},{6,5},{7,6},{8,11},{9,8},{10,9... | collective-permute-start | bytes 196616 | tf_op jit(solution)/shard_map/ppermute | solution.py:37
  19.9 3.9 %collective-permute-start.8 = (bf16[128,256]{1,0:T(8,128)(2,1)S(1)}, bf16[128,256]{1,0:T(8,128)(2,1)S(1)}, u32[]{:S(2)}, u32[]{:S(2)}) collective-permute-start(bf16[128,256]{1,0:T(8,128)(2,1)S(1)} %arrive.1.refs_7_), channel_id=1, source_target_pairs={{0,2},{1,3},{2,0},{3,1},{4,6},{5,7},{6,4},{7,5},{8,10},{9,11},{10,... | collective-permute-start | bytes 196616 | tf_op jit(solution)/shard_map/ppermute | solution.py:37
  20.8 2.9 %collective-permute-start.7 = (bf16[128,256]{1,0:T(8,128)(2,1)S(1)}, bf16[128,256]{1,0:T(8,128)(2,1)S(1)}, u32[]{:S(2)}, u32[]{:S(2)}) collective-permute-start(bf16[128,256]{1,0:T(8,128)(2,1)S(1)} %arrive.1.refs_7_), channel_id=1, source_target_pairs={{0,1},{1,2},{2,3},{3,0},{4,5},{5,6},{6,7},{7,4},{8,9},{9,10},{10,1... | collective-permute-start | bytes 196616 | tf_op jit(solution)/shard_map/ppermute | solution.py:37
  24.9 12.9 %collective-permute-start.10 = (bf16[128,256]{1,0:T(8,128)(2,1)S(1)}, bf16[128,256]{1,0:T(8,128)(2,1)S(1)}, u32[]{:S(2)}, u32[]{:S(2)}) collective-permute-start(bf16[128,256]{1,0:T(8,128)(2,1)S(1)} %get-tuple-element.93), channel_id=1, source_target_pairs={{0,1},{1,2},{2,3},{3,0},{4,5},{5,6},{6,7},{7,4},{8,9},{9,10},{10,1... | collective-permute-start | bytes 196616 | tf_op jit(solution)/shard_map/ppermute | solution.py:37
  31.7 8.6 %collective-permute-start.11 = (bf16[128,256]{1,0:T(8,128)(2,1)S(1)}, bf16[128,256]{1,0:T(8,128)(2,1)S(1)}, u32[]{:S(2)}, u32[]{:S(2)}) collective-permute-start(bf16[128,256]{1,0:T(8,128)(2,1)S(1)} %get-tuple-element.94), channel_id=1, source_target_pairs={{0,2},{1,3},{2,0},{3,1},{4,6},{5,7},{6,4},{7,5},{8,10},{9,11},{10,... | collective-permute-start | bytes 196616 | tf_op jit(solution)/shard_map/ppermute | solution.py:37
  37.1 3.7 %collective-permute-start.12 = (bf16[128,256]{1,0:T(8,128)(2,1)S(1)}, bf16[128,256]{1,0:T(8,128)(2,1)S(1)}, u32[]{:S(2)}, u32[]{:S(2)}) collective-permute-start(bf16[128,256]{1,0:T(8,128)(2,1)S(1)} %get-tuple-element.95), channel_id=1, source_target_pairs={{0,3},{1,0},{2,1},{3,2},{4,7},{5,4},{6,5},{7,6},{8,11},{9,8},{10,9... | collective-permute-start | bytes 196616 | tf_op jit(solution)/shard_map/ppermute | solution.py:37
  40.9 21.2 %collective-permute-start.16 = (bf16[4,128,256]{2,1,0:T(8,128)(2,1)S(1)}, bf16[4,128,256]{2,1,0:T(8,128)(2,1)S(1)}, u32[]{:S(2)}, u32[]{:S(2)}) collective-permute-start(bf16[4,128,256]{2,1,0:T(8,128)(2,1)S(1)} %get-tuple-element.105), channel_id=1, source_target_pairs={{1,0},{2,1},{3,2},{5,4},{6,5},{7,6},{9,8},{10,9},{11,10},{13,12},{... | collective-permute-start | bytes 786440 | tf_op jit(solution)/shard_map/ppermute | solution.py:32
  42.8 6.0 %collective-permute-start.15 = (bf16[128,256]{1,0:T(8,128)(2,1)S(1)}, bf16[128,256]{1,0:T(8,128)(2,1)S(1)}, u32[]{:S(2)}, u32[]{:S(2)}) collective-permute-start(bf16[128,256]{1,0:T(8,128)(2,1)S(1)} %gather.1.here_ref), channel_id=1, source_target_pairs={{0,20},{4,24},{8,28},{12,0},{16,4},{20,8},{24,12},{28,16},{1,21},{... | collective-permute-start | bytes 196616 | tf_op jit(solution)/shard_map/ppermute | solution.py:37
  44.9 3.9 %collective-permute-start.14 = (bf16[128,256]{1,0:T(8,128)(2,1)S(1)}, bf16[128,256]{1,0:T(8,128)(2,1)S(1)}, u32[]{:S(2)}, u32[]{:S(2)}) collective-permute-start(bf16[128,256]{1,0:T(8,128)(2,1)S(1)} %gather.1.here_ref), channel_id=1, source_target_pairs={{0,24},{4,28},{8,0},{12,4},{16,8},{20,12},{24,16},{28,20},{1,25},{... | collective-permute-start | bytes 196616 | tf_op jit(solution)/shard_map/ppermute | solution.py:37
  47.5 4.2 %collective-permute-start.13 = (bf16[128,256]{1,0:T(8,128)(2,1)S(1)}, bf16[128,256]{1,0:T(8,128)(2,1)S(1)}, u32[]{:S(2)}, u32[]{:S(2)}) collective-permute-start(bf16[128,256]{1,0:T(8,128)(2,1)S(1)} %gather.1.here_ref), channel_id=1, source_target_pairs={{0,28},{4,0},{8,4},{12,8},{16,12},{20,16},{24,20},{28,24},{1,29},{... | collective-permute-start | bytes 196616 | tf_op jit(solution)/shard_map/ppermute | solution.py:37
  52.1 6.8 %collective-permute-start.18 = (bf16[256,256]{1,0:T(8,128)(2,1)S(1)}, bf16[256,256]{1,0:T(8,128)(2,1)S(1)}, u32[]{:S(2)}, u32[]{:S(2)}) collective-permute-start(bf16[256,256]{1,0:T(8,128)(2,1)S(1)} %get-tuple-element.109), channel_id=1, source_target_pairs={{0,1},{1,2},{2,3},{3,0},{4,5},{5,6},{6,7},{7,4},{8,9},{9,10},{10,1... | collective-permute-start | bytes 393224 | tf_op jit(solution)/shard_map/ppermute | solution.py:37
  53.5 8.0 %collective-permute-start.19 = (bf16[256,256]{1,0:T(8,128)(2,1)S(1)}, bf16[256,256]{1,0:T(8,128)(2,1)S(1)}, u32[]{:S(2)}, u32[]{:S(2)}) collective-permute-start(bf16[256,256]{1,0:T(8,128)(2,1)S(1)} %get-tuple-element.110), channel_id=1, source_target_pairs={{0,2},{1,3},{2,0},{3,1},{4,6},{5,7},{6,4},{7,5},{8,10},{9,11},{10,... | collective-permute-start | bytes 393224 | tf_op jit(solution)/shard_map/ppermute | solution.py:37
  55.6 6.6 %collective-permute-start.20 = (bf16[256,256]{1,0:T(8,128)(2,1)S(1)}, bf16[256,256]{1,0:T(8,128)(2,1)S(1)}, u32[]{:S(2)}, u32[]{:S(2)}) collective-permute-start(bf16[256,256]{1,0:T(8,128)(2,1)S(1)} %get-tuple-element.111), channel_id=1, source_target_pairs={{0,3},{1,0},{2,1},{3,2},{4,7},{5,4},{6,5},{7,6},{8,11},{9,8},{10,9... | collective-permute-start | bytes 393224 | tf_op jit(solution)/shard_map/ppermute | solution.py:37
  55.6 3.4 %collective-permute-start.17 = (f32[8,128]{1,0:T(8,128)S(1)}, f32[8,128]{1,0:T(8,128)S(1)}, u32[]{:S(2)}, u32[]{:S(2)}) collective-permute-start(f32[8,128]{1,0:T(8,128)S(1)} %get-tuple-element.102.sink_ref), channel_id=1, source_target_pairs={{0,16},{4,20},{8,24},{12,28},{16,0},{20,4},{24,8},{28,12},{1,17},{... | collective-permute-start | bytes 12296 | tf_op jit(solution)/shard_map/ppermute | solution.py:37

commit v8 on v7

--- a/solution.py
+++ b/solution.py
@@ -206,7 +206,7 @@
     head = lax.axis_index("head")
     states = [planned_block(inputs[0], block) for block in range(blocks_here)]
     for step, tail_ref in zip(steps, tail_refs):
-        tails[lax.rem(head - step + slots, slots)] = tail_ref[...]
+        tails[lax.rem(head + step, slots)] = tail_ref[...]
 
     def step(place, carry):
         pair = place // blocks_here
@@ -633,7 +633,7 @@
             close(keys),
             close(values),
             halo,
-            *(tails[step] for step in steps),
+            *(tails[-step % head_count] for step in steps),
             *(close(value) for value in joined),
         )
         base = 1 + len(inputs) - len(joined)
@@ -671,21 +671,27 @@
 
     if per_slot == 2:
         *joined, own_tail = attend((0,), 1, 0, spread[1], ())
-        *results, tail_1, tail_2, tail_3 = attend((1, 2, 3), PAIRS - 1, 1, halo, joined)
+        *joined, tail_1, tail_2 = attend((1, 2), 2, 1, halo, joined)
+        *results, tail_3 = attend((3,), 1, 3, halo, joined)
         dtail = [own_tail, tail_1, tail_2, tail_3]
     else:
         results = attend(tuple(range(head_count)), PAIRS, None, halo, ())
         results, dtail = results[:5], list(results[5:])
     attended, query_grad, dk, dv, dhalo = results
     parts = swap(dtail, "head")
-    quarter_grad = pl.pallas_call(
-        gather_kernel,
-        out_shape=shape((WINDOW, width)),
-        in_specs=[VMEM] * head_count,
-        out_specs=VMEM,
-        compiler_params=PARAMS,
-        name="gather",
-    )(*parts)
+
+    def gather(values):
+        return pl.pallas_call(
+            gather_kernel,
+            out_shape=shape((WINDOW, width)),
+            in_specs=[VMEM] * len(values),
+            out_specs=VMEM,
+            compiler_params=PARAMS,
+            name="gather",
+        )(*values)
+
+    quarter_grad = gather([gather(parts[:-1]), parts[-1]])
+
     def flush(value):
         return pl.pallas_call(
             stage_kernel,
@@ -701,7 +707,6 @@
     attended, _ = lax.optimization_barrier((attended, quarter_grad))
     attended = flush(attended)
     attended, *returned = lax.optimization_barrier((attended, *returned))
-    dhalo, _ = lax.optimization_barrier((dhalo, quarter_grad))
     halo_back = shift(dhalo, "head", -1)
     *landed, sink_near = pl.pallas_call(
         functools.partial(land_kernel, blocks),

time: 63.8 us -> 59.1 us (0.926)
  the two profiles are of different devices: /device:TPU:7 before, /device:TPU:3 now
where the time goes in v8:
time: 59.1 us; the launch traced here: 58.9 us
  starting transfers between devices  30.6 us (52%)
  Pallas kernels  16.9 us (29%)
  waiting for transfers between devices  10.5 us (18%)
  between operations  0.78 us (1%)
    ppermute x19, starting transfers between devices, ring(): lax.ppermute(value, axis, [(source, (source + steps) % count) for source...  25.3 us
    ppermute x19, waiting for transfers between devices, ring(): lax.ppermute(value, axis, [(source, (source + steps) % count) for source...  10.5 us
    pallas_call x3, Pallas kernels, attend(): pl.pallas_call(functools.partial(attend_kernel, blocks_here, head_count,...  7.72 us
    ppermute x2, starting transfers between devices, shift(): lax.ppermute(value, axis, [(source, source + steps) for source in range(l...  5.31 us
    pallas_call x2, Pallas kernels, flush(): pl.pallas_call(stage_kernel, out_shape=pltpu.HBM(value.shape, BF16), in_s...  2.65 us
    pallas_call x1, Pallas kernels, local(): pl.pallas_call(stage_kernel, out_shape=(pltpu.VMEM(queries.shape, BF16),)...  2.26 us
  transfers between devices with their start and end apart: 21, of which 11 were waited for; matrix products, arithmetic and copies ran while one was open for 0% of the time, Pallas kernels for 25%

profile of v8, /device:TPU:3, one launch (start us, length us, event | category | flops | bytes accessed | tf_op | source)
XLA Modules:
  0.0 58.9 jit_solution(1015295748534204484)
XLA Ops:
  0.6 1.2 %pack.1 = (bf16[256,256]{1,0:T(8,128)(2,1)S(1)}, bf16[256,256]{1,0:T(8,128)(2,1)S(1)}, bf16[256,256]{1,0:T(8,128)(2,1)S(1)}, bf16[256,256]{1,0:T(8,128)(2,1)S(1)...) custom-call(f32[16]{0:T(128)} %sink_hbm.1, ...), custom_call_target="tpu_custom_call" | custom-call | tf_op jit(solution)/shard_map/pack/pallas_call | solution.py:561
  1.8 1.9 %collective-permute-start = (bf16[256,256]{1,0:T(8,128)(2,1)S(1)}, bf16[256,256]{1,0:T(8,128)(2,1)S(1)}, u32[]{:S(2)}, u32[]{:S(2)}) collective-permute-start(bf16[256,256]{1,0:T(8,128)(2,1)S(1)} %get-tuple-element.65), channel_id=1, source_target_pairs={{0,1},{1,2},{2,3},{3,0},{4,5},{5,6},{6,7},{7,4},{8,9},{9,10},{10,1... | collective-permute-start | bytes 393224 | tf_op jit(solution)/shard_map/ppermute | solution.py:37
  4.1 3.4 %collective-permute-start.6 = (bf16[4,128,256]{2,1,0:T(8,128)(2,1)S(1)}, bf16[4,128,256]{2,1,0:T(8,128)(2,1)S(1)}, u32[]{:S(2)}, u32[]{:S(2)}) collective-permute-start(bf16[4,128,256]{2,1,0:T(8,128)(2,1)S(1)} %get-tuple-element.86), channel_id=1, source_target_pairs={{0,1},{1,2},{2,3},{4,5},{5,6},{6,7},{8,9},{9,10},{10,11},{12,13},{... | collective-permute-start | bytes 786440 | tf_op jit(solution)/shard_map/ppermute | solution.py:32
  8.3 1.5 %collective-permute-done.1.refs_2_ = bf16[256,256]{1,0:T(8,128)(2,1)S(1)} collective-permute-done((bf16[256,256]{1,0:T(8,128)(2,1)S(1)}, bf16[256,256]{1,0:T(8,128)(2,1)S(1)}, u32[]{:S(2)}, u32[]{:S(2)}) %collective-permute-start.1) | collective-permute-done | bytes 131104 | tf_op jit(solution)/shard_map/ppermute | solution.py:37
  10.9 2.3 %collective-permute-start.3 = (bf16[128,256]{1,0:T(8,128)(2,1)S(1)}, bf16[128,256]{1,0:T(8,128)(2,1)S(1)}, u32[]{:S(2)}, u32[]{:S(2)}) collective-permute-start(bf16[128,256]{1,0:T(8,128)(2,1)S(1)} %get-tuple-element.75), channel_id=1, source_target_pairs={{0,12},{4,16},{8,20},{12,24},{16,28},{20,0},{24,4},{28,8},{1,13},{... | collective-permute-start | bytes 196616 | tf_op jit(solution)/shard_map/ppermute | solution.py:37
  13.2 1.3 %collective-permute-start.4 = (bf16[128,256]{1,0:T(8,128)(2,1)S(1)}, bf16[128,256]{1,0:T(8,128)(2,1)S(1)}, u32[]{:S(2)}, u32[]{:S(2)}) collective-permute-start(bf16[128,256]{1,0:T(8,128)(2,1)S(1)} %get-tuple-element.76), channel_id=1, source_target_pairs={{0,8},{4,12},{8,16},{12,20},{16,24},{20,28},{24,0},{28,4},{1,9},{5... | collective-permute-start | bytes 196616 | tf_op jit(solution)/shard_map/ppermute | solution.py:37
  14.5 1.2 %collective-permute-start.5 = (bf16[128,256]{1,0:T(8,128)(2,1)S(1)}, bf16[128,256]{1,0:T(8,128)(2,1)S(1)}, u32[]{:S(2)}, u32[]{:S(2)}) collective-permute-start(bf16[128,256]{1,0:T(8,128)(2,1)S(1)} %get-tuple-element.77), channel_id=1, source_target_pairs={{0,4},{4,8},{8,12},{12,16},{16,20},{20,24},{24,28},{28,0},{1,5},{5... | collective-permute-start | bytes 196616 | tf_op jit(solution)/shard_map/ppermute | solution.py:37
  15.9 2.3 %stage.1 = (bf16[256,4096]{1,0:T(8,128)(2,1)S(1)}, bf16[256,4096]{1,0:T(8,128)(2,1)S(1)}) custom-call(bf16[256,4096]{1,0:T(8,128)(2,1)} %refs_0_, bf16[256,4096]{1,0:T(8,128)(2,1)} %refs_1_), custom_call_target="tpu_custom_call" | custom-call | tf_op jit(solution)/shard_map/stage/pallas_call | solution.py:606
  18.4 2.8 %collective-permute-start.9 = (bf16[128,256]{1,0:T(8,128)(2,1)S(1)}, bf16[128,256]{1,0:T(8,128)(2,1)S(1)}, u32[]{:S(2)}, u32[]{:S(2)}) collective-permute-start(bf16[128,256]{1,0:T(8,128)(2,1)S(1)} %arrive.1.refs_7_), channel_id=1, source_target_pairs={{0,2},{1,3},{2,0},{3,1},{4,6},{5,7},{6,4},{7,5},{8,10},{9,11},{10,... | collective-permute-start | bytes 196616 | tf_op jit(solution)/shard_map/ppermute | solution.py:37
  21.1 1.7 %collective-permute-start.7 = (bf16[128,256]{1,0:T(8,128)(2,1)S(1)}, bf16[128,256]{1,0:T(8,128)(2,1)S(1)}, u32[]{:S(2)}, u32[]{:S(2)}) collective-permute-start(bf16[128,256]{1,0:T(8,128)(2,1)S(1)} %arrive.1.refs_7_), channel_id=1, source_target_pairs={{0,1},{1,2},{2,3},{3,0},{4,5},{5,6},{6,7},{7,4},{8,9},{9,10},{10,1... | collective-permute-start | bytes 196616 | tf_op jit(solution)/shard_map/ppermute | solution.py:37
  22.8 2.0 %attend.3 = (bf16[256,4096]{1,0:T(8,128)(2,1)S(1)}, bf16[256,4096]{1,0:T(8,128)(2,1)S(1)}, f32[256,512]{1,0:T(8,128)S(1)}, f32[256,512]{1,0:T(8,128)S(1)}, bf16[...) custom-call(s32[8,128]{1,0:T(8,128)S(1)} %plan.1.plan_ref.refs_0_, f32[64,128]{1,0:T(8,128)S(1)} %sinks.1.refs_1_, ...), custom_call_target="tpu_custom_call" | custom-call | tf_op jit(solution)/shard_map/attend/pallas_call | solution.py:640
  25.6 3.8 %attend.4 = (bf16[256,4096]{1,0:T(8,128)(2,1)S(1)}, bf16[256,4096]{1,0:T(8,128)(2,1)S(1)}, f32[256,512]{1,0:T(8,128)S(1)}, f32[256,512]{1,0:T(8,128)S(1)}, bf16[...) custom-call(s32[8,128]{1,0:T(8,128)S(1)} %plan.1.plan_ref.refs_0_, ...), custom_call_target="tpu_custom_call", output_to_operand_aliasing={{0}: (9, {}), {1}: (10, {}), {2}: (11, {}), {3}: (12, {}), ... | custom-call | tf_op jit(solution)/shard_map/attend/pallas_call | solution.py:640
  29.4 3.8 %collective-permute-start.10 = (bf16[128,256]{1,0:T(8,128)(2,1)S(1)}, bf16[128,256]{1,0:T(8,128)(2,1)S(1)}, u32[]{:S(2)}, u32[]{:S(2)}) collective-permute-start(bf16[128,256]{1,0:T(8,128)(2,1)S(1)} %get-tuple-element.102), channel_id=1, source_target_pairs={{0,1},{1,2},{2,3},{3,0},{4,5},{5,6},{6,7},{7,4},{8,9},{9,10},{10,1... | collective-permute-start | bytes 196616 | tf_op jit(solution)/shard_map/ppermute | solution.py:37
  33.5 2.0 %attend.5 = (bf16[256,4096]{1,0:T(8,128)(2,1)S(1)}, bf16[256,4096]{1,0:T(8,128)(2,1)S(1)}, f32[256,512]{1,0:T(8,128)S(1)}, f32[256,512]{1,0:T(8,128)S(1)}, bf16[...) custom-call(s32[8,128]{1,0:T(8,128)S(1)} %plan.1.plan_ref.refs_0_, ...), custom_call_target="tpu_custom_call", output_to_operand_aliasing={{0}: (8, {}), {1}: (9, {}), {2}: (10, {}), {3}: (11, {}), {... | custom-call | tf_op jit(solution)/shard_map/attend/pallas_call | solution.py:640
  35.5 1.6 %collective-permute-start.12 = (bf16[128,256]{1,0:T(8,128)(2,1)S(1)}, bf16[128,256]{1,0:T(8,128)(2,1)S(1)}, u32[]{:S(2)}, u32[]{:S(2)}) collective-permute-start(bf16[128,256]{1,0:T(8,128)(2,1)S(1)} %get-tuple-element.104), channel_id=1, source_target_pairs={{0,3},{1,0},{2,1},{3,2},{4,7},{5,4},{6,5},{7,6},{8,11},{9,8},{10,9... | collective-permute-start | bytes 196616 | tf_op jit(solution)/shard_map/ppermute | solution.py:37
  37.1 1.9 %collective-permute-start.16 = (bf16[4,128,256]{2,1,0:T(8,128)(2,1)S(1)}, bf16[4,128,256]{2,1,0:T(8,128)(2,1)S(1)}, u32[]{:S(2)}, u32[]{:S(2)}) collective-permute-start(bf16[4,128,256]{2,1,0:T(8,128)(2,1)S(1)} %get-tuple-element.113), channel_id=1, source_target_pairs={{1,0},{2,1},{3,2},{5,4},{6,5},{7,6},{9,8},{10,9},{11,10},{13,12},{... | collective-permute-start | bytes 786440 | tf_op jit(solution)/shard_map/ppermute | solution.py:32
  39.5 4.0 %collective-permute-start.15 = (bf16[128,256]{1,0:T(8,128)(2,1)S(1)}, bf16[128,256]{1,0:T(8,128)(2,1)S(1)}, u32[]{:S(2)}, u32[]{:S(2)}) collective-permute-start(bf16[128,256]{1,0:T(8,128)(2,1)S(1)} %gather.3.here_ref), channel_id=1, source_target_pairs={{0,20},{4,24},{8,28},{12,0},{16,4},{20,8},{24,12},{28,16},{1,21},{... | collective-permute-start | bytes 196616 | tf_op jit(solution)/shard_map/ppermute | solution.py:37
  43.5 1.5 %collective-permute-start.14 = (bf16[128,256]{1,0:T(8,128)(2,1)S(1)}, bf16[128,256]{1,0:T(8,128)(2,1)S(1)}, u32[]{:S(2)}, u32[]{:S(2)}) collective-permute-start(bf16[128,256]{1,0:T(8,128)(2,1)S(1)} %gather.3.here_ref), channel_id=1, source_target_pairs={{0,24},{4,28},{8,0},{12,4},{16,8},{20,12},{24,16},{28,20},{1,25},{... | collective-permute-start | bytes 196616 | tf_op jit(solution)/shard_map/ppermute | solution.py:37
  44.9 1.3 %flush.2 = bf16[256,4096]{1,0:T(8,128)(2,1)} custom-call(bf16[256,4096]{1,0:T(8,128)(2,1)S(1)} %get-tuple-element.105.refs_0_), custom_call_target="tpu_custom_call" | custom-call | tf_op jit(solution)/shard_map/flush/pallas_call | solution.py:696
  47.0 2.2 %collective-permute-done.13.refs_0_ = bf16[128,256]{1,0:T(8,128)(2,1)S(1)} collective-permute-done((bf16[128,256]{1,0:T(8,128)(2,1)S(1)}, bf16[128,256]{1,0:T(8,128)(2,1)S(1)}, u32[]{:S(2)}, u32[]{:S(2)}) %collective-permute-start.13) | collective-permute-done | bytes 65568 | tf_op jit(solution)/shard_map/ppermute | solution.py:37
  49.6 1.7 %collective-permute-start.18 = (bf16[256,256]{1,0:T(8,128)(2,1)S(1)}, bf16[256,256]{1,0:T(8,128)(2,1)S(1)}, u32[]{:S(2)}, u32[]{:S(2)}) collective-permute-start(bf16[256,256]{1,0:T(8,128)(2,1)S(1)} %get-tuple-element.117), channel_id=1, source_target_pairs={{0,1},{1,2},{2,3},{3,0},{4,5},{5,6},{6,7},{7,4},{8,9},{9,10},{10,1... | collective-permute-start | bytes 393224 | tf_op jit(solution)/shard_map/ppermute | solution.py:37
  52.1 1.3 %flush.3 = bf16[256,4096]{1,0:T(8,128)(2,1)} custom-call(bf16[256,4096]{1,0:T(8,128)(2,1)S(1)} %get-tuple-element.112.refs_0_), custom_call_target="tpu_custom_call" | custom-call | tf_op jit(solution)/shard_map/flush/pallas_call | solution.py:696
  53.4 1.7 %collective-permute-done.17.far_ref = f32[8,128]{1,0:T(8,128)S(1)} collective-permute-done((f32[8,128]{1,0:T(8,128)S(1)}, f32[8,128]{1,0:T(8,128)S(1)}, u32[]{:S(2)}, u32[]{:S(2)}) %collective-permute-start.17) | collective-permute-done | bytes 4128 | tf_op jit(solution)/shard_map/ppermute | solution.py:37
  55.1 2.1 %collective-permute-done.19.refs_2_ = bf16[256,256]{1,0:T(8,128)(2,1)S(1)} collective-permute-done((bf16[256,256]{1,0:T(8,128)(2,1)S(1)}, bf16[256,256]{1,0:T(8,128)(2,1)S(1)}, u32[]{:S(2)}, u32[]{:S(2)}) %collective-permute-start.19) | collective-permute-done | bytes 131104 | tf_op jit(solution)/shard_map/ppermute | solution.py:37
  (33 shorter events, 7.7 us)
Async XLA Ops:
  1.8 6.5 %collective-permute-start = (bf16[256,256]{1,0:T(8,128)(2,1)S(1)}, bf16[256,256]{1,0:T(8,128)(2,1)S(1)}, u32[]{:S(2)}, u32[]{:S(2)}) collective-permute-start(bf16[256,256]{1,0:T(8,128)(2,1)S(1)} %get-tuple-element.65), channel_id=1, source_target_pairs={{0,1},{1,2},{2,3},{3,0},{4,5},{5,6},{6,7},{7,4},{8,9},{9,10},{10,1... | collective-permute-start | bytes 393224 | tf_op jit(solution)/shard_map/ppermute | solution.py:37
  3.7 6.2 %collective-permute-start.1 = (bf16[256,256]{1,0:T(8,128)(2,1)S(1)}, bf16[256,256]{1,0:T(8,128)(2,1)S(1)}, u32[]{:S(2)}, u32[]{:S(2)}) collective-permute-start(bf16[256,256]{1,0:T(8,128)(2,1)S(1)} %get-tuple-element.66), channel_id=1, source_target_pairs={{0,2},{1,3},{2,0},{3,1},{4,6},{5,7},{6,4},{7,5},{8,10},{9,11},{10,... | collective-permute-start | bytes 393224 | tf_op jit(solution)/shard_map/ppermute | solution.py:37
  3.9 6.6 %collective-permute-start.2 = (bf16[256,256]{1,0:T(8,128)(2,1)S(1)}, bf16[256,256]{1,0:T(8,128)(2,1)S(1)}, u32[]{:S(2)}, u32[]{:S(2)}) collective-permute-start(bf16[256,256]{1,0:T(8,128)(2,1)S(1)} %get-tuple-element.67), channel_id=1, source_target_pairs={{0,3},{1,0},{2,1},{3,2},{4,7},{5,4},{6,5},{7,6},{8,11},{9,8},{10,9... | collective-permute-start | bytes 393224 | tf_op jit(solution)/shard_map/ppermute | solution.py:37
  4.1 20.7 %collective-permute-start.6 = (bf16[4,128,256]{2,1,0:T(8,128)(2,1)S(1)}, bf16[4,128,256]{2,1,0:T(8,128)(2,1)S(1)}, u32[]{:S(2)}, u32[]{:S(2)}) collective-permute-start(bf16[4,128,256]{2,1,0:T(8,128)(2,1)S(1)} %get-tuple-element.86), channel_id=1, source_target_pairs={{0,1},{1,2},{2,3},{4,5},{5,6},{6,7},{8,9},{9,10},{10,11},{12,13},{... | collective-permute-start | bytes 786440 | tf_op jit(solution)/shard_map/ppermute | solution.py:32
  10.9 7.3 %collective-permute-start.3 = (bf16[128,256]{1,0:T(8,128)(2,1)S(1)}, bf16[128,256]{1,0:T(8,128)(2,1)S(1)}, u32[]{:S(2)}, u32[]{:S(2)}) collective-permute-start(bf16[128,256]{1,0:T(8,128)(2,1)S(1)} %get-tuple-element.75), channel_id=1, source_target_pairs={{0,12},{4,16},{8,20},{12,24},{16,28},{20,0},{24,4},{28,8},{1,13},{... | collective-permute-start | bytes 196616 | tf_op jit(solution)/shard_map/ppermute | solution.py:37
  13.2 4.9 %collective-permute-start.4 = (bf16[128,256]{1,0:T(8,128)(2,1)S(1)}, bf16[128,256]{1,0:T(8,128)(2,1)S(1)}, u32[]{:S(2)}, u32[]{:S(2)}) collective-permute-start(bf16[128,256]{1,0:T(8,128)(2,1)S(1)} %get-tuple-element.76), channel_id=1, source_target_pairs={{0,8},{4,12},{8,16},{12,20},{16,24},{20,28},{24,0},{28,4},{1,9},{5... | collective-permute-start | bytes 196616 | tf_op jit(solution)/shard_map/ppermute | solution.py:37
  14.5 3.7 %collective-permute-start.5 = (bf16[128,256]{1,0:T(8,128)(2,1)S(1)}, bf16[128,256]{1,0:T(8,128)(2,1)S(1)}, u32[]{:S(2)}, u32[]{:S(2)}) collective-permute-start(bf16[128,256]{1,0:T(8,128)(2,1)S(1)} %get-tuple-element.77), channel_id=1, source_target_pairs={{0,4},{4,8},{8,12},{12,16},{16,20},{20,24},{24,28},{28,0},{1,5},{5... | collective-permute-start | bytes 196616 | tf_op jit(solution)/shard_map/ppermute | solution.py:37
  18.4 6.5 %collective-permute-start.9 = (bf16[128,256]{1,0:T(8,128)(2,1)S(1)}, bf16[128,256]{1,0:T(8,128)(2,1)S(1)}, u32[]{:S(2)}, u32[]{:S(2)}) collective-permute-start(bf16[128,256]{1,0:T(8,128)(2,1)S(1)} %arrive.1.refs_7_), channel_id=1, source_target_pairs={{0,2},{1,3},{2,0},{3,1},{4,6},{5,7},{6,4},{7,5},{8,10},{9,11},{10,... | collective-permute-start | bytes 196616 | tf_op jit(solution)/shard_map/ppermute | solution.py:37
  21.1 4.5 %collective-permute-start.8 = (bf16[128,256]{1,0:T(8,128)(2,1)S(1)}, bf16[128,256]{1,0:T(8,128)(2,1)S(1)}, u32[]{:S(2)}, u32[]{:S(2)}) collective-permute-start(bf16[128,256]{1,0:T(8,128)(2,1)S(1)} %arrive.1.refs_7_), channel_id=1, source_target_pairs={{0,3},{1,0},{2,1},{3,2},{4,7},{5,4},{6,5},{7,6},{8,11},{9,8},{10,9... | collective-permute-start | bytes 196616 | tf_op jit(solution)/shard_map/ppermute | solution.py:37
  21.1 12.4 %collective-permute-start.7 = (bf16[128,256]{1,0:T(8,128)(2,1)S(1)}, bf16[128,256]{1,0:T(8,128)(2,1)S(1)}, u32[]{:S(2)}, u32[]{:S(2)}) collective-permute-start(bf16[128,256]{1,0:T(8,128)(2,1)S(1)} %arrive.1.refs_7_), channel_id=1, source_target_pairs={{0,1},{1,2},{2,3},{3,0},{4,5},{5,6},{6,7},{7,4},{8,9},{9,10},{10,1... | collective-permute-start | bytes 196616 | tf_op jit(solution)/shard_map/ppermute | solution.py:37
  29.4 9.6 %collective-permute-start.10 = (bf16[128,256]{1,0:T(8,128)(2,1)S(1)}, bf16[128,256]{1,0:T(8,128)(2,1)S(1)}, u32[]{:S(2)}, u32[]{:S(2)}) collective-permute-start(bf16[128,256]{1,0:T(8,128)(2,1)S(1)} %get-tuple-element.102), channel_id=1, source_target_pairs={{0,1},{1,2},{2,3},{3,0},{4,5},{5,6},{6,7},{7,4},{8,9},{9,10},{10,1... | collective-permute-start | bytes 196616 | tf_op jit(solution)/shard_map/ppermute | solution.py:37
  33.2 5.9 %collective-permute-start.11 = (bf16[128,256]{1,0:T(8,128)(2,1)S(1)}, bf16[128,256]{1,0:T(8,128)(2,1)S(1)}, u32[]{:S(2)}, u32[]{:S(2)}) collective-permute-start(bf16[128,256]{1,0:T(8,128)(2,1)S(1)} %get-tuple-element.103), channel_id=1, source_target_pairs={{0,2},{1,3},{2,0},{3,1},{4,6},{5,7},{6,4},{7,5},{8,10},{9,11},{10,... | collective-permute-start | bytes 196616 | tf_op jit(solution)/shard_map/ppermute | solution.py:37
  35.5 3.8 %collective-permute-start.12 = (bf16[128,256]{1,0:T(8,128)(2,1)S(1)}, bf16[128,256]{1,0:T(8,128)(2,1)S(1)}, u32[]{:S(2)}, u32[]{:S(2)}) collective-permute-start(bf16[128,256]{1,0:T(8,128)(2,1)S(1)} %get-tuple-element.104), channel_id=1, source_target_pairs={{0,3},{1,0},{2,1},{3,2},{4,7},{5,4},{6,5},{7,6},{8,11},{9,8},{10,9... | collective-permute-start | bytes 196616 | tf_op jit(solution)/shard_map/ppermute | solution.py:37
  37.1 18.0 %collective-permute-start.16 = (bf16[4,128,256]{2,1,0:T(8,128)(2,1)S(1)}, bf16[4,128,256]{2,1,0:T(8,128)(2,1)S(1)}, u32[]{:S(2)}, u32[]{:S(2)}) collective-permute-start(bf16[4,128,256]{2,1,0:T(8,128)(2,1)S(1)} %get-tuple-element.113), channel_id=1, source_target_pairs={{1,0},{2,1},{3,2},{5,4},{6,5},{7,6},{9,8},{10,9},{11,10},{13,12},{... | collective-permute-start | bytes 786440 | tf_op jit(solution)/shard_map/ppermute | solution.py:32
  39.5 7.3 %collective-permute-start.15 = (bf16[128,256]{1,0:T(8,128)(2,1)S(1)}, bf16[128,256]{1,0:T(8,128)(2,1)S(1)}, u32[]{:S(2)}, u32[]{:S(2)}) collective-permute-start(bf16[128,256]{1,0:T(8,128)(2,1)S(1)} %gather.3.here_ref), channel_id=1, source_target_pairs={{0,20},{4,24},{8,28},{12,0},{16,4},{20,8},{24,12},{28,16},{1,21},{... | collective-permute-start | bytes 196616 | tf_op jit(solution)/shard_map/ppermute | solution.py:37
  43.5 3.5 %collective-permute-start.14 = (bf16[128,256]{1,0:T(8,128)(2,1)S(1)}, bf16[128,256]{1,0:T(8,128)(2,1)S(1)}, u32[]{:S(2)}, u32[]{:S(2)}) collective-permute-start(bf16[128,256]{1,0:T(8,128)(2,1)S(1)} %gather.3.here_ref), channel_id=1, source_target_pairs={{0,24},{4,28},{8,0},{12,4},{16,8},{20,12},{24,16},{28,20},{1,25},{... | collective-permute-start | bytes 196616 | tf_op jit(solution)/shard_map/ppermute | solution.py:37
  44.9 4.3 %collective-permute-start.13 = (bf16[128,256]{1,0:T(8,128)(2,1)S(1)}, bf16[128,256]{1,0:T(8,128)(2,1)S(1)}, u32[]{:S(2)}, u32[]{:S(2)}) collective-permute-start(bf16[128,256]{1,0:T(8,128)(2,1)S(1)} %gather.3.here_ref), channel_id=1, source_target_pairs={{0,28},{4,0},{8,4},{12,8},{16,12},{20,16},{24,20},{28,24},{1,29},{... | collective-permute-start | bytes 196616 | tf_op jit(solution)/shard_map/ppermute | solution.py:37
  49.6 5.5 %collective-permute-start.18 = (bf16[256,256]{1,0:T(8,128)(2,1)S(1)}, bf16[256,256]{1,0:T(8,128)(2,1)S(1)}, u32[]{:S(2)}, u32[]{:S(2)}) collective-permute-start(bf16[256,256]{1,0:T(8,128)(2,1)S(1)} %get-tuple-element.117), channel_id=1, source_target_pairs={{0,1},{1,2},{2,3},{3,0},{4,5},{5,6},{6,7},{7,4},{8,9},{9,10},{10,1... | collective-permute-start | bytes 393224 | tf_op jit(solution)/shard_map/ppermute | solution.py:37
  51.3 6.0 %collective-permute-start.19 = (bf16[256,256]{1,0:T(8,128)(2,1)S(1)}, bf16[256,256]{1,0:T(8,128)(2,1)S(1)}, u32[]{:S(2)}, u32[]{:S(2)}) collective-permute-start(bf16[256,256]{1,0:T(8,128)(2,1)S(1)} %get-tuple-element.118), channel_id=1, source_target_pairs={{0,2},{1,3},{2,0},{3,1},{4,6},{5,7},{6,4},{7,5},{8,10},{9,11},{10,... | collective-permute-start | bytes 393224 | tf_op jit(solution)/shard_map/ppermute | solution.py:37
  51.4 6.6 %collective-permute-start.20 = (bf16[256,256]{1,0:T(8,128)(2,1)S(1)}, bf16[256,256]{1,0:T(8,128)(2,1)S(1)}, u32[]{:S(2)}, u32[]{:S(2)}) collective-permute-start(bf16[256,256]{1,0:T(8,128)(2,1)S(1)} %get-tuple-element.119), channel_id=1, source_target_pairs={{0,3},{1,0},{2,1},{3,2},{4,7},{5,4},{6,5},{7,6},{8,11},{9,8},{10,9... | collective-permute-start | bytes 393224 | tf_op jit(solution)/shard_map/ppermute | solution.py:37
  51.8 3.4 %collective-permute-start.17 = (f32[8,128]{1,0:T(8,128)S(1)}, f32[8,128]{1,0:T(8,128)S(1)}, u32[]{:S(2)}, u32[]{:S(2)}) collective-permute-start(f32[8,128]{1,0:T(8,128)S(1)} %get-tuple-element.111.sink_ref), channel_id=1, source_target_pairs={{0,16},{4,20},{8,24},{12,28},{16,0},{20,4},{24,8},{28,12},{1,17},{... | collective-permute-start | bytes 12296 | tf_op jit(solution)/shard_map/ppermute | solution.py:37

commit v9 on v8

--- a/solution.py
+++ b/solution.py
@@ -332,28 +332,33 @@
         def stacked(ref, unit, half):
             return jnp.concatenate([ref[corner] for corner in corners(unit, half)], axis=0)
 
-        def products(index):
+        def product(padded, ref, index):
             unit, half = items[index]
-            score, dp = (
-                lax.dot_general(
-                    padded[half][unit],
-                    stacked(ref, unit, half),
-                    turn,
-                    preferred_element_type=F32,
-                )
-                for padded, ref in ((padded_k, q_ref), (padded_v, g_ref))
+            return lax.dot_general(
+                padded[half][unit], stacked(ref, unit, half), turn, preferred_element_type=F32
             )
-            parts = []
-            for base in (0, seen):
-                near, far = slice(base, base + HALF), slice(base + HALF, base + 2 * HALF)
-                rest = slice(base + 2 * HALF, base + 3 * HALF)
+
+        def parts_of(odd):
+            base = odd * seen
+            return (
+                slice(base, base + HALF),
+                slice(base + HALF, base + 2 * HALF),
+                slice(base + 2 * HALF, base + seen),
+            )
+
+        def scores(index):
+            half = items[index][1]
+            score = product(padded_k, q_ref, index)
+            pairs = []
+            for near, far, rest in (parts_of(0), parts_of(1)):
                 edge = jnp.where(own, score[near], score[far] + bias)
-                whole = score[rest] + bias if half == 0 else score[rest]
-                parts.append((edge, whole, jnp.where(own, dp[near], dp[far]), dp[rest]))
-            return parts
-
-        def weigh(index, odd, edge, whole, dp_edge, dp_whole):
-            unit, half = items[index]
+                pairs.append((edge, score[rest] + bias if half == 0 else score[rest]))
+            return pairs
+
+        def weigh(index, odd, edge, whole, dp):
+            near, far, rest = parts_of(odd)
+            dp_edge, dp_whole = jnp.where(own, dp[near], dp[far]), dp[rest]
+            unit = items[index][0]
             base = odd * seen
             row = unit * GROUP + odd
             sink = jnp.concatenate(
@@ -423,13 +428,13 @@
             )
             return total + pltpu.roll(total, HEAD_DIM, 1)
 
-        ahead, parts = products(0), []
+        ahead, parts = scores(0), []
         for index in range(len(items)):
-            now = ahead
-            weigh(index, 0, *now[0])
+            now, dp = ahead, product(padded_v, g_ref, index)
+            weigh(index, 0, *now[0], dp)
             if index + 1 < len(items):
-                ahead = products(index + 1)
-            weigh(index, 1, *now[1])
+                ahead = scores(index + 1)
+            weigh(index, 1, *now[1], dp)
             if index >= 1:
                 finish(index - 1)
             parts.append(reduce(index))

time: 59.1 us -> 60.5 us (1.024); the launches traced: 58.9 us -> 59.3 us
  Pallas kernels: 16.9 us -> 24.2 us
  starting transfers between devices: 30.6 us -> 24.2 us
    pallas_call x3, Pallas kernels: 7.72 us -> 15 us  [attend(): pl.pallas_call(functools.partial(attend_kernel, blocks_here, head_count,...]
    ppermute x19, starting transfers between devices: 25.3 us -> 18.9 us  [ring(): lax.ppermute(value, axis, [(source, (source + steps) % count) for source...]
  transfers between devices with their start and end apart: 21 -> 21, of which waited for: 11 -> 9; matrix products, arithmetic and copies ran while one was open for 0% -> 0% of each run, Pallas kernels for 25% -> 37%
where the time goes in v9:
time: 60.5 us; the launch traced here: 59.3 us
  Pallas kernels  24.2 us (40%)
  starting transfers between devices  24.2 us (40%)
  waiting for transfers between devices  10.1 us (17%)
  between operations  0.78 us (1%)
    ppermute x19, starting transfers between devices, ring(): lax.ppermute(value, axis, [(source, (source + steps) % count) for source...  18.9 us
    pallas_call x3, Pallas kernels, attend(): pl.pallas_call(functools.partial(attend_kernel, blocks_here, head_count,...  15 us
    ppermute x19, waiting for transfers between devices, ring(): lax.ppermute(value, axis, [(source, (source + steps) % count) for source...  10.1 us
    ppermute x2, starting transfers between devices, shift(): lax.ppermute(value, axis, [(source, source + steps) for source in range(l...  5.31 us
    pallas_call x2, Pallas kernels, flush(): pl.pallas_call(stage_kernel, out_shape=pltpu.HBM(value.shape, BF16), in_s...  2.65 us
    pallas_call x1, Pallas kernels, local(): pl.pallas_call(stage_kernel, out_shape=(pltpu.VMEM(queries.shape, BF16),)...  2.26 us
  transfers between devices with their start and end apart: 21, of which 9 were waited for; matrix products, arithmetic and copies ran while one was open for 0% of the time, Pallas kernels for 37%

profile of v9, /device:TPU:3, one launch (start us, length us, event | category | flops | bytes accessed | tf_op | source)
XLA Modules:
  0.0 59.3 jit_solution(10862117383775666613)
XLA Ops:
  0.6 1.2 %pack.1 = (bf16[256,256]{1,0:T(8,128)(2,1)S(1)}, bf16[256,256]{1,0:T(8,128)(2,1)S(1)}, bf16[256,256]{1,0:T(8,128)(2,1)S(1)}, bf16[256,256]{1,0:T(8,128)(2,1)S(1)...) custom-call(f32[16]{0:T(128)} %sink_hbm.1, ...), custom_call_target="tpu_custom_call" | custom-call | tf_op jit(solution)/shard_map/pack/pallas_call | solution.py:566
  1.8 1.9 %collective-permute-start = (bf16[256,256]{1,0:T(8,128)(2,1)S(1)}, bf16[256,256]{1,0:T(8,128)(2,1)S(1)}, u32[]{:S(2)}, u32[]{:S(2)}) collective-permute-start(bf16[256,256]{1,0:T(8,128)(2,1)S(1)} %get-tuple-element.65), channel_id=1, source_target_pairs={{0,1},{1,2},{2,3},{3,0},{4,5},{5,6},{6,7},{7,4},{8,9},{9,10},{10,1... | collective-permute-start | bytes 393224 | tf_op jit(solution)/shard_map/ppermute | solution.py:37
  4.1 3.4 %collective-permute-start.6 = (bf16[4,128,256]{2,1,0:T(8,128)(2,1)S(1)}, bf16[4,128,256]{2,1,0:T(8,128)(2,1)S(1)}, u32[]{:S(2)}, u32[]{:S(2)}) collective-permute-start(bf16[4,128,256]{2,1,0:T(8,128)(2,1)S(1)} %get-tuple-element.86), channel_id=1, source_target_pairs={{0,1},{1,2},{2,3},{4,5},{5,6},{6,7},{8,9},{9,10},{10,11},{12,13},{... | collective-permute-start | bytes 786440 | tf_op jit(solution)/shard_map/ppermute | solution.py:32
  8.3 1.5 %collective-permute-done.1.refs_2_ = bf16[256,256]{1,0:T(8,128)(2,1)S(1)} collective-permute-done((bf16[256,256]{1,0:T(8,128)(2,1)S(1)}, bf16[256,256]{1,0:T(8,128)(2,1)S(1)}, u32[]{:S(2)}, u32[]{:S(2)}) %collective-permute-start.1) | collective-permute-done | bytes 131104 | tf_op jit(solution)/shard_map/ppermute | solution.py:37
  10.9 2.3 %collective-permute-start.3 = (bf16[128,256]{1,0:T(8,128)(2,1)S(1)}, bf16[128,256]{1,0:T(8,128)(2,1)S(1)}, u32[]{:S(2)}, u32[]{:S(2)}) collective-permute-start(bf16[128,256]{1,0:T(8,128)(2,1)S(1)} %get-tuple-element.75), channel_id=1, source_target_pairs={{0,12},{4,16},{8,20},{12,24},{16,28},{20,0},{24,4},{28,8},{1,13},{... | collective-permute-start | bytes 196616 | tf_op jit(solution)/shard_map/ppermute | solution.py:37
  13.2 1.3 %collective-permute-start.4 = (bf16[128,256]{1,0:T(8,128)(2,1)S(1)}, bf16[128,256]{1,0:T(8,128)(2,1)S(1)}, u32[]{:S(2)}, u32[]{:S(2)}) collective-permute-start(bf16[128,256]{1,0:T(8,128)(2,1)S(1)} %get-tuple-element.76), channel_id=1, source_target_pairs={{0,8},{4,12},{8,16},{12,20},{16,24},{20,28},{24,0},{28,4},{1,9},{5... | collective-permute-start | bytes 196616 | tf_op jit(solution)/shard_map/ppermute | solution.py:37
  14.5 1.2 %collective-permute-start.5 = (bf16[128,256]{1,0:T(8,128)(2,1)S(1)}, bf16[128,256]{1,0:T(8,128)(2,1)S(1)}, u32[]{:S(2)}, u32[]{:S(2)}) collective-permute-start(bf16[128,256]{1,0:T(8,128)(2,1)S(1)} %get-tuple-element.77), channel_id=1, source_target_pairs={{0,4},{4,8},{8,12},{12,16},{16,20},{20,24},{24,28},{28,0},{1,5},{5... | collective-permute-start | bytes 196616 | tf_op jit(solution)/shard_map/ppermute | solution.py:37
  15.9 2.3 %stage.1 = (bf16[256,4096]{1,0:T(8,128)(2,1)S(1)}, bf16[256,4096]{1,0:T(8,128)(2,1)S(1)}) custom-call(bf16[256,4096]{1,0:T(8,128)(2,1)} %refs_0_, bf16[256,4096]{1,0:T(8,128)(2,1)} %refs_1_), custom_call_target="tpu_custom_call" | custom-call | tf_op jit(solution)/shard_map/stage/pallas_call | solution.py:611
  18.4 2.8 %collective-permute-start.9 = (bf16[128,256]{1,0:T(8,128)(2,1)S(1)}, bf16[128,256]{1,0:T(8,128)(2,1)S(1)}, u32[]{:S(2)}, u32[]{:S(2)}) collective-permute-start(bf16[128,256]{1,0:T(8,128)(2,1)S(1)} %arrive.1.refs_7_), channel_id=1, source_target_pairs={{0,2},{1,3},{2,0},{3,1},{4,6},{5,7},{6,4},{7,5},{8,10},{9,11},{10,... | collective-permute-start | bytes 196616 | tf_op jit(solution)/shard_map/ppermute | solution.py:37
  21.1 1.7 %collective-permute-start.7 = (bf16[128,256]{1,0:T(8,128)(2,1)S(1)}, bf16[128,256]{1,0:T(8,128)(2,1)S(1)}, u32[]{:S(2)}, u32[]{:S(2)}) collective-permute-start(bf16[128,256]{1,0:T(8,128)(2,1)S(1)} %arrive.1.refs_7_), channel_id=1, source_target_pairs={{0,1},{1,2},{2,3},{3,0},{4,5},{5,6},{6,7},{7,4},{8,9},{9,10},{10,1... | collective-permute-start | bytes 196616 | tf_op jit(solution)/shard_map/ppermute | solution.py:37
  22.8 3.8 %attend.3 = (bf16[256,4096]{1,0:T(8,128)(2,1)S(1)}, bf16[256,4096]{1,0:T(8,128)(2,1)S(1)}, f32[256,512]{1,0:T(8,128)S(1)}, f32[256,512]{1,0:T(8,128)S(1)}, bf16[...) custom-call(s32[8,128]{1,0:T(8,128)S(1)} %plan.1.plan_ref.refs_0_, f32[64,128]{1,0:T(8,128)S(1)} %sinks.1.refs_1_, ...), custom_call_target="tpu_custom_call" | custom-call | tf_op jit(solution)/shard_map/attend/pallas_call | solution.py:645
  26.6 7.5 %attend.4 = (bf16[256,4096]{1,0:T(8,128)(2,1)S(1)}, bf16[256,4096]{1,0:T(8,128)(2,1)S(1)}, f32[256,512]{1,0:T(8,128)S(1)}, f32[256,512]{1,0:T(8,128)S(1)}, bf16[...) custom-call(s32[8,128]{1,0:T(8,128)S(1)} %plan.1.plan_ref.refs_0_, ...), custom_call_target="tpu_custom_call", output_to_operand_aliasing={{0}: (9, {}), {1}: (10, {}), {2}: (11, {}), {3}: (12, {}), ... | custom-call | tf_op jit(solution)/shard_map/attend/pallas_call | solution.py:645
  34.3 3.8 %attend.5 = (bf16[256,4096]{1,0:T(8,128)(2,1)S(1)}, bf16[256,4096]{1,0:T(8,128)(2,1)S(1)}, f32[256,512]{1,0:T(8,128)S(1)}, f32[256,512]{1,0:T(8,128)S(1)}, bf16[...) custom-call(s32[8,128]{1,0:T(8,128)S(1)} %plan.1.plan_ref.refs_0_, ...), custom_call_target="tpu_custom_call", output_to_operand_aliasing={{0}: (8, {}), {1}: (9, {}), {2}: (10, {}), {3}: (11, {}), {... | custom-call | tf_op jit(solution)/shard_map/attend/pallas_call | solution.py:645
  38.5 1.9 %collective-permute-start.16 = (bf16[4,128,256]{2,1,0:T(8,128)(2,1)S(1)}, bf16[4,128,256]{2,1,0:T(8,128)(2,1)S(1)}, u32[]{:S(2)}, u32[]{:S(2)}) collective-permute-start(bf16[4,128,256]{2,1,0:T(8,128)(2,1)S(1)} %get-tuple-element.113), channel_id=1, source_target_pairs={{1,0},{2,1},{3,2},{5,4},{6,5},{7,6},{9,8},{10,9},{11,10},{13,12},{... | collective-permute-start | bytes 786440 | tf_op jit(solution)/shard_map/ppermute | solution.py:32
  40.6 1.4 %collective-permute-done.12.refs_1_ = bf16[128,256]{1,0:T(8,128)(2,1)S(1)} collective-permute-done((bf16[128,256]{1,0:T(8,128)(2,1)S(1)}, bf16[128,256]{1,0:T(8,128)(2,1)S(1)}, u32[]{:S(2)}, u32[]{:S(2)}) %collective-permute-start.12) | collective-permute-done | bytes 65568 | tf_op jit(solution)/shard_map/ppermute | solution.py:37
  42.2 2.5 %collective-permute-start.15 = (bf16[128,256]{1,0:T(8,128)(2,1)S(1)}, bf16[128,256]{1,0:T(8,128)(2,1)S(1)}, u32[]{:S(2)}, u32[]{:S(2)}) collective-permute-start(bf16[128,256]{1,0:T(8,128)(2,1)S(1)} %gather.3.here_ref), channel_id=1, source_target_pairs={{0,20},{4,24},{8,28},{12,0},{16,4},{20,8},{24,12},{28,16},{1,21},{... | collective-permute-start | bytes 196616 | tf_op jit(solution)/shard_map/ppermute | solution.py:37
  45.2 1.3 %flush.2 = bf16[256,4096]{1,0:T(8,128)(2,1)} custom-call(bf16[256,4096]{1,0:T(8,128)(2,1)S(1)} %get-tuple-element.105.refs_0_), custom_call_target="tpu_custom_call" | custom-call | tf_op jit(solution)/shard_map/flush/pallas_call | solution.py:701
  46.5 1.6 %collective-permute-done.15.refs_2_ = bf16[128,256]{1,0:T(8,128)(2,1)S(1)} collective-permute-done((bf16[128,256]{1,0:T(8,128)(2,1)S(1)}, bf16[128,256]{1,0:T(8,128)(2,1)S(1)}, u32[]{:S(2)}, u32[]{:S(2)}) %collective-permute-start.15) | collective-permute-done | bytes 65568 | tf_op jit(solution)/shard_map/ppermute | solution.py:37
  48.2 1.4 %collective-permute-done.13.refs_0_ = bf16[128,256]{1,0:T(8,128)(2,1)S(1)} collective-permute-done((bf16[128,256]{1,0:T(8,128)(2,1)S(1)}, bf16[128,256]{1,0:T(8,128)(2,1)S(1)}, u32[]{:S(2)}, u32[]{:S(2)}) %collective-permute-start.13) | collective-permute-done | bytes 65568 | tf_op jit(solution)/shard_map/ppermute | solution.py:37
  50.0 2.0 %collective-permute-start.18 = (bf16[256,256]{1,0:T(8,128)(2,1)S(1)}, bf16[256,256]{1,0:T(8,128)(2,1)S(1)}, u32[]{:S(2)}, u32[]{:S(2)}) collective-permute-start(bf16[256,256]{1,0:T(8,128)(2,1)S(1)} %get-tuple-element.117), channel_id=1, source_target_pairs={{0,1},{1,2},{2,3},{3,0},{4,5},{5,6},{6,7},{7,4},{8,9},{9,10},{10,1... | collective-permute-start | bytes 393224 | tf_op jit(solution)/shard_map/ppermute | solution.py:37
  52.5 1.1 %collective-permute-start.17 = (f32[8,128]{1,0:T(8,128)S(1)}, f32[8,128]{1,0:T(8,128)S(1)}, u32[]{:S(2)}, u32[]{:S(2)}) collective-permute-start(f32[8,128]{1,0:T(8,128)S(1)} %get-tuple-element.111.sink_ref), channel_id=1, source_target_pairs={{0,16},{4,20},{8,24},{12,28},{16,0},{20,4},{24,8},{28,12},{1,17},{... | collective-permute-start | bytes 12296 | tf_op jit(solution)/shard_map/ppermute | solution.py:37
  53.6 1.3 %flush.3 = bf16[256,4096]{1,0:T(8,128)(2,1)} custom-call(bf16[256,4096]{1,0:T(8,128)(2,1)S(1)} %get-tuple-element.112.refs_0_), custom_call_target="tpu_custom_call" | custom-call | tf_op jit(solution)/shard_map/flush/pallas_call | solution.py:701
  55.8 2.1 %collective-permute-done.19.refs_2_ = bf16[256,256]{1,0:T(8,128)(2,1)S(1)} collective-permute-done((bf16[256,256]{1,0:T(8,128)(2,1)S(1)}, bf16[256,256]{1,0:T(8,128)(2,1)S(1)}, u32[]{:S(2)}, u32[]{:S(2)}) %collective-permute-start.19) | collective-permute-done | bytes 131104 | tf_op jit(solution)/shard_map/ppermute | solution.py:37
  58.3 0.9 %total.1 = (bf16[256,512]{1,0:T(8,128)(2,1)}, bf16[256,512]{1,0:T(8,128)(2,1)}, f32[16]{0:T(128)}) custom-call(bf16[4,128,256]{2,1,0:T(8,128)(2,1)S(1)} %collective-permute-done.16.halo_ref, f32[256,512]{1,0:T(8,128)S(1)} %get-tuple-element.114.dk_ref, f32[256,512]{1,0:T(8,128)S(1)} %get-tuple-element.115.dv_ref, f32[8,128]{1,0:T(8,128)S(1)} %get-tuple-element.111.sink_ref, ...), custom_call_target="tpu_custom_call" | custom-call | tf_op jit(solution)/shard_map/total/pallas_call | solution.py:732
  (33 shorter events, 6.2 us)
Async XLA Ops:
  1.8 6.5 %collective-permute-start = (bf16[256,256]{1,0:T(8,128)(2,1)S(1)}, bf16[256,256]{1,0:T(8,128)(2,1)S(1)}, u32[]{:S(2)}, u32[]{:S(2)}) collective-permute-start(bf16[256,256]{1,0:T(8,128)(2,1)S(1)} %get-tuple-element.65), channel_id=1, source_target_pairs={{0,1},{1,2},{2,3},{3,0},{4,5},{5,6},{6,7},{7,4},{8,9},{9,10},{10,1... | collective-permute-start | bytes 393224 | tf_op jit(solution)/shard_map/ppermute | solution.py:37
  3.7 6.2 %collective-permute-start.1 = (bf16[256,256]{1,0:T(8,128)(2,1)S(1)}, bf16[256,256]{1,0:T(8,128)(2,1)S(1)}, u32[]{:S(2)}, u32[]{:S(2)}) collective-permute-start(bf16[256,256]{1,0:T(8,128)(2,1)S(1)} %get-tuple-element.66), channel_id=1, source_target_pairs={{0,2},{1,3},{2,0},{3,1},{4,6},{5,7},{6,4},{7,5},{8,10},{9,11},{10,... | collective-permute-start | bytes 393224 | tf_op jit(solution)/shard_map/ppermute | solution.py:37
  3.9 6.6 %collective-permute-start.2 = (bf16[256,256]{1,0:T(8,128)(2,1)S(1)}, bf16[256,256]{1,0:T(8,128)(2,1)S(1)}, u32[]{:S(2)}, u32[]{:S(2)}) collective-permute-start(bf16[256,256]{1,0:T(8,128)(2,1)S(1)} %get-tuple-element.67), channel_id=1, source_target_pairs={{0,3},{1,0},{2,1},{3,2},{4,7},{5,4},{6,5},{7,6},{8,11},{9,8},{10,9... | collective-permute-start | bytes 393224 | tf_op jit(solution)/shard_map/ppermute | solution.py:37
  4.1 22.5 %collective-permute-start.6 = (bf16[4,128,256]{2,1,0:T(8,128)(2,1)S(1)}, bf16[4,128,256]{2,1,0:T(8,128)(2,1)S(1)}, u32[]{:S(2)}, u32[]{:S(2)}) collective-permute-start(bf16[4,128,256]{2,1,0:T(8,128)(2,1)S(1)} %get-tuple-element.86), channel_id=1, source_target_pairs={{0,1},{1,2},{2,3},{4,5},{5,6},{6,7},{8,9},{9,10},{10,11},{12,13},{... | collective-permute-start | bytes 786440 | tf_op jit(solution)/shard_map/ppermute | solution.py:32
  10.9 7.3 %collective-permute-start.3 = (bf16[128,256]{1,0:T(8,128)(2,1)S(1)}, bf16[128,256]{1,0:T(8,128)(2,1)S(1)}, u32[]{:S(2)}, u32[]{:S(2)}) collective-permute-start(bf16[128,256]{1,0:T(8,128)(2,1)S(1)} %get-tuple-element.75), channel_id=1, source_target_pairs={{0,12},{4,16},{8,20},{12,24},{16,28},{20,0},{24,4},{28,8},{1,13},{... | collective-permute-start | bytes 196616 | tf_op jit(solution)/shard_map/ppermute | solution.py:37
  13.2 4.9 %collective-permute-start.4 = (bf16[128,256]{1,0:T(8,128)(2,1)S(1)}, bf16[128,256]{1,0:T(8,128)(2,1)S(1)}, u32[]{:S(2)}, u32[]{:S(2)}) collective-permute-start(bf16[128,256]{1,0:T(8,128)(2,1)S(1)} %get-tuple-element.76), channel_id=1, source_target_pairs={{0,8},{4,12},{8,16},{12,20},{16,24},{20,28},{24,0},{28,4},{1,9},{5... | collective-permute-start | bytes 196616 | tf_op jit(solution)/shard_map/ppermute | solution.py:37
  14.5 3.7 %collective-permute-start.5 = (bf16[128,256]{1,0:T(8,128)(2,1)S(1)}, bf16[128,256]{1,0:T(8,128)(2,1)S(1)}, u32[]{:S(2)}, u32[]{:S(2)}) collective-permute-start(bf16[128,256]{1,0:T(8,128)(2,1)S(1)} %get-tuple-element.77), channel_id=1, source_target_pairs={{0,4},{4,8},{8,12},{12,16},{16,20},{20,24},{24,28},{28,0},{1,5},{5... | collective-permute-start | bytes 196616 | tf_op jit(solution)/shard_map/ppermute | solution.py:37
  18.4 8.3 %collective-permute-start.9 = (bf16[128,256]{1,0:T(8,128)(2,1)S(1)}, bf16[128,256]{1,0:T(8,128)(2,1)S(1)}, u32[]{:S(2)}, u32[]{:S(2)}) collective-permute-start(bf16[128,256]{1,0:T(8,128)(2,1)S(1)} %arrive.1.refs_7_), channel_id=1, source_target_pairs={{0,2},{1,3},{2,0},{3,1},{4,6},{5,7},{6,4},{7,5},{8,10},{9,11},{10,... | collective-permute-start | bytes 196616 | tf_op jit(solution)/shard_map/ppermute | solution.py:37
  21.1 5.5 %collective-permute-start.8 = (bf16[128,256]{1,0:T(8,128)(2,1)S(1)}, bf16[128,256]{1,0:T(8,128)(2,1)S(1)}, u32[]{:S(2)}, u32[]{:S(2)}) collective-permute-start(bf16[128,256]{1,0:T(8,128)(2,1)S(1)} %arrive.1.refs_7_), channel_id=1, source_target_pairs={{0,3},{1,0},{2,1},{3,2},{4,7},{5,4},{6,5},{7,6},{8,11},{9,8},{10,9... | collective-permute-start | bytes 196616 | tf_op jit(solution)/shard_map/ppermute | solution.py:37
  21.1 13.2 %collective-permute-start.7 = (bf16[128,256]{1,0:T(8,128)(2,1)S(1)}, bf16[128,256]{1,0:T(8,128)(2,1)S(1)}, u32[]{:S(2)}, u32[]{:S(2)}) collective-permute-start(bf16[128,256]{1,0:T(8,128)(2,1)S(1)} %arrive.1.refs_7_), channel_id=1, source_target_pairs={{0,1},{1,2},{2,3},{3,0},{4,5},{5,6},{6,7},{7,4},{8,9},{9,10},{10,1... | collective-permute-start | bytes 196616 | tf_op jit(solution)/shard_map/ppermute | solution.py:37
  34.1 6.3 %collective-permute-start.10 = (bf16[128,256]{1,0:T(8,128)(2,1)S(1)}, bf16[128,256]{1,0:T(8,128)(2,1)S(1)}, u32[]{:S(2)}, u32[]{:S(2)}) collective-permute-start(bf16[128,256]{1,0:T(8,128)(2,1)S(1)} %get-tuple-element.102), channel_id=1, source_target_pairs={{0,1},{1,2},{2,3},{3,0},{4,5},{5,6},{6,7},{7,4},{8,9},{9,10},{10,1... | collective-permute-start | bytes 196616 | tf_op jit(solution)/shard_map/ppermute | solution.py:37
  34.2 6.2 %collective-permute-start.11 = (bf16[128,256]{1,0:T(8,128)(2,1)S(1)}, bf16[128,256]{1,0:T(8,128)(2,1)S(1)}, u32[]{:S(2)}, u32[]{:S(2)}) collective-permute-start(bf16[128,256]{1,0:T(8,128)(2,1)S(1)} %get-tuple-element.103), channel_id=1, source_target_pairs={{0,2},{1,3},{2,0},{3,1},{4,6},{5,7},{6,4},{7,5},{8,10},{9,11},{10,... | collective-permute-start | bytes 196616 | tf_op jit(solution)/shard_map/ppermute | solution.py:37
  38.0 4.0 %collective-permute-start.12 = (bf16[128,256]{1,0:T(8,128)(2,1)S(1)}, bf16[128,256]{1,0:T(8,128)(2,1)S(1)}, u32[]{:S(2)}, u32[]{:S(2)}) collective-permute-start(bf16[128,256]{1,0:T(8,128)(2,1)S(1)} %get-tuple-element.104), channel_id=1, source_target_pairs={{0,3},{1,0},{2,1},{3,2},{4,7},{5,4},{6,5},{7,6},{8,11},{9,8},{10,9... | collective-permute-start | bytes 196616 | tf_op jit(solution)/shard_map/ppermute | solution.py:37
  38.5 17.3 %collective-permute-start.16 = (bf16[4,128,256]{2,1,0:T(8,128)(2,1)S(1)}, bf16[4,128,256]{2,1,0:T(8,128)(2,1)S(1)}, u32[]{:S(2)}, u32[]{:S(2)}) collective-permute-start(bf16[4,128,256]{2,1,0:T(8,128)(2,1)S(1)} %get-tuple-element.113), channel_id=1, source_target_pairs={{1,0},{2,1},{3,2},{5,4},{6,5},{7,6},{9,8},{10,9},{11,10},{13,12},{... | collective-permute-start | bytes 786440 | tf_op jit(solution)/shard_map/ppermute | solution.py:32
  42.2 6.0 %collective-permute-start.15 = (bf16[128,256]{1,0:T(8,128)(2,1)S(1)}, bf16[128,256]{1,0:T(8,128)(2,1)S(1)}, u32[]{:S(2)}, u32[]{:S(2)}) collective-permute-start(bf16[128,256]{1,0:T(8,128)(2,1)S(1)} %gather.3.here_ref), channel_id=1, source_target_pairs={{0,20},{4,24},{8,28},{12,0},{16,4},{20,8},{24,12},{28,16},{1,21},{... | collective-permute-start | bytes 196616 | tf_op jit(solution)/shard_map/ppermute | solution.py:37
  44.7 3.4 %collective-permute-start.14 = (bf16[128,256]{1,0:T(8,128)(2,1)S(1)}, bf16[128,256]{1,0:T(8,128)(2,1)S(1)}, u32[]{:S(2)}, u32[]{:S(2)}) collective-permute-start(bf16[128,256]{1,0:T(8,128)(2,1)S(1)} %gather.3.here_ref), channel_id=1, source_target_pairs={{0,24},{4,28},{8,0},{12,4},{16,8},{20,12},{24,16},{28,20},{1,25},{... | collective-permute-start | bytes 196616 | tf_op jit(solution)/shard_map/ppermute | solution.py:37
  44.8 4.8 %collective-permute-start.13 = (bf16[128,256]{1,0:T(8,128)(2,1)S(1)}, bf16[128,256]{1,0:T(8,128)(2,1)S(1)}, u32[]{:S(2)}, u32[]{:S(2)}) collective-permute-start(bf16[128,256]{1,0:T(8,128)(2,1)S(1)} %gather.3.here_ref), channel_id=1, source_target_pairs={{0,28},{4,0},{8,4},{12,8},{16,12},{20,16},{24,20},{28,24},{1,29},{... | collective-permute-start | bytes 196616 | tf_op jit(solution)/shard_map/ppermute | solution.py:37
  50.0 5.9 %collective-permute-start.18 = (bf16[256,256]{1,0:T(8,128)(2,1)S(1)}, bf16[256,256]{1,0:T(8,128)(2,1)S(1)}, u32[]{:S(2)}, u32[]{:S(2)}) collective-permute-start(bf16[256,256]{1,0:T(8,128)(2,1)S(1)} %get-tuple-element.117), channel_id=1, source_target_pairs={{0,1},{1,2},{2,3},{3,0},{4,5},{5,6},{6,7},{7,4},{8,9},{9,10},{10,1... | collective-permute-start | bytes 393224 | tf_op jit(solution)/shard_map/ppermute | solution.py:37
  52.0 6.0 %collective-permute-start.19 = (bf16[256,256]{1,0:T(8,128)(2,1)S(1)}, bf16[256,256]{1,0:T(8,128)(2,1)S(1)}, u32[]{:S(2)}, u32[]{:S(2)}) collective-permute-start(bf16[256,256]{1,0:T(8,128)(2,1)S(1)} %get-tuple-element.118), channel_id=1, source_target_pairs={{0,2},{1,3},{2,0},{3,1},{4,6},{5,7},{6,4},{7,5},{8,10},{9,11},{10,... | collective-permute-start | bytes 393224 | tf_op jit(solution)/shard_map/ppermute | solution.py:37
  52.0 6.3 %collective-permute-start.20 = (bf16[256,256]{1,0:T(8,128)(2,1)S(1)}, bf16[256,256]{1,0:T(8,128)(2,1)S(1)}, u32[]{:S(2)}, u32[]{:S(2)}) collective-permute-start(bf16[256,256]{1,0:T(8,128)(2,1)S(1)} %get-tuple-element.119), channel_id=1, source_target_pairs={{0,3},{1,0},{2,1},{3,2},{4,7},{5,4},{6,5},{7,6},{8,11},{9,8},{10,9... | collective-permute-start | bytes 393224 | tf_op jit(solution)/shard_map/ppermute | solution.py:37
  52.5 3.4 %collective-permute-start.17 = (f32[8,128]{1,0:T(8,128)S(1)}, f32[8,128]{1,0:T(8,128)S(1)}, u32[]{:S(2)}, u32[]{:S(2)}) collective-permute-start(f32[8,128]{1,0:T(8,128)S(1)} %get-tuple-element.111.sink_ref), channel_id=1, source_target_pairs={{0,16},{4,20},{8,24},{12,28},{16,0},{20,4},{24,8},{28,12},{1,17},{... | collective-permute-start | bytes 12296 | tf_op jit(solution)/shard_map/ppermute | solution.py:37

commit v10 on v8

--- a/solution.py
+++ b/solution.py
@@ -423,12 +423,12 @@
             )
             return total + pltpu.roll(total, HEAD_DIM, 1)
 
-        ahead, parts = products(0), []
+        ahead, parts = [products(0), products(1)], []
         for index in range(len(items)):
-            now = ahead
+            now = ahead.pop(0)
             weigh(index, 0, *now[0])
-            if index + 1 < len(items):
-                ahead = products(index + 1)
+            if index + 2 < len(items):
+                ahead.append(products(index + 2))
             weigh(index, 1, *now[1])
             if index >= 1:
                 finish(index - 1)

time: 59.1 us -> 61.3 us (1.037)
  Pallas kernels: 16.9 us -> 24.1 us
  starting transfers between devices: 30.6 us -> 24.1 us
  waiting for transfers between devices: 10.5 us -> 12.5 us
    pallas_call x3, Pallas kernels: 7.72 us -> 14.9 us  [attend(): pl.pallas_call(functools.partial(attend_kernel, blocks_here, head_count,...]
    ppermute x19, starting transfers between devices: 25.3 us -> 18.8 us  [ring(): lax.ppermute(value, axis, [(source, (source + steps) % count) for source...]
    ppermute x19, waiting for transfers between devices: 10.5 us -> 12.5 us  [ring(): lax.ppermute(value, axis, [(source, (source + steps) % count) for source...]
  transfers between devices with their start and end apart: 21 -> 21, of which waited for: 11 -> 9; matrix products, arithmetic and copies ran while one was open for 0% -> 0% of each run, Pallas kernels for 25% -> 36%
where the time goes in v10:
time: 61.3 us; the launch traced here: 61.5 us
  Pallas kernels  24.1 us (39%)
  starting transfers between devices  24.1 us (39%)
  waiting for transfers between devices  12.5 us (20%)
  between operations  0.78 us (1%)
    ppermute x19, starting transfers between devices, ring(): lax.ppermute(value, axis, [(source, (source + steps) % count) for source...  18.8 us
    pallas_call x3, Pallas kernels, attend(): pl.pallas_call(functools.partial(attend_kernel, blocks_here, head_count,...  14.9 us
    ppermute x19, waiting for transfers between devices, ring(): lax.ppermute(value, axis, [(source, (source + steps) % count) for source...  12.5 us
    ppermute x2, starting transfers between devices, shift(): lax.ppermute(value, axis, [(source, source + steps) for source in range(l...  5.31 us
    pallas_call x2, Pallas kernels, flush(): pl.pallas_call(stage_kernel, out_shape=pltpu.HBM(value.shape, BF16), in_s...  2.65 us
    pallas_call x1, Pallas kernels, local(): pl.pallas_call(stage_kernel, out_shape=(pltpu.VMEM(queries.shape, BF16),)...  2.26 us
  transfers between devices with their start and end apart: 21, of which 9 were waited for; matrix products, arithmetic and copies ran while one was open for 0% of the time, Pallas kernels for 36%

profile of v10, /device:TPU:3, one launch (start us, length us, event | category | flops | bytes accessed | tf_op | source)
XLA Modules:
  0.0 61.5 jit_solution(16760704833142473262)
XLA Ops:
  0.6 1.2 %pack.1 = (bf16[256,256]{1,0:T(8,128)(2,1)S(1)}, bf16[256,256]{1,0:T(8,128)(2,1)S(1)}, bf16[256,256]{1,0:T(8,128)(2,1)S(1)}, bf16[256,256]{1,0:T(8,128)(2,1)S(1)...) custom-call(f32[16]{0:T(128)} %sink_hbm.1, ...), custom_call_target="tpu_custom_call" | custom-call | tf_op jit(solution)/shard_map/pack/pallas_call | solution.py:561
  1.8 1.9 %collective-permute-start = (bf16[256,256]{1,0:T(8,128)(2,1)S(1)}, bf16[256,256]{1,0:T(8,128)(2,1)S(1)}, u32[]{:S(2)}, u32[]{:S(2)}) collective-permute-start(bf16[256,256]{1,0:T(8,128)(2,1)S(1)} %get-tuple-element.65), channel_id=1, source_target_pairs={{0,1},{1,2},{2,3},{3,0},{4,5},{5,6},{6,7},{7,4},{8,9},{9,10},{10,1... | collective-permute-start | bytes 393224 | tf_op jit(solution)/shard_map/ppermute | solution.py:37
  4.1 3.4 %collective-permute-start.6 = (bf16[4,128,256]{2,1,0:T(8,128)(2,1)S(1)}, bf16[4,128,256]{2,1,0:T(8,128)(2,1)S(1)}, u32[]{:S(2)}, u32[]{:S(2)}) collective-permute-start(bf16[4,128,256]{2,1,0:T(8,128)(2,1)S(1)} %get-tuple-element.86), channel_id=1, source_target_pairs={{0,1},{1,2},{2,3},{4,5},{5,6},{6,7},{8,9},{9,10},{10,11},{12,13},{... | collective-permute-start | bytes 786440 | tf_op jit(solution)/shard_map/ppermute | solution.py:32
  8.3 1.5 %collective-permute-done.1.refs_2_ = bf16[256,256]{1,0:T(8,128)(2,1)S(1)} collective-permute-done((bf16[256,256]{1,0:T(8,128)(2,1)S(1)}, bf16[256,256]{1,0:T(8,128)(2,1)S(1)}, u32[]{:S(2)}, u32[]{:S(2)}) %collective-permute-start.1) | collective-permute-done | bytes 131104 | tf_op jit(solution)/shard_map/ppermute | solution.py:37
  10.9 2.3 %collective-permute-start.3 = (bf16[128,256]{1,0:T(8,128)(2,1)S(1)}, bf16[128,256]{1,0:T(8,128)(2,1)S(1)}, u32[]{:S(2)}, u32[]{:S(2)}) collective-permute-start(bf16[128,256]{1,0:T(8,128)(2,1)S(1)} %get-tuple-element.75), channel_id=1, source_target_pairs={{0,12},{4,16},{8,20},{12,24},{16,28},{20,0},{24,4},{28,8},{1,13},{... | collective-permute-start | bytes 196616 | tf_op jit(solution)/shard_map/ppermute | solution.py:37
  13.2 1.3 %collective-permute-start.4 = (bf16[128,256]{1,0:T(8,128)(2,1)S(1)}, bf16[128,256]{1,0:T(8,128)(2,1)S(1)}, u32[]{:S(2)}, u32[]{:S(2)}) collective-permute-start(bf16[128,256]{1,0:T(8,128)(2,1)S(1)} %get-tuple-element.76), channel_id=1, source_target_pairs={{0,8},{4,12},{8,16},{12,20},{16,24},{20,28},{24,0},{28,4},{1,9},{5... | collective-permute-start | bytes 196616 | tf_op jit(solution)/shard_map/ppermute | solution.py:37
  14.5 1.2 %collective-permute-start.5 = (bf16[128,256]{1,0:T(8,128)(2,1)S(1)}, bf16[128,256]{1,0:T(8,128)(2,1)S(1)}, u32[]{:S(2)}, u32[]{:S(2)}) collective-permute-start(bf16[128,256]{1,0:T(8,128)(2,1)S(1)} %get-tuple-element.77), channel_id=1, source_target_pairs={{0,4},{4,8},{8,12},{12,16},{16,20},{20,24},{24,28},{28,0},{1,5},{5... | collective-permute-start | bytes 196616 | tf_op jit(solution)/shard_map/ppermute | solution.py:37
  15.9 2.3 %stage.1 = (bf16[256,4096]{1,0:T(8,128)(2,1)S(1)}, bf16[256,4096]{1,0:T(8,128)(2,1)S(1)}) custom-call(bf16[256,4096]{1,0:T(8,128)(2,1)} %refs_0_, bf16[256,4096]{1,0:T(8,128)(2,1)} %refs_1_), custom_call_target="tpu_custom_call" | custom-call | tf_op jit(solution)/shard_map/stage/pallas_call | solution.py:606
  18.4 2.8 %collective-permute-start.9 = (bf16[128,256]{1,0:T(8,128)(2,1)S(1)}, bf16[128,256]{1,0:T(8,128)(2,1)S(1)}, u32[]{:S(2)}, u32[]{:S(2)}) collective-permute-start(bf16[128,256]{1,0:T(8,128)(2,1)S(1)} %arrive.1.refs_7_), channel_id=1, source_target_pairs={{0,2},{1,3},{2,0},{3,1},{4,6},{5,7},{6,4},{7,5},{8,10},{9,11},{10,... | collective-permute-start | bytes 196616 | tf_op jit(solution)/shard_map/ppermute | solution.py:37
  21.1 1.7 %collective-permute-start.7 = (bf16[128,256]{1,0:T(8,128)(2,1)S(1)}, bf16[128,256]{1,0:T(8,128)(2,1)S(1)}, u32[]{:S(2)}, u32[]{:S(2)}) collective-permute-start(bf16[128,256]{1,0:T(8,128)(2,1)S(1)} %arrive.1.refs_7_), channel_id=1, source_target_pairs={{0,1},{1,2},{2,3},{3,0},{4,5},{5,6},{6,7},{7,4},{8,9},{9,10},{10,1... | collective-permute-start | bytes 196616 | tf_op jit(solution)/shard_map/ppermute | solution.py:37
  22.8 3.7 %attend.3 = (bf16[256,4096]{1,0:T(8,128)(2,1)S(1)}, bf16[256,4096]{1,0:T(8,128)(2,1)S(1)}, f32[256,512]{1,0:T(8,128)S(1)}, f32[256,512]{1,0:T(8,128)S(1)}, bf16[...) custom-call(s32[8,128]{1,0:T(8,128)S(1)} %plan.1.plan_ref.refs_0_, f32[64,128]{1,0:T(8,128)S(1)} %sinks.1.refs_1_, ...), custom_call_target="tpu_custom_call" | custom-call | tf_op jit(solution)/shard_map/attend/pallas_call | solution.py:640
  26.6 7.4 %attend.4 = (bf16[256,4096]{1,0:T(8,128)(2,1)S(1)}, bf16[256,4096]{1,0:T(8,128)(2,1)S(1)}, f32[256,512]{1,0:T(8,128)S(1)}, f32[256,512]{1,0:T(8,128)S(1)}, bf16[...) custom-call(s32[8,128]{1,0:T(8,128)S(1)} %plan.1.plan_ref.refs_0_, ...), custom_call_target="tpu_custom_call", output_to_operand_aliasing={{0}: (9, {}), {1}: (10, {}), {2}: (11, {}), {3}: (12, {}), ... | custom-call | tf_op jit(solution)/shard_map/attend/pallas_call | solution.py:640
  34.2 3.8 %attend.5 = (bf16[256,4096]{1,0:T(8,128)(2,1)S(1)}, bf16[256,4096]{1,0:T(8,128)(2,1)S(1)}, f32[256,512]{1,0:T(8,128)S(1)}, f32[256,512]{1,0:T(8,128)S(1)}, bf16[...) custom-call(s32[8,128]{1,0:T(8,128)S(1)} %plan.1.plan_ref.refs_0_, ...), custom_call_target="tpu_custom_call", output_to_operand_aliasing={{0}: (8, {}), {1}: (9, {}), {2}: (10, {}), {3}: (11, {}), {... | custom-call | tf_op jit(solution)/shard_map/attend/pallas_call | solution.py:640
  38.4 1.9 %collective-permute-start.16 = (bf16[4,128,256]{2,1,0:T(8,128)(2,1)S(1)}, bf16[4,128,256]{2,1,0:T(8,128)(2,1)S(1)}, u32[]{:S(2)}, u32[]{:S(2)}) collective-permute-start(bf16[4,128,256]{2,1,0:T(8,128)(2,1)S(1)} %get-tuple-element.113), channel_id=1, source_target_pairs={{1,0},{2,1},{3,2},{5,4},{6,5},{7,6},{9,8},{10,9},{11,10},{13,12},{... | collective-permute-start | bytes 786440 | tf_op jit(solution)/shard_map/ppermute | solution.py:32
  40.5 1.4 %collective-permute-done.12.refs_1_ = bf16[128,256]{1,0:T(8,128)(2,1)S(1)} collective-permute-done((bf16[128,256]{1,0:T(8,128)(2,1)S(1)}, bf16[128,256]{1,0:T(8,128)(2,1)S(1)}, u32[]{:S(2)}, u32[]{:S(2)}) %collective-permute-start.12) | collective-permute-done | bytes 65568 | tf_op jit(solution)/shard_map/ppermute | solution.py:37
  42.1 2.1 %collective-permute-start.15 = (bf16[128,256]{1,0:T(8,128)(2,1)S(1)}, bf16[128,256]{1,0:T(8,128)(2,1)S(1)}, u32[]{:S(2)}, u32[]{:S(2)}) collective-permute-start(bf16[128,256]{1,0:T(8,128)(2,1)S(1)} %gather.3.here_ref), channel_id=1, source_target_pairs={{0,20},{4,24},{8,28},{12,0},{16,4},{20,8},{24,12},{28,16},{1,21},{... | collective-permute-start | bytes 196616 | tf_op jit(solution)/shard_map/ppermute | solution.py:37
  44.2 2.5 %collective-permute-start.14 = (bf16[128,256]{1,0:T(8,128)(2,1)S(1)}, bf16[128,256]{1,0:T(8,128)(2,1)S(1)}, u32[]{:S(2)}, u32[]{:S(2)}) collective-permute-start(bf16[128,256]{1,0:T(8,128)(2,1)S(1)} %gather.3.here_ref), channel_id=1, source_target_pairs={{0,24},{4,28},{8,0},{12,4},{16,8},{20,12},{24,16},{28,20},{1,25},{... | collective-permute-start | bytes 196616 | tf_op jit(solution)/shard_map/ppermute | solution.py:37
  46.8 1.3 %flush.2 = bf16[256,4096]{1,0:T(8,128)(2,1)} custom-call(bf16[256,4096]{1,0:T(8,128)(2,1)S(1)} %get-tuple-element.105.refs_0_), custom_call_target="tpu_custom_call" | custom-call | tf_op jit(solution)/shard_map/flush/pallas_call | solution.py:696
  48.6 3.2 %collective-permute-done.13.refs_0_ = bf16[128,256]{1,0:T(8,128)(2,1)S(1)} collective-permute-done((bf16[128,256]{1,0:T(8,128)(2,1)S(1)}, bf16[128,256]{1,0:T(8,128)(2,1)S(1)}, u32[]{:S(2)}, u32[]{:S(2)}) %collective-permute-start.13) | collective-permute-done | bytes 65568 | tf_op jit(solution)/shard_map/ppermute | solution.py:37
  52.2 0.9 %collective-permute-start.18 = (bf16[256,256]{1,0:T(8,128)(2,1)S(1)}, bf16[256,256]{1,0:T(8,128)(2,1)S(1)}, u32[]{:S(2)}, u32[]{:S(2)}) collective-permute-start(bf16[256,256]{1,0:T(8,128)(2,1)S(1)} %get-tuple-element.117), channel_id=1, source_target_pairs={{0,1},{1,2},{2,3},{3,0},{4,5},{5,6},{6,7},{7,4},{8,9},{9,10},{10,1... | collective-permute-start | bytes 393224 | tf_op jit(solution)/shard_map/ppermute | solution.py:37
  54.0 1.3 %flush.3 = bf16[256,4096]{1,0:T(8,128)(2,1)} custom-call(bf16[256,4096]{1,0:T(8,128)(2,1)S(1)} %get-tuple-element.112.refs_0_), custom_call_target="tpu_custom_call" | custom-call | tf_op jit(solution)/shard_map/flush/pallas_call | solution.py:696
  55.4 2.0 %collective-permute-done.17.far_ref = f32[8,128]{1,0:T(8,128)S(1)} collective-permute-done((f32[8,128]{1,0:T(8,128)S(1)}, f32[8,128]{1,0:T(8,128)S(1)}, u32[]{:S(2)}, u32[]{:S(2)}) %collective-permute-start.17) | collective-permute-done | bytes 4128 | tf_op jit(solution)/shard_map/ppermute | solution.py:37
  57.4 2.5 %collective-permute-done.19.refs_2_ = bf16[256,256]{1,0:T(8,128)(2,1)S(1)} collective-permute-done((bf16[256,256]{1,0:T(8,128)(2,1)S(1)}, bf16[256,256]{1,0:T(8,128)(2,1)S(1)}, u32[]{:S(2)}, u32[]{:S(2)}) %collective-permute-start.19) | collective-permute-done | bytes 131104 | tf_op jit(solution)/shard_map/ppermute | solution.py:37
  60.6 0.9 %total.1 = (bf16[256,512]{1,0:T(8,128)(2,1)}, bf16[256,512]{1,0:T(8,128)(2,1)}, f32[16]{0:T(128)}) custom-call(bf16[4,128,256]{2,1,0:T(8,128)(2,1)S(1)} %collective-permute-done.16.halo_ref, f32[256,512]{1,0:T(8,128)S(1)} %get-tuple-element.114.dk_ref, f32[256,512]{1,0:T(8,128)S(1)} %get-tuple-element.115.dv_ref, f32[8,128]{1,0:T(8,128)S(1)} %get-tuple-element.111.sink_ref, ...), custom_call_target="tpu_custom_call" | custom-call | tf_op jit(solution)/shard_map/total/pallas_call | solution.py:727
  (33 shorter events, 6.0 us)
Async XLA Ops:
  1.8 6.5 %collective-permute-start = (bf16[256,256]{1,0:T(8,128)(2,1)S(1)}, bf16[256,256]{1,0:T(8,128)(2,1)S(1)}, u32[]{:S(2)}, u32[]{:S(2)}) collective-permute-start(bf16[256,256]{1,0:T(8,128)(2,1)S(1)} %get-tuple-element.65), channel_id=1, source_target_pairs={{0,1},{1,2},{2,3},{3,0},{4,5},{5,6},{6,7},{7,4},{8,9},{9,10},{10,1... | collective-permute-start | bytes 393224 | tf_op jit(solution)/shard_map/ppermute | solution.py:37
  3.7 6.2 %collective-permute-start.1 = (bf16[256,256]{1,0:T(8,128)(2,1)S(1)}, bf16[256,256]{1,0:T(8,128)(2,1)S(1)}, u32[]{:S(2)}, u32[]{:S(2)}) collective-permute-start(bf16[256,256]{1,0:T(8,128)(2,1)S(1)} %get-tuple-element.66), channel_id=1, source_target_pairs={{0,2},{1,3},{2,0},{3,1},{4,6},{5,7},{6,4},{7,5},{8,10},{9,11},{10,... | collective-permute-start | bytes 393224 | tf_op jit(solution)/shard_map/ppermute | solution.py:37
  3.9 6.6 %collective-permute-start.2 = (bf16[256,256]{1,0:T(8,128)(2,1)S(1)}, bf16[256,256]{1,0:T(8,128)(2,1)S(1)}, u32[]{:S(2)}, u32[]{:S(2)}) collective-permute-start(bf16[256,256]{1,0:T(8,128)(2,1)S(1)} %get-tuple-element.67), channel_id=1, source_target_pairs={{0,3},{1,0},{2,1},{3,2},{4,7},{5,4},{6,5},{7,6},{8,11},{9,8},{10,9... | collective-permute-start | bytes 393224 | tf_op jit(solution)/shard_map/ppermute | solution.py:37
  4.1 22.5 %collective-permute-start.6 = (bf16[4,128,256]{2,1,0:T(8,128)(2,1)S(1)}, bf16[4,128,256]{2,1,0:T(8,128)(2,1)S(1)}, u32[]{:S(2)}, u32[]{:S(2)}) collective-permute-start(bf16[4,128,256]{2,1,0:T(8,128)(2,1)S(1)} %get-tuple-element.86), channel_id=1, source_target_pairs={{0,1},{1,2},{2,3},{4,5},{5,6},{6,7},{8,9},{9,10},{10,11},{12,13},{... | collective-permute-start | bytes 786440 | tf_op jit(solution)/shard_map/ppermute | solution.py:32
  10.9 7.3 %collective-permute-start.3 = (bf16[128,256]{1,0:T(8,128)(2,1)S(1)}, bf16[128,256]{1,0:T(8,128)(2,1)S(1)}, u32[]{:S(2)}, u32[]{:S(2)}) collective-permute-start(bf16[128,256]{1,0:T(8,128)(2,1)S(1)} %get-tuple-element.75), channel_id=1, source_target_pairs={{0,12},{4,16},{8,20},{12,24},{16,28},{20,0},{24,4},{28,8},{1,13},{... | collective-permute-start | bytes 196616 | tf_op jit(solution)/shard_map/ppermute | solution.py:37
  13.2 4.9 %collective-permute-start.4 = (bf16[128,256]{1,0:T(8,128)(2,1)S(1)}, bf16[128,256]{1,0:T(8,128)(2,1)S(1)}, u32[]{:S(2)}, u32[]{:S(2)}) collective-permute-start(bf16[128,256]{1,0:T(8,128)(2,1)S(1)} %get-tuple-element.76), channel_id=1, source_target_pairs={{0,8},{4,12},{8,16},{12,20},{16,24},{20,28},{24,0},{28,4},{1,9},{5... | collective-permute-start | bytes 196616 | tf_op jit(solution)/shard_map/ppermute | solution.py:37
  14.5 3.7 %collective-permute-start.5 = (bf16[128,256]{1,0:T(8,128)(2,1)S(1)}, bf16[128,256]{1,0:T(8,128)(2,1)S(1)}, u32[]{:S(2)}, u32[]{:S(2)}) collective-permute-start(bf16[128,256]{1,0:T(8,128)(2,1)S(1)} %get-tuple-element.77), channel_id=1, source_target_pairs={{0,4},{4,8},{8,12},{12,16},{16,20},{20,24},{24,28},{28,0},{1,5},{5... | collective-permute-start | bytes 196616 | tf_op jit(solution)/shard_map/ppermute | solution.py:37
  18.4 8.3 %collective-permute-start.9 = (bf16[128,256]{1,0:T(8,128)(2,1)S(1)}, bf16[128,256]{1,0:T(8,128)(2,1)S(1)}, u32[]{:S(2)}, u32[]{:S(2)}) collective-permute-start(bf16[128,256]{1,0:T(8,128)(2,1)S(1)} %arrive.1.refs_7_), channel_id=1, source_target_pairs={{0,2},{1,3},{2,0},{3,1},{4,6},{5,7},{6,4},{7,5},{8,10},{9,11},{10,... | collective-permute-start | bytes 196616 | tf_op jit(solution)/shard_map/ppermute | solution.py:37
  21.1 5.5 %collective-permute-start.8 = (bf16[128,256]{1,0:T(8,128)(2,1)S(1)}, bf16[128,256]{1,0:T(8,128)(2,1)S(1)}, u32[]{:S(2)}, u32[]{:S(2)}) collective-permute-start(bf16[128,256]{1,0:T(8,128)(2,1)S(1)} %arrive.1.refs_7_), channel_id=1, source_target_pairs={{0,3},{1,0},{2,1},{3,2},{4,7},{5,4},{6,5},{7,6},{8,11},{9,8},{10,9... | collective-permute-start | bytes 196616 | tf_op jit(solution)/shard_map/ppermute | solution.py:37
  21.1 13.1 %collective-permute-start.7 = (bf16[128,256]{1,0:T(8,128)(2,1)S(1)}, bf16[128,256]{1,0:T(8,128)(2,1)S(1)}, u32[]{:S(2)}, u32[]{:S(2)}) collective-permute-start(bf16[128,256]{1,0:T(8,128)(2,1)S(1)} %arrive.1.refs_7_), channel_id=1, source_target_pairs={{0,1},{1,2},{2,3},{3,0},{4,5},{5,6},{6,7},{7,4},{8,9},{9,10},{10,1... | collective-permute-start | bytes 196616 | tf_op jit(solution)/shard_map/ppermute | solution.py:37
  34.0 6.3 %collective-permute-start.10 = (bf16[128,256]{1,0:T(8,128)(2,1)S(1)}, bf16[128,256]{1,0:T(8,128)(2,1)S(1)}, u32[]{:S(2)}, u32[]{:S(2)}) collective-permute-start(bf16[128,256]{1,0:T(8,128)(2,1)S(1)} %get-tuple-element.102), channel_id=1, source_target_pairs={{0,1},{1,2},{2,3},{3,0},{4,5},{5,6},{6,7},{7,4},{8,9},{9,10},{10,1... | collective-permute-start | bytes 196616 | tf_op jit(solution)/shard_map/ppermute | solution.py:37
  34.1 6.2 %collective-permute-start.11 = (bf16[128,256]{1,0:T(8,128)(2,1)S(1)}, bf16[128,256]{1,0:T(8,128)(2,1)S(1)}, u32[]{:S(2)}, u32[]{:S(2)}) collective-permute-start(bf16[128,256]{1,0:T(8,128)(2,1)S(1)} %get-tuple-element.103), channel_id=1, source_target_pairs={{0,2},{1,3},{2,0},{3,1},{4,6},{5,7},{6,4},{7,5},{8,10},{9,11},{10,... | collective-permute-start | bytes 196616 | tf_op jit(solution)/shard_map/ppermute | solution.py:37
  37.9 4.0 %collective-permute-start.12 = (bf16[128,256]{1,0:T(8,128)(2,1)S(1)}, bf16[128,256]{1,0:T(8,128)(2,1)S(1)}, u32[]{:S(2)}, u32[]{:S(2)}) collective-permute-start(bf16[128,256]{1,0:T(8,128)(2,1)S(1)} %get-tuple-element.104), channel_id=1, source_target_pairs={{0,3},{1,0},{2,1},{3,2},{4,7},{5,4},{6,5},{7,6},{8,11},{9,8},{10,9... | collective-permute-start | bytes 196616 | tf_op jit(solution)/shard_map/ppermute | solution.py:37
  38.4 19.0 %collective-permute-start.16 = (bf16[4,128,256]{2,1,0:T(8,128)(2,1)S(1)}, bf16[4,128,256]{2,1,0:T(8,128)(2,1)S(1)}, u32[]{:S(2)}, u32[]{:S(2)}) collective-permute-start(bf16[4,128,256]{2,1,0:T(8,128)(2,1)S(1)} %get-tuple-element.113), channel_id=1, source_target_pairs={{1,0},{2,1},{3,2},{5,4},{6,5},{7,6},{9,8},{10,9},{11,10},{13,12},{... | collective-permute-start | bytes 786440 | tf_op jit(solution)/shard_map/ppermute | solution.py:32
  42.1 6.5 %collective-permute-start.15 = (bf16[128,256]{1,0:T(8,128)(2,1)S(1)}, bf16[128,256]{1,0:T(8,128)(2,1)S(1)}, u32[]{:S(2)}, u32[]{:S(2)}) collective-permute-start(bf16[128,256]{1,0:T(8,128)(2,1)S(1)} %gather.3.here_ref), channel_id=1, source_target_pairs={{0,20},{4,24},{8,28},{12,0},{16,4},{20,8},{24,12},{28,16},{1,21},{... | collective-permute-start | bytes 196616 | tf_op jit(solution)/shard_map/ppermute | solution.py:37
  44.2 4.4 %collective-permute-start.14 = (bf16[128,256]{1,0:T(8,128)(2,1)S(1)}, bf16[128,256]{1,0:T(8,128)(2,1)S(1)}, u32[]{:S(2)}, u32[]{:S(2)}) collective-permute-start(bf16[128,256]{1,0:T(8,128)(2,1)S(1)} %gather.3.here_ref), channel_id=1, source_target_pairs={{0,24},{4,28},{8,0},{12,4},{16,8},{20,12},{24,16},{28,20},{1,25},{... | collective-permute-start | bytes 196616 | tf_op jit(solution)/shard_map/ppermute | solution.py:37
  46.8 5.0 %collective-permute-start.13 = (bf16[128,256]{1,0:T(8,128)(2,1)S(1)}, bf16[128,256]{1,0:T(8,128)(2,1)S(1)}, u32[]{:S(2)}, u32[]{:S(2)}) collective-permute-start(bf16[128,256]{1,0:T(8,128)(2,1)S(1)} %gather.3.here_ref), channel_id=1, source_target_pairs={{0,28},{4,0},{8,4},{12,8},{16,12},{20,16},{24,20},{28,24},{1,29},{... | collective-permute-start | bytes 196616 | tf_op jit(solution)/shard_map/ppermute | solution.py:37
  52.2 5.2 %collective-permute-start.18 = (bf16[256,256]{1,0:T(8,128)(2,1)S(1)}, bf16[256,256]{1,0:T(8,128)(2,1)S(1)}, u32[]{:S(2)}, u32[]{:S(2)}) collective-permute-start(bf16[256,256]{1,0:T(8,128)(2,1)S(1)} %get-tuple-element.117), channel_id=1, source_target_pairs={{0,1},{1,2},{2,3},{3,0},{4,5},{5,6},{6,7},{7,4},{8,9},{9,10},{10,1... | collective-permute-start | bytes 393224 | tf_op jit(solution)/shard_map/ppermute | solution.py:37
  53.1 6.8 %collective-permute-start.19 = (bf16[256,256]{1,0:T(8,128)(2,1)S(1)}, bf16[256,256]{1,0:T(8,128)(2,1)S(1)}, u32[]{:S(2)}, u32[]{:S(2)}) collective-permute-start(bf16[256,256]{1,0:T(8,128)(2,1)S(1)} %get-tuple-element.118), channel_id=1, source_target_pairs={{0,2},{1,3},{2,0},{3,1},{4,6},{5,7},{6,4},{7,5},{8,10},{9,11},{10,... | collective-permute-start | bytes 393224 | tf_op jit(solution)/shard_map/ppermute | solution.py:37
  54.0 6.6 %collective-permute-start.20 = (bf16[256,256]{1,0:T(8,128)(2,1)S(1)}, bf16[256,256]{1,0:T(8,128)(2,1)S(1)}, u32[]{:S(2)}, u32[]{:S(2)}) collective-permute-start(bf16[256,256]{1,0:T(8,128)(2,1)S(1)} %get-tuple-element.119), channel_id=1, source_target_pairs={{0,3},{1,0},{2,1},{3,2},{4,7},{5,4},{6,5},{7,6},{8,11},{9,8},{10,9... | collective-permute-start | bytes 393224 | tf_op jit(solution)/shard_map/ppermute | solution.py:37
  54.0 3.4 %collective-permute-start.17 = (f32[8,128]{1,0:T(8,128)S(1)}, f32[8,128]{1,0:T(8,128)S(1)}, u32[]{:S(2)}, u32[]{:S(2)}) collective-permute-start(f32[8,128]{1,0:T(8,128)S(1)} %get-tuple-element.111.sink_ref), channel_id=1, source_target_pairs={{0,16},{4,20},{8,24},{12,28},{16,0},{20,4},{24,8},{28,12},{1,17},{... | collective-permute-start | bytes 12296 | tf_op jit(solution)/shard_map/ppermute | solution.py:37

commit v11 on v8

--- a/solution.py
+++ b/solution.py
@@ -369,17 +369,18 @@
             sink_weight = jnp.exp(sink - peak)
             inverse = 1.0 / (jnp.sum(edge + whole, axis=0, keepdims=True) + sink_weight)
             edge, whole = edge * inverse, whole * inverse
-            term_edge, term_whole = edge * dp_edge, whole * dp_whole
-            delta = jnp.sum(term_edge + term_whole, axis=0, keepdims=True)
-            for target, at_edge, at_whole in (
-                (prob2, edge, whole),
-                (slope2, term_edge - edge * delta, term_whole - whole * delta),
+            delta = jnp.sum(edge * dp_edge + whole * dp_whole, axis=0, keepdims=True)
+            edge16, whole16 = edge.astype(BF16), whole.astype(BF16)
+            edge_own = edge16 * own16
+            edge_prev = edge16 - edge_own
+            away_edge, away_whole = (dp_edge - delta).astype(BF16), (dp_whole - delta).astype(BF16)
+            for target, rows in (
+                (prob2, (edge_own, edge_prev, whole16)),
+                (slope2, (edge_own * away_edge, edge_prev * away_edge, whole16 * away_whole)),
             ):
-                edge16 = at_edge.astype(BF16)
-                edge_own = edge16 * own16
-                target[base : base + HALF, wide(index)] = edge_own
-                target[base + HALF : base + 2 * HALF, wide(index)] = edge16 - edge_own
-                target[base + 2 * HALF : base + seen, wide(index)] = at_whole.astype(BF16)
+                for by, value in enumerate(rows):
+                    at = base + by * HALF
+                    target[at : at + HALF, wide(index)] = value
             sink_term = sink_weight * inverse * delta
             for at, lanes in ((row, slice(0, 128)), (row + 4, slice(128, 256))):
                 part = sink_term[:, lanes]

time: 59.1 us -> 59.4 us (level); the launches traced: 58.9 us -> 59.9 us
  starting transfers between devices: 30.6 us -> 23.8 us
  Pallas kernels: 16.9 us -> 22.5 us
  waiting for transfers between devices: 10.5 us -> 12.8 us
    ppermute x19, starting transfers between devices: 25.3 us -> 18.5 us  [ring(): lax.ppermute(value, axis, [(source, (source + steps) % count) for source...]
    pallas_call x3, Pallas kernels: 7.72 us -> 13.3 us  [attend(): pl.pallas_call(functools.partial(attend_kernel, blocks_here, head_count,...]
    ppermute x19, waiting for transfers between devices: 10.5 us -> 12.8 us  [ring(): lax.ppermute(value, axis, [(source, (source + steps) % count) for source...]
  transfers between devices with their start and end apart: 21 -> 21, of which waited for: 11 -> 9; matrix products, arithmetic and copies ran while one was open for 0% -> 0% of each run, Pallas kernels for 25% -> 34%
where the time goes in v11:
time: 59.4 us; the launch traced here: 59.9 us
  starting transfers between devices  23.8 us (40%)
  Pallas kernels  22.5 us (38%)
  waiting for transfers between devices  12.8 us (22%)
  between operations  0.81 us (1%)
    ppermute x19, starting transfers between devices, ring(): lax.ppermute(value, axis, [(source, (source + steps) % count) for source...  18.5 us
    pallas_call x3, Pallas kernels, attend(): pl.pallas_call(functools.partial(attend_kernel, blocks_here, head_count,...  13.3 us
    ppermute x19, waiting for transfers between devices, ring(): lax.ppermute(value, axis, [(source, (source + steps) % count) for source...  12.8 us
    ppermute x2, starting transfers between devices, shift(): lax.ppermute(value, axis, [(source, source + steps) for source in range(l...  5.31 us
    pallas_call x2, Pallas kernels, flush(): pl.pallas_call(stage_kernel, out_shape=pltpu.HBM(value.shape, BF16), in_s...  2.65 us
    pallas_call x1, Pallas kernels, local(): pl.pallas_call(stage_kernel, out_shape=(pltpu.VMEM(queries.shape, BF16),)...  2.26 us
  transfers between devices with their start and end apart: 21, of which 9 were waited for; matrix products, arithmetic and copies ran while one was open for 0% of the time, Pallas kernels for 34%

profile of v11, /device:TPU:3, one launch (start us, length us, event | category | flops | bytes accessed | tf_op | source)
XLA Modules:
  0.0 59.9 jit_solution(13778629263394965842)
XLA Ops:
  0.6 1.2 %pack.1 = (bf16[256,256]{1,0:T(8,128)(2,1)S(1)}, bf16[256,256]{1,0:T(8,128)(2,1)S(1)}, bf16[256,256]{1,0:T(8,128)(2,1)S(1)}, bf16[256,256]{1,0:T(8,128)(2,1)S(1)...) custom-call(f32[16]{0:T(128)} %sink_hbm.1, ...), custom_call_target="tpu_custom_call" | custom-call | tf_op jit(solution)/shard_map/pack/pallas_call | solution.py:562
  1.8 1.9 %collective-permute-start = (bf16[256,256]{1,0:T(8,128)(2,1)S(1)}, bf16[256,256]{1,0:T(8,128)(2,1)S(1)}, u32[]{:S(2)}, u32[]{:S(2)}) collective-permute-start(bf16[256,256]{1,0:T(8,128)(2,1)S(1)} %get-tuple-element.65), channel_id=1, source_target_pairs={{0,1},{1,2},{2,3},{3,0},{4,5},{5,6},{6,7},{7,4},{8,9},{9,10},{10,1... | collective-permute-start | bytes 393224 | tf_op jit(solution)/shard_map/ppermute | solution.py:37
  4.1 3.4 %collective-permute-start.6 = (bf16[4,128,256]{2,1,0:T(8,128)(2,1)S(1)}, bf16[4,128,256]{2,1,0:T(8,128)(2,1)S(1)}, u32[]{:S(2)}, u32[]{:S(2)}) collective-permute-start(bf16[4,128,256]{2,1,0:T(8,128)(2,1)S(1)} %get-tuple-element.86), channel_id=1, source_target_pairs={{0,1},{1,2},{2,3},{4,5},{5,6},{6,7},{8,9},{9,10},{10,11},{12,13},{... | collective-permute-start | bytes 786440 | tf_op jit(solution)/shard_map/ppermute | solution.py:32
  8.3 1.5 %collective-permute-done.1.refs_2_ = bf16[256,256]{1,0:T(8,128)(2,1)S(1)} collective-permute-done((bf16[256,256]{1,0:T(8,128)(2,1)S(1)}, bf16[256,256]{1,0:T(8,128)(2,1)S(1)}, u32[]{:S(2)}, u32[]{:S(2)}) %collective-permute-start.1) | collective-permute-done | bytes 131104 | tf_op jit(solution)/shard_map/ppermute | solution.py:37
  10.9 2.3 %collective-permute-start.3 = (bf16[128,256]{1,0:T(8,128)(2,1)S(1)}, bf16[128,256]{1,0:T(8,128)(2,1)S(1)}, u32[]{:S(2)}, u32[]{:S(2)}) collective-permute-start(bf16[128,256]{1,0:T(8,128)(2,1)S(1)} %get-tuple-element.75), channel_id=1, source_target_pairs={{0,12},{4,16},{8,20},{12,24},{16,28},{20,0},{24,4},{28,8},{1,13},{... | collective-permute-start | bytes 196616 | tf_op jit(solution)/shard_map/ppermute | solution.py:37
  13.2 1.3 %collective-permute-start.4 = (bf16[128,256]{1,0:T(8,128)(2,1)S(1)}, bf16[128,256]{1,0:T(8,128)(2,1)S(1)}, u32[]{:S(2)}, u32[]{:S(2)}) collective-permute-start(bf16[128,256]{1,0:T(8,128)(2,1)S(1)} %get-tuple-element.76), channel_id=1, source_target_pairs={{0,8},{4,12},{8,16},{12,20},{16,24},{20,28},{24,0},{28,4},{1,9},{5... | collective-permute-start | bytes 196616 | tf_op jit(solution)/shard_map/ppermute | solution.py:37
  14.5 1.2 %collective-permute-start.5 = (bf16[128,256]{1,0:T(8,128)(2,1)S(1)}, bf16[128,256]{1,0:T(8,128)(2,1)S(1)}, u32[]{:S(2)}, u32[]{:S(2)}) collective-permute-start(bf16[128,256]{1,0:T(8,128)(2,1)S(1)} %get-tuple-element.77), channel_id=1, source_target_pairs={{0,4},{4,8},{8,12},{12,16},{16,20},{20,24},{24,28},{28,0},{1,5},{5... | collective-permute-start | bytes 196616 | tf_op jit(solution)/shard_map/ppermute | solution.py:37
  15.9 2.3 %stage.1 = (bf16[256,4096]{1,0:T(8,128)(2,1)S(1)}, bf16[256,4096]{1,0:T(8,128)(2,1)S(1)}) custom-call(bf16[256,4096]{1,0:T(8,128)(2,1)} %refs_0_, bf16[256,4096]{1,0:T(8,128)(2,1)} %refs_1_), custom_call_target="tpu_custom_call" | custom-call | tf_op jit(solution)/shard_map/stage/pallas_call | solution.py:607
  18.4 2.8 %collective-permute-start.9 = (bf16[128,256]{1,0:T(8,128)(2,1)S(1)}, bf16[128,256]{1,0:T(8,128)(2,1)S(1)}, u32[]{:S(2)}, u32[]{:S(2)}) collective-permute-start(bf16[128,256]{1,0:T(8,128)(2,1)S(1)} %arrive.1.refs_7_), channel_id=1, source_target_pairs={{0,2},{1,3},{2,0},{3,1},{4,6},{5,7},{6,4},{7,5},{8,10},{9,11},{10,... | collective-permute-start | bytes 196616 | tf_op jit(solution)/shard_map/ppermute | solution.py:37
  21.1 1.7 %collective-permute-start.7 = (bf16[128,256]{1,0:T(8,128)(2,1)S(1)}, bf16[128,256]{1,0:T(8,128)(2,1)S(1)}, u32[]{:S(2)}, u32[]{:S(2)}) collective-permute-start(bf16[128,256]{1,0:T(8,128)(2,1)S(1)} %arrive.1.refs_7_), channel_id=1, source_target_pairs={{0,1},{1,2},{2,3},{3,0},{4,5},{5,6},{6,7},{7,4},{8,9},{9,10},{10,1... | collective-permute-start | bytes 196616 | tf_op jit(solution)/shard_map/ppermute | solution.py:37
  22.8 3.3 %attend.3 = (bf16[256,4096]{1,0:T(8,128)(2,1)S(1)}, bf16[256,4096]{1,0:T(8,128)(2,1)S(1)}, f32[256,512]{1,0:T(8,128)S(1)}, f32[256,512]{1,0:T(8,128)S(1)}, bf16[...) custom-call(s32[8,128]{1,0:T(8,128)S(1)} %plan.1.plan_ref.refs_0_, f32[64,128]{1,0:T(8,128)S(1)} %sinks.1.refs_1_, ...), custom_call_target="tpu_custom_call" | custom-call | tf_op jit(solution)/shard_map/attend/pallas_call | solution.py:641
  26.2 6.6 %attend.4 = (bf16[256,4096]{1,0:T(8,128)(2,1)S(1)}, bf16[256,4096]{1,0:T(8,128)(2,1)S(1)}, f32[256,512]{1,0:T(8,128)S(1)}, f32[256,512]{1,0:T(8,128)S(1)}, bf16[...) custom-call(s32[8,128]{1,0:T(8,128)S(1)} %plan.1.plan_ref.refs_0_, ...), custom_call_target="tpu_custom_call", output_to_operand_aliasing={{0}: (9, {}), {1}: (10, {}), {2}: (11, {}), {3}: (12, {}), ... | custom-call | tf_op jit(solution)/shard_map/attend/pallas_call | solution.py:641
  33.0 3.4 %attend.5 = (bf16[256,4096]{1,0:T(8,128)(2,1)S(1)}, bf16[256,4096]{1,0:T(8,128)(2,1)S(1)}, f32[256,512]{1,0:T(8,128)S(1)}, f32[256,512]{1,0:T(8,128)S(1)}, bf16[...) custom-call(s32[8,128]{1,0:T(8,128)S(1)} %plan.1.plan_ref.refs_0_, ...), custom_call_target="tpu_custom_call", output_to_operand_aliasing={{0}: (8, {}), {1}: (9, {}), {2}: (10, {}), {3}: (11, {}), {... | custom-call | tf_op jit(solution)/shard_map/attend/pallas_call | solution.py:641
  36.3 1.9 %collective-permute-start.16 = (bf16[4,128,256]{2,1,0:T(8,128)(2,1)S(1)}, bf16[4,128,256]{2,1,0:T(8,128)(2,1)S(1)}, u32[]{:S(2)}, u32[]{:S(2)}) collective-permute-start(bf16[4,128,256]{2,1,0:T(8,128)(2,1)S(1)} %get-tuple-element.113), channel_id=1, source_target_pairs={{1,0},{2,1},{3,2},{5,4},{6,5},{7,6},{9,8},{10,9},{11,10},{13,12},{... | collective-permute-start | bytes 786440 | tf_op jit(solution)/shard_map/ppermute | solution.py:32
  38.4 1.9 %collective-permute-done.12.refs_1_ = bf16[128,256]{1,0:T(8,128)(2,1)S(1)} collective-permute-done((bf16[128,256]{1,0:T(8,128)(2,1)S(1)}, bf16[128,256]{1,0:T(8,128)(2,1)S(1)}, u32[]{:S(2)}, u32[]{:S(2)}) %collective-permute-start.12) | collective-permute-done | bytes 65568 | tf_op jit(solution)/shard_map/ppermute | solution.py:37
  40.5 1.9 %collective-permute-start.15 = (bf16[128,256]{1,0:T(8,128)(2,1)S(1)}, bf16[128,256]{1,0:T(8,128)(2,1)S(1)}, u32[]{:S(2)}, u32[]{:S(2)}) collective-permute-start(bf16[128,256]{1,0:T(8,128)(2,1)S(1)} %gather.3.here_ref), channel_id=1, source_target_pairs={{0,20},{4,24},{8,28},{12,0},{16,4},{20,8},{24,12},{28,16},{1,21},{... | collective-permute-start | bytes 196616 | tf_op jit(solution)/shard_map/ppermute | solution.py:37
  42.4 2.8 %collective-permute-start.14 = (bf16[128,256]{1,0:T(8,128)(2,1)S(1)}, bf16[128,256]{1,0:T(8,128)(2,1)S(1)}, u32[]{:S(2)}, u32[]{:S(2)}) collective-permute-start(bf16[128,256]{1,0:T(8,128)(2,1)S(1)} %gather.3.here_ref), channel_id=1, source_target_pairs={{0,24},{4,28},{8,0},{12,4},{16,8},{20,12},{24,16},{28,20},{1,25},{... | collective-permute-start | bytes 196616 | tf_op jit(solution)/shard_map/ppermute | solution.py:37
  45.2 1.3 %flush.2 = bf16[256,4096]{1,0:T(8,128)(2,1)} custom-call(bf16[256,4096]{1,0:T(8,128)(2,1)S(1)} %get-tuple-element.105.refs_0_), custom_call_target="tpu_custom_call" | custom-call | tf_op jit(solution)/shard_map/flush/pallas_call | solution.py:697
  47.1 2.9 %collective-permute-done.13.refs_0_ = bf16[128,256]{1,0:T(8,128)(2,1)S(1)} collective-permute-done((bf16[128,256]{1,0:T(8,128)(2,1)S(1)}, bf16[128,256]{1,0:T(8,128)(2,1)S(1)}, u32[]{:S(2)}, u32[]{:S(2)}) %collective-permute-start.13) | collective-permute-done | bytes 65568 | tf_op jit(solution)/shard_map/ppermute | solution.py:37
  50.4 1.1 %collective-permute-start.18 = (bf16[256,256]{1,0:T(8,128)(2,1)S(1)}, bf16[256,256]{1,0:T(8,128)(2,1)S(1)}, u32[]{:S(2)}, u32[]{:S(2)}) collective-permute-start(bf16[256,256]{1,0:T(8,128)(2,1)S(1)} %get-tuple-element.117), channel_id=1, source_target_pairs={{0,1},{1,2},{2,3},{3,0},{4,5},{5,6},{6,7},{7,4},{8,9},{9,10},{10,1... | collective-permute-start | bytes 393224 | tf_op jit(solution)/shard_map/ppermute | solution.py:37
  52.4 1.3 %flush.3 = bf16[256,4096]{1,0:T(8,128)(2,1)} custom-call(bf16[256,4096]{1,0:T(8,128)(2,1)S(1)} %get-tuple-element.112.refs_0_), custom_call_target="tpu_custom_call" | custom-call | tf_op jit(solution)/shard_map/flush/pallas_call | solution.py:697
  53.8 2.0 %collective-permute-done.17.far_ref = f32[8,128]{1,0:T(8,128)S(1)} collective-permute-done((f32[8,128]{1,0:T(8,128)S(1)}, f32[8,128]{1,0:T(8,128)S(1)}, u32[]{:S(2)}, u32[]{:S(2)}) %collective-permute-start.17) | collective-permute-done | bytes 4128 | tf_op jit(solution)/shard_map/ppermute | solution.py:37
  55.8 2.6 %collective-permute-done.19.refs_2_ = bf16[256,256]{1,0:T(8,128)(2,1)S(1)} collective-permute-done((bf16[256,256]{1,0:T(8,128)(2,1)S(1)}, bf16[256,256]{1,0:T(8,128)(2,1)S(1)}, u32[]{:S(2)}, u32[]{:S(2)}) %collective-permute-start.19) | collective-permute-done | bytes 131104 | tf_op jit(solution)/shard_map/ppermute | solution.py:37
  59.0 0.9 %total.1 = (bf16[256,512]{1,0:T(8,128)(2,1)}, bf16[256,512]{1,0:T(8,128)(2,1)}, f32[16]{0:T(128)}) custom-call(bf16[4,128,256]{2,1,0:T(8,128)(2,1)S(1)} %collective-permute-done.16.halo_ref, f32[256,512]{1,0:T(8,128)S(1)} %get-tuple-element.114.dk_ref, f32[256,512]{1,0:T(8,128)S(1)} %get-tuple-element.115.dv_ref, f32[8,128]{1,0:T(8,128)S(1)} %get-tuple-element.111.sink_ref, ...), custom_call_target="tpu_custom_call" | custom-call | tf_op jit(solution)/shard_map/total/pallas_call | solution.py:728
  (33 shorter events, 5.6 us)
Async XLA Ops:
  1.8 6.5 %collective-permute-start = (bf16[256,256]{1,0:T(8,128)(2,1)S(1)}, bf16[256,256]{1,0:T(8,128)(2,1)S(1)}, u32[]{:S(2)}, u32[]{:S(2)}) collective-permute-start(bf16[256,256]{1,0:T(8,128)(2,1)S(1)} %get-tuple-element.65), channel_id=1, source_target_pairs={{0,1},{1,2},{2,3},{3,0},{4,5},{5,6},{6,7},{7,4},{8,9},{9,10},{10,1... | collective-permute-start | bytes 393224 | tf_op jit(solution)/shard_map/ppermute | solution.py:37
  3.7 6.2 %collective-permute-start.1 = (bf16[256,256]{1,0:T(8,128)(2,1)S(1)}, bf16[256,256]{1,0:T(8,128)(2,1)S(1)}, u32[]{:S(2)}, u32[]{:S(2)}) collective-permute-start(bf16[256,256]{1,0:T(8,128)(2,1)S(1)} %get-tuple-element.66), channel_id=1, source_target_pairs={{0,2},{1,3},{2,0},{3,1},{4,6},{5,7},{6,4},{7,5},{8,10},{9,11},{10,... | collective-permute-start | bytes 393224 | tf_op jit(solution)/shard_map/ppermute | solution.py:37
  3.9 6.6 %collective-permute-start.2 = (bf16[256,256]{1,0:T(8,128)(2,1)S(1)}, bf16[256,256]{1,0:T(8,128)(2,1)S(1)}, u32[]{:S(2)}, u32[]{:S(2)}) collective-permute-start(bf16[256,256]{1,0:T(8,128)(2,1)S(1)} %get-tuple-element.67), channel_id=1, source_target_pairs={{0,3},{1,0},{2,1},{3,2},{4,7},{5,4},{6,5},{7,6},{8,11},{9,8},{10,9... | collective-permute-start | bytes 393224 | tf_op jit(solution)/shard_map/ppermute | solution.py:37
  4.1 22.1 %collective-permute-start.6 = (bf16[4,128,256]{2,1,0:T(8,128)(2,1)S(1)}, bf16[4,128,256]{2,1,0:T(8,128)(2,1)S(1)}, u32[]{:S(2)}, u32[]{:S(2)}) collective-permute-start(bf16[4,128,256]{2,1,0:T(8,128)(2,1)S(1)} %get-tuple-element.86), channel_id=1, source_target_pairs={{0,1},{1,2},{2,3},{4,5},{5,6},{6,7},{8,9},{9,10},{10,11},{12,13},{... | collective-permute-start | bytes 786440 | tf_op jit(solution)/shard_map/ppermute | solution.py:32
  10.9 7.3 %collective-permute-start.3 = (bf16[128,256]{1,0:T(8,128)(2,1)S(1)}, bf16[128,256]{1,0:T(8,128)(2,1)S(1)}, u32[]{:S(2)}, u32[]{:S(2)}) collective-permute-start(bf16[128,256]{1,0:T(8,128)(2,1)S(1)} %get-tuple-element.75), channel_id=1, source_target_pairs={{0,12},{4,16},{8,20},{12,24},{16,28},{20,0},{24,4},{28,8},{1,13},{... | collective-permute-start | bytes 196616 | tf_op jit(solution)/shard_map/ppermute | solution.py:37
  13.2 4.9 %collective-permute-start.4 = (bf16[128,256]{1,0:T(8,128)(2,1)S(1)}, bf16[128,256]{1,0:T(8,128)(2,1)S(1)}, u32[]{:S(2)}, u32[]{:S(2)}) collective-permute-start(bf16[128,256]{1,0:T(8,128)(2,1)S(1)} %get-tuple-element.76), channel_id=1, source_target_pairs={{0,8},{4,12},{8,16},{12,20},{16,24},{20,28},{24,0},{28,4},{1,9},{5... | collective-permute-start | bytes 196616 | tf_op jit(solution)/shard_map/ppermute | solution.py:37
  14.5 3.7 %collective-permute-start.5 = (bf16[128,256]{1,0:T(8,128)(2,1)S(1)}, bf16[128,256]{1,0:T(8,128)(2,1)S(1)}, u32[]{:S(2)}, u32[]{:S(2)}) collective-permute-start(bf16[128,256]{1,0:T(8,128)(2,1)S(1)} %get-tuple-element.77), channel_id=1, source_target_pairs={{0,4},{4,8},{8,12},{12,16},{16,20},{20,24},{24,28},{28,0},{1,5},{5... | collective-permute-start | bytes 196616 | tf_op jit(solution)/shard_map/ppermute | solution.py:37
  18.4 7.8 %collective-permute-start.9 = (bf16[128,256]{1,0:T(8,128)(2,1)S(1)}, bf16[128,256]{1,0:T(8,128)(2,1)S(1)}, u32[]{:S(2)}, u32[]{:S(2)}) collective-permute-start(bf16[128,256]{1,0:T(8,128)(2,1)S(1)} %arrive.1.refs_7_), channel_id=1, source_target_pairs={{0,2},{1,3},{2,0},{3,1},{4,6},{5,7},{6,4},{7,5},{8,10},{9,11},{10,... | collective-permute-start | bytes 196616 | tf_op jit(solution)/shard_map/ppermute | solution.py:37
  21.1 5.1 %collective-permute-start.8 = (bf16[128,256]{1,0:T(8,128)(2,1)S(1)}, bf16[128,256]{1,0:T(8,128)(2,1)S(1)}, u32[]{:S(2)}, u32[]{:S(2)}) collective-permute-start(bf16[128,256]{1,0:T(8,128)(2,1)S(1)} %arrive.1.refs_7_), channel_id=1, source_target_pairs={{0,3},{1,0},{2,1},{3,2},{4,7},{5,4},{6,5},{7,6},{8,11},{9,8},{10,9... | collective-permute-start | bytes 196616 | tf_op jit(solution)/shard_map/ppermute | solution.py:37
  21.1 11.9 %collective-permute-start.7 = (bf16[128,256]{1,0:T(8,128)(2,1)S(1)}, bf16[128,256]{1,0:T(8,128)(2,1)S(1)}, u32[]{:S(2)}, u32[]{:S(2)}) collective-permute-start(bf16[128,256]{1,0:T(8,128)(2,1)S(1)} %arrive.1.refs_7_), channel_id=1, source_target_pairs={{0,1},{1,2},{2,3},{3,0},{4,5},{5,6},{6,7},{7,4},{8,9},{9,10},{10,1... | collective-permute-start | bytes 196616 | tf_op jit(solution)/shard_map/ppermute | solution.py:37
  32.8 5.4 %collective-permute-start.10 = (bf16[128,256]{1,0:T(8,128)(2,1)S(1)}, bf16[128,256]{1,0:T(8,128)(2,1)S(1)}, u32[]{:S(2)}, u32[]{:S(2)}) collective-permute-start(bf16[128,256]{1,0:T(8,128)(2,1)S(1)} %get-tuple-element.102), channel_id=1, source_target_pairs={{0,1},{1,2},{2,3},{3,0},{4,5},{5,6},{6,7},{7,4},{8,9},{9,10},{10,1... | collective-permute-start | bytes 196616 | tf_op jit(solution)/shard_map/ppermute | solution.py:37
  32.9 5.4 %collective-permute-start.11 = (bf16[128,256]{1,0:T(8,128)(2,1)S(1)}, bf16[128,256]{1,0:T(8,128)(2,1)S(1)}, u32[]{:S(2)}, u32[]{:S(2)}) collective-permute-start(bf16[128,256]{1,0:T(8,128)(2,1)S(1)} %get-tuple-element.103), channel_id=1, source_target_pairs={{0,2},{1,3},{2,0},{3,1},{4,6},{5,7},{6,4},{7,5},{8,10},{9,11},{10,... | collective-permute-start | bytes 196616 | tf_op jit(solution)/shard_map/ppermute | solution.py:37
  36.3 4.0 %collective-permute-start.12 = (bf16[128,256]{1,0:T(8,128)(2,1)S(1)}, bf16[128,256]{1,0:T(8,128)(2,1)S(1)}, u32[]{:S(2)}, u32[]{:S(2)}) collective-permute-start(bf16[128,256]{1,0:T(8,128)(2,1)S(1)} %get-tuple-element.104), channel_id=1, source_target_pairs={{0,3},{1,0},{2,1},{3,2},{4,7},{5,4},{6,5},{7,6},{8,11},{9,8},{10,9... | collective-permute-start | bytes 196616 | tf_op jit(solution)/shard_map/ppermute | solution.py:37
  36.3 19.5 %collective-permute-start.16 = (bf16[4,128,256]{2,1,0:T(8,128)(2,1)S(1)}, bf16[4,128,256]{2,1,0:T(8,128)(2,1)S(1)}, u32[]{:S(2)}, u32[]{:S(2)}) collective-permute-start(bf16[4,128,256]{2,1,0:T(8,128)(2,1)S(1)} %get-tuple-element.113), channel_id=1, source_target_pairs={{1,0},{2,1},{3,2},{5,4},{6,5},{7,6},{9,8},{10,9},{11,10},{13,12},{... | collective-permute-start | bytes 786440 | tf_op jit(solution)/shard_map/ppermute | solution.py:32
  40.5 6.0 %collective-permute-start.15 = (bf16[128,256]{1,0:T(8,128)(2,1)S(1)}, bf16[128,256]{1,0:T(8,128)(2,1)S(1)}, u32[]{:S(2)}, u32[]{:S(2)}) collective-permute-start(bf16[128,256]{1,0:T(8,128)(2,1)S(1)} %gather.3.here_ref), channel_id=1, source_target_pairs={{0,20},{4,24},{8,28},{12,0},{16,4},{20,8},{24,12},{28,16},{1,21},{... | collective-permute-start | bytes 196616 | tf_op jit(solution)/shard_map/ppermute | solution.py:37
  42.4 4.7 %collective-permute-start.14 = (bf16[128,256]{1,0:T(8,128)(2,1)S(1)}, bf16[128,256]{1,0:T(8,128)(2,1)S(1)}, u32[]{:S(2)}, u32[]{:S(2)}) collective-permute-start(bf16[128,256]{1,0:T(8,128)(2,1)S(1)} %gather.3.here_ref), channel_id=1, source_target_pairs={{0,24},{4,28},{8,0},{12,4},{16,8},{20,12},{24,16},{28,20},{1,25},{... | collective-permute-start | bytes 196616 | tf_op jit(solution)/shard_map/ppermute | solution.py:37
  45.2 4.8 %collective-permute-start.13 = (bf16[128,256]{1,0:T(8,128)(2,1)S(1)}, bf16[128,256]{1,0:T(8,128)(2,1)S(1)}, u32[]{:S(2)}, u32[]{:S(2)}) collective-permute-start(bf16[128,256]{1,0:T(8,128)(2,1)S(1)} %gather.3.here_ref), channel_id=1, source_target_pairs={{0,28},{4,0},{8,4},{12,8},{16,12},{20,16},{24,20},{28,24},{1,29},{... | collective-permute-start | bytes 196616 | tf_op jit(solution)/shard_map/ppermute | solution.py:37
  50.4 5.4 %collective-permute-start.18 = (bf16[256,256]{1,0:T(8,128)(2,1)S(1)}, bf16[256,256]{1,0:T(8,128)(2,1)S(1)}, u32[]{:S(2)}, u32[]{:S(2)}) collective-permute-start(bf16[256,256]{1,0:T(8,128)(2,1)S(1)} %get-tuple-element.117), channel_id=1, source_target_pairs={{0,1},{1,2},{2,3},{3,0},{4,5},{5,6},{6,7},{7,4},{8,9},{9,10},{10,1... | collective-permute-start | bytes 393224 | tf_op jit(solution)/shard_map/ppermute | solution.py:37
  51.6 6.8 %collective-permute-start.19 = (bf16[256,256]{1,0:T(8,128)(2,1)S(1)}, bf16[256,256]{1,0:T(8,128)(2,1)S(1)}, u32[]{:S(2)}, u32[]{:S(2)}) collective-permute-start(bf16[256,256]{1,0:T(8,128)(2,1)S(1)} %get-tuple-element.118), channel_id=1, source_target_pairs={{0,2},{1,3},{2,0},{3,1},{4,6},{5,7},{6,4},{7,5},{8,10},{9,11},{10,... | collective-permute-start | bytes 393224 | tf_op jit(solution)/shard_map/ppermute | solution.py:37
  52.4 6.6 %collective-permute-start.20 = (bf16[256,256]{1,0:T(8,128)(2,1)S(1)}, bf16[256,256]{1,0:T(8,128)(2,1)S(1)}, u32[]{:S(2)}, u32[]{:S(2)}) collective-permute-start(bf16[256,256]{1,0:T(8,128)(2,1)S(1)} %get-tuple-element.119), channel_id=1, source_target_pairs={{0,3},{1,0},{2,1},{3,2},{4,7},{5,4},{6,5},{7,6},{8,11},{9,8},{10,9... | collective-permute-start | bytes 393224 | tf_op jit(solution)/shard_map/ppermute | solution.py:37
  52.4 3.4 %collective-permute-start.17 = (f32[8,128]{1,0:T(8,128)S(1)}, f32[8,128]{1,0:T(8,128)S(1)}, u32[]{:S(2)}, u32[]{:S(2)}) collective-permute-start(f32[8,128]{1,0:T(8,128)S(1)} %get-tuple-element.111.sink_ref), channel_id=1, source_target_pairs={{0,16},{4,20},{8,24},{12,28},{16,0},{20,4},{24,8},{28,12},{1,17},{... | collective-permute-start | bytes 12296 | tf_op jit(solution)/shard_map/ppermute | solution.py:37

commit v12 on v11

--- a/solution.py
+++ b/solution.py
@@ -206,12 +206,12 @@
     head = lax.axis_index("head")
     states = [planned_block(inputs[0], block) for block in range(blocks_here)]
     for step, tail_ref in zip(steps, tail_refs):
-        tails[lax.rem(head + step, slots)] = tail_ref[...]
+        tails[head ^ step] = tail_ref[...]
 
     def step(place, carry):
         pair = place // blocks_here
         if offset is not None:
-            pair = lax.rem(head + pair + offset, PAIRS)
+            pair = head ^ (pair + offset)
         block = place % blocks_here
         state = states[0]
         for other in range(1, blocks_here):
@@ -471,7 +471,7 @@
             rows = jnp.concatenate([rows, jnp.zeros((128 - heads, WINDOW), F32)], axis=0)
             sink_row = jnp.sum(rows.T, axis=0, keepdims=True)
             tail = with_row(tail, sink_row)
-            wanted = lax.rem(pair * (2 // per_slot) + part - head + slots, slots)
+            wanted = (pair * (2 // per_slot) + part) ^ head
             for step, dtail_ref in dtails:
 
                 @pl.when(wanted == step)
@@ -538,6 +538,14 @@
 
 def swap(values, axis):
     return [values[0]] + [ring(values[step], axis, step) for step in range(1, len(values))]
+
+
+def trade(values, axis):
+    places = range(lax.axis_size(axis))
+    return [values[0]] + [
+        lax.ppermute(values[bits], axis, [(place, place ^ bits) for place in places])
+        for bits in range(1, len(values))
+    ]
 
 
 def local(
@@ -624,7 +632,7 @@
         compiler_params=PARAMS,
         name="arrive",
     )(plan, *arrived)
-    tails = swap([quarter] * head_count, "head")
+    tails = trade([quarter] * head_count, "head")
 
     def attend(steps, pairs, offset, halo, joined):
         inputs = (
@@ -634,7 +642,7 @@
             close(keys),
             close(values),
             halo,
-            *(tails[-step % head_count] for step in steps),
+            *(tails[step] for step in steps),
             *(close(value) for value in joined),
         )
         base = 1 + len(inputs) - len(joined)
@@ -672,14 +680,14 @@
 
     if per_slot == 2:
         *joined, own_tail = attend((0,), 1, 0, spread[1], ())
-        *joined, tail_1, tail_2 = attend((1, 2), 2, 1, halo, joined)
-        *results, tail_3 = attend((3,), 1, 3, halo, joined)
+        *joined, tail_2, tail_3 = attend((2, 3), 2, 2, halo, joined)
+        *results, tail_1 = attend((1,), 1, 1, halo, joined)
         dtail = [own_tail, tail_1, tail_2, tail_3]
     else:
         results = attend(tuple(range(head_count)), PAIRS, None, halo, ())
         results, dtail = results[:5], list(results[5:])
     attended, query_grad, dk, dv, dhalo = results
-    parts = swap(dtail, "head")
+    parts = trade(dtail, "head")
 
     def gather(values):
         return pl.pallas_call(
@@ -691,7 +699,7 @@
             name="gather",
         )(*values)
 
-    quarter_grad = gather([gather(parts[:-1]), parts[-1]])
+    quarter_grad = gather([gather([parts[0], *parts[2:]]), parts[1]])
 
     def flush(value):
         return pl.pallas_call(

time: 59.4 us -> 59.3 us (level); the launches traced: 59.9 us -> 58.5 us
  starting transfers between devices: 23.8 us -> 30.8 us
  Pallas kernels: 22.5 us -> 16.7 us
  waiting for transfers between devices: 12.8 us -> 10.2 us
    ppermute x0 -> x6, starting transfers between devices: none -> 10.9 us  [trade(): lax.ppermute(values[bits], axis, [(place, place ^ bits) for place in plac...]
    pallas_call x3, Pallas kernels: 13.3 us -> 7.46 us  [attend(): pl.pallas_call(functools.partial(attend_kernel, blocks_here, head_count,...]
    ppermute x19 -> x13, starting transfers between devices: 18.5 us -> 14.5 us  [ring(): lax.ppermute(value, axis, [(source, (source + steps) % count) for source...]
    ppermute x19 -> x13, waiting for transfers between devices: 12.8 us -> 9.76 us  [ring(): lax.ppermute(value, axis, [(source, (source + steps) % count) for source...]
  transfers between devices with their start and end apart: 21 -> 21, of which waited for: 9 -> 10; matrix products, arithmetic and copies ran while one was open for 0% -> 0% of each run, Pallas kernels for 34% -> 25%
where the time goes in v12:
time: 59.3 us; the launch traced here: 58.5 us
  starting transfers between devices  30.8 us (52%)
  Pallas kernels  16.7 us (28%)
  waiting for transfers between devices  10.2 us (17%)
  between operations  0.79 us (1%)
    ppermute x13, starting transfers between devices, ring(): lax.ppermute(value, axis, [(source, (source + steps) % count) for source...  14.5 us
    ppermute x6, starting transfers between devices, trade(): lax.ppermute(values[bits], axis, [(place, place ^ bits) for place in plac...  10.9 us
    ppermute x13, waiting for transfers between devices, ring(): lax.ppermute(value, axis, [(source, (source + steps) % count) for source...  9.76 us
    pallas_call x3, Pallas kernels, attend(): pl.pallas_call(functools.partial(attend_kernel, blocks_here, head_count,...  7.46 us
    ppermute x2, starting transfers between devices, shift(): lax.ppermute(value, axis, [(source, source + steps) for source in range(l...  5.32 us
    pallas_call x2, Pallas kernels, flush(): pl.pallas_call(stage_kernel, out_shape=pltpu.HBM(value.shape, BF16), in_s...  2.65 us
    pallas_call x1, Pallas kernels, local(): pl.pallas_call(stage_kernel, out_shape=(pltpu.VMEM(queries.shape, BF16),)...  2.26 us
  transfers between devices with their start and end apart: 21, of which 10 were waited for; matrix products, arithmetic and copies ran while one was open for 0% of the time, Pallas kernels for 25%

profile of v12, /device:TPU:3, one launch (start us, length us, event | category | flops | bytes accessed | tf_op | source)
XLA Modules:
  0.0 58.5 jit_solution(3769502225712269455)
XLA Ops:
  0.6 1.2 %pack.1 = (bf16[256,256]{1,0:T(8,128)(2,1)S(1)}, bf16[256,256]{1,0:T(8,128)(2,1)S(1)}, bf16[256,256]{1,0:T(8,128)(2,1)S(1)}, bf16[256,256]{1,0:T(8,128)(2,1)S(1)...) custom-call(f32[16]{0:T(128)} %sink_hbm.1, ...), custom_call_target="tpu_custom_call" | custom-call | tf_op jit(solution)/shard_map/pack/pallas_call | solution.py:570
  1.8 1.9 %collective-permute-start = (bf16[256,256]{1,0:T(8,128)(2,1)S(1)}, bf16[256,256]{1,0:T(8,128)(2,1)S(1)}, u32[]{:S(2)}, u32[]{:S(2)}) collective-permute-start(bf16[256,256]{1,0:T(8,128)(2,1)S(1)} %get-tuple-element.65), channel_id=1, source_target_pairs={{0,1},{1,2},{2,3},{3,0},{4,5},{5,6},{6,7},{7,4},{8,9},{9,10},{10,1... | collective-permute-start | bytes 393224 | tf_op jit(solution)/shard_map/ppermute | solution.py:37
  4.1 3.4 %collective-permute-start.6 = (bf16[4,128,256]{2,1,0:T(8,128)(2,1)S(1)}, bf16[4,128,256]{2,1,0:T(8,128)(2,1)S(1)}, u32[]{:S(2)}, u32[]{:S(2)}) collective-permute-start(bf16[4,128,256]{2,1,0:T(8,128)(2,1)S(1)} %get-tuple-element.86), channel_id=1, source_target_pairs={{0,1},{1,2},{2,3},{4,5},{5,6},{6,7},{8,9},{9,10},{10,11},{12,13},{... | collective-permute-start | bytes 786440 | tf_op jit(solution)/shard_map/ppermute | solution.py:32
  8.3 1.5 %collective-permute-done.1.refs_2_ = bf16[256,256]{1,0:T(8,128)(2,1)S(1)} collective-permute-done((bf16[256,256]{1,0:T(8,128)(2,1)S(1)}, bf16[256,256]{1,0:T(8,128)(2,1)S(1)}, u32[]{:S(2)}, u32[]{:S(2)}) %collective-permute-start.1) | collective-permute-done | bytes 131104 | tf_op jit(solution)/shard_map/ppermute | solution.py:37
  10.9 2.3 %collective-permute-start.3 = (bf16[128,256]{1,0:T(8,128)(2,1)S(1)}, bf16[128,256]{1,0:T(8,128)(2,1)S(1)}, u32[]{:S(2)}, u32[]{:S(2)}) collective-permute-start(bf16[128,256]{1,0:T(8,128)(2,1)S(1)} %get-tuple-element.75), channel_id=1, source_target_pairs={{0,12},{4,16},{8,20},{12,24},{16,28},{20,0},{24,4},{28,8},{1,13},{... | collective-permute-start | bytes 196616 | tf_op jit(solution)/shard_map/ppermute | solution.py:37
  13.2 1.3 %collective-permute-start.4 = (bf16[128,256]{1,0:T(8,128)(2,1)S(1)}, bf16[128,256]{1,0:T(8,128)(2,1)S(1)}, u32[]{:S(2)}, u32[]{:S(2)}) collective-permute-start(bf16[128,256]{1,0:T(8,128)(2,1)S(1)} %get-tuple-element.76), channel_id=1, source_target_pairs={{0,8},{4,12},{8,16},{12,20},{16,24},{20,28},{24,0},{28,4},{1,9},{5... | collective-permute-start | bytes 196616 | tf_op jit(solution)/shard_map/ppermute | solution.py:37
  14.5 1.2 %collective-permute-start.5 = (bf16[128,256]{1,0:T(8,128)(2,1)S(1)}, bf16[128,256]{1,0:T(8,128)(2,1)S(1)}, u32[]{:S(2)}, u32[]{:S(2)}) collective-permute-start(bf16[128,256]{1,0:T(8,128)(2,1)S(1)} %get-tuple-element.77), channel_id=1, source_target_pairs={{0,4},{4,8},{8,12},{12,16},{16,20},{20,24},{24,28},{28,0},{1,5},{5... | collective-permute-start | bytes 196616 | tf_op jit(solution)/shard_map/ppermute | solution.py:37
  15.9 2.3 %stage.1 = (bf16[256,4096]{1,0:T(8,128)(2,1)S(1)}, bf16[256,4096]{1,0:T(8,128)(2,1)S(1)}) custom-call(bf16[256,4096]{1,0:T(8,128)(2,1)} %refs_0_, bf16[256,4096]{1,0:T(8,128)(2,1)} %refs_1_), custom_call_target="tpu_custom_call" | custom-call | tf_op jit(solution)/shard_map/stage/pallas_call | solution.py:615
  18.4 1.4 %collective-permute-start.9 = (bf16[128,256]{1,0:T(8,128)(2,1)S(1)}, bf16[128,256]{1,0:T(8,128)(2,1)S(1)}, u32[]{:S(2)}, u32[]{:S(2)}) collective-permute-start(bf16[128,256]{1,0:T(8,128)(2,1)S(1)} %arrive.1.refs_7_), channel_id=1, source_target_pairs={{0,3},{1,2},{2,1},{3,0},{4,7},{5,6},{6,5},{7,4},{8,11},{9,10},{10,... | collective-permute-start | bytes 196616 | tf_op jit(solution)/shard_map/ppermute | solution.py:546
  19.8 2.2 %collective-permute-start.8 = (bf16[128,256]{1,0:T(8,128)(2,1)S(1)}, bf16[128,256]{1,0:T(8,128)(2,1)S(1)}, u32[]{:S(2)}, u32[]{:S(2)}) collective-permute-start(bf16[128,256]{1,0:T(8,128)(2,1)S(1)} %arrive.1.refs_7_), channel_id=1, source_target_pairs={{0,2},{1,3},{2,0},{3,1},{4,6},{5,7},{6,4},{7,5},{8,10},{9,11},{10,... | collective-permute-start | bytes 196616 | tf_op jit(solution)/shard_map/ppermute | solution.py:546
  22.0 1.9 %attend.3 = (bf16[256,4096]{1,0:T(8,128)(2,1)S(1)}, bf16[256,4096]{1,0:T(8,128)(2,1)S(1)}, f32[256,512]{1,0:T(8,128)S(1)}, f32[256,512]{1,0:T(8,128)S(1)}, bf16[...) custom-call(s32[8,128]{1,0:T(8,128)S(1)} %plan.1.plan_ref.refs_0_, f32[64,128]{1,0:T(8,128)S(1)} %sinks.1.refs_1_, ...), custom_call_target="tpu_custom_call" | custom-call | tf_op jit(solution)/shard_map/attend/pallas_call | solution.py:649
  24.3 3.7 %attend.4 = (bf16[256,4096]{1,0:T(8,128)(2,1)S(1)}, bf16[256,4096]{1,0:T(8,128)(2,1)S(1)}, f32[256,512]{1,0:T(8,128)S(1)}, f32[256,512]{1,0:T(8,128)S(1)}, bf16[...) custom-call(s32[8,128]{1,0:T(8,128)S(1)} %plan.1.plan_ref.refs_0_, ...), custom_call_target="tpu_custom_call", output_to_operand_aliasing={{0}: (9, {}), {1}: (10, {}), {2}: (11, {}), {3}: (12, {}), ... | custom-call | tf_op jit(solution)/shard_map/attend/pallas_call | solution.py:649
  28.1 6.1 %collective-permute-start.11 = (bf16[128,256]{1,0:T(8,128)(2,1)S(1)}, bf16[128,256]{1,0:T(8,128)(2,1)S(1)}, u32[]{:S(2)}, u32[]{:S(2)}) collective-permute-start(bf16[128,256]{1,0:T(8,128)(2,1)S(1)} %get-tuple-element.103), channel_id=1, source_target_pairs={{0,3},{1,2},{2,1},{3,0},{4,7},{5,6},{6,5},{7,4},{8,11},{9,10},{10,... | collective-permute-start | bytes 196616 | tf_op jit(solution)/shard_map/ppermute | solution.py:546
  34.2 1.9 %attend.5 = (bf16[256,4096]{1,0:T(8,128)(2,1)S(1)}, bf16[256,4096]{1,0:T(8,128)(2,1)S(1)}, f32[256,512]{1,0:T(8,128)S(1)}, f32[256,512]{1,0:T(8,128)S(1)}, bf16[...) custom-call(s32[8,128]{1,0:T(8,128)S(1)} %plan.1.plan_ref.refs_0_, ...), custom_call_target="tpu_custom_call", output_to_operand_aliasing={{0}: (8, {}), {1}: (9, {}), {2}: (10, {}), {3}: (11, {}), {... | custom-call | tf_op jit(solution)/shard_map/attend/pallas_call | solution.py:649
  36.1 1.2 %collective-permute-start.12 = (bf16[128,256]{1,0:T(8,128)(2,1)S(1)}, bf16[128,256]{1,0:T(8,128)(2,1)S(1)}, u32[]{:S(2)}, u32[]{:S(2)}) collective-permute-start(bf16[128,256]{1,0:T(8,128)(2,1)S(1)} %get-tuple-element.104), channel_id=1, source_target_pairs={{0,1},{1,0},{2,3},{3,2},{4,5},{5,4},{6,7},{7,6},{8,9},{9,8},{10,11... | collective-permute-start | bytes 196616 | tf_op jit(solution)/shard_map/ppermute | solution.py:546
  37.2 1.9 %collective-permute-start.16 = (bf16[4,128,256]{2,1,0:T(8,128)(2,1)S(1)}, bf16[4,128,256]{2,1,0:T(8,128)(2,1)S(1)}, u32[]{:S(2)}, u32[]{:S(2)}) collective-permute-start(bf16[4,128,256]{2,1,0:T(8,128)(2,1)S(1)} %get-tuple-element.113), channel_id=1, source_target_pairs={{1,0},{2,1},{3,2},{5,4},{6,5},{7,6},{9,8},{10,9},{11,10},{13,12},{... | collective-permute-start | bytes 786440 | tf_op jit(solution)/shard_map/ppermute | solution.py:32
  39.5 3.9 %collective-permute-start.15 = (bf16[128,256]{1,0:T(8,128)(2,1)S(1)}, bf16[128,256]{1,0:T(8,128)(2,1)S(1)}, u32[]{:S(2)}, u32[]{:S(2)}) collective-permute-start(bf16[128,256]{1,0:T(8,128)(2,1)S(1)} %gather.3.here_ref), channel_id=1, source_target_pairs={{0,20},{4,24},{8,28},{12,0},{16,4},{20,8},{24,12},{28,16},{1,21},{... | collective-permute-start | bytes 196616 | tf_op jit(solution)/shard_map/ppermute | solution.py:37
  43.8 1.3 %flush.2 = bf16[256,4096]{1,0:T(8,128)(2,1)} custom-call(bf16[256,4096]{1,0:T(8,128)(2,1)S(1)} %get-tuple-element.105.refs_0_), custom_call_target="tpu_custom_call" | custom-call | tf_op jit(solution)/shard_map/flush/pallas_call | solution.py:705
  45.1 1.4 %collective-permute-done.15.refs_2_ = bf16[128,256]{1,0:T(8,128)(2,1)S(1)} collective-permute-done((bf16[128,256]{1,0:T(8,128)(2,1)S(1)}, bf16[128,256]{1,0:T(8,128)(2,1)S(1)}, u32[]{:S(2)}, u32[]{:S(2)}) %collective-permute-start.15) | collective-permute-done | bytes 65568 | tf_op jit(solution)/shard_map/ppermute | solution.py:37
  47.4 1.0 %collective-permute-done.13.refs_0_ = bf16[128,256]{1,0:T(8,128)(2,1)S(1)} collective-permute-done((bf16[128,256]{1,0:T(8,128)(2,1)S(1)}, bf16[128,256]{1,0:T(8,128)(2,1)S(1)}, u32[]{:S(2)}, u32[]{:S(2)}) %collective-permute-start.13) | collective-permute-done | bytes 65568 | tf_op jit(solution)/shard_map/ppermute | solution.py:37
  48.8 2.3 %collective-permute-start.18 = (bf16[256,256]{1,0:T(8,128)(2,1)S(1)}, bf16[256,256]{1,0:T(8,128)(2,1)S(1)}, u32[]{:S(2)}, u32[]{:S(2)}) collective-permute-start(bf16[256,256]{1,0:T(8,128)(2,1)S(1)} %get-tuple-element.117), channel_id=1, source_target_pairs={{0,1},{1,2},{2,3},{3,0},{4,5},{5,6},{6,7},{7,4},{8,9},{9,10},{10,1... | collective-permute-start | bytes 393224 | tf_op jit(solution)/shard_map/ppermute | solution.py:37
  51.9 1.3 %flush.3 = bf16[256,4096]{1,0:T(8,128)(2,1)} custom-call(bf16[256,4096]{1,0:T(8,128)(2,1)S(1)} %get-tuple-element.112.refs_0_), custom_call_target="tpu_custom_call" | custom-call | tf_op jit(solution)/shard_map/flush/pallas_call | solution.py:705
  53.2 1.8 %collective-permute-done.17.far_ref = f32[8,128]{1,0:T(8,128)S(1)} collective-permute-done((f32[8,128]{1,0:T(8,128)S(1)}, f32[8,128]{1,0:T(8,128)S(1)}, u32[]{:S(2)}, u32[]{:S(2)}) %collective-permute-start.17) | collective-permute-done | bytes 4128 | tf_op jit(solution)/shard_map/ppermute | solution.py:37
  55.0 2.1 %collective-permute-done.19.refs_2_ = bf16[256,256]{1,0:T(8,128)(2,1)S(1)} collective-permute-done((bf16[256,256]{1,0:T(8,128)(2,1)S(1)}, bf16[256,256]{1,0:T(8,128)(2,1)S(1)}, u32[]{:S(2)}, u32[]{:S(2)}) %collective-permute-start.19) | collective-permute-done | bytes 131104 | tf_op jit(solution)/shard_map/ppermute | solution.py:37
  (33 shorter events, 7.2 us)
Async XLA Ops:
  1.8 6.5 %collective-permute-start = (bf16[256,256]{1,0:T(8,128)(2,1)S(1)}, bf16[256,256]{1,0:T(8,128)(2,1)S(1)}, u32[]{:S(2)}, u32[]{:S(2)}) collective-permute-start(bf16[256,256]{1,0:T(8,128)(2,1)S(1)} %get-tuple-element.65), channel_id=1, source_target_pairs={{0,1},{1,2},{2,3},{3,0},{4,5},{5,6},{6,7},{7,4},{8,9},{9,10},{10,1... | collective-permute-start | bytes 393224 | tf_op jit(solution)/shard_map/ppermute | solution.py:37
  3.7 6.2 %collective-permute-start.1 = (bf16[256,256]{1,0:T(8,128)(2,1)S(1)}, bf16[256,256]{1,0:T(8,128)(2,1)S(1)}, u32[]{:S(2)}, u32[]{:S(2)}) collective-permute-start(bf16[256,256]{1,0:T(8,128)(2,1)S(1)} %get-tuple-element.66), channel_id=1, source_target_pairs={{0,2},{1,3},{2,0},{3,1},{4,6},{5,7},{6,4},{7,5},{8,10},{9,11},{10,... | collective-permute-start | bytes 393224 | tf_op jit(solution)/shard_map/ppermute | solution.py:37
  3.9 6.6 %collective-permute-start.2 = (bf16[256,256]{1,0:T(8,128)(2,1)S(1)}, bf16[256,256]{1,0:T(8,128)(2,1)S(1)}, u32[]{:S(2)}, u32[]{:S(2)}) collective-permute-start(bf16[256,256]{1,0:T(8,128)(2,1)S(1)} %get-tuple-element.67), channel_id=1, source_target_pairs={{0,3},{1,0},{2,1},{3,2},{4,7},{5,4},{6,5},{7,6},{8,11},{9,8},{10,9... | collective-permute-start | bytes 393224 | tf_op jit(solution)/shard_map/ppermute | solution.py:37
  4.1 19.7 %collective-permute-start.6 = (bf16[4,128,256]{2,1,0:T(8,128)(2,1)S(1)}, bf16[4,128,256]{2,1,0:T(8,128)(2,1)S(1)}, u32[]{:S(2)}, u32[]{:S(2)}) collective-permute-start(bf16[4,128,256]{2,1,0:T(8,128)(2,1)S(1)} %get-tuple-element.86), channel_id=1, source_target_pairs={{0,1},{1,2},{2,3},{4,5},{5,6},{6,7},{8,9},{9,10},{10,11},{12,13},{... | collective-permute-start | bytes 786440 | tf_op jit(solution)/shard_map/ppermute | solution.py:32
  10.9 7.3 %collective-permute-start.3 = (bf16[128,256]{1,0:T(8,128)(2,1)S(1)}, bf16[128,256]{1,0:T(8,128)(2,1)S(1)}, u32[]{:S(2)}, u32[]{:S(2)}) collective-permute-start(bf16[128,256]{1,0:T(8,128)(2,1)S(1)} %get-tuple-element.75), channel_id=1, source_target_pairs={{0,12},{4,16},{8,20},{12,24},{16,28},{20,0},{24,4},{28,8},{1,13},{... | collective-permute-start | bytes 196616 | tf_op jit(solution)/shard_map/ppermute | solution.py:37
  13.2 4.9 %collective-permute-start.4 = (bf16[128,256]{1,0:T(8,128)(2,1)S(1)}, bf16[128,256]{1,0:T(8,128)(2,1)S(1)}, u32[]{:S(2)}, u32[]{:S(2)}) collective-permute-start(bf16[128,256]{1,0:T(8,128)(2,1)S(1)} %get-tuple-element.76), channel_id=1, source_target_pairs={{0,8},{4,12},{8,16},{12,20},{16,24},{20,28},{24,0},{28,4},{1,9},{5... | collective-permute-start | bytes 196616 | tf_op jit(solution)/shard_map/ppermute | solution.py:37
  14.5 3.7 %collective-permute-start.5 = (bf16[128,256]{1,0:T(8,128)(2,1)S(1)}, bf16[128,256]{1,0:T(8,128)(2,1)S(1)}, u32[]{:S(2)}, u32[]{:S(2)}) collective-permute-start(bf16[128,256]{1,0:T(8,128)(2,1)S(1)} %get-tuple-element.77), channel_id=1, source_target_pairs={{0,4},{4,8},{8,12},{12,16},{16,20},{20,24},{24,28},{28,0},{1,5},{5... | collective-permute-start | bytes 196616 | tf_op jit(solution)/shard_map/ppermute | solution.py:37
  18.4 5.5 %collective-permute-start.9 = (bf16[128,256]{1,0:T(8,128)(2,1)S(1)}, bf16[128,256]{1,0:T(8,128)(2,1)S(1)}, u32[]{:S(2)}, u32[]{:S(2)}) collective-permute-start(bf16[128,256]{1,0:T(8,128)(2,1)S(1)} %arrive.1.refs_7_), channel_id=1, source_target_pairs={{0,3},{1,2},{2,1},{3,0},{4,7},{5,6},{6,5},{7,4},{8,11},{9,10},{10,... | collective-permute-start | bytes 196616 | tf_op jit(solution)/shard_map/ppermute | solution.py:546
  19.8 4.6 %collective-permute-start.8 = (bf16[128,256]{1,0:T(8,128)(2,1)S(1)}, bf16[128,256]{1,0:T(8,128)(2,1)S(1)}, u32[]{:S(2)}, u32[]{:S(2)}) collective-permute-start(bf16[128,256]{1,0:T(8,128)(2,1)S(1)} %arrive.1.refs_7_), channel_id=1, source_target_pairs={{0,2},{1,3},{2,0},{3,1},{4,6},{5,7},{6,4},{7,5},{8,10},{9,11},{10,... | collective-permute-start | bytes 196616 | tf_op jit(solution)/shard_map/ppermute | solution.py:546
  22.0 12.2 %collective-permute-start.7 = (bf16[128,256]{1,0:T(8,128)(2,1)S(1)}, bf16[128,256]{1,0:T(8,128)(2,1)S(1)}, u32[]{:S(2)}, u32[]{:S(2)}) collective-permute-start(bf16[128,256]{1,0:T(8,128)(2,1)S(1)} %arrive.1.refs_7_), channel_id=1, source_target_pairs={{0,1},{1,0},{2,3},{3,2},{4,5},{5,4},{6,7},{7,6},{8,9},{9,8},{10,11... | collective-permute-start | bytes 196616 | tf_op jit(solution)/shard_map/ppermute | solution.py:546
  28.0 11.1 %collective-permute-start.10 = (bf16[128,256]{1,0:T(8,128)(2,1)S(1)}, bf16[128,256]{1,0:T(8,128)(2,1)S(1)}, u32[]{:S(2)}, u32[]{:S(2)}) collective-permute-start(bf16[128,256]{1,0:T(8,128)(2,1)S(1)} %get-tuple-element.102), channel_id=1, source_target_pairs={{0,2},{1,3},{2,0},{3,1},{4,6},{5,7},{6,4},{7,5},{8,10},{9,11},{10,... | collective-permute-start | bytes 196616 | tf_op jit(solution)/shard_map/ppermute | solution.py:546
  28.1 11.1 %collective-permute-start.11 = (bf16[128,256]{1,0:T(8,128)(2,1)S(1)}, bf16[128,256]{1,0:T(8,128)(2,1)S(1)}, u32[]{:S(2)}, u32[]{:S(2)}) collective-permute-start(bf16[128,256]{1,0:T(8,128)(2,1)S(1)} %get-tuple-element.103), channel_id=1, source_target_pairs={{0,3},{1,2},{2,1},{3,0},{4,7},{5,6},{6,5},{7,4},{8,11},{9,10},{10,... | collective-permute-start | bytes 196616 | tf_op jit(solution)/shard_map/ppermute | solution.py:546
  36.1 3.3 %collective-permute-start.12 = (bf16[128,256]{1,0:T(8,128)(2,1)S(1)}, bf16[128,256]{1,0:T(8,128)(2,1)S(1)}, u32[]{:S(2)}, u32[]{:S(2)}) collective-permute-start(bf16[128,256]{1,0:T(8,128)(2,1)S(1)} %get-tuple-element.104), channel_id=1, source_target_pairs={{0,1},{1,0},{2,3},{3,2},{4,5},{5,4},{6,7},{7,6},{8,9},{9,8},{10,11... | collective-permute-start | bytes 196616 | tf_op jit(solution)/shard_map/ppermute | solution.py:546
  37.2 17.8 %collective-permute-start.16 = (bf16[4,128,256]{2,1,0:T(8,128)(2,1)S(1)}, bf16[4,128,256]{2,1,0:T(8,128)(2,1)S(1)}, u32[]{:S(2)}, u32[]{:S(2)}) collective-permute-start(bf16[4,128,256]{2,1,0:T(8,128)(2,1)S(1)} %get-tuple-element.113), channel_id=1, source_target_pairs={{1,0},{2,1},{3,2},{5,4},{6,5},{7,6},{9,8},{10,9},{11,10},{13,12},{... | collective-permute-start | bytes 786440 | tf_op jit(solution)/shard_map/ppermute | solution.py:32
  39.5 7.0 %collective-permute-start.15 = (bf16[128,256]{1,0:T(8,128)(2,1)S(1)}, bf16[128,256]{1,0:T(8,128)(2,1)S(1)}, u32[]{:S(2)}, u32[]{:S(2)}) collective-permute-start(bf16[128,256]{1,0:T(8,128)(2,1)S(1)} %gather.3.here_ref), channel_id=1, source_target_pairs={{0,20},{4,24},{8,28},{12,0},{16,4},{20,8},{24,12},{28,16},{1,21},{... | collective-permute-start | bytes 196616 | tf_op jit(solution)/shard_map/ppermute | solution.py:37
  43.4 4.0 %collective-permute-start.14 = (bf16[128,256]{1,0:T(8,128)(2,1)S(1)}, bf16[128,256]{1,0:T(8,128)(2,1)S(1)}, u32[]{:S(2)}, u32[]{:S(2)}) collective-permute-start(bf16[128,256]{1,0:T(8,128)(2,1)S(1)} %gather.3.here_ref), channel_id=1, source_target_pairs={{0,24},{4,28},{8,0},{12,4},{16,8},{20,12},{24,16},{28,20},{1,25},{... | collective-permute-start | bytes 196616 | tf_op jit(solution)/shard_map/ppermute | solution.py:37
  43.7 4.7 %collective-permute-start.13 = (bf16[128,256]{1,0:T(8,128)(2,1)S(1)}, bf16[128,256]{1,0:T(8,128)(2,1)S(1)}, u32[]{:S(2)}, u32[]{:S(2)}) collective-permute-start(bf16[128,256]{1,0:T(8,128)(2,1)S(1)} %gather.3.here_ref), channel_id=1, source_target_pairs={{0,28},{4,0},{8,4},{12,8},{16,12},{20,16},{24,20},{28,24},{1,29},{... | collective-permute-start | bytes 196616 | tf_op jit(solution)/shard_map/ppermute | solution.py:37
  48.8 6.2 %collective-permute-start.18 = (bf16[256,256]{1,0:T(8,128)(2,1)S(1)}, bf16[256,256]{1,0:T(8,128)(2,1)S(1)}, u32[]{:S(2)}, u32[]{:S(2)}) collective-permute-start(bf16[256,256]{1,0:T(8,128)(2,1)S(1)} %get-tuple-element.117), channel_id=1, source_target_pairs={{0,1},{1,2},{2,3},{3,0},{4,5},{5,6},{6,7},{7,4},{8,9},{9,10},{10,1... | collective-permute-start | bytes 393224 | tf_op jit(solution)/shard_map/ppermute | solution.py:37
  51.2 6.0 %collective-permute-start.19 = (bf16[256,256]{1,0:T(8,128)(2,1)S(1)}, bf16[256,256]{1,0:T(8,128)(2,1)S(1)}, u32[]{:S(2)}, u32[]{:S(2)}) collective-permute-start(bf16[256,256]{1,0:T(8,128)(2,1)S(1)} %get-tuple-element.118), channel_id=1, source_target_pairs={{0,2},{1,3},{2,0},{3,1},{4,6},{5,7},{6,4},{7,5},{8,10},{9,11},{10,... | collective-permute-start | bytes 393224 | tf_op jit(solution)/shard_map/ppermute | solution.py:37
  51.2 6.3 %collective-permute-start.20 = (bf16[256,256]{1,0:T(8,128)(2,1)S(1)}, bf16[256,256]{1,0:T(8,128)(2,1)S(1)}, u32[]{:S(2)}, u32[]{:S(2)}) collective-permute-start(bf16[256,256]{1,0:T(8,128)(2,1)S(1)} %get-tuple-element.119), channel_id=1, source_target_pairs={{0,3},{1,0},{2,1},{3,2},{4,7},{5,4},{6,5},{7,6},{8,11},{9,8},{10,9... | collective-permute-start | bytes 393224 | tf_op jit(solution)/shard_map/ppermute | solution.py:37
  51.7 3.4 %collective-permute-start.17 = (f32[8,128]{1,0:T(8,128)S(1)}, f32[8,128]{1,0:T(8,128)S(1)}, u32[]{:S(2)}, u32[]{:S(2)}) collective-permute-start(f32[8,128]{1,0:T(8,128)S(1)} %get-tuple-element.111.sink_ref), channel_id=1, source_target_pairs={{0,16},{4,20},{8,24},{12,28},{16,0},{20,4},{24,8},{28,12},{1,17},{... | collective-permute-start | bytes 12296 | tf_op jit(solution)/shard_map/ppermute | solution.py:37

commit v13 on v12

--- a/solution.py
+++ b/solution.py
@@ -500,7 +500,7 @@
     for distance, in_ref in enumerate(in_refs, 1):
         valid, place = planned_tail(plan_ref, distance)
         sink_row = sink_row + row_join(in_ref[:16])
-        wanted = lax.rem(place // blocks_here - head + slots, slots)
+        wanted = (place // blocks_here) ^ head
         here = pl.ds(pl.multiple_of(place % blocks_here * WINDOW, WINDOW), WINDOW)
         for step, out_ref in enumerate(out_refs):
 
@@ -517,8 +517,8 @@
     slots, rows = len(tail_refs), dk_ref.shape[0]
     width = tails.shape[2] // 2
     head = lax.axis_index("head")
-    for step, tail_ref in enumerate(tail_refs):
-        tails[lax.rem(head - step + slots, slots)] = tail_ref[...]
+    for bits, tail_ref in zip((*range(2, slots), 1, 0), tail_refs):
+        tails[head ^ bits] = tail_ref[...]
     halo_k = jnp.concatenate([halo_ref[pair][:, :128] for pair in range(PAIRS)], axis=1)
     halo_v = jnp.concatenate([halo_ref[pair][:, 128:] for pair in range(PAIRS)], axis=1)
     for in_ref, halo, at, out_ref in (
@@ -725,7 +725,8 @@
         compiler_params=PARAMS,
         name="land",
     )(plan, quarter_grad, *returned)
-    tails_back = swap(landed, "head")
+    back = trade(landed, "head")
+    tails_back = [*back[2:], back[1], back[0]]
     query_grad, _ = lax.optimization_barrier((query_grad, sink_near))
     query_grad = flush(query_grad)
     span = LAG + 1

time: 59.3 us -> 59 us (level)
  Pallas kernels: 16.7 us -> 22.6 us
  starting transfers between devices: 30.8 us -> 25.2 us
  waiting for transfers between devices: 10.2 us -> 9.44 us
    pallas_call x3, Pallas kernels: 7.46 us -> 13.4 us  [attend(): pl.pallas_call(functools.partial(attend_kernel, blocks_here, head_count,...]
    ppermute x6 -> x9, starting transfers between devices: 10.9 us -> 7.73 us  [trade(): lax.ppermute(values[bits], axis, [(place, place ^ bits) for place in plac...]
    ppermute x13 -> x10, starting transfers between devices: 14.5 us -> 11.7 us  [ring(): lax.ppermute(value, axis, [(source, (source + steps) % count) for source...]
    ppermute x13 -> x10, waiting for transfers between devices: 9.76 us -> 7.33 us  [ring(): lax.ppermute(value, axis, [(source, (source + steps) % count) for source...]
    ppermute x6 -> x9, waiting for transfers between devices: 0.46 us -> 2.11 us  [trade(): lax.ppermute(values[bits], axis, [(place, place ^ bits) for place in plac...]
  transfers between devices with their start and end apart: 21 -> 21, of which waited for: 10 -> 7; matrix products, arithmetic and copies ran while one was open for 0% -> 0% of each run, Pallas kernels for 25% -> 35%
where the time goes in v13:
time: 59 us; the launch traced here: 58 us
  starting transfers between devices  25.2 us (43%)
  Pallas kernels  22.6 us (38%)
  waiting for transfers between devices  9.44 us (16%)
  between operations  0.79 us (1%)
    pallas_call x3, Pallas kernels, attend(): pl.pallas_call(functools.partial(attend_kernel, blocks_here, head_count,...  13.4 us
    ppermute x10, starting transfers between devices, ring(): lax.ppermute(value, axis, [(source, (source + steps) % count) for source...  11.7 us
    ppermute x9, starting transfers between devices, trade(): lax.ppermute(values[bits], axis, [(place, place ^ bits) for place in plac...  7.73 us
    ppermute x10, waiting for transfers between devices, ring(): lax.ppermute(value, axis, [(source, (source + steps) % count) for source...  7.33 us
    ppermute x2, starting transfers between devices, shift(): lax.ppermute(value, axis, [(source, source + steps) for source in range(l...  5.79 us
    pallas_call x2, Pallas kernels, flush(): pl.pallas_call(stage_kernel, out_shape=pltpu.HBM(value.shape, BF16), in_s...  2.65 us
    pallas_call x1, Pallas kernels, local(): pl.pallas_call(stage_kernel, out_shape=(pltpu.VMEM(queries.shape, BF16),)...  2.26 us
    ppermute x9, waiting for transfers between devices, trade(): lax.ppermute(values[bits], axis, [(place, place ^ bits) for place in plac...  2.11 us
  transfers between devices with their start and end apart: 21, of which 7 were waited for; matrix products, arithmetic and copies ran while one was open for 0% of the time, Pallas kernels for 35%

profile of v13, /device:TPU:3, one launch (start us, length us, event | category | flops | bytes accessed | tf_op | source)
XLA Modules:
  0.0 58.0 jit_solution(817758767323874716)
XLA Ops:
  0.6 1.2 %pack.1 = (bf16[256,256]{1,0:T(8,128)(2,1)S(1)}, bf16[256,256]{1,0:T(8,128)(2,1)S(1)}, bf16[256,256]{1,0:T(8,128)(2,1)S(1)}, bf16[256,256]{1,0:T(8,128)(2,1)S(1)...) custom-call(f32[16]{0:T(128)} %sink_hbm.1, ...), custom_call_target="tpu_custom_call" | custom-call | tf_op jit(solution)/shard_map/pack/pallas_call | solution.py:570
  1.8 1.9 %collective-permute-start = (bf16[256,256]{1,0:T(8,128)(2,1)S(1)}, bf16[256,256]{1,0:T(8,128)(2,1)S(1)}, u32[]{:S(2)}, u32[]{:S(2)}) collective-permute-start(bf16[256,256]{1,0:T(8,128)(2,1)S(1)} %get-tuple-element.65), channel_id=1, source_target_pairs={{0,1},{1,2},{2,3},{3,0},{4,5},{5,6},{6,7},{7,4},{8,9},{9,10},{10,1... | collective-permute-start | bytes 393224 | tf_op jit(solution)/shard_map/ppermute | solution.py:37
  4.1 3.4 %collective-permute-start.6 = (bf16[4,128,256]{2,1,0:T(8,128)(2,1)S(1)}, bf16[4,128,256]{2,1,0:T(8,128)(2,1)S(1)}, u32[]{:S(2)}, u32[]{:S(2)}) collective-permute-start(bf16[4,128,256]{2,1,0:T(8,128)(2,1)S(1)} %get-tuple-element.86), channel_id=1, source_target_pairs={{0,1},{1,2},{2,3},{4,5},{5,6},{6,7},{8,9},{9,10},{10,11},{12,13},{... | collective-permute-start | bytes 786440 | tf_op jit(solution)/shard_map/ppermute | solution.py:32
  8.3 1.5 %collective-permute-done.1.refs_2_ = bf16[256,256]{1,0:T(8,128)(2,1)S(1)} collective-permute-done((bf16[256,256]{1,0:T(8,128)(2,1)S(1)}, bf16[256,256]{1,0:T(8,128)(2,1)S(1)}, u32[]{:S(2)}, u32[]{:S(2)}) %collective-permute-start.1) | collective-permute-done | bytes 131104 | tf_op jit(solution)/shard_map/ppermute | solution.py:37
  10.9 2.3 %collective-permute-start.3 = (bf16[128,256]{1,0:T(8,128)(2,1)S(1)}, bf16[128,256]{1,0:T(8,128)(2,1)S(1)}, u32[]{:S(2)}, u32[]{:S(2)}) collective-permute-start(bf16[128,256]{1,0:T(8,128)(2,1)S(1)} %get-tuple-element.75), channel_id=1, source_target_pairs={{0,12},{4,16},{8,20},{12,24},{16,28},{20,0},{24,4},{28,8},{1,13},{... | collective-permute-start | bytes 196616 | tf_op jit(solution)/shard_map/ppermute | solution.py:37
  13.2 1.3 %collective-permute-start.4 = (bf16[128,256]{1,0:T(8,128)(2,1)S(1)}, bf16[128,256]{1,0:T(8,128)(2,1)S(1)}, u32[]{:S(2)}, u32[]{:S(2)}) collective-permute-start(bf16[128,256]{1,0:T(8,128)(2,1)S(1)} %get-tuple-element.76), channel_id=1, source_target_pairs={{0,8},{4,12},{8,16},{12,20},{16,24},{20,28},{24,0},{28,4},{1,9},{5... | collective-permute-start | bytes 196616 | tf_op jit(solution)/shard_map/ppermute | solution.py:37
  14.5 1.2 %collective-permute-start.5 = (bf16[128,256]{1,0:T(8,128)(2,1)S(1)}, bf16[128,256]{1,0:T(8,128)(2,1)S(1)}, u32[]{:S(2)}, u32[]{:S(2)}) collective-permute-start(bf16[128,256]{1,0:T(8,128)(2,1)S(1)} %get-tuple-element.77), channel_id=1, source_target_pairs={{0,4},{4,8},{8,12},{12,16},{16,20},{20,24},{24,28},{28,0},{1,5},{5... | collective-permute-start | bytes 196616 | tf_op jit(solution)/shard_map/ppermute | solution.py:37
  15.9 2.3 %stage.1 = (bf16[256,4096]{1,0:T(8,128)(2,1)S(1)}, bf16[256,4096]{1,0:T(8,128)(2,1)S(1)}) custom-call(bf16[256,4096]{1,0:T(8,128)(2,1)} %refs_0_, bf16[256,4096]{1,0:T(8,128)(2,1)} %refs_1_), custom_call_target="tpu_custom_call" | custom-call | tf_op jit(solution)/shard_map/stage/pallas_call | solution.py:615
  18.4 1.4 %collective-permute-start.9 = (bf16[128,256]{1,0:T(8,128)(2,1)S(1)}, bf16[128,256]{1,0:T(8,128)(2,1)S(1)}, u32[]{:S(2)}, u32[]{:S(2)}) collective-permute-start(bf16[128,256]{1,0:T(8,128)(2,1)S(1)} %arrive.1.refs_7_), channel_id=1, source_target_pairs={{0,3},{1,2},{2,1},{3,0},{4,7},{5,6},{6,5},{7,4},{8,11},{9,10},{10,... | collective-permute-start | bytes 196616 | tf_op jit(solution)/shard_map/ppermute | solution.py:546
  19.8 2.2 %collective-permute-start.8 = (bf16[128,256]{1,0:T(8,128)(2,1)S(1)}, bf16[128,256]{1,0:T(8,128)(2,1)S(1)}, u32[]{:S(2)}, u32[]{:S(2)}) collective-permute-start(bf16[128,256]{1,0:T(8,128)(2,1)S(1)} %arrive.1.refs_7_), channel_id=1, source_target_pairs={{0,2},{1,3},{2,0},{3,1},{4,6},{5,7},{6,4},{7,5},{8,10},{9,11},{10,... | collective-permute-start | bytes 196616 | tf_op jit(solution)/shard_map/ppermute | solution.py:546
  22.0 3.4 %attend.3 = (bf16[256,4096]{1,0:T(8,128)(2,1)S(1)}, bf16[256,4096]{1,0:T(8,128)(2,1)S(1)}, f32[256,512]{1,0:T(8,128)S(1)}, f32[256,512]{1,0:T(8,128)S(1)}, bf16[...) custom-call(s32[8,128]{1,0:T(8,128)S(1)} %plan.1.plan_ref.refs_0_, f32[64,128]{1,0:T(8,128)S(1)} %sinks.1.refs_1_, ...), custom_call_target="tpu_custom_call" | custom-call | tf_op jit(solution)/shard_map/attend/pallas_call | solution.py:649
  25.4 6.6 %attend.4 = (bf16[256,4096]{1,0:T(8,128)(2,1)S(1)}, bf16[256,4096]{1,0:T(8,128)(2,1)S(1)}, f32[256,512]{1,0:T(8,128)S(1)}, f32[256,512]{1,0:T(8,128)S(1)}, bf16[...) custom-call(s32[8,128]{1,0:T(8,128)S(1)} %plan.1.plan_ref.refs_0_, ...), custom_call_target="tpu_custom_call", output_to_operand_aliasing={{0}: (9, {}), {1}: (10, {}), {2}: (11, {}), {3}: (12, {}), ... | custom-call | tf_op jit(solution)/shard_map/attend/pallas_call | solution.py:649
  32.0 1.3 %collective-permute-start.10 = (bf16[128,256]{1,0:T(8,128)(2,1)S(1)}, bf16[128,256]{1,0:T(8,128)(2,1)S(1)}, u32[]{:S(2)}, u32[]{:S(2)}) collective-permute-start(bf16[128,256]{1,0:T(8,128)(2,1)S(1)} %get-tuple-element.102), channel_id=1, source_target_pairs={{0,2},{1,3},{2,0},{3,1},{4,6},{5,7},{6,4},{7,5},{8,10},{9,11},{10,... | collective-permute-start | bytes 196616 | tf_op jit(solution)/shard_map/ppermute | solution.py:546
  33.3 3.4 %attend.5 = (bf16[256,4096]{1,0:T(8,128)(2,1)S(1)}, bf16[256,4096]{1,0:T(8,128)(2,1)S(1)}, f32[256,512]{1,0:T(8,128)S(1)}, f32[256,512]{1,0:T(8,128)S(1)}, bf16[...) custom-call(s32[8,128]{1,0:T(8,128)S(1)} %plan.1.plan_ref.refs_0_, ...), custom_call_target="tpu_custom_call", output_to_operand_aliasing={{0}: (8, {}), {1}: (9, {}), {2}: (10, {}), {3}: (11, {}), {... | custom-call | tf_op jit(solution)/shard_map/attend/pallas_call | solution.py:649
  36.7 2.4 %collective-permute-start.16 = (bf16[4,128,256]{2,1,0:T(8,128)(2,1)S(1)}, bf16[4,128,256]{2,1,0:T(8,128)(2,1)S(1)}, u32[]{:S(2)}, u32[]{:S(2)}) collective-permute-start(bf16[4,128,256]{2,1,0:T(8,128)(2,1)S(1)} %get-tuple-element.113), channel_id=1, source_target_pairs={{1,0},{2,1},{3,2},{5,4},{6,5},{7,6},{9,8},{10,9},{11,10},{13,12},{... | collective-permute-start | bytes 786440 | tf_op jit(solution)/shard_map/ppermute | solution.py:32
  40.4 3.4 %collective-permute-start.14 = (bf16[128,256]{1,0:T(8,128)(2,1)S(1)}, bf16[128,256]{1,0:T(8,128)(2,1)S(1)}, u32[]{:S(2)}, u32[]{:S(2)}) collective-permute-start(bf16[128,256]{1,0:T(8,128)(2,1)S(1)} %gather.3.here_ref), channel_id=1, source_target_pairs={{0,24},{4,28},{8,0},{12,4},{16,8},{20,12},{24,16},{28,20},{1,25},{... | collective-permute-start | bytes 196616 | tf_op jit(solution)/shard_map/ppermute | solution.py:37
  43.7 1.3 %flush.2 = bf16[256,4096]{1,0:T(8,128)(2,1)} custom-call(bf16[256,4096]{1,0:T(8,128)(2,1)S(1)} %get-tuple-element.105.refs_0_), custom_call_target="tpu_custom_call" | custom-call | tf_op jit(solution)/shard_map/flush/pallas_call | solution.py:705
  45.0 1.4 %collective-permute-done.15.refs_2_ = bf16[128,256]{1,0:T(8,128)(2,1)S(1)} collective-permute-done((bf16[128,256]{1,0:T(8,128)(2,1)S(1)}, bf16[128,256]{1,0:T(8,128)(2,1)S(1)}, u32[]{:S(2)}, u32[]{:S(2)}) %collective-permute-start.15) | collective-permute-done | bytes 65568 | tf_op jit(solution)/shard_map/ppermute | solution.py:37
  46.5 1.9 %collective-permute-done.13.refs_0_ = bf16[128,256]{1,0:T(8,128)(2,1)S(1)} collective-permute-done((bf16[128,256]{1,0:T(8,128)(2,1)S(1)}, bf16[128,256]{1,0:T(8,128)(2,1)S(1)}, u32[]{:S(2)}, u32[]{:S(2)}) %collective-permute-start.13) | collective-permute-done | bytes 65568 | tf_op jit(solution)/shard_map/ppermute | solution.py:37
  49.1 2.2 %collective-permute-start.19 = (bf16[256,256]{1,0:T(8,128)(2,1)S(1)}, bf16[256,256]{1,0:T(8,128)(2,1)S(1)}, u32[]{:S(2)}, u32[]{:S(2)}) collective-permute-start(bf16[256,256]{1,0:T(8,128)(2,1)S(1)} %get-tuple-element.117), channel_id=1, source_target_pairs={{0,3},{1,2},{2,1},{3,0},{4,7},{5,6},{6,5},{7,4},{8,11},{9,10},{10,... | collective-permute-start | bytes 393224 | tf_op jit(solution)/shard_map/ppermute | solution.py:546
  51.8 1.3 %flush.3 = bf16[256,4096]{1,0:T(8,128)(2,1)} custom-call(bf16[256,4096]{1,0:T(8,128)(2,1)S(1)} %get-tuple-element.112.refs_0_), custom_call_target="tpu_custom_call" | custom-call | tf_op jit(solution)/shard_map/flush/pallas_call | solution.py:705
  53.2 1.8 %collective-permute-done.17.far_ref = f32[8,128]{1,0:T(8,128)S(1)} collective-permute-done((f32[8,128]{1,0:T(8,128)S(1)}, f32[8,128]{1,0:T(8,128)S(1)}, u32[]{:S(2)}, u32[]{:S(2)}) %collective-permute-start.17) | collective-permute-done | bytes 4128 | tf_op jit(solution)/shard_map/ppermute | solution.py:37
  54.9 2.1 %collective-permute-done.19.refs_1_ = bf16[256,256]{1,0:T(8,128)(2,1)S(1)} collective-permute-done((bf16[256,256]{1,0:T(8,128)(2,1)S(1)}, bf16[256,256]{1,0:T(8,128)(2,1)S(1)}, u32[]{:S(2)}, u32[]{:S(2)}) %collective-permute-start.19) | collective-permute-done | bytes 131104 | tf_op jit(solution)/shard_map/ppermute | solution.py:546
  57.0 0.9 %total.1 = (bf16[256,512]{1,0:T(8,128)(2,1)}, bf16[256,512]{1,0:T(8,128)(2,1)}, f32[16]{0:T(128)}) custom-call(bf16[4,128,256]{2,1,0:T(8,128)(2,1)S(1)} %collective-permute-done.16.halo_ref, f32[256,512]{1,0:T(8,128)S(1)} %get-tuple-element.114.dk_ref, f32[256,512]{1,0:T(8,128)S(1)} %get-tuple-element.115.dv_ref, f32[8,128]{1,0:T(8,128)S(1)} %get-tuple-element.111.sink_ref, ...), custom_call_target="tpu_custom_call" | custom-call | tf_op jit(solution)/shard_map/total/pallas_call | solution.py:737
  (33 shorter events, 5.1 us)
Async XLA Ops:
  1.8 6.5 %collective-permute-start = (bf16[256,256]{1,0:T(8,128)(2,1)S(1)}, bf16[256,256]{1,0:T(8,128)(2,1)S(1)}, u32[]{:S(2)}, u32[]{:S(2)}) collective-permute-start(bf16[256,256]{1,0:T(8,128)(2,1)S(1)} %get-tuple-element.65), channel_id=1, source_target_pairs={{0,1},{1,2},{2,3},{3,0},{4,5},{5,6},{6,7},{7,4},{8,9},{9,10},{10,1... | collective-permute-start | bytes 393224 | tf_op jit(solution)/shard_map/ppermute | solution.py:37
  3.7 6.2 %collective-permute-start.1 = (bf16[256,256]{1,0:T(8,128)(2,1)S(1)}, bf16[256,256]{1,0:T(8,128)(2,1)S(1)}, u32[]{:S(2)}, u32[]{:S(2)}) collective-permute-start(bf16[256,256]{1,0:T(8,128)(2,1)S(1)} %get-tuple-element.66), channel_id=1, source_target_pairs={{0,2},{1,3},{2,0},{3,1},{4,6},{5,7},{6,4},{7,5},{8,10},{9,11},{10,... | collective-permute-start | bytes 393224 | tf_op jit(solution)/shard_map/ppermute | solution.py:37
  3.9 6.6 %collective-permute-start.2 = (bf16[256,256]{1,0:T(8,128)(2,1)S(1)}, bf16[256,256]{1,0:T(8,128)(2,1)S(1)}, u32[]{:S(2)}, u32[]{:S(2)}) collective-permute-start(bf16[256,256]{1,0:T(8,128)(2,1)S(1)} %get-tuple-element.67), channel_id=1, source_target_pairs={{0,3},{1,0},{2,1},{3,2},{4,7},{5,4},{6,5},{7,6},{8,11},{9,8},{10,9... | collective-permute-start | bytes 393224 | tf_op jit(solution)/shard_map/ppermute | solution.py:37
  4.1 21.2 %collective-permute-start.6 = (bf16[4,128,256]{2,1,0:T(8,128)(2,1)S(1)}, bf16[4,128,256]{2,1,0:T(8,128)(2,1)S(1)}, u32[]{:S(2)}, u32[]{:S(2)}) collective-permute-start(bf16[4,128,256]{2,1,0:T(8,128)(2,1)S(1)} %get-tuple-element.86), channel_id=1, source_target_pairs={{0,1},{1,2},{2,3},{4,5},{5,6},{6,7},{8,9},{9,10},{10,11},{12,13},{... | collective-permute-start | bytes 786440 | tf_op jit(solution)/shard_map/ppermute | solution.py:32
  10.9 7.3 %collective-permute-start.3 = (bf16[128,256]{1,0:T(8,128)(2,1)S(1)}, bf16[128,256]{1,0:T(8,128)(2,1)S(1)}, u32[]{:S(2)}, u32[]{:S(2)}) collective-permute-start(bf16[128,256]{1,0:T(8,128)(2,1)S(1)} %get-tuple-element.75), channel_id=1, source_target_pairs={{0,12},{4,16},{8,20},{12,24},{16,28},{20,0},{24,4},{28,8},{1,13},{... | collective-permute-start | bytes 196616 | tf_op jit(solution)/shard_map/ppermute | solution.py:37
  13.2 4.9 %collective-permute-start.4 = (bf16[128,256]{1,0:T(8,128)(2,1)S(1)}, bf16[128,256]{1,0:T(8,128)(2,1)S(1)}, u32[]{:S(2)}, u32[]{:S(2)}) collective-permute-start(bf16[128,256]{1,0:T(8,128)(2,1)S(1)} %get-tuple-element.76), channel_id=1, source_target_pairs={{0,8},{4,12},{8,16},{12,20},{16,24},{20,28},{24,0},{28,4},{1,9},{5... | collective-permute-start | bytes 196616 | tf_op jit(solution)/shard_map/ppermute | solution.py:37
  14.5 3.7 %collective-permute-start.5 = (bf16[128,256]{1,0:T(8,128)(2,1)S(1)}, bf16[128,256]{1,0:T(8,128)(2,1)S(1)}, u32[]{:S(2)}, u32[]{:S(2)}) collective-permute-start(bf16[128,256]{1,0:T(8,128)(2,1)S(1)} %get-tuple-element.77), channel_id=1, source_target_pairs={{0,4},{4,8},{8,12},{12,16},{16,20},{20,24},{24,28},{28,0},{1,5},{5... | collective-permute-start | bytes 196616 | tf_op jit(solution)/shard_map/ppermute | solution.py:37
  18.4 7.0 %collective-permute-start.9 = (bf16[128,256]{1,0:T(8,128)(2,1)S(1)}, bf16[128,256]{1,0:T(8,128)(2,1)S(1)}, u32[]{:S(2)}, u32[]{:S(2)}) collective-permute-start(bf16[128,256]{1,0:T(8,128)(2,1)S(1)} %arrive.1.refs_7_), channel_id=1, source_target_pairs={{0,3},{1,2},{2,1},{3,0},{4,7},{5,6},{6,5},{7,4},{8,11},{9,10},{10,... | collective-permute-start | bytes 196616 | tf_op jit(solution)/shard_map/ppermute | solution.py:546
  19.8 5.6 %collective-permute-start.8 = (bf16[128,256]{1,0:T(8,128)(2,1)S(1)}, bf16[128,256]{1,0:T(8,128)(2,1)S(1)}, u32[]{:S(2)}, u32[]{:S(2)}) collective-permute-start(bf16[128,256]{1,0:T(8,128)(2,1)S(1)} %arrive.1.refs_7_), channel_id=1, source_target_pairs={{0,2},{1,3},{2,0},{3,1},{4,6},{5,7},{6,4},{7,5},{8,10},{9,11},{10,... | collective-permute-start | bytes 196616 | tf_op jit(solution)/shard_map/ppermute | solution.py:546
  22.0 11.4 %collective-permute-start.7 = (bf16[128,256]{1,0:T(8,128)(2,1)S(1)}, bf16[128,256]{1,0:T(8,128)(2,1)S(1)}, u32[]{:S(2)}, u32[]{:S(2)}) collective-permute-start(bf16[128,256]{1,0:T(8,128)(2,1)S(1)} %arrive.1.refs_7_), channel_id=1, source_target_pairs={{0,1},{1,0},{2,3},{3,2},{4,5},{5,4},{6,7},{7,6},{8,9},{9,8},{10,11... | collective-permute-start | bytes 196616 | tf_op jit(solution)/shard_map/ppermute | solution.py:546
  32.0 7.1 %collective-permute-start.10 = (bf16[128,256]{1,0:T(8,128)(2,1)S(1)}, bf16[128,256]{1,0:T(8,128)(2,1)S(1)}, u32[]{:S(2)}, u32[]{:S(2)}) collective-permute-start(bf16[128,256]{1,0:T(8,128)(2,1)S(1)} %get-tuple-element.102), channel_id=1, source_target_pairs={{0,2},{1,3},{2,0},{3,1},{4,6},{5,7},{6,4},{7,5},{8,10},{9,11},{10,... | collective-permute-start | bytes 196616 | tf_op jit(solution)/shard_map/ppermute | solution.py:546
  33.3 5.8 %collective-permute-start.11 = (bf16[128,256]{1,0:T(8,128)(2,1)S(1)}, bf16[128,256]{1,0:T(8,128)(2,1)S(1)}, u32[]{:S(2)}, u32[]{:S(2)}) collective-permute-start(bf16[128,256]{1,0:T(8,128)(2,1)S(1)} %get-tuple-element.103), channel_id=1, source_target_pairs={{0,3},{1,2},{2,1},{3,0},{4,7},{5,6},{6,5},{7,4},{8,11},{9,10},{10,... | collective-permute-start | bytes 196616 | tf_op jit(solution)/shard_map/ppermute | solution.py:546
  36.7 2.6 %collective-permute-start.12 = (bf16[128,256]{1,0:T(8,128)(2,1)S(1)}, bf16[128,256]{1,0:T(8,128)(2,1)S(1)}, u32[]{:S(2)}, u32[]{:S(2)}) collective-permute-start(bf16[128,256]{1,0:T(8,128)(2,1)S(1)} %get-tuple-element.104), channel_id=1, source_target_pairs={{0,1},{1,0},{2,3},{3,2},{4,5},{5,4},{6,7},{7,6},{8,9},{9,8},{10,11... | collective-permute-start | bytes 196616 | tf_op jit(solution)/shard_map/ppermute | solution.py:546
  36.7 18.2 %collective-permute-start.16 = (bf16[4,128,256]{2,1,0:T(8,128)(2,1)S(1)}, bf16[4,128,256]{2,1,0:T(8,128)(2,1)S(1)}, u32[]{:S(2)}, u32[]{:S(2)}) collective-permute-start(bf16[4,128,256]{2,1,0:T(8,128)(2,1)S(1)} %get-tuple-element.113), channel_id=1, source_target_pairs={{1,0},{2,1},{3,2},{5,4},{6,5},{7,6},{9,8},{10,9},{11,10},{13,12},{... | collective-permute-start | bytes 786440 | tf_op jit(solution)/shard_map/ppermute | solution.py:32
  39.5 7.0 %collective-permute-start.15 = (bf16[128,256]{1,0:T(8,128)(2,1)S(1)}, bf16[128,256]{1,0:T(8,128)(2,1)S(1)}, u32[]{:S(2)}, u32[]{:S(2)}) collective-permute-start(bf16[128,256]{1,0:T(8,128)(2,1)S(1)} %gather.3.here_ref), channel_id=1, source_target_pairs={{0,20},{4,24},{8,28},{12,0},{16,4},{20,8},{24,12},{28,16},{1,21},{... | collective-permute-start | bytes 196616 | tf_op jit(solution)/shard_map/ppermute | solution.py:37
  40.4 6.2 %collective-permute-start.14 = (bf16[128,256]{1,0:T(8,128)(2,1)S(1)}, bf16[128,256]{1,0:T(8,128)(2,1)S(1)}, u32[]{:S(2)}, u32[]{:S(2)}) collective-permute-start(bf16[128,256]{1,0:T(8,128)(2,1)S(1)} %gather.3.here_ref), channel_id=1, source_target_pairs={{0,24},{4,28},{8,0},{12,4},{16,8},{20,12},{24,16},{28,20},{1,25},{... | collective-permute-start | bytes 196616 | tf_op jit(solution)/shard_map/ppermute | solution.py:37
  43.7 4.7 %collective-permute-start.13 = (bf16[128,256]{1,0:T(8,128)(2,1)S(1)}, bf16[128,256]{1,0:T(8,128)(2,1)S(1)}, u32[]{:S(2)}, u32[]{:S(2)}) collective-permute-start(bf16[128,256]{1,0:T(8,128)(2,1)S(1)} %gather.3.here_ref), channel_id=1, source_target_pairs={{0,28},{4,0},{8,4},{12,8},{16,12},{20,16},{24,20},{28,24},{1,29},{... | collective-permute-start | bytes 196616 | tf_op jit(solution)/shard_map/ppermute | solution.py:37
  48.8 6.1 %collective-permute-start.18 = (bf16[256,256]{1,0:T(8,128)(2,1)S(1)}, bf16[256,256]{1,0:T(8,128)(2,1)S(1)}, u32[]{:S(2)}, u32[]{:S(2)}) collective-permute-start(bf16[256,256]{1,0:T(8,128)(2,1)S(1)} %get-tuple-element.116), channel_id=1, source_target_pairs={{0,2},{1,3},{2,0},{3,1},{4,6},{5,7},{6,4},{7,5},{8,10},{9,11},{10,... | collective-permute-start | bytes 393224 | tf_op jit(solution)/shard_map/ppermute | solution.py:546
  49.1 8.0 %collective-permute-start.19 = (bf16[256,256]{1,0:T(8,128)(2,1)S(1)}, bf16[256,256]{1,0:T(8,128)(2,1)S(1)}, u32[]{:S(2)}, u32[]{:S(2)}) collective-permute-start(bf16[256,256]{1,0:T(8,128)(2,1)S(1)} %get-tuple-element.117), channel_id=1, source_target_pairs={{0,3},{1,2},{2,1},{3,0},{4,7},{5,6},{6,5},{7,4},{8,11},{9,10},{10,... | collective-permute-start | bytes 393224 | tf_op jit(solution)/shard_map/ppermute | solution.py:546
  51.3 5.8 %collective-permute-start.20 = (bf16[256,256]{1,0:T(8,128)(2,1)S(1)}, bf16[256,256]{1,0:T(8,128)(2,1)S(1)}, u32[]{:S(2)}, u32[]{:S(2)}) collective-permute-start(bf16[256,256]{1,0:T(8,128)(2,1)S(1)} %get-tuple-element.118), channel_id=1, source_target_pairs={{0,1},{1,0},{2,3},{3,2},{4,5},{5,4},{6,7},{7,6},{8,9},{9,8},{10,11... | collective-permute-start | bytes 393224 | tf_op jit(solution)/shard_map/ppermute | solution.py:546
  51.6 3.4 %collective-permute-start.17 = (f32[8,128]{1,0:T(8,128)S(1)}, f32[8,128]{1,0:T(8,128)S(1)}, u32[]{:S(2)}, u32[]{:S(2)}) collective-permute-start(f32[8,128]{1,0:T(8,128)S(1)} %get-tuple-element.111.sink_ref), channel_id=1, source_target_pairs={{0,16},{4,20},{8,24},{12,28},{16,0},{20,4},{24,8},{28,12},{1,17},{... | collective-permute-start | bytes 12296 | tf_op jit(solution)/shard_map/ppermute | solution.py:37

commit v14 on v12

--- a/solution.py
+++ b/solution.py
@@ -427,12 +427,12 @@
         ahead, parts = products(0), []
         for index in range(len(items)):
             now = ahead
-            weigh(index, 0, *now[0])
             if index + 1 < len(items):
                 ahead = products(index + 1)
-            weigh(index, 1, *now[1])
+            weigh(index, 0, *now[0])
             if index >= 1:
                 finish(index - 1)
+            weigh(index, 1, *now[1])
             parts.append(reduce(index))
         finish(len(items) - 1)
         grads = [

time: 59.3 us -> 60.1 us (1.013)
  starting transfers between devices: 30.8 us -> 24.8 us
  Pallas kernels: 16.7 us -> 22.6 us
    ppermute x6, starting transfers between devices: 10.9 us -> 4.98 us  [trade(): lax.ppermute(values[bits], axis, [(place, place ^ bits) for place in plac...]
    pallas_call x3, Pallas kernels: 7.46 us -> 13.4 us  [attend(): pl.pallas_call(functools.partial(attend_kernel, blocks_here, head_count,...]
    ppermute x13, waiting for transfers between devices: 9.76 us -> 10.7 us  [ring(): lax.ppermute(value, axis, [(source, (source + steps) % count) for source...]
  transfers between devices with their start and end apart: 21 -> 21, of which waited for: 10 -> 9; matrix products, arithmetic and copies ran while one was open for 0% -> 0% of each run, Pallas kernels for 25% -> 35%
where the time goes in v14:
time: 60.1 us; the launch traced here: 58.9 us
  starting transfers between devices  24.8 us (41%)
  Pallas kernels  22.6 us (38%)
  waiting for transfers between devices  10.7 us (18%)
  between operations  0.79 us (1%)
    ppermute x13, starting transfers between devices, ring(): lax.ppermute(value, axis, [(source, (source + steps) % count) for source...  14.1 us
    pallas_call x3, Pallas kernels, attend(): pl.pallas_call(functools.partial(attend_kernel, blocks_here, head_count,...  13.4 us
    ppermute x13, waiting for transfers between devices, ring(): lax.ppermute(value, axis, [(source, (source + steps) % count) for source...  10.7 us
    ppermute x2, starting transfers between devices, shift(): lax.ppermute(value, axis, [(source, source + steps) for source in range(l...  5.79 us
    ppermute x6, starting transfers between devices, trade(): lax.ppermute(values[bits], axis, [(place, place ^ bits) for place in plac...  4.98 us
    pallas_call x2, Pallas kernels, flush(): pl.pallas_call(stage_kernel, out_shape=pltpu.HBM(value.shape, BF16), in_s...  2.65 us
    pallas_call x1, Pallas kernels, local(): pl.pallas_call(stage_kernel, out_shape=(pltpu.VMEM(queries.shape, BF16),)...  2.26 us
  transfers between devices with their start and end apart: 21, of which 9 were waited for; matrix products, arithmetic and copies ran while one was open for 0% of the time, Pallas kernels for 35%

profile of v14, /device:TPU:3, one launch (start us, length us, event | category | flops | bytes accessed | tf_op | source)
XLA Modules:
  0.0 58.9 jit_solution(3769502225712269455)
XLA Ops:
  0.6 1.2 %pack.1 = (bf16[256,256]{1,0:T(8,128)(2,1)S(1)}, bf16[256,256]{1,0:T(8,128)(2,1)S(1)}, bf16[256,256]{1,0:T(8,128)(2,1)S(1)}, bf16[256,256]{1,0:T(8,128)(2,1)S(1)...) custom-call(f32[16]{0:T(128)} %sink_hbm.1, ...), custom_call_target="tpu_custom_call" | custom-call | tf_op jit(solution)/shard_map/pack/pallas_call | solution.py:570
  1.8 1.9 %collective-permute-start = (bf16[256,256]{1,0:T(8,128)(2,1)S(1)}, bf16[256,256]{1,0:T(8,128)(2,1)S(1)}, u32[]{:S(2)}, u32[]{:S(2)}) collective-permute-start(bf16[256,256]{1,0:T(8,128)(2,1)S(1)} %get-tuple-element.65), channel_id=1, source_target_pairs={{0,1},{1,2},{2,3},{3,0},{4,5},{5,6},{6,7},{7,4},{8,9},{9,10},{10,1... | collective-permute-start | bytes 393224 | tf_op jit(solution)/shard_map/ppermute | solution.py:37
  4.1 3.4 %collective-permute-start.6 = (bf16[4,128,256]{2,1,0:T(8,128)(2,1)S(1)}, bf16[4,128,256]{2,1,0:T(8,128)(2,1)S(1)}, u32[]{:S(2)}, u32[]{:S(2)}) collective-permute-start(bf16[4,128,256]{2,1,0:T(8,128)(2,1)S(1)} %get-tuple-element.86), channel_id=1, source_target_pairs={{0,1},{1,2},{2,3},{4,5},{5,6},{6,7},{8,9},{9,10},{10,11},{12,13},{... | collective-permute-start | bytes 786440 | tf_op jit(solution)/shard_map/ppermute | solution.py:32
  8.3 1.5 %collective-permute-done.1.refs_2_ = bf16[256,256]{1,0:T(8,128)(2,1)S(1)} collective-permute-done((bf16[256,256]{1,0:T(8,128)(2,1)S(1)}, bf16[256,256]{1,0:T(8,128)(2,1)S(1)}, u32[]{:S(2)}, u32[]{:S(2)}) %collective-permute-start.1) | collective-permute-done | bytes 131104 | tf_op jit(solution)/shard_map/ppermute | solution.py:37
  10.9 2.3 %collective-permute-start.3 = (bf16[128,256]{1,0:T(8,128)(2,1)S(1)}, bf16[128,256]{1,0:T(8,128)(2,1)S(1)}, u32[]{:S(2)}, u32[]{:S(2)}) collective-permute-start(bf16[128,256]{1,0:T(8,128)(2,1)S(1)} %get-tuple-element.75), channel_id=1, source_target_pairs={{0,12},{4,16},{8,20},{12,24},{16,28},{20,0},{24,4},{28,8},{1,13},{... | collective-permute-start | bytes 196616 | tf_op jit(solution)/shard_map/ppermute | solution.py:37
  13.2 1.3 %collective-permute-start.4 = (bf16[128,256]{1,0:T(8,128)(2,1)S(1)}, bf16[128,256]{1,0:T(8,128)(2,1)S(1)}, u32[]{:S(2)}, u32[]{:S(2)}) collective-permute-start(bf16[128,256]{1,0:T(8,128)(2,1)S(1)} %get-tuple-element.76), channel_id=1, source_target_pairs={{0,8},{4,12},{8,16},{12,20},{16,24},{20,28},{24,0},{28,4},{1,9},{5... | collective-permute-start | bytes 196616 | tf_op jit(solution)/shard_map/ppermute | solution.py:37
  14.5 1.2 %collective-permute-start.5 = (bf16[128,256]{1,0:T(8,128)(2,1)S(1)}, bf16[128,256]{1,0:T(8,128)(2,1)S(1)}, u32[]{:S(2)}, u32[]{:S(2)}) collective-permute-start(bf16[128,256]{1,0:T(8,128)(2,1)S(1)} %get-tuple-element.77), channel_id=1, source_target_pairs={{0,4},{4,8},{8,12},{12,16},{16,20},{20,24},{24,28},{28,0},{1,5},{5... | collective-permute-start | bytes 196616 | tf_op jit(solution)/shard_map/ppermute | solution.py:37
  15.9 2.3 %stage.1 = (bf16[256,4096]{1,0:T(8,128)(2,1)S(1)}, bf16[256,4096]{1,0:T(8,128)(2,1)S(1)}) custom-call(bf16[256,4096]{1,0:T(8,128)(2,1)} %refs_0_, bf16[256,4096]{1,0:T(8,128)(2,1)} %refs_1_), custom_call_target="tpu_custom_call" | custom-call | tf_op jit(solution)/shard_map/stage/pallas_call | solution.py:615
  18.4 1.4 %collective-permute-start.9 = (bf16[128,256]{1,0:T(8,128)(2,1)S(1)}, bf16[128,256]{1,0:T(8,128)(2,1)S(1)}, u32[]{:S(2)}, u32[]{:S(2)}) collective-permute-start(bf16[128,256]{1,0:T(8,128)(2,1)S(1)} %arrive.1.refs_7_), channel_id=1, source_target_pairs={{0,3},{1,2},{2,1},{3,0},{4,7},{5,6},{6,5},{7,4},{8,11},{9,10},{10,... | collective-permute-start | bytes 196616 | tf_op jit(solution)/shard_map/ppermute | solution.py:546
  19.8 2.2 %collective-permute-start.8 = (bf16[128,256]{1,0:T(8,128)(2,1)S(1)}, bf16[128,256]{1,0:T(8,128)(2,1)S(1)}, u32[]{:S(2)}, u32[]{:S(2)}) collective-permute-start(bf16[128,256]{1,0:T(8,128)(2,1)S(1)} %arrive.1.refs_7_), channel_id=1, source_target_pairs={{0,2},{1,3},{2,0},{3,1},{4,6},{5,7},{6,4},{7,5},{8,10},{9,11},{10,... | collective-permute-start | bytes 196616 | tf_op jit(solution)/shard_map/ppermute | solution.py:546
  22.0 3.4 %attend.3 = (bf16[256,4096]{1,0:T(8,128)(2,1)S(1)}, bf16[256,4096]{1,0:T(8,128)(2,1)S(1)}, f32[256,512]{1,0:T(8,128)S(1)}, f32[256,512]{1,0:T(8,128)S(1)}, bf16[...) custom-call(s32[8,128]{1,0:T(8,128)S(1)} %plan.1.plan_ref.refs_0_, f32[64,128]{1,0:T(8,128)S(1)} %sinks.1.refs_1_, ...), custom_call_target="tpu_custom_call" | custom-call | tf_op jit(solution)/shard_map/attend/pallas_call | solution.py:649
  25.4 6.6 %attend.4 = (bf16[256,4096]{1,0:T(8,128)(2,1)S(1)}, bf16[256,4096]{1,0:T(8,128)(2,1)S(1)}, f32[256,512]{1,0:T(8,128)S(1)}, f32[256,512]{1,0:T(8,128)S(1)}, bf16[...) custom-call(s32[8,128]{1,0:T(8,128)S(1)} %plan.1.plan_ref.refs_0_, ...), custom_call_target="tpu_custom_call", output_to_operand_aliasing={{0}: (9, {}), {1}: (10, {}), {2}: (11, {}), {3}: (12, {}), ... | custom-call | tf_op jit(solution)/shard_map/attend/pallas_call | solution.py:649
  32.0 1.3 %collective-permute-start.10 = (bf16[128,256]{1,0:T(8,128)(2,1)S(1)}, bf16[128,256]{1,0:T(8,128)(2,1)S(1)}, u32[]{:S(2)}, u32[]{:S(2)}) collective-permute-start(bf16[128,256]{1,0:T(8,128)(2,1)S(1)} %get-tuple-element.102), channel_id=1, source_target_pairs={{0,2},{1,3},{2,0},{3,1},{4,6},{5,7},{6,4},{7,5},{8,10},{9,11},{10,... | collective-permute-start | bytes 196616 | tf_op jit(solution)/shard_map/ppermute | solution.py:546
  33.3 3.4 %attend.5 = (bf16[256,4096]{1,0:T(8,128)(2,1)S(1)}, bf16[256,4096]{1,0:T(8,128)(2,1)S(1)}, f32[256,512]{1,0:T(8,128)S(1)}, f32[256,512]{1,0:T(8,128)S(1)}, bf16[...) custom-call(s32[8,128]{1,0:T(8,128)S(1)} %plan.1.plan_ref.refs_0_, ...), custom_call_target="tpu_custom_call", output_to_operand_aliasing={{0}: (8, {}), {1}: (9, {}), {2}: (10, {}), {3}: (11, {}), {... | custom-call | tf_op jit(solution)/shard_map/attend/pallas_call | solution.py:649
  36.7 2.4 %collective-permute-start.16 = (bf16[4,128,256]{2,1,0:T(8,128)(2,1)S(1)}, bf16[4,128,256]{2,1,0:T(8,128)(2,1)S(1)}, u32[]{:S(2)}, u32[]{:S(2)}) collective-permute-start(bf16[4,128,256]{2,1,0:T(8,128)(2,1)S(1)} %get-tuple-element.113), channel_id=1, source_target_pairs={{1,0},{2,1},{3,2},{5,4},{6,5},{7,6},{9,8},{10,9},{11,10},{13,12},{... | collective-permute-start | bytes 786440 | tf_op jit(solution)/shard_map/ppermute | solution.py:32
  39.5 3.9 %collective-permute-start.15 = (bf16[128,256]{1,0:T(8,128)(2,1)S(1)}, bf16[128,256]{1,0:T(8,128)(2,1)S(1)}, u32[]{:S(2)}, u32[]{:S(2)}) collective-permute-start(bf16[128,256]{1,0:T(8,128)(2,1)S(1)} %gather.3.here_ref), channel_id=1, source_target_pairs={{0,20},{4,24},{8,28},{12,0},{16,4},{20,8},{24,12},{28,16},{1,21},{... | collective-permute-start | bytes 196616 | tf_op jit(solution)/shard_map/ppermute | solution.py:37
  43.9 1.3 %flush.2 = bf16[256,4096]{1,0:T(8,128)(2,1)} custom-call(bf16[256,4096]{1,0:T(8,128)(2,1)S(1)} %get-tuple-element.105.refs_0_), custom_call_target="tpu_custom_call" | custom-call | tf_op jit(solution)/shard_map/flush/pallas_call | solution.py:705
  45.2 1.3 %collective-permute-done.15.refs_2_ = bf16[128,256]{1,0:T(8,128)(2,1)S(1)} collective-permute-done((bf16[128,256]{1,0:T(8,128)(2,1)S(1)}, bf16[128,256]{1,0:T(8,128)(2,1)S(1)}, u32[]{:S(2)}, u32[]{:S(2)}) %collective-permute-start.15) | collective-permute-done | bytes 65568 | tf_op jit(solution)/shard_map/ppermute | solution.py:37
  47.4 1.6 %collective-permute-done.13.refs_0_ = bf16[128,256]{1,0:T(8,128)(2,1)S(1)} collective-permute-done((bf16[128,256]{1,0:T(8,128)(2,1)S(1)}, bf16[128,256]{1,0:T(8,128)(2,1)S(1)}, u32[]{:S(2)}, u32[]{:S(2)}) %collective-permute-start.13) | collective-permute-done | bytes 65568 | tf_op jit(solution)/shard_map/ppermute | solution.py:37
  49.5 2.0 %collective-permute-start.18 = (bf16[256,256]{1,0:T(8,128)(2,1)S(1)}, bf16[256,256]{1,0:T(8,128)(2,1)S(1)}, u32[]{:S(2)}, u32[]{:S(2)}) collective-permute-start(bf16[256,256]{1,0:T(8,128)(2,1)S(1)} %get-tuple-element.117), channel_id=1, source_target_pairs={{0,1},{1,2},{2,3},{3,0},{4,5},{5,6},{6,7},{7,4},{8,9},{9,10},{10,1... | collective-permute-start | bytes 393224 | tf_op jit(solution)/shard_map/ppermute | solution.py:37
  52.0 1.3 %flush.3 = bf16[256,4096]{1,0:T(8,128)(2,1)} custom-call(bf16[256,4096]{1,0:T(8,128)(2,1)S(1)} %get-tuple-element.112.refs_0_), custom_call_target="tpu_custom_call" | custom-call | tf_op jit(solution)/shard_map/flush/pallas_call | solution.py:705
  53.3 2.0 %collective-permute-done.17.far_ref = f32[8,128]{1,0:T(8,128)S(1)} collective-permute-done((f32[8,128]{1,0:T(8,128)S(1)}, f32[8,128]{1,0:T(8,128)S(1)}, u32[]{:S(2)}, u32[]{:S(2)}) %collective-permute-start.17) | collective-permute-done | bytes 4128 | tf_op jit(solution)/shard_map/ppermute | solution.py:37
  55.3 2.1 %collective-permute-done.19.refs_2_ = bf16[256,256]{1,0:T(8,128)(2,1)S(1)} collective-permute-done((bf16[256,256]{1,0:T(8,128)(2,1)S(1)}, bf16[256,256]{1,0:T(8,128)(2,1)S(1)}, u32[]{:S(2)}, u32[]{:S(2)}) %collective-permute-start.19) | collective-permute-done | bytes 131104 | tf_op jit(solution)/shard_map/ppermute | solution.py:37
  58.0 0.9 %total.1 = (bf16[256,512]{1,0:T(8,128)(2,1)}, bf16[256,512]{1,0:T(8,128)(2,1)}, f32[16]{0:T(128)}) custom-call(bf16[4,128,256]{2,1,0:T(8,128)(2,1)S(1)} %collective-permute-done.16.halo_ref, f32[256,512]{1,0:T(8,128)S(1)} %get-tuple-element.114.dk_ref, f32[256,512]{1,0:T(8,128)S(1)} %get-tuple-element.115.dv_ref, f32[8,128]{1,0:T(8,128)S(1)} %get-tuple-element.111.sink_ref, ...), custom_call_target="tpu_custom_call" | custom-call | tf_op jit(solution)/shard_map/total/pallas_call | solution.py:736
  (33 shorter events, 5.7 us)
Async XLA Ops:
  1.8 6.5 %collective-permute-start = (bf16[256,256]{1,0:T(8,128)(2,1)S(1)}, bf16[256,256]{1,0:T(8,128)(2,1)S(1)}, u32[]{:S(2)}, u32[]{:S(2)}) collective-permute-start(bf16[256,256]{1,0:T(8,128)(2,1)S(1)} %get-tuple-element.65), channel_id=1, source_target_pairs={{0,1},{1,2},{2,3},{3,0},{4,5},{5,6},{6,7},{7,4},{8,9},{9,10},{10,1... | collective-permute-start | bytes 393224 | tf_op jit(solution)/shard_map/ppermute | solution.py:37
  3.7 6.2 %collective-permute-start.1 = (bf16[256,256]{1,0:T(8,128)(2,1)S(1)}, bf16[256,256]{1,0:T(8,128)(2,1)S(1)}, u32[]{:S(2)}, u32[]{:S(2)}) collective-permute-start(bf16[256,256]{1,0:T(8,128)(2,1)S(1)} %get-tuple-element.66), channel_id=1, source_target_pairs={{0,2},{1,3},{2,0},{3,1},{4,6},{5,7},{6,4},{7,5},{8,10},{9,11},{10,... | collective-permute-start | bytes 393224 | tf_op jit(solution)/shard_map/ppermute | solution.py:37
  3.9 6.6 %collective-permute-start.2 = (bf16[256,256]{1,0:T(8,128)(2,1)S(1)}, bf16[256,256]{1,0:T(8,128)(2,1)S(1)}, u32[]{:S(2)}, u32[]{:S(2)}) collective-permute-start(bf16[256,256]{1,0:T(8,128)(2,1)S(1)} %get-tuple-element.67), channel_id=1, source_target_pairs={{0,3},{1,0},{2,1},{3,2},{4,7},{5,4},{6,5},{7,6},{8,11},{9,8},{10,9... | collective-permute-start | bytes 393224 | tf_op jit(solution)/shard_map/ppermute | solution.py:37
  4.1 21.2 %collective-permute-start.6 = (bf16[4,128,256]{2,1,0:T(8,128)(2,1)S(1)}, bf16[4,128,256]{2,1,0:T(8,128)(2,1)S(1)}, u32[]{:S(2)}, u32[]{:S(2)}) collective-permute-start(bf16[4,128,256]{2,1,0:T(8,128)(2,1)S(1)} %get-tuple-element.86), channel_id=1, source_target_pairs={{0,1},{1,2},{2,3},{4,5},{5,6},{6,7},{8,9},{9,10},{10,11},{12,13},{... | collective-permute-start | bytes 786440 | tf_op jit(solution)/shard_map/ppermute | solution.py:32
  10.9 7.3 %collective-permute-start.3 = (bf16[128,256]{1,0:T(8,128)(2,1)S(1)}, bf16[128,256]{1,0:T(8,128)(2,1)S(1)}, u32[]{:S(2)}, u32[]{:S(2)}) collective-permute-start(bf16[128,256]{1,0:T(8,128)(2,1)S(1)} %get-tuple-element.75), channel_id=1, source_target_pairs={{0,12},{4,16},{8,20},{12,24},{16,28},{20,0},{24,4},{28,8},{1,13},{... | collective-permute-start | bytes 196616 | tf_op jit(solution)/shard_map/ppermute | solution.py:37
  13.2 4.9 %collective-permute-start.4 = (bf16[128,256]{1,0:T(8,128)(2,1)S(1)}, bf16[128,256]{1,0:T(8,128)(2,1)S(1)}, u32[]{:S(2)}, u32[]{:S(2)}) collective-permute-start(bf16[128,256]{1,0:T(8,128)(2,1)S(1)} %get-tuple-element.76), channel_id=1, source_target_pairs={{0,8},{4,12},{8,16},{12,20},{16,24},{20,28},{24,0},{28,4},{1,9},{5... | collective-permute-start | bytes 196616 | tf_op jit(solution)/shard_map/ppermute | solution.py:37
  14.5 3.7 %collective-permute-start.5 = (bf16[128,256]{1,0:T(8,128)(2,1)S(1)}, bf16[128,256]{1,0:T(8,128)(2,1)S(1)}, u32[]{:S(2)}, u32[]{:S(2)}) collective-permute-start(bf16[128,256]{1,0:T(8,128)(2,1)S(1)} %get-tuple-element.77), channel_id=1, source_target_pairs={{0,4},{4,8},{8,12},{12,16},{16,20},{20,24},{24,28},{28,0},{1,5},{5... | collective-permute-start | bytes 196616 | tf_op jit(solution)/shard_map/ppermute | solution.py:37
  18.4 7.0 %collective-permute-start.9 = (bf16[128,256]{1,0:T(8,128)(2,1)S(1)}, bf16[128,256]{1,0:T(8,128)(2,1)S(1)}, u32[]{:S(2)}, u32[]{:S(2)}) collective-permute-start(bf16[128,256]{1,0:T(8,128)(2,1)S(1)} %arrive.1.refs_7_), channel_id=1, source_target_pairs={{0,3},{1,2},{2,1},{3,0},{4,7},{5,6},{6,5},{7,4},{8,11},{9,10},{10,... | collective-permute-start | bytes 196616 | tf_op jit(solution)/shard_map/ppermute | solution.py:546
  19.8 5.6 %collective-permute-start.8 = (bf16[128,256]{1,0:T(8,128)(2,1)S(1)}, bf16[128,256]{1,0:T(8,128)(2,1)S(1)}, u32[]{:S(2)}, u32[]{:S(2)}) collective-permute-start(bf16[128,256]{1,0:T(8,128)(2,1)S(1)} %arrive.1.refs_7_), channel_id=1, source_target_pairs={{0,2},{1,3},{2,0},{3,1},{4,6},{5,7},{6,4},{7,5},{8,10},{9,11},{10,... | collective-permute-start | bytes 196616 | tf_op jit(solution)/shard_map/ppermute | solution.py:546
  22.0 11.4 %collective-permute-start.7 = (bf16[128,256]{1,0:T(8,128)(2,1)S(1)}, bf16[128,256]{1,0:T(8,128)(2,1)S(1)}, u32[]{:S(2)}, u32[]{:S(2)}) collective-permute-start(bf16[128,256]{1,0:T(8,128)(2,1)S(1)} %arrive.1.refs_7_), channel_id=1, source_target_pairs={{0,1},{1,0},{2,3},{3,2},{4,5},{5,4},{6,7},{7,6},{8,9},{9,8},{10,11... | collective-permute-start | bytes 196616 | tf_op jit(solution)/shard_map/ppermute | solution.py:546
  32.0 7.1 %collective-permute-start.10 = (bf16[128,256]{1,0:T(8,128)(2,1)S(1)}, bf16[128,256]{1,0:T(8,128)(2,1)S(1)}, u32[]{:S(2)}, u32[]{:S(2)}) collective-permute-start(bf16[128,256]{1,0:T(8,128)(2,1)S(1)} %get-tuple-element.102), channel_id=1, source_target_pairs={{0,2},{1,3},{2,0},{3,1},{4,6},{5,7},{6,4},{7,5},{8,10},{9,11},{10,... | collective-permute-start | bytes 196616 | tf_op jit(solution)/shard_map/ppermute | solution.py:546
  33.3 5.8 %collective-permute-start.11 = (bf16[128,256]{1,0:T(8,128)(2,1)S(1)}, bf16[128,256]{1,0:T(8,128)(2,1)S(1)}, u32[]{:S(2)}, u32[]{:S(2)}) collective-permute-start(bf16[128,256]{1,0:T(8,128)(2,1)S(1)} %get-tuple-element.103), channel_id=1, source_target_pairs={{0,3},{1,2},{2,1},{3,0},{4,7},{5,6},{6,5},{7,4},{8,11},{9,10},{10,... | collective-permute-start | bytes 196616 | tf_op jit(solution)/shard_map/ppermute | solution.py:546
  36.7 2.6 %collective-permute-start.12 = (bf16[128,256]{1,0:T(8,128)(2,1)S(1)}, bf16[128,256]{1,0:T(8,128)(2,1)S(1)}, u32[]{:S(2)}, u32[]{:S(2)}) collective-permute-start(bf16[128,256]{1,0:T(8,128)(2,1)S(1)} %get-tuple-element.104), channel_id=1, source_target_pairs={{0,1},{1,0},{2,3},{3,2},{4,5},{5,4},{6,7},{7,6},{8,9},{9,8},{10,11... | collective-permute-start | bytes 196616 | tf_op jit(solution)/shard_map/ppermute | solution.py:546
  36.7 18.6 %collective-permute-start.16 = (bf16[4,128,256]{2,1,0:T(8,128)(2,1)S(1)}, bf16[4,128,256]{2,1,0:T(8,128)(2,1)S(1)}, u32[]{:S(2)}, u32[]{:S(2)}) collective-permute-start(bf16[4,128,256]{2,1,0:T(8,128)(2,1)S(1)} %get-tuple-element.113), channel_id=1, source_target_pairs={{1,0},{2,1},{3,2},{5,4},{6,5},{7,6},{9,8},{10,9},{11,10},{13,12},{... | collective-permute-start | bytes 786440 | tf_op jit(solution)/shard_map/ppermute | solution.py:32
  39.5 7.0 %collective-permute-start.15 = (bf16[128,256]{1,0:T(8,128)(2,1)S(1)}, bf16[128,256]{1,0:T(8,128)(2,1)S(1)}, u32[]{:S(2)}, u32[]{:S(2)}) collective-permute-start(bf16[128,256]{1,0:T(8,128)(2,1)S(1)} %gather.3.here_ref), channel_id=1, source_target_pairs={{0,20},{4,24},{8,28},{12,0},{16,4},{20,8},{24,12},{28,16},{1,21},{... | collective-permute-start | bytes 196616 | tf_op jit(solution)/shard_map/ppermute | solution.py:37
  43.4 4.0 %collective-permute-start.14 = (bf16[128,256]{1,0:T(8,128)(2,1)S(1)}, bf16[128,256]{1,0:T(8,128)(2,1)S(1)}, u32[]{:S(2)}, u32[]{:S(2)}) collective-permute-start(bf16[128,256]{1,0:T(8,128)(2,1)S(1)} %gather.3.here_ref), channel_id=1, source_target_pairs={{0,24},{4,28},{8,0},{12,4},{16,8},{20,12},{24,16},{28,20},{1,25},{... | collective-permute-start | bytes 196616 | tf_op jit(solution)/shard_map/ppermute | solution.py:37
  43.8 5.2 %collective-permute-start.13 = (bf16[128,256]{1,0:T(8,128)(2,1)S(1)}, bf16[128,256]{1,0:T(8,128)(2,1)S(1)}, u32[]{:S(2)}, u32[]{:S(2)}) collective-permute-start(bf16[128,256]{1,0:T(8,128)(2,1)S(1)} %gather.3.here_ref), channel_id=1, source_target_pairs={{0,28},{4,0},{8,4},{12,8},{16,12},{20,16},{24,20},{28,24},{1,29},{... | collective-permute-start | bytes 196616 | tf_op jit(solution)/shard_map/ppermute | solution.py:37
  49.5 5.9 %collective-permute-start.18 = (bf16[256,256]{1,0:T(8,128)(2,1)S(1)}, bf16[256,256]{1,0:T(8,128)(2,1)S(1)}, u32[]{:S(2)}, u32[]{:S(2)}) collective-permute-start(bf16[256,256]{1,0:T(8,128)(2,1)S(1)} %get-tuple-element.117), channel_id=1, source_target_pairs={{0,1},{1,2},{2,3},{3,0},{4,5},{5,6},{6,7},{7,4},{8,9},{9,10},{10,1... | collective-permute-start | bytes 393224 | tf_op jit(solution)/shard_map/ppermute | solution.py:37
  51.5 6.0 %collective-permute-start.19 = (bf16[256,256]{1,0:T(8,128)(2,1)S(1)}, bf16[256,256]{1,0:T(8,128)(2,1)S(1)}, u32[]{:S(2)}, u32[]{:S(2)}) collective-permute-start(bf16[256,256]{1,0:T(8,128)(2,1)S(1)} %get-tuple-element.118), channel_id=1, source_target_pairs={{0,2},{1,3},{2,0},{3,1},{4,6},{5,7},{6,4},{7,5},{8,10},{9,11},{10,... | collective-permute-start | bytes 393224 | tf_op jit(solution)/shard_map/ppermute | solution.py:37
  51.5 6.5 %collective-permute-start.20 = (bf16[256,256]{1,0:T(8,128)(2,1)S(1)}, bf16[256,256]{1,0:T(8,128)(2,1)S(1)}, u32[]{:S(2)}, u32[]{:S(2)}) collective-permute-start(bf16[256,256]{1,0:T(8,128)(2,1)S(1)} %get-tuple-element.119), channel_id=1, source_target_pairs={{0,3},{1,0},{2,1},{3,2},{4,7},{5,4},{6,5},{7,6},{8,11},{9,8},{10,9... | collective-permute-start | bytes 393224 | tf_op jit(solution)/shard_map/ppermute | solution.py:37
  52.0 3.4 %collective-permute-start.17 = (f32[8,128]{1,0:T(8,128)S(1)}, f32[8,128]{1,0:T(8,128)S(1)}, u32[]{:S(2)}, u32[]{:S(2)}) collective-permute-start(f32[8,128]{1,0:T(8,128)S(1)} %get-tuple-element.111.sink_ref), channel_id=1, source_target_pairs={{0,16},{4,20},{8,24},{12,28},{16,0},{20,4},{24,8},{28,12},{1,17},{... | collective-permute-start | bytes 12296 | tf_op jit(solution)/shard_map/ppermute | solution.py:37
